TPU v7x, 32 devices: a whole 2x2x4 slice. The times are simulated.
32 devices in a mesh: groups: 2 (over y), ctx: 4 (over z), head: 4 (over x, core).
Axes of the slice: x: 2, y: 2, z: 4, core: 2. Of those that a mesh axis runs over, the one named last changes fastest.
Arguments:
- queries: bfloat16 [1024, 8192], P(('groups', 'ctx'), 'head'), parts along dimension 0, may hold values from -145 to 145
- stretch_keys: bfloat16 [1024, 1024], P(('groups', 'ctx'), 'head'), parts along dimension 0, may hold values from -4.5 to 4.5
- stretch_values: bfloat16 [1024, 1024], P(('groups', 'ctx'), 'head'), parts along dimension 0, may hold values from -4 to 4
- cache_keys: bfloat16 [2048, 1024], P(('groups', 'ctx'), 'head'), parts along dimension 0, may hold values from -4 to 4
- cache_values: bfloat16 [2048, 1024], P(('groups', 'ctx'), 'head'), parts along dimension 0, may hold values from -4 to 4
- prefix_length: int32 [2], P('groups'), parts along dimension 0, may hold values from 256 to 1024
- page_targets: int32 [64], P('groups'), parts along dimension 0, may hold values from 0 to 31, as said below
- pool_keys: bfloat16 [1024, 16, 1024], P(('groups', 'ctx'), None, 'head'), parts along dimension 0, may hold values from -4.5 to 4.5
- pool_values: bfloat16 [1024, 16, 1024], P(('groups', 'ctx'), None, 'head'), parts along dimension 0, may hold values from -4 to 4
- decode_queries: bfloat16 [64, 8192], P(('groups', 'ctx'), 'head'), parts along dimension 0, may hold values from -145 to 145
- page_lists: int32 [64, 32], P(('groups', 'ctx')), parts along dimension 0, may hold values from 0 to 135, as said below
- context_length: int32 [64], P(('groups', 'ctx')), parts along dimension 0, may hold values from 32 to 512
Outputs:
- prefill_attention: bfloat16 [1024, 8192], P(('groups', 'ctx'), 'head'), parts along dimension 0
- decode_attention: bfloat16 [64, 8192], P(('groups', 'ctx'), 'head'), parts along dimension 0
There are 2 independent parts, one for each index of `groups`. A program takes and returns all parts, laid end to end along the dimension named above; each array names one. Nothing has to cross between parts.
Inputs may be any that keep to these rules, and one draw needn't show every extreme that they name: `page_targets`: targets are distinct; every owner receives exactly 8 new pages, and the 8 pages of one index of ctx go to owners 2 at a time, so that exactly 2 of them share each of their owners. `page_lists`: entry 0 of every row names one of the 128 held pages; entry 1 of row r names new slot 128 + (r % 8) % 8.
All inputs are finite; a program needn't handle non-finite values.
Results may differ from a plain program's by a relative error of at most 0.006.
Values may be sent and summed in bfloat16 or wider, within the bound.
No kernel may reach another device: no remote copies, remote signals or barrier semaphores. Data moves between devices by JAX's collectives and lax.ppermute only.
A program may use at most 64 MiB of HBM per device.

v0:
```python
import functools

import jax
import jax.numpy as jnp
from jax import lax
from jax.experimental import pallas as pl
from jax.experimental.pallas import tpu as pltpu
from jax.sharding import PartitionSpec as P

HEADS = 64
KV_HEADS = 8
HEAD_DIM = 128
GROUP = HEADS // KV_HEADS
PAGE = 16
P_DEV = 8
EXP2_SCALE = HEAD_DIM ** (-0.5) * 1.4426950408889634
HIDDEN = -1e30
VMEM_BYTES = 48 * 1024 * 1024

VMEM = pl.BlockSpec(memory_space=pltpu.VMEM)
SMEM = pl.BlockSpec(memory_space=pltpu.SMEM)


def attend(qt_ref, head, cols, keys, values_t, seen, state):
    scores = jnp.dot(keys, qt_ref[head, :, cols], preferred_element_type=jnp.float32)
    scores = jnp.where(seen, scores, jnp.float32(HIDDEN))
    high = jnp.max(scores, axis=0, keepdims=True)
    if state is not None:
        old_high, old_total, old_accum = state
        high = jnp.maximum(high, old_high)
    weights = jnp.exp2((scores - high) * EXP2_SCALE)
    total = jnp.sum(weights, axis=0, keepdims=True)
    accum = jnp.dot(values_t, weights.astype(jnp.bfloat16), preferred_element_type=jnp.float32)
    if state is not None:
        decay = jnp.exp2((old_high - high) * EXP2_SCALE)
        total = total + old_total * decay
        accum = accum + old_accum * decay
    return high, total, accum


def near_kernel(
    own_ref, limit_ref, q_ref, stretch_ref, cache_ref, qt_ref, high_ref, total_ref, accum_ref
):
    kv_local, _, rows = qt_ref.shape
    count, s_rows, _ = stretch_ref.shape
    s_rows = s_rows // 2
    c_rows = cache_ref.shape[0] // 2
    tokens = q_ref.shape[0]
    own = own_ref[0]
    for head in range(kv_local):
        for sub in range(GROUP):
            col = (head * GROUP + sub) * HEAD_DIM
            qt_ref[head, :, sub * tokens : (sub + 1) * tokens] = q_ref[:, col : col + HEAD_DIM].T
    width = min(2 * tokens, rows)
    keys_all = count * s_rows + c_rows
    place = lax.broadcasted_iota(jnp.int32, (keys_all, width), 0)
    token = lax.rem(lax.broadcasted_iota(jnp.int32, (keys_all, width), 1), tokens)
    held = place - count * s_rows
    seen = ((held < 0) & (place <= own * tokens + token)) | (
        (held >= 0) & (held < limit_ref[0] - own * c_rows)
    )
    for head in range(kv_local):
        feats = slice(head * HEAD_DIM, (head + 1) * HEAD_DIM)
        keys = jnp.concatenate(
            [stretch_ref[shard, :s_rows, feats] for shard in range(count)] + [cache_ref[:c_rows, feats]], axis=0
        )
        values = jnp.concatenate(
            [stretch_ref[shard, s_rows:, feats] for shard in range(count)] + [cache_ref[c_rows:, feats]], axis=0
        )
        values_t = values.T
        for start in range(0, rows, width):
            cols = slice(start, start + width)
            high, total, accum = attend(qt_ref, head, cols, keys, values_t, seen, None)
            high_ref[head, :, cols] = high
            total_ref[head, :, cols] = total
            accum_ref[head, :, cols] = accum


def far_kernel(count, own_ref, limit_ref, qt_ref, cache_ref, high_ref, total_ref, accum_ref, out_ref):
    kv_local, _, rows = qt_ref.shape
    c_rows = cache_ref.shape[1] // 2
    tokens = out_ref.shape[0]
    width = min(2 * tokens, rows)
    own = own_ref[0]
    limit = limit_ref[0]
    shards = [lax.rem(own + hop, count) for hop in range(1, count)]
    place = lax.broadcasted_iota(jnp.int32, (c_rows, width), 0)
    seen = jnp.concatenate([place < limit - shard * c_rows for shard in shards], axis=0)
    for head in range(kv_local):
        feats = slice(head * HEAD_DIM, (head + 1) * HEAD_DIM)
        keys = jnp.concatenate([cache_ref[shard, :c_rows, feats] for shard in shards], axis=0)
        values_t = jnp.concatenate([cache_ref[shard, c_rows:, feats] for shard in shards], axis=0).T
        for start in range(0, rows, width):
            cols = slice(start, start + width)
            state = (high_ref[head, :, cols], total_ref[head, :, cols], accum_ref[head, :, cols])
            _, total, accum = attend(qt_ref, head, cols, keys, values_t, seen, state)
            mixed = accum / total
            for piece in range(width // tokens):
                col = (head * GROUP + start // tokens + piece) * HEAD_DIM
                out_ref[:, col : col + HEAD_DIM] = (
                    mixed[:, piece * tokens : (piece + 1) * tokens].T.astype(jnp.bfloat16)
                )


def decode_kernel(slots_ref, q_ref, lists_ref, length_ref, pool_k, pool_v, stretch_ref, out_ref):
    rows, q_width = q_ref.shape
    heads = q_width // HEAD_DIM
    kv_local = heads // GROUP
    span = lists_ref.shape[1]
    lists = lists_ref[...]
    lengths = length_ref[...]

    queries = q_ref[...].astype(jnp.float32)
    stacked = []
    for head in range(heads):
        piece = queries[:, head * HEAD_DIM : (head + 1) * HEAD_DIM]
        blank = jnp.zeros_like(piece)
        stacked.append(
            jnp.concatenate([piece if kv == head // GROUP else blank for kv in range(kv_local)], axis=1)
        )
    wide_queries = jnp.concatenate(stacked, axis=0).astype(jnp.bfloat16)

    def copies(slot):
        tokens = slot.shape[1]
        offset = lax.rem(lax.broadcasted_iota(jnp.int32, (rows, tokens), 1), PAGE)
        tally = jnp.zeros((rows, tokens), jnp.float32)
        for entry in range(span):
            hit = (slot == lists[:, entry : entry + 1]) & (offset < lengths - entry * PAGE)
            tally = tally + jnp.where(hit, jnp.float32(1.0), jnp.float32(0.0))
        return tally

    parts = []

    def add_part(keys, values, slot):
        scores = lax.dot_general(
            wide_queries, keys, (((1,), (1,)), ((), ())), preferred_element_type=jnp.float32
        )
        tally = copies(slot)[None]
        scores = scores.reshape(heads, rows, -1)
        scores = jnp.where(tally > 0, scores, jnp.float32(HIDDEN))
        parts.append((scores, tally, values))

    held = pool_k.shape[0] * PAGE
    held_slot = lax.broadcasted_iota(jnp.int32, (rows, held), 1) // PAGE
    add_part(pool_k[...].reshape(held, -1), pool_v[...].reshape(held, -1), held_slot)
    count, s_rows, kv_width = stretch_ref.shape
    s_rows = s_rows // 2
    fresh = count * s_rows
    add_part(
        stretch_ref[:, :s_rows, :].reshape(fresh, kv_width),
        stretch_ref[:, s_rows:, :].reshape(fresh, kv_width),
        jnp.broadcast_to(slots_ref[...], (rows, fresh)),
    )

    high = functools.reduce(
        jnp.maximum, [jnp.max(scores, axis=-1, keepdims=True) for scores, _, _ in parts]
    )
    total = 0.0
    mixed = 0.0
    for scores, tally, values in parts:
        weights = jnp.exp2((scores - high) * EXP2_SCALE) * tally
        total = total + jnp.sum(weights, axis=-1, keepdims=True)
        mixed = mixed + jnp.dot(
            weights.reshape(heads * rows, -1).astype(jnp.bfloat16),
            values,
            preferred_element_type=jnp.float32,
        )
    for head in range(heads):
        kv = head // GROUP
        piece = mixed[head * rows : (head + 1) * rows, kv * HEAD_DIM : (kv + 1) * HEAD_DIM]
        out_ref[:, head * HEAD_DIM : (head + 1) * HEAD_DIM] = (piece / total[head]).astype(jnp.bfloat16)


def per_device(
    count,
    queries,
    stretch_keys,
    stretch_values,
    cache_keys,
    cache_values,
    prefix_length,
    page_targets,
    pool_keys,
    pool_values,
    decode_queries,
    page_lists,
    context_length,
):
    own = lax.axis_index("ctx")
    own_array = jnp.full((1,), own, jnp.int32)
    tokens, width = queries.shape
    kv_local = stretch_keys.shape[1] // HEAD_DIM
    rows = GROUP * tokens
    c_rows = cache_keys.shape[0]
    f32 = jnp.float32
    params = pltpu.CompilerParams(vmem_limit_bytes=VMEM_BYTES)

    own_c = jnp.concatenate([cache_keys, cache_values], axis=0)
    own_s = jnp.concatenate([stretch_keys, stretch_values], axis=0)
    all_c = lax.all_gather(own_c, "ctx", axis=0, tiled=True).reshape(count, 2 * c_rows, -1)
    all_s = lax.all_gather(own_s, "ctx", axis=0, tiled=True).reshape(count, 2 * tokens, -1)

    def cost(keys):
        pairs = kv_local * rows * keys
        return pl.CostEstimate(
            flops=4 * pairs * HEAD_DIM, bytes_accessed=4 * rows * kv_local * HEAD_DIM, transcendentals=pairs
        )

    qt, high, total, accum = pl.pallas_call(
        near_kernel,
        out_shape=(
            jax.ShapeDtypeStruct((kv_local, HEAD_DIM, rows), jnp.bfloat16),
            jax.ShapeDtypeStruct((kv_local, 1, rows), f32),
            jax.ShapeDtypeStruct((kv_local, 1, rows), f32),
            jax.ShapeDtypeStruct((kv_local, HEAD_DIM, rows), f32),
        ),
        in_specs=[SMEM, SMEM] + [VMEM] * 3,
        out_specs=(VMEM,) * 4,
        compiler_params=params,
        cost_estimate=cost(count * tokens + c_rows),
        name="stretch_and_own_cache",
    )(own_array, prefix_length, queries, all_s, own_c)

    slots = jnp.where(page_targets // P_DEV == own, pool_keys.shape[0] + page_targets % P_DEV, -1)
    slots = jnp.repeat(slots, PAGE).reshape(1, -1)
    decoded = pl.pallas_call(
        decode_kernel,
        out_shape=jax.ShapeDtypeStruct(decode_queries.shape, jnp.bfloat16),
        in_specs=[VMEM] * 7,
        out_specs=VMEM,
        compiler_params=params,
        cost_estimate=pl.CostEstimate(
            flops=4 * 128 * 2048 * 256, bytes_accessed=4 * pool_keys.size, transcendentals=128 * 2560
        ),
        name="decode_rows",
    )(
        slots, decode_queries, page_lists, context_length.reshape(-1, 1),
        pool_keys, pool_values, all_s,
    )

    prefill = pl.pallas_call(
        functools.partial(far_kernel, count),
        out_shape=jax.ShapeDtypeStruct((tokens, width), jnp.bfloat16),
        in_specs=[SMEM, SMEM] + [VMEM] * 5,
        out_specs=VMEM,
        compiler_params=params,
        cost_estimate=cost((count - 1) * c_rows),
        name="other_cache_shards",
    )(own_array, prefix_length, qt, all_c, high, total, accum)
    return (prefill, decoded)


def solution(mesh):
    in_specs = (
        P(("groups", "ctx"), "head"),
        P(("groups", "ctx"), "head"),
        P(("groups", "ctx"), "head"),
        P(("groups", "ctx"), "head"),
        P(("groups", "ctx"), "head"),
        P("groups"),
        P("groups"),
        P(("groups", "ctx"), None, "head"),
        P(("groups", "ctx"), None, "head"),
        P(("groups", "ctx"), "head"),
        P(("groups", "ctx"), None),
        P(("groups", "ctx")),
    )
    out_specs = (P(("groups", "ctx"), "head"), P(("groups", "ctx"), "head"))
    return jax.shard_map(
        functools.partial(per_device, mesh.shape["ctx"]),
        mesh=mesh,
        in_specs=in_specs,
        out_specs=out_specs,
        check_vma=False,
    )
```

profile of v0, /device:TPU:0, one launch (start us, length us, event | category | flops | bytes accessed | tf_op | source)
XLA Modules:
  0.0 58.0 jit_solution(4808285211954671108)
XLA Ops:
  7.2 0.0 copy-start.8
  7.2 0.0 copy-start.9
  7.2 0.0 copy-start.10
  7.2 0.0 all-gather.2.cloned.1.call-start
  7.3 1.0 %constant_dynamic-update-slice_fusion.1 = bf16[512,256]{1,0:T(8,128)(2,1)S(1)} fusion(bf16[256,256]{1,0:T(8,128)(2,1)} %param.15), kind=kLoop, calls=%fused_computation.2 | loop fusion | bytes 262144
  8.3 0.0 copy-done.8
  8.3 0.0 copy-start.3
  8.3 0.7 %copy-done.3 = bf16[512,256]{1,0:T(8,128)(2,1)} copy-done((bf16[512,256]{1,0:T(8,128)(2,1)}, bf16[512,256]{1,0:T(8,128)(2,1)S(1)}, u32[]{:S(2)}) %copy-start.3) | copy-done | bytes 262168
  9.0 0.0 all-gather.2.cloned.1.call-update
  9.7 0.7 %copy.15.length_ref = s32[8,1]{1,0:T(8,128)S(1)} copy(s32[8,1]{0,1:T(1,128)} %bitcast.7) | data formatting | bytes 64 | tf_op jit(solution)/shard_map/reshape | solution.py:237
  10.4 0.7 %compare_select_fusion = s32[32]{0:T(128)S(1)} fusion(s32[32]{0:T(128)} %param.18, s32[]{:T(128)} %axis_index.15), kind=kLoop, calls=%fused_computation.4 | loop fusion | flops 704 | bytes 260 | tf_op jit(solution)/shard_map/jit(_where)/select_n | solution.py:224
  11.1 0.1 broadcast_in_dim.9
  11.1 0.1 reshape_reshape.3.slots_ref
  11.3 0.0 copy-start.5
  11.3 0.0 copy-start.6
  11.3 22.2 %all_gather.6 = bf16[1024,256]{1,0:T(8,128)(2,1)S(1)} all-gather(bf16[256,256]{1,0:T(8,128)(2,1)S(1)} %pad_maximum_fusion), channel_id=1, replica_groups=mesh['groups'=2,'ctx'=4,'head'=4] {'ctx'}, dimensions={0}, use_global_device_ids=true | all-gather | bytes 655360 | tf_op jit(solution)/shard_map/all_gather | solution.py:201
  33.5 0.0 copy-done
  33.5 0.0 copy-start.1
  33.5 1.2 %copy-done.1 = bf16[128,16,256]{2,1,0:T(8,128)(2,1)S(1)} copy-done((bf16[128,16,256]{2,1,0:T(8,128)(2,1)S(1)}, bf16[128,16,256]{2,1,0:T(8,128)(2,1)}, u32[]{:S(2)}) %copy-start.1) | copy-done | bytes 1048600
  34.7 2.0 %decode_rows.1 = bf16[8,2048]{1,0:T(8,128)(2,1)} custom-call(s32[1,512]{1,0:T(1,128)S(1)} %reshape_reshape.3.slots_ref, bf16[8,2048]{1,0:T(8,128)(2,1)S(1)} %copy-done.5, s32[8,32]{1,0:T(8,128)S(1)} %copy-done.6, s32[8,1]{1,0:T(8,128)S(1)} %copy.15.length_ref, bf16[128,16,256]{2,1,0:T(8,128)(2,1)S(1)} %copy-done, bf16[128,16,256]{2,1,0:T(8,128)(2,1)S(1)} %copy-done.1, ...), custom_call_target="tpu_custom_call" | custom-call | flops 268435456 | bytes 2097152 | tf_op jit(solution)/shard_map/decode_rows/pallas_call | solution.py:226
  36.8 4.6 %stretch_and_own_cache.1 = (bf16[2,128,1024]{2,1,0:T(8,128)(2,1)S(1)}, f32[2,1,1024]{2,1,0:T(1,128)S(1)}, f32[2,1,1024]{2,1,0:T(1,128)S(1)}, f32[2,128,1024]{2,1,0:T(8,128)S(1)}) custom-call(s32[1]{0:T(128)} %bitcast.own_ref, s32[1]{0:T(128)S(6)} %copy.17.limit_ref, bf16[128,2048]{1,0:T(8,128)(2,1)S(1)} %copy-done.7, bf16[4,256,256]{2,1,0:T(8,128)(2,1)S(1)} %bitcast.5, ...), custom_call_target="tpu_custom_call" | custom-call | flops 805306368 | bytes 1048576 | tf_op jit(solution)/shard_map/stretch_and_own_cache/pallas_call | solution.py:209
  41.4 3.1 %all-gather.2.cloned.1.call-done = bf16[2048,256]{1,0:T(8,128)(2,1)} async-done(((bf16[512,256]{1,0:T(8,128)(2,1)}), bf16[2048,256]{1,0:T(8,128)(2,1)}) %all-gather.2.cloned.1.call-update) | async-done | bytes 1048592 | tf_op jit(solution)/shard_map/all_gather | solution.py:200
  44.5 1.2 %copy-done.2 = bf16[2048,256]{1,0:T(8,128)(2,1)S(1)} copy-done((bf16[2048,256]{1,0:T(8,128)(2,1)S(1)}, bf16[2048,256]{1,0:T(8,128)(2,1)}, u32[]{:S(2)}) %copy-start.2) | copy-done | bytes 1048600
  45.7 5.5 %other_cache_shards.1 = bf16[128,2048]{1,0:T(8,128)(2,1)} custom-call(s32[1]{0:T(128)} %bitcast.own_ref, s32[1]{0:T(128)S(6)} %copy.17.limit_ref, bf16[2,128,1024]{2,1,0:T(8,128)(2,1)S(1)} %get-tuple-element.6.qt_ref, bf16[4,512,256]{2,1,0:T(8,128)(2,1)S(1)} %bitcast.6, f32[2,1,1024]{2,1,0:T(1,128)S(1)} %get-tuple-element.7.high_ref, ...), custom_call_target="tpu_custom_call" | custom-call | flops 805306368 | bytes 1048576 | tf_op jit(solution)/shard_map/other_cache_shards/pallas_call | solution.py:241
  (12 shorter events, 0.0 us)
Async XLA Ops:
  7.2 1.1 %copy-start.8 = (bf16[256,256]{1,0:T(8,128)(2,1)S(1)}, bf16[256,256]{1,0:T(8,128)(2,1)}, u32[]{:S(2)}) copy-start(bf16[256,256]{1,0:T(8,128)(2,1)} %param.16) | copy-start | bytes 393220
  7.2 4.1 %copy-start.9 = (bf16[128,256]{1,0:T(8,128)(2,1)S(1)}, bf16[128,256]{1,0:T(8,128)(2,1)}, u32[]{:S(2)}) copy-start(bf16[128,256]{1,0:T(8,128)(2,1)} %param.14) | copy-start | bytes 196612
  7.2 4.0 %copy-start.10 = (bf16[128,256]{1,0:T(8,128)(2,1)S(1)}, bf16[128,256]{1,0:T(8,128)(2,1)}, u32[]{:S(2)}) copy-start(bf16[128,256]{1,0:T(8,128)(2,1)} %param.13) | copy-start | bytes 196612
  7.2 26.3 %copy-start = (bf16[128,16,256]{2,1,0:T(8,128)(2,1)S(1)}, bf16[128,16,256]{2,1,0:T(8,128)(2,1)}, u32[]{:S(2)}) copy-start(bf16[128,16,256]{2,1,0:T(8,128)(2,1)} %pool_k.1) | copy-start | bytes 3145732
  7.2 37.3 %all-gather.2.cloned.1.call-start = ((), (), s32[]{:S(2)}) async-start(), calls=%async_computation | async-start | bytes 1310720 | tf_op jit(solution)/shard_map/all_gather | solution.py:200
  8.3 0.7 %copy-start.3 = (bf16[512,256]{1,0:T(8,128)(2,1)}, bf16[512,256]{1,0:T(8,128)(2,1)S(1)}, u32[]{:S(2)}) copy-start(bf16[512,256]{1,0:T(8,128)(2,1)S(1)} %constant_dynamic-update-slice_fusion.cache_ref) | copy-start | bytes 786436
  11.3 22.2 %copy-start.5 = (bf16[8,2048]{1,0:T(8,128)(2,1)S(1)}, bf16[8,2048]{1,0:T(8,128)(2,1)}, u32[]{:S(2)}) copy-start(bf16[8,2048]{1,0:T(8,128)(2,1)} %q_ref.3) | copy-start | bytes 98308
  11.3 22.2 %copy-start.6 = (s32[8,32]{1,0:T(8,128)S(1)}, s32[8,32]{1,0:T(8,128)}, u32[]{:S(2)}) copy-start(s32[8,32]{1,0:T(8,128)} %lists_ref.1) | copy-start | bytes 3076
  33.5 1.2 %copy-start.1 = (bf16[128,16,256]{2,1,0:T(8,128)(2,1)S(1)}, bf16[128,16,256]{2,1,0:T(8,128)(2,1)}, u32[]{:S(2)}) copy-start(bf16[128,16,256]{2,1,0:T(8,128)(2,1)} %pool_v.1) | copy-start | bytes 3145732
  34.7 2.0 %copy-start.4 = (bf16[512,256]{1,0:T(8,128)(2,1)S(1)}, bf16[512,256]{1,0:T(8,128)(2,1)}, u32[]{:S(2)}) copy-start(bf16[512,256]{1,0:T(8,128)(2,1)} %copy-done.3) | copy-start | bytes 786436
  34.7 2.0 %copy-start.7 = (bf16[128,2048]{1,0:T(8,128)(2,1)S(1)}, bf16[128,2048]{1,0:T(8,128)(2,1)}, u32[]{:S(2)}) copy-start(bf16[128,2048]{1,0:T(8,128)(2,1)} %q_ref.2) | copy-start | bytes 1572868
  44.5 1.2 %copy-start.2 = (bf16[2048,256]{1,0:T(8,128)(2,1)S(1)}, bf16[2048,256]{1,0:T(8,128)(2,1)}, u32[]{:S(2)}) copy-start(bf16[2048,256]{1,0:T(8,128)(2,1)} %all-gather.2.cloned.1.call-done) | copy-start | bytes 3145732
Sparse Core Ops, SparseCore 0:
  10.2 34.2 all-gather.1
where the time goes:
time: 58.3 us; the launch traced here: 58 us
  blocking collectives  22.2 us (38%)
  between operations  14.8 us (25%)
  Pallas kernels  12.1 us (21%)
  local copies, waits for them, and re-layouts  5.1 us (9%)
  waiting for transfers between devices  3.08 us (5%)
  other arithmetic  0.68 us (1%)
    all_gather x1, blocking collectives, per_device(): lax.all_gather(own_s, 'ctx', axis=0, tiled=True)  22.2 us
    pallas_call x1, Pallas kernels, per_device(): pl.pallas_call(functools.partial(far_kernel, count), out_shape=jax.ShapeD...  5.47 us
    pallas_call x1, Pallas kernels, per_device(): pl.pallas_call(near_kernel, out_shape=(jax.ShapeDtypeStruct((kv_local, HE...  4.64 us
    unnamed x23, local copies, waits for them, and re-layouts  4.21 us
    all_gather x1, waiting for transfers between devices, per_device(): lax.all_gather(own_c, 'ctx', axis=0, tiled=True)  3.07 us
    pallas_call x1, Pallas kernels, per_device(): pl.pallas_call(decode_kernel, out_shape=jax.ShapeDtypeStruct(decode_queri...  2.04 us
  transfers between devices with their start and end apart: 1, of which 1 were waited for; matrix products, arithmetic and copies ran while one was open for 3% of the time, Pallas kernels for 12%

commit v1 on v0

v1 whole, which is shorter than its diff:
```python
import functools

import jax
import jax.numpy as jnp
from jax import lax
from jax.experimental import pallas as pl
from jax.experimental.pallas import tpu as pltpu
from jax.sharding import PartitionSpec as P

HEADS = 64
KV_HEADS = 8
HEAD_DIM = 128
GROUP = HEADS // KV_HEADS
PAGE = 16
P_DEV = 8
EXP2_SCALE = HEAD_DIM ** (-0.5) * 1.4426950408889634
HIDDEN = -1e30
VMEM_BYTES = 48 * 1024 * 1024

VMEM = pl.BlockSpec(memory_space=pltpu.VMEM)
SMEM = pl.BlockSpec(memory_space=pltpu.SMEM)


def attend(qt_ref, head, cols, keys, values_t, state):
    tokens = keys.shape[1] - HEAD_DIM
    queries = qt_ref[head, :, cols]
    place = lax.broadcasted_iota(jnp.int32, (tokens, queries.shape[1]), 0)
    token = lax.rem(lax.broadcasted_iota(jnp.int32, (tokens, queries.shape[1]), 1), tokens)
    pick = jnp.where(place == token, jnp.float32(1.0), jnp.float32(0.0)).astype(jnp.bfloat16)
    queries = jnp.concatenate([queries, pick], axis=0)
    scores = jnp.dot(keys, queries, preferred_element_type=jnp.float32)
    high = jnp.max(scores, axis=0, keepdims=True)
    if state is not None:
        old_high, old_total, old_accum = state
        high = jnp.maximum(high, old_high)
    weights = jnp.exp2((scores - high) * EXP2_SCALE)
    total = jnp.sum(weights, axis=0, keepdims=True)
    accum = jnp.dot(values_t, weights.astype(jnp.bfloat16), preferred_element_type=jnp.float32)
    if state is not None:
        decay = jnp.exp2((old_high - high) * EXP2_SCALE)
        total = total + old_total * decay
        accum = accum + old_accum * decay
    return high, total, accum


def hidden(seen):
    return jnp.where(seen, jnp.float32(0.0), jnp.float32(HIDDEN)).astype(jnp.bfloat16)


def shard_mask(shard, own, limit, tokens, keys):
    c_rows = keys - tokens
    place = lax.broadcasted_iota(jnp.int32, (keys, tokens), 0)
    token = lax.broadcasted_iota(jnp.int32, (keys, tokens), 1)
    stretch = place - token <= (own - shard) * tokens
    cached = place - tokens < limit - shard * c_rows
    return hidden(((place < tokens) & stretch) | ((place >= tokens) & cached))


def wide_queries(q_ref, kv_local):
    heads = q_ref.shape[1] // HEAD_DIM
    queries = q_ref[...].astype(jnp.float32)
    stacked = []
    for head in range(heads):
        piece = queries[:, head * HEAD_DIM : (head + 1) * HEAD_DIM]
        blank = jnp.zeros_like(piece)
        stacked.append(
            jnp.concatenate([piece if kv == head // GROUP else blank for kv in range(kv_local)], axis=1)
        )
    return jnp.concatenate(stacked, axis=0).astype(jnp.bfloat16)


def decode_attend(queries, lists, lengths, parts, state):
    rows, span = lists.shape
    heads = queries.shape[0] // rows
    done = []
    for keys, values, slot in parts:
        tokens = slot.shape[1]
        offset = lax.rem(lax.broadcasted_iota(jnp.int32, (rows, tokens), 1), PAGE)
        tally = jnp.zeros((rows, tokens), jnp.float32)
        for entry in range(span):
            hit = (slot == lists[:, entry : entry + 1]) & (offset < lengths - entry * PAGE)
            tally = tally + jnp.where(hit, jnp.float32(1.0), jnp.float32(0.0))
        tally = tally[None]
        scores = lax.dot_general(
            queries, keys, (((1,), (1,)), ((), ())), preferred_element_type=jnp.float32
        ).reshape(heads, rows, tokens)
        done.append((jnp.where(tally > 0, scores, jnp.float32(HIDDEN)), tally, values))
    highs = [jnp.max(scores, axis=-1, keepdims=True) for scores, _, _ in done]
    if state is not None:
        old_high, old_total, old_mixed = state
        highs.append(old_high)
    high = functools.reduce(jnp.maximum, highs)
    total, mixed = 0.0, 0.0
    if state is not None:
        decay = jnp.exp2((old_high - high) * EXP2_SCALE)
        total = old_total * decay
        mixed = old_mixed * decay
    for scores, tally, values in done:
        weights = jnp.exp2((scores - high) * EXP2_SCALE) * tally
        total = total + jnp.sum(weights, axis=-1, keepdims=True)
        mixed = mixed + jnp.dot(
            weights.reshape(heads * rows, -1).astype(jnp.bfloat16),
            values,
            preferred_element_type=jnp.float32,
        ).reshape(heads, rows, -1)
    return high, total, mixed


def own_kernel(own_ref, limit_ref, q_ref, shard_ref, qt_ref, high_ref, total_ref, accum_ref):
    kv_local, _, rows = qt_ref.shape
    tokens = q_ref.shape[0]
    for head in range(kv_local):
        for sub in range(GROUP):
            col = (head * GROUP + sub) * HEAD_DIM
            qt_ref[head, :, sub * tokens : (sub + 1) * tokens] = q_ref[:, col : col + HEAD_DIM].T
    half = shard_ref.shape[0] // 2
    width = min(2 * tokens, rows)
    mask = shard_mask(own_ref[0], own_ref[0], limit_ref[0], tokens, half)
    for head in range(kv_local):
        feats = slice(head * HEAD_DIM, (head + 1) * HEAD_DIM)
        keys = jnp.concatenate([shard_ref[:half, feats], mask], axis=1)
        values_t = shard_ref[half:, feats].T
        for start in range(0, rows, width):
            cols = slice(start, start + width)
            high, total, accum = attend(qt_ref, head, cols, keys, values_t, None)
            high_ref[head, :, cols] = high
            total_ref[head, :, cols] = total
            accum_ref[head, :, cols] = accum


def held_kernel(
    own_ref, q_ref, lists_ref, length_ref, slots_ref, pool_k, pool_v, shard_ref,
    wide_ref, high_ref, total_ref, mixed_ref,
):
    rows = q_ref.shape[0]
    tokens = slots_ref.shape[1]
    half, kv_width = shard_ref.shape
    half = half // 2
    held = pool_k.shape[0] * PAGE
    queries = wide_queries(q_ref, kv_width // HEAD_DIM)
    wide_ref[...] = queries
    held_slot = lax.broadcasted_iota(jnp.int32, (rows, held), 1) // PAGE
    own_slot = jnp.broadcast_to(slots_ref[pl.ds(own_ref[0], 1), :], (rows, tokens))
    parts = [
        (pool_k[...].reshape(held, kv_width), pool_v[...].reshape(held, kv_width), held_slot),
        (shard_ref[:tokens], shard_ref[half : half + tokens], own_slot),
    ]
    high_ref[...], total_ref[...], mixed_ref[...] = decode_attend(
        queries, lists_ref[...], length_ref[...], parts, None
    )


def hop_kernel(count, hops, last, *refs):
    own_ref, limit_ref, qt_ref, wide_ref, lists_ref, length_ref, slots_ref = refs[:7]
    shard_refs = refs[7 : 7 + len(hops)]
    high_in, total_in, accum_in, dec_high, dec_total, dec_mixed = refs[7 + len(hops) : 13 + len(hops)]
    outs = refs[13 + len(hops) :]
    own = own_ref[0]
    limit = limit_ref[0]
    kv_local, _, rows = qt_ref.shape
    tokens = slots_ref.shape[1]
    half = shard_refs[0].shape[0] // 2
    width = min(2 * tokens, rows)
    shards = [lax.rem(own + hop + count, count) for hop in hops]

    dec_rows = lists_ref.shape[0]
    parts = [
        (
            ref[:tokens],
            ref[half : half + tokens],
            jnp.broadcast_to(slots_ref[pl.ds(shard, 1), :], (dec_rows, tokens)),
        )
        for shard, ref in zip(shards, shard_refs)
    ]
    state = (dec_high[...], dec_total[...], dec_mixed[...])
    state = decode_attend(wide_ref[...], lists_ref[...], length_ref[...], parts, state)
    if last:
        _, total, mixed = state
        for head in range(kv_local * GROUP):
            kv = head // GROUP
            piece = mixed[head, :, kv * HEAD_DIM : (kv + 1) * HEAD_DIM] / total[head]
            outs[1][:, head * HEAD_DIM : (head + 1) * HEAD_DIM] = piece.astype(jnp.bfloat16)
    else:
        outs[3][...], outs[4][...], outs[5][...] = state

    mask = jnp.concatenate([shard_mask(shard, own, limit, tokens, half) for shard in shards], axis=0)
    for head in range(kv_local):
        feats = slice(head * HEAD_DIM, (head + 1) * HEAD_DIM)
        keys = jnp.concatenate([ref[:half, feats] for ref in shard_refs], axis=0)
        keys = jnp.concatenate([keys, mask], axis=1)
        values_t = jnp.concatenate([ref[half:, feats] for ref in shard_refs], axis=0).T
        for start in range(0, rows, width):
            cols = slice(start, start + width)
            state = (high_in[head, :, cols], total_in[head, :, cols], accum_in[head, :, cols])
            high, total, accum = attend(qt_ref, head, cols, keys, values_t, state)
            if last:
                mixed = (accum / total).astype(jnp.bfloat16)
                for piece in range(width // tokens):
                    col = (head * GROUP + start // tokens + piece) * HEAD_DIM
                    outs[0][:, col : col + HEAD_DIM] = mixed[:, piece * tokens : (piece + 1) * tokens].T
            else:
                outs[0][head, :, cols] = high
                outs[1][head, :, cols] = total
                outs[2][head, :, cols] = accum


def per_device(
    count,
    queries,
    stretch_keys,
    stretch_values,
    cache_keys,
    cache_values,
    prefix_length,
    page_targets,
    pool_keys,
    pool_values,
    decode_queries,
    page_lists,
    context_length,
):
    own = lax.axis_index("ctx")
    own_array = jnp.full((1,), own, jnp.int32)
    tokens, width = queries.shape
    kv_width = stretch_keys.shape[1]
    kv_local = kv_width // HEAD_DIM
    rows = GROUP * tokens
    heads = kv_local * GROUP
    dec_rows = decode_queries.shape[0]
    half = tokens + cache_keys.shape[0]
    f32 = jnp.float32
    params = pltpu.CompilerParams(vmem_limit_bytes=VMEM_BYTES)

    up_pairs = [(i, (i + 1) % count) for i in range(count)]
    down_pairs = [(i, (i - 1) % count) for i in range(count)]
    shard = jnp.concatenate([stretch_keys, cache_keys, stretch_values, cache_values], axis=0)
    ups, downs = [shard], [shard]
    for hop in range(1, count // 2 + 1):
        ups.append(lax.ppermute(ups[-1], "ctx", up_pairs))
        if hop <= (count - 1) // 2:
            downs.append(lax.ppermute(downs[-1], "ctx", down_pairs))

    def cost(keys):
        pairs = kv_local * rows * keys
        return pl.CostEstimate(
            flops=4 * pairs * HEAD_DIM, bytes_accessed=4 * rows * kv_local * HEAD_DIM, transcendentals=pairs
        )

    state_shapes = (
        jax.ShapeDtypeStruct((kv_local, 1, rows), f32),
        jax.ShapeDtypeStruct((kv_local, 1, rows), f32),
        jax.ShapeDtypeStruct((kv_local, HEAD_DIM, rows), f32),
    )
    dec_shapes = (
        jax.ShapeDtypeStruct((heads, dec_rows, 1), f32),
        jax.ShapeDtypeStruct((heads, dec_rows, 1), f32),
        jax.ShapeDtypeStruct((heads, dec_rows, kv_width), f32),
    )
    qt, *state = pl.pallas_call(
        own_kernel,
        out_shape=(jax.ShapeDtypeStruct((kv_local, HEAD_DIM, rows), jnp.bfloat16),) + state_shapes,
        in_specs=[SMEM, SMEM, VMEM, VMEM],
        out_specs=(VMEM,) * 4,
        compiler_params=params,
        cost_estimate=cost(half),
        name="own_shard",
    )(own_array, prefix_length, queries, shard)

    slots = jnp.where(page_targets // P_DEV == own, pool_keys.shape[0] + page_targets % P_DEV, -1)
    slots = jnp.repeat(slots, PAGE).reshape(count, tokens)
    lengths = context_length.reshape(-1, 1)
    wide, *dec_state = pl.pallas_call(
        held_kernel,
        out_shape=(jax.ShapeDtypeStruct((heads * dec_rows, kv_width), jnp.bfloat16),) + dec_shapes,
        in_specs=[SMEM] + [VMEM] * 7,
        out_specs=(VMEM,) * 4,
        compiler_params=params,
        cost_estimate=pl.CostEstimate(
            flops=4 * 128 * 2048 * 256, bytes_accessed=4 * pool_keys.size, transcendentals=128 * 2560
        ),
        name="decode_held_pages",
    )(own_array, decode_queries, page_lists, lengths, slots, pool_keys, pool_values, shard)

    for hop in range(1, count // 2 + 1):
        last = hop == count // 2
        hops, shards = [-hop], [ups[hop]]
        if hop < len(downs):
            hops.append(hop)
            shards.append(downs[hop])
        out_shape = state_shapes + dec_shapes
        if last:
            out_shape = (
                jax.ShapeDtypeStruct((tokens, width), jnp.bfloat16),
                jax.ShapeDtypeStruct(decode_queries.shape, jnp.bfloat16),
            )
        results = pl.pallas_call(
            functools.partial(hop_kernel, count, hops, last),
            out_shape=out_shape,
            in_specs=[SMEM, SMEM] + [VMEM] * (11 + len(hops)),
            out_specs=(VMEM,) * len(out_shape),
            compiler_params=params,
            cost_estimate=cost(half * len(hops)),
            name="shards_" + str(hop) + "_away",
        )(
            own_array, prefix_length, qt, wide, page_lists, lengths, slots,
            *shards, *state, *dec_state,
        )
        if last:
            return tuple(results)
        state, dec_state = results[:3], results[3:]


def solution(mesh):
    in_specs = (
        P(("groups", "ctx"), "head"),
        P(("groups", "ctx"), "head"),
        P(("groups", "ctx"), "head"),
        P(("groups", "ctx"), "head"),
        P(("groups", "ctx"), "head"),
        P("groups"),
        P("groups"),
        P(("groups", "ctx"), None, "head"),
        P(("groups", "ctx"), None, "head"),
        P(("groups", "ctx"), "head"),
        P(("groups", "ctx"), None),
        P(("groups", "ctx")),
    )
    out_specs = (P(("groups", "ctx"), "head"), P(("groups", "ctx"), "head"))
    return jax.shard_map(
        functools.partial(per_device, mesh.shape["ctx"]),
        mesh=mesh,
        in_specs=in_specs,
        out_specs=out_specs,
        check_vma=False,
    )
```

time: 58.3 us -> 40.4 us (0.69)
  the two profiles are of different devices: /device:TPU:0 before, /device:TPU:22 now
where the time goes in v1:
time: 40.4 us; the launch traced here: 40.1 us
  waiting for transfers between devices  16.2 us (40%)
  Pallas kernels  13.4 us (33%)
  local copies, waits for them, and re-layouts  5.32 us (13%)
  starting transfers between devices  3.79 us (9%)
  between operations  1.39 us (3%)
    ppermute x2, waiting for transfers between devices, per_device(): ups.append(lax.ppermute(ups[-1], 'ctx', up_pairs))  16.2 us
    pallas_call x2, Pallas kernels, per_device(): pl.pallas_call(functools.partial(hop_kernel, count, hops, last), out_shap...  8.89 us
    unnamed x23, local copies, waits for them, and re-layouts  4.99 us
    ppermute x2, starting transfers between devices, per_device(): ups.append(lax.ppermute(ups[-1], 'ctx', up_pairs))  3.34 us
    pallas_call x1, Pallas kernels, per_device(): pl.pallas_call(own_kernel, out_shape=(jax.ShapeDtypeStruct((kv_local, HEA...  3.24 us
    pallas_call x1, Pallas kernels, per_device(): pl.pallas_call(held_kernel, out_shape=(jax.ShapeDtypeStruct((heads * dec_...  1.3 us
  transfers between devices with their start and end apart: 3, of which 1 were waited for; matrix products, arithmetic and copies ran while one was open for 1% of the time, Pallas kernels for 23%

profile of v1, /device:TPU:22, one launch (start us, length us, event | category | flops | bytes accessed | tf_op | source)
XLA Modules:
  0.0 40.1 jit_solution(14188498211929363054)
XLA Ops:
  0.6 0.9 %constant_dynamic-update-slice_fusion.3 = bf16[768,256]{1,0:T(8,128)(2,1)S(1)} fusion(bf16[128,256]{1,0:T(8,128)(2,1)} %param.13), kind=kLoop, calls=%fused_computation.3 | loop fusion | bytes 131072
  1.5 0.0 copy-done.5
  1.6 0.8 %copy-done.7 = bf16[128,256]{1,0:T(8,128)(2,1)S(1)} copy-done((bf16[128,256]{1,0:T(8,128)(2,1)S(1)}, bf16[128,256]{1,0:T(8,128)(2,1)}, u32[]{:S(2)}) %copy-start.7) | copy-done | bytes 65560
  2.4 0.1 copy-done.6
  2.5 0.0 copy-start.2
  2.5 1.6 %collective-permute-start = (bf16[768,256]{1,0:T(8,128)(2,1)S(1)}, bf16[768,256]{1,0:T(8,128)(2,1)S(1)}, u32[]{:S(2)}, u32[]{:S(2)}) collective-permute-start(bf16[768,256]{1,0:T(8,128)(2,1)S(1)} %constant_dynamic-update-slice_fusion.shard_ref), channel_id=1, source_target_pairs={{0,4},{4,8},{8,12},{12,0},{1,5},{5,9},{9,13},{13,1},{2,6},{6,10},{... | collective-permute-start | bytes 1179656 | tf_op jit(solution)/shard_map/ppermute | solution.py:239
  4.2 0.4 %collective-permute-start.2 = (bf16[768,256]{1,0:T(8,128)(2,1)S(1)}, bf16[768,256]{1,0:T(8,128)(2,1)S(1)}, u32[]{:S(2)}, u32[]{:S(2)}) collective-permute-start(bf16[768,256]{1,0:T(8,128)(2,1)S(1)} %constant_dynamic-update-slice_fusion.shard_ref), channel_id=1, source_target_pairs={{0,12},{4,0},{8,4},{12,8},{1,13},{5,1},{9,5},{13,9},{2,14},{6,2},{... | collective-permute-start | bytes 1179656 | tf_op jit(solution)/shard_map/ppermute | solution.py:241
  4.6 16.2 %collective-permute-done.refs_7_ = bf16[768,256]{1,0:T(8,128)(2,1)S(1)} collective-permute-done((bf16[768,256]{1,0:T(8,128)(2,1)S(1)}, bf16[768,256]{1,0:T(8,128)(2,1)S(1)}, u32[]{:S(2)}, u32[]{:S(2)}) %collective-permute-start) | collective-permute-done | bytes 393248 | tf_op jit(solution)/shard_map/ppermute | solution.py:239
  20.8 1.7 %collective-permute-start.1 = (bf16[768,256]{1,0:T(8,128)(2,1)S(1)}, bf16[768,256]{1,0:T(8,128)(2,1)S(1)}, u32[]{:S(2)}, u32[]{:S(2)}) collective-permute-start(bf16[768,256]{1,0:T(8,128)(2,1)S(1)} %collective-permute-done.refs_7_), channel_id=1, source_target_pairs={{0,4},{4,8},{8,12},{12,0},{1,5},{5,9},{9,13},{13,1},{2,6},{6,10},{... | collective-permute-start | bytes 1179656 | tf_op jit(solution)/shard_map/ppermute | solution.py:239
  22.5 0.1 broadcast_in_dim.13
  22.6 0.1 broadcast_in_dim.14
  22.7 0.1 broadcast_in_dim.15.slots_ref.refs_6_
  22.7 0.7 %copy-done.8 = s32[8]{0:T(128)S(1)} copy-done((s32[8]{0:T(128)S(1)}, s32[8]{0:T(128)}, u32[]{:S(2)}) %copy-start.8) | copy-done | bytes 56
  23.4 0.1 copy.14.length_ref.refs_5_
  24.1 0.0 copy-done.2
  24.2 0.0 copy-start
  24.2 1.2 %copy-done = bf16[128,16,256]{2,1,0:T(8,128)(2,1)S(1)} copy-done((bf16[128,16,256]{2,1,0:T(8,128)(2,1)S(1)}, bf16[128,16,256]{2,1,0:T(8,128)(2,1)}, u32[]{:S(2)}) %copy-start) | copy-done | bytes 1048600
  25.4 1.2 %copy-done.1 = bf16[128,16,256]{2,1,0:T(8,128)(2,1)S(1)} copy-done((bf16[128,16,256]{2,1,0:T(8,128)(2,1)S(1)}, bf16[128,16,256]{2,1,0:T(8,128)(2,1)}, u32[]{:S(2)}) %copy-start.1) | copy-done | bytes 1048600
  26.6 1.3 %decode_held_pages.1 = (bf16[128,256]{1,0:T(8,128)(2,1)S(1)}, f32[16,8,1]{2,1,0:T(8,128)S(1)}, f32[16,8,1]{2,1,0:T(8,128)S(1)}, f32[16,8,256]{2,1,0:T(8,128)S(1)}) custom-call(s32[1]{0:T(128)} %bitcast.own_ref.refs_0_, bf16[8,2048]{1,0:T(8,128)(2,1)S(1)} %copy-done.2, s32[8,32]{1,0:T(8,128)S(1)} %copy-done.3, s32[8,1]{1,0:T(8,128)S(1)} %copy.14.length_ref.refs_5_, ...), custom_call_target="tpu_custom_call" | custom-call | flops 268435456 | bytes 2097152 | tf_op jit(solution)/shard_map/decode_held_pages/pallas_call | solution.py:272
  27.9 3.2 %own_shard.1 = (bf16[2,128,1024]{2,1,0:T(8,128)(2,1)S(1)}, f32[2,1,1024]{2,1,0:T(1,128)S(1)}, f32[2,1,1024]{2,1,0:T(1,128)S(1)}, f32[2,128,1024]{2,1,0:T(8,128)S(1)}) custom-call(s32[1]{0:T(128)} %bitcast.own_ref.refs_0_, s32[1]{0:T(128)S(6)} %copy.20.limit_ref.refs_1_, bf16[128,2048]{1,0:T(8,128)(2,1)S(1)} %copy-done.4, ...), custom_call_target="tpu_custom_call" | custom-call | flops 402653184 | bytes 1048576 | tf_op jit(solution)/shard_map/own_shard/pallas_call | solution.py:259
  31.2 0.0 collective-permute-done.2.refs_8_
  31.2 4.6 %shards_1_away.1 = (f32[2,1,1024]{2,1,0:T(1,128)S(1)}, f32[2,1,1024]{2,1,0:T(1,128)S(1)}, f32[2,128,1024]{2,1,0:T(8,128)S(1)}, f32[16,8,1]{2,1,0:T(8,128)S(1)}, ...) custom-call(s32[1]{0:T(128)} %bitcast.own_ref.refs_0_, s32[1]{0:T(128)S(6)} %copy.20.limit_ref.refs_1_, ...), custom_call_target="tpu_custom_call" | custom-call | flops 805306368 | bytes 1048576 | tf_op jit(solution)/shard_map/shards_1_away/pallas_call | solution.py:296
  35.8 0.0 collective-permute-done.1.refs_7_
  35.8 4.3 %shards_2_away.1 = (bf16[128,2048]{1,0:T(8,128)(2,1)}, bf16[8,2048]{1,0:T(8,128)(2,1)}) custom-call(s32[1]{0:T(128)} %bitcast.own_ref.refs_0_, s32[1]{0:T(128)S(6)} %copy.20.limit_ref.refs_1_, bf16[2,128,1024]{2,1,0:T(8,128)(2,1)S(1)} %get-tuple-element.16.refs_2_, bf16[128,256]{1,0:T(8,128)(2,1)S(1)} %get-tuple-element.17.refs_3_, s32[8,32]{1,0:T(8,128)S(1)} %copy-done.3, ...), custom_call_target="tpu_custom_call" | custom-call | flops 402653184 | bytes 1048576 | tf_op jit(solution)/shard_map/shards_2_away/pallas_call | solution.py:296
  (15 shorter events, 0.1 us)
Async XLA Ops:
  0.6 0.9 %copy-start.5 = (bf16[256,256]{1,0:T(8,128)(2,1)S(1)}, bf16[256,256]{1,0:T(8,128)(2,1)}, u32[]{:S(2)}) copy-start(bf16[256,256]{1,0:T(8,128)(2,1)} %param.15) | copy-start | bytes 393220
  1.6 0.8 %copy-start.7 = (bf16[128,256]{1,0:T(8,128)(2,1)S(1)}, bf16[128,256]{1,0:T(8,128)(2,1)}, u32[]{:S(2)}) copy-start(bf16[128,256]{1,0:T(8,128)(2,1)} %param.14) | copy-start | bytes 196612
  1.6 0.9 %copy-start.6 = (bf16[256,256]{1,0:T(8,128)(2,1)S(1)}, bf16[256,256]{1,0:T(8,128)(2,1)}, u32[]{:S(2)}) copy-start(bf16[256,256]{1,0:T(8,128)(2,1)} %param.16) | copy-start | bytes 393220
  2.5 20.0 %copy-start.9 = (s32[32]{0:T(128)S(1)}, s32[32]{0:T(128)}, u32[]{:S(2)}) copy-start(s32[32]{0:T(128)} %param.18) | copy-start | bytes 388
  2.5 21.6 %copy-start.2 = (bf16[8,2048]{1,0:T(8,128)(2,1)S(1)}, bf16[8,2048]{1,0:T(8,128)(2,1)}, u32[]{:S(2)}) copy-start(bf16[8,2048]{1,0:T(8,128)(2,1)} %q_ref.3) | copy-start | bytes 98308
  2.5 18.2 %collective-permute-start = (bf16[768,256]{1,0:T(8,128)(2,1)S(1)}, bf16[768,256]{1,0:T(8,128)(2,1)S(1)}, u32[]{:S(2)}, u32[]{:S(2)}) collective-permute-start(bf16[768,256]{1,0:T(8,128)(2,1)S(1)} %constant_dynamic-update-slice_fusion.shard_ref), channel_id=1, source_target_pairs={{0,4},{4,8},{8,12},{12,0},{1,5},{5,9},{9,13},{13,1},{2,6},{6,10},{... | collective-permute-start | bytes 1179656 | tf_op jit(solution)/shard_map/ppermute | solution.py:239
  4.2 27.0 %collective-permute-start.2 = (bf16[768,256]{1,0:T(8,128)(2,1)S(1)}, bf16[768,256]{1,0:T(8,128)(2,1)S(1)}, u32[]{:S(2)}, u32[]{:S(2)}) collective-permute-start(bf16[768,256]{1,0:T(8,128)(2,1)S(1)} %constant_dynamic-update-slice_fusion.shard_ref), channel_id=1, source_target_pairs={{0,12},{4,0},{8,4},{12,8},{1,13},{5,1},{9,5},{13,9},{2,14},{6,2},{... | collective-permute-start | bytes 1179656 | tf_op jit(solution)/shard_map/ppermute | solution.py:241
  20.8 15.0 %collective-permute-start.1 = (bf16[768,256]{1,0:T(8,128)(2,1)S(1)}, bf16[768,256]{1,0:T(8,128)(2,1)S(1)}, u32[]{:S(2)}, u32[]{:S(2)}) collective-permute-start(bf16[768,256]{1,0:T(8,128)(2,1)S(1)} %collective-permute-done.refs_7_), channel_id=1, source_target_pairs={{0,4},{4,8},{8,12},{12,0},{1,5},{5,9},{9,13},{13,1},{2,6},{6,10},{... | collective-permute-start | bytes 1179656 | tf_op jit(solution)/shard_map/ppermute | solution.py:239
  22.7 0.7 %copy-start.8 = (s32[8]{0:T(128)S(1)}, s32[8]{0:T(128)}, u32[]{:S(2)}) copy-start(s32[8]{0:T(128)} %param.23) | copy-start | bytes 100
  23.4 0.7 %copy-start.3 = (s32[8,32]{1,0:T(8,128)S(1)}, s32[8,32]{1,0:T(8,128)}, u32[]{:S(2)}) copy-start(s32[8,32]{1,0:T(8,128)} %refs_4_.3) | copy-start | bytes 3076
  24.2 1.2 %copy-start = (bf16[128,16,256]{2,1,0:T(8,128)(2,1)S(1)}, bf16[128,16,256]{2,1,0:T(8,128)(2,1)}, u32[]{:S(2)}) copy-start(bf16[128,16,256]{2,1,0:T(8,128)(2,1)} %pool_k.1) | copy-start | bytes 3145732
  25.4 1.2 %copy-start.1 = (bf16[128,16,256]{2,1,0:T(8,128)(2,1)S(1)}, bf16[128,16,256]{2,1,0:T(8,128)(2,1)}, u32[]{:S(2)}) copy-start(bf16[128,16,256]{2,1,0:T(8,128)(2,1)} %pool_v.1) | copy-start | bytes 3145732
  26.6 1.3 %copy-start.4 = (bf16[128,2048]{1,0:T(8,128)(2,1)S(1)}, bf16[128,2048]{1,0:T(8,128)(2,1)}, u32[]{:S(2)}) copy-start(bf16[128,2048]{1,0:T(8,128)(2,1)} %q_ref.2) | copy-start | bytes 1572868

commit v2 on v1

--- a/solution.py
+++ b/solution.py
@@ -234,11 +234,8 @@
     up_pairs = [(i, (i + 1) % count) for i in range(count)]
     down_pairs = [(i, (i - 1) % count) for i in range(count)]
     shard = jnp.concatenate([stretch_keys, cache_keys, stretch_values, cache_values], axis=0)
-    ups, downs = [shard], [shard]
-    for hop in range(1, count // 2 + 1):
-        ups.append(lax.ppermute(ups[-1], "ctx", up_pairs))
-        if hop <= (count - 1) // 2:
-            downs.append(lax.ppermute(downs[-1], "ctx", down_pairs))
+    ups = [shard, lax.ppermute(shard, "ctx", up_pairs)]
+    downs = [shard, lax.ppermute(shard, "ctx", down_pairs)]
 
     def cost(keys):
         pairs = kv_local * rows * keys
@@ -280,6 +277,12 @@
         ),
         name="decode_held_pages",
     )(own_array, decode_queries, page_lists, lengths, slots, pool_keys, pool_values, shard)
+
+    ups[1], state, dec_state = lax.optimization_barrier((ups[1], state, dec_state))
+    for hop in range(2, count // 2 + 1):
+        ups.append(lax.ppermute(ups[-1], "ctx", up_pairs))
+        if hop <= (count - 1) // 2:
+            downs.append(lax.ppermute(downs[-1], "ctx", down_pairs))
 
     for hop in range(1, count // 2 + 1):
         last = hop == count // 2

time: 40.4 us -> 38.2 us (0.946)
  the two profiles are of different devices: /device:TPU:22 before, /device:TPU:0 now
where the time goes in v2:
time: 38.2 us; the launch traced here: 37.9 us
  Pallas kernels  13.4 us (35%)
  waiting for transfers between devices  12.7 us (33%)
  local copies, waits for them, and re-layouts  5.26 us (14%)
  starting transfers between devices  5.17 us (14%)
  between operations  1.35 us (4%)
    pallas_call x2, Pallas kernels, per_device(): pl.pallas_call(functools.partial(hop_kernel, count, hops, last), out_shap...  8.88 us
    ppermute x1, waiting for transfers between devices, per_device(): downs = [shard, lax.ppermute(shard, 'ctx', down_pairs)]  7.2 us
    unnamed x23, local copies, waits for them, and re-layouts  4.94 us
    ppermute x1, waiting for transfers between devices, per_device(): ups.append(lax.ppermute(ups[-1], 'ctx', up_pairs))  4.22 us
    pallas_call x1, Pallas kernels, per_device(): pl.pallas_call(own_kernel, out_shape=(jax.ShapeDtypeStruct((kv_local, HEA...  3.23 us
    ppermute x1, starting transfers between devices, per_device(): ups = [shard, lax.ppermute(shard, 'ctx', up_pairs)]  3.08 us
    ppermute x1, starting transfers between devices, per_device(): downs = [shard, lax.ppermute(shard, 'ctx', down_pairs)]  2.09 us
    ppermute x1, waiting for transfers between devices, per_device(): ups = [shard, lax.ppermute(shard, 'ctx', up_pairs)]  1.32 us
  transfers between devices with their start and end apart: 3, of which 3 were waited for; matrix products, arithmetic and copies ran while one was open for 1% of the time, Pallas kernels for 24%

profile of v2, /device:TPU:0, one launch (start us, length us, event | category | flops | bytes accessed | tf_op | source)
XLA Modules:
  0.0 37.9 jit_solution(17582042847531146354)
XLA Ops:
  0.6 0.0 copy-start.5
  0.6 0.9 %constant_dynamic-update-slice_fusion.3 = bf16[768,256]{1,0:T(8,128)(2,1)S(1)} fusion(bf16[128,256]{1,0:T(8,128)(2,1)} %param.13), kind=kLoop, calls=%fused_computation.3 | loop fusion | bytes 131072
  1.5 0.0 copy-done.5
  1.6 0.8 %copy-done.7 = bf16[128,256]{1,0:T(8,128)(2,1)S(1)} copy-done((bf16[128,256]{1,0:T(8,128)(2,1)S(1)}, bf16[128,256]{1,0:T(8,128)(2,1)}, u32[]{:S(2)}) %copy-start.7) | copy-done | bytes 65560
  2.4 0.1 copy-done.6
  2.5 0.0 copy-start.2
  2.5 3.1 %collective-permute-start = (bf16[768,256]{1,0:T(8,128)(2,1)S(1)}, bf16[768,256]{1,0:T(8,128)(2,1)S(1)}, u32[]{:S(2)}, u32[]{:S(2)}) collective-permute-start(bf16[768,256]{1,0:T(8,128)(2,1)S(1)} %constant_dynamic-update-slice_fusion.shard_ref), channel_id=1, source_target_pairs={{0,4},{4,8},{8,12},{12,0},{1,5},{5,9},{9,13},{13,1},{2,6},{6,10},{... | collective-permute-start | bytes 1179656 | tf_op jit(solution)/shard_map/ppermute | solution.py:237
  5.6 2.1 %collective-permute-start.2 = (bf16[768,256]{1,0:T(8,128)(2,1)S(1)}, bf16[768,256]{1,0:T(8,128)(2,1)S(1)}, u32[]{:S(2)}, u32[]{:S(2)}) collective-permute-start(bf16[768,256]{1,0:T(8,128)(2,1)S(1)} %constant_dynamic-update-slice_fusion.shard_ref), channel_id=1, source_target_pairs={{0,12},{4,0},{8,4},{12,8},{1,13},{5,1},{9,5},{13,9},{2,14},{6,2},{... | collective-permute-start | bytes 1179656 | tf_op jit(solution)/shard_map/ppermute | solution.py:238
  8.4 0.1 broadcast_in_dim.13
  8.5 0.0 copy-done.8
  8.5 0.1 copy.14.length_ref.refs_5_
  8.5 0.1 broadcast_in_dim.14
  8.6 0.1 broadcast_in_dim.15.slots_ref.refs_6_
  8.7 0.6 %copy-done.3 = s32[8,32]{1,0:T(8,128)S(1)} copy-done((s32[8,32]{1,0:T(8,128)S(1)}, s32[8,32]{1,0:T(8,128)}, u32[]{:S(2)}) %copy-start.3) | copy-done | bytes 1048
  9.3 1.2 %copy-done = bf16[128,16,256]{2,1,0:T(8,128)(2,1)S(1)} copy-done((bf16[128,16,256]{2,1,0:T(8,128)(2,1)S(1)}, bf16[128,16,256]{2,1,0:T(8,128)(2,1)}, u32[]{:S(2)}) %copy-start) | copy-done | bytes 1048600
  10.5 1.2 %copy-done.1 = bf16[128,16,256]{2,1,0:T(8,128)(2,1)S(1)} copy-done((bf16[128,16,256]{2,1,0:T(8,128)(2,1)S(1)}, bf16[128,16,256]{2,1,0:T(8,128)(2,1)}, u32[]{:S(2)}) %copy-start.1) | copy-done | bytes 1048600
  11.8 1.3 %decode_held_pages.1 = (bf16[128,256]{1,0:T(8,128)(2,1)S(1)}, f32[16,8,1]{2,1,0:T(8,128)S(1)}, f32[16,8,1]{2,1,0:T(8,128)S(1)}, f32[16,8,256]{2,1,0:T(8,128)S(1)}) custom-call(s32[1]{0:T(128)} %bitcast.own_ref.refs_0_, bf16[8,2048]{1,0:T(8,128)(2,1)S(1)} %copy-done.2, s32[8,32]{1,0:T(8,128)S(1)} %copy-done.3, s32[8,1]{1,0:T(8,128)S(1)} %copy.14.length_ref.refs_5_, ...), custom_call_target="tpu_custom_call" | custom-call | flops 268435456 | bytes 2097152 | tf_op jit(solution)/shard_map/decode_held_pages/pallas_call | solution.py:269
  13.1 3.2 %own_shard.1 = (bf16[2,128,1024]{2,1,0:T(8,128)(2,1)S(1)}, f32[2,1,1024]{2,1,0:T(1,128)S(1)}, f32[2,1,1024]{2,1,0:T(1,128)S(1)}, f32[2,128,1024]{2,1,0:T(8,128)S(1)}) custom-call(s32[1]{0:T(128)} %bitcast.own_ref.refs_0_, s32[1]{0:T(128)S(6)} %copy.20.limit_ref.refs_1_, bf16[128,2048]{1,0:T(8,128)(2,1)S(1)} %copy-done.4, ...), custom_call_target="tpu_custom_call" | custom-call | flops 402653184 | bytes 1048576 | tf_op jit(solution)/shard_map/own_shard/pallas_call | solution.py:256
  16.3 1.3 %collective-permute-done.refs_7_ = bf16[768,256]{1,0:T(8,128)(2,1)S(1)} collective-permute-done((bf16[768,256]{1,0:T(8,128)(2,1)S(1)}, bf16[768,256]{1,0:T(8,128)(2,1)S(1)}, u32[]{:S(2)}, u32[]{:S(2)}) %collective-permute-start) | collective-permute-done | bytes 393248 | tf_op jit(solution)/shard_map/ppermute | solution.py:237
  17.6 0.0 collective-permute-start.1
  17.6 7.2 %collective-permute-done.2.refs_8_ = bf16[768,256]{1,0:T(8,128)(2,1)S(1)} collective-permute-done((bf16[768,256]{1,0:T(8,128)(2,1)S(1)}, bf16[768,256]{1,0:T(8,128)(2,1)S(1)}, u32[]{:S(2)}, u32[]{:S(2)}) %collective-permute-start.2) | collective-permute-done | bytes 393248 | tf_op jit(solution)/shard_map/ppermute | solution.py:238
  24.8 4.6 %shards_1_away.1 = (f32[2,1,1024]{2,1,0:T(1,128)S(1)}, f32[2,1,1024]{2,1,0:T(1,128)S(1)}, f32[2,128,1024]{2,1,0:T(8,128)S(1)}, f32[16,8,1]{2,1,0:T(8,128)S(1)}, ...) custom-call(s32[1]{0:T(128)} %bitcast.own_ref.refs_0_, s32[1]{0:T(128)S(6)} %copy.20.limit_ref.refs_1_, ...), custom_call_target="tpu_custom_call" | custom-call | flops 805306368 | bytes 1048576 | tf_op jit(solution)/shard_map/shards_1_away/pallas_call | solution.py:299
  29.4 4.2 %collective-permute-done.1.refs_7_ = bf16[768,256]{1,0:T(8,128)(2,1)S(1)} collective-permute-done((bf16[768,256]{1,0:T(8,128)(2,1)S(1)}, bf16[768,256]{1,0:T(8,128)(2,1)S(1)}, u32[]{:S(2)}, u32[]{:S(2)}) %collective-permute-start.1) | collective-permute-done | bytes 393248 | tf_op jit(solution)/shard_map/ppermute | solution.py:283
  33.7 4.3 %shards_2_away.1 = (bf16[128,2048]{1,0:T(8,128)(2,1)}, bf16[8,2048]{1,0:T(8,128)(2,1)}) custom-call(s32[1]{0:T(128)} %bitcast.own_ref.refs_0_, s32[1]{0:T(128)S(6)} %copy.20.limit_ref.refs_1_, bf16[2,128,1024]{2,1,0:T(8,128)(2,1)S(1)} %get-tuple-element.23.refs_2_, bf16[128,256]{1,0:T(8,128)(2,1)S(1)} %get-tuple-element.24.refs_3_, s32[8,32]{1,0:T(8,128)S(1)} %copy-done.3, ...), custom_call_target="tpu_custom_call" | custom-call | flops 402653184 | bytes 1048576 | tf_op jit(solution)/shard_map/shards_2_away/pallas_call | solution.py:299
  (15 shorter events, 0.1 us)
Async XLA Ops:
  0.6 0.9 %copy-start.5 = (bf16[256,256]{1,0:T(8,128)(2,1)S(1)}, bf16[256,256]{1,0:T(8,128)(2,1)}, u32[]{:S(2)}) copy-start(bf16[256,256]{1,0:T(8,128)(2,1)} %param.15) | copy-start | bytes 393220
  1.6 0.8 %copy-start.7 = (bf16[128,256]{1,0:T(8,128)(2,1)S(1)}, bf16[128,256]{1,0:T(8,128)(2,1)}, u32[]{:S(2)}) copy-start(bf16[128,256]{1,0:T(8,128)(2,1)} %param.14) | copy-start | bytes 196612
  1.6 0.9 %copy-start.6 = (bf16[256,256]{1,0:T(8,128)(2,1)S(1)}, bf16[256,256]{1,0:T(8,128)(2,1)}, u32[]{:S(2)}) copy-start(bf16[256,256]{1,0:T(8,128)(2,1)} %param.16) | copy-start | bytes 393220
  2.5 5.2 %copy-start.9 = (s32[32]{0:T(128)S(1)}, s32[32]{0:T(128)}, u32[]{:S(2)}) copy-start(s32[32]{0:T(128)} %param.18) | copy-start | bytes 388
  2.5 5.9 %copy-start.8 = (s32[8]{0:T(128)S(1)}, s32[8]{0:T(128)}, u32[]{:S(2)}) copy-start(s32[8]{0:T(128)} %param.23) | copy-start | bytes 100
  2.5 6.2 %copy-start.2 = (bf16[8,2048]{1,0:T(8,128)(2,1)S(1)}, bf16[8,2048]{1,0:T(8,128)(2,1)}, u32[]{:S(2)}) copy-start(bf16[8,2048]{1,0:T(8,128)(2,1)} %q_ref.3) | copy-start | bytes 98308
  2.5 15.1 %collective-permute-start = (bf16[768,256]{1,0:T(8,128)(2,1)S(1)}, bf16[768,256]{1,0:T(8,128)(2,1)S(1)}, u32[]{:S(2)}, u32[]{:S(2)}) collective-permute-start(bf16[768,256]{1,0:T(8,128)(2,1)S(1)} %constant_dynamic-update-slice_fusion.shard_ref), channel_id=1, source_target_pairs={{0,4},{4,8},{8,12},{12,0},{1,5},{5,9},{9,13},{13,1},{2,6},{6,10},{... | collective-permute-start | bytes 1179656 | tf_op jit(solution)/shard_map/ppermute | solution.py:237
  5.6 19.2 %collective-permute-start.2 = (bf16[768,256]{1,0:T(8,128)(2,1)S(1)}, bf16[768,256]{1,0:T(8,128)(2,1)S(1)}, u32[]{:S(2)}, u32[]{:S(2)}) collective-permute-start(bf16[768,256]{1,0:T(8,128)(2,1)S(1)} %constant_dynamic-update-slice_fusion.shard_ref), channel_id=1, source_target_pairs={{0,12},{4,0},{8,4},{12,8},{1,13},{5,1},{9,5},{13,9},{2,14},{6,2},{... | collective-permute-start | bytes 1179656 | tf_op jit(solution)/shard_map/ppermute | solution.py:238
  8.6 0.7 %copy-start.3 = (s32[8,32]{1,0:T(8,128)S(1)}, s32[8,32]{1,0:T(8,128)}, u32[]{:S(2)}) copy-start(s32[8,32]{1,0:T(8,128)} %refs_4_.3) | copy-start | bytes 3076
  9.3 1.2 %copy-start = (bf16[128,16,256]{2,1,0:T(8,128)(2,1)S(1)}, bf16[128,16,256]{2,1,0:T(8,128)(2,1)}, u32[]{:S(2)}) copy-start(bf16[128,16,256]{2,1,0:T(8,128)(2,1)} %pool_k.1) | copy-start | bytes 3145732
  10.5 1.2 %copy-start.1 = (bf16[128,16,256]{2,1,0:T(8,128)(2,1)S(1)}, bf16[128,16,256]{2,1,0:T(8,128)(2,1)}, u32[]{:S(2)}) copy-start(bf16[128,16,256]{2,1,0:T(8,128)(2,1)} %pool_v.1) | copy-start | bytes 3145732
  11.8 1.3 %copy-start.4 = (bf16[128,2048]{1,0:T(8,128)(2,1)S(1)}, bf16[128,2048]{1,0:T(8,128)(2,1)}, u32[]{:S(2)}) copy-start(bf16[128,2048]{1,0:T(8,128)(2,1)} %q_ref.2) | copy-start | bytes 1572868
  17.6 16.0 %collective-permute-start.1 = (bf16[768,256]{1,0:T(8,128)(2,1)S(1)}, bf16[768,256]{1,0:T(8,128)(2,1)S(1)}, u32[]{:S(2)}, u32[]{:S(2)}) collective-permute-start(bf16[768,256]{1,0:T(8,128)(2,1)S(1)} %collective-permute-done.refs_7_), channel_id=1, source_target_pairs={{0,4},{4,8},{8,12},{12,0},{1,5},{5,9},{9,13},{13,1},{2,6},{6,10},{... | collective-permute-start | bytes 1179656 | tf_op jit(solution)/shard_map/ppermute | solution.py:283

commit v3 on v2

v3 whole, which is shorter than its diff:
```python
import functools

import jax
import jax.numpy as jnp
from jax import lax
from jax.experimental import pallas as pl
from jax.experimental.pallas import tpu as pltpu
from jax.sharding import PartitionSpec as P

HEADS = 64
KV_HEADS = 8
HEAD_DIM = 128
GROUP = HEADS // KV_HEADS
PAGE = 16
P_DEV = 8
EXP2_SCALE = HEAD_DIM ** (-0.5) * 1.4426950408889634
HIDDEN = -1e30
VMEM_BYTES = 48 * 1024 * 1024

VMEM = pl.BlockSpec(memory_space=pltpu.VMEM)
SMEM = pl.BlockSpec(memory_space=pltpu.SMEM)
HBM = pl.BlockSpec(memory_space=pltpu.HBM)


def attend(qt_ref, cols, keys, values_t, state):
    tokens = keys.shape[1] - HEAD_DIM
    queries = qt_ref[:, cols]
    place = lax.broadcasted_iota(jnp.int32, (tokens, queries.shape[1]), 0)
    token = lax.rem(lax.broadcasted_iota(jnp.int32, (tokens, queries.shape[1]), 1), tokens)
    pick = jnp.where(place == token, jnp.float32(1.0), jnp.float32(0.0)).astype(jnp.bfloat16)
    queries = jnp.concatenate([queries, pick], axis=0)
    scores = jnp.dot(keys, queries, preferred_element_type=jnp.float32)
    high = jnp.max(scores, axis=0, keepdims=True)
    if state is not None:
        old_high, old_total, old_accum = state
        high = jnp.maximum(high, old_high)
    weights = jnp.exp2((scores - high) * EXP2_SCALE)
    total = jnp.sum(weights, axis=0, keepdims=True)
    accum = jnp.dot(values_t, weights.astype(jnp.bfloat16), preferred_element_type=jnp.float32)
    if state is not None:
        decay = jnp.exp2((old_high - high) * EXP2_SCALE)
        total = total + old_total * decay
        accum = accum + old_accum * decay
    return high, total, accum


def hidden(seen):
    return jnp.where(seen, jnp.float32(0.0), jnp.float32(HIDDEN)).astype(jnp.bfloat16)


def shard_mask(shard, own, limit, tokens, keys):
    c_rows = keys - tokens
    place = lax.broadcasted_iota(jnp.int32, (keys, tokens), 0)
    token = lax.broadcasted_iota(jnp.int32, (keys, tokens), 1)
    stretch = place - token <= (own - shard) * tokens
    cached = place - tokens < limit - shard * c_rows
    return hidden(((place < tokens) & stretch) | ((place >= tokens) & cached))


def slot_row(targets_ref, shard, own, tokens, pool):
    page = lax.broadcasted_iota(jnp.int32, (1, tokens), 1) // PAGE
    slots = jnp.full((1, tokens), -1, jnp.int32)
    for index in range(tokens // PAGE):
        target = targets_ref[shard * (tokens // PAGE) + index]
        slot = jnp.where(target // P_DEV == own, pool + target % P_DEV, -1)
        slots = jnp.where(page == index, slot, slots)
    return slots


def length_column(length_ref):
    rows = length_ref.shape[0]
    place = lax.broadcasted_iota(jnp.int32, (rows, 1), 0)
    lengths = jnp.zeros((rows, 1), jnp.int32)
    for row in range(rows):
        lengths = jnp.where(place == row, length_ref[row], lengths)
    return lengths


def tally_of(lists, lengths, slot):
    rows, span = lists.shape
    tokens = slot.shape[1]
    slot = jnp.broadcast_to(slot, (rows, tokens))
    offset = lax.rem(lax.broadcasted_iota(jnp.int32, (rows, tokens), 1), PAGE)
    tally = jnp.zeros((rows, tokens), jnp.float32)
    for entry in range(span):
        hit = (slot == lists[:, entry : entry + 1]) & (offset < lengths - entry * PAGE)
        tally = tally + jnp.where(hit, jnp.float32(1.0), jnp.float32(0.0))
    return tally[None]


def decode_attend(queries, parts, state):
    done = []
    for keys, values, tally in parts:
        scores = lax.dot_general(
            queries, keys, (((1,), (1,)), ((), ())), preferred_element_type=jnp.float32
        ).reshape(-1, tally.shape[1], tally.shape[2])
        done.append((jnp.where(tally > 0, scores, jnp.float32(HIDDEN)), tally, values))
    highs = [jnp.max(scores, axis=-1, keepdims=True) for scores, _, _ in done]
    if state is not None:
        old_high, old_total, old_mixed = state
        highs.append(old_high)
    high = functools.reduce(jnp.maximum, highs)
    total, mixed = 0.0, 0.0
    if state is not None:
        decay = jnp.exp2((old_high - high) * EXP2_SCALE)
        total = old_total * decay
        mixed = old_mixed * decay
    for scores, tally, values in done:
        weights = jnp.exp2((scores - high) * EXP2_SCALE) * tally
        total = total + jnp.sum(weights, axis=-1, keepdims=True)
        mixed = mixed + jnp.dot(
            weights.reshape(queries.shape[0], -1).astype(jnp.bfloat16),
            values,
            preferred_element_type=jnp.float32,
        ).reshape(high.shape[0], high.shape[1], -1)
    return high, total, mixed


def pack_kernel(sk_ref, ck_ref, sv_ref, cv_ref, *refs):
    outs, sems = refs[:-1], refs[-1]
    copies = []
    for head, out_ref in enumerate(outs):
        feats = pl.ds(head * HEAD_DIM, HEAD_DIM)
        start = 0
        for place, ref in enumerate((sk_ref, ck_ref, sv_ref, cv_ref)):
            rows = ref.shape[0]
            copies.append(
                pltpu.make_async_copy(
                    ref.at[:, feats], out_ref.at[pl.ds(start, rows), :], sems.at[head, place]
                )
            )
            start += rows
    for copy in copies:
        copy.start()
    for copy in copies:
        copy.wait()


def own_kernel(kv_local, own_ref, limit_ref, q_ref, *refs):
    shard_refs, outs = refs[:kv_local], refs[kv_local:]
    tokens = q_ref.shape[0]
    rows = GROUP * tokens
    half = shard_refs[0].shape[0] // 2
    width = min(2 * tokens, rows)
    mask = shard_mask(own_ref[0], own_ref[0], limit_ref[0], tokens, half)
    for head in range(kv_local):
        qt_ref, high_ref, total_ref, accum_ref = outs[4 * head : 4 * head + 4]
        for sub in range(GROUP):
            col = (head * GROUP + sub) * HEAD_DIM
            qt_ref[:, sub * tokens : (sub + 1) * tokens] = q_ref[:, col : col + HEAD_DIM].T
        keys = jnp.concatenate([shard_refs[head][:half], mask], axis=1)
        values_t = shard_refs[head][half:].T
        for start in range(0, rows, width):
            cols = slice(start, start + width)
            high, total, accum = attend(qt_ref, cols, keys, values_t, None)
            high_ref[:, cols] = high
            total_ref[:, cols] = total
            accum_ref[:, cols] = accum


def held_kernel(kv_local, own_ref, targets_ref, length_ref, q_ref, lists_ref, pool_k, pool_v, *refs):
    shard_refs = refs[:kv_local]
    outs = refs[kv_local:-3]
    keys_ref, values_ref, sems = refs[-3:]
    copies = []
    for place, (source, target) in enumerate(((pool_k, keys_ref), (pool_v, values_ref))):
        pages = source.shape[0] // 2
        for part in range(2):
            span = pl.ds(part * pages, pages)
            copies.append(pltpu.make_async_copy(source.at[span], target.at[span], sems.at[place, part]))
    for copy in copies:
        copy.start()
    dec_rows = q_ref.shape[0]
    half = shard_refs[0].shape[0] // 2
    pool = keys_ref.shape[0]
    held = pool * PAGE
    tokens = PAGE * P_DEV
    own = own_ref[0]
    lists = lists_ref[...]
    lengths = length_column(length_ref)
    held_tally = tally_of(lists, lengths, lax.broadcasted_iota(jnp.int32, (1, held), 1) // PAGE)
    own_tally = tally_of(lists, lengths, slot_row(targets_ref, own, own, tokens, pool))
    queries = q_ref[...].astype(jnp.float32)
    for head in range(kv_local):
        pieces = [
            queries[:, (head * GROUP + sub) * HEAD_DIM : (head * GROUP + sub + 1) * HEAD_DIM]
            for sub in range(GROUP)
        ]
        outs[4 * head][...] = jnp.concatenate(pieces, axis=0).astype(jnp.bfloat16)
    for copy in copies:
        copy.wait()
    for head in range(kv_local):
        feats = slice(head * HEAD_DIM, (head + 1) * HEAD_DIM)
        rows_ref, high_ref, total_ref, mixed_ref = outs[4 * head : 4 * head + 4]
        parts = [
            (keys_ref[:, :, feats].reshape(held, -1), values_ref[:, :, feats].reshape(held, -1), held_tally),
            (shard_refs[head][:tokens], shard_refs[head][half : half + tokens], own_tally),
        ]
        high_ref[...], total_ref[...], mixed_ref[...] = decode_attend(rows_ref[...], parts, None)


def hop_kernel(count, hops, pool, last, first_out, *refs):
    own_ref, limit_ref, targets_ref, length_ref, lists_ref = refs[:5]
    shard_refs = refs[5 : 5 + len(hops)]
    qt_ref, high_in, total_in, accum_in, dec_q, dec_high, dec_total, dec_mixed = refs[5 + len(hops) : 13 + len(hops)]
    outs = refs[first_out:]
    own = own_ref[0]
    limit = limit_ref[0]
    rows = qt_ref.shape[1]
    tokens = rows // GROUP
    half = shard_refs[0].shape[0] // 2
    width = min(2 * tokens, rows)
    shards = [lax.rem(own + hop + count, count) for hop in hops]

    lists = lists_ref[...]
    lengths = length_column(length_ref)
    parts = [
        (
            ref[:tokens],
            ref[half : half + tokens],
            tally_of(lists, lengths, slot_row(targets_ref, shard, own, tokens, pool)),
        )
        for shard, ref in zip(shards, shard_refs)
    ]
    state = decode_attend(dec_q[...], parts, (dec_high[...], dec_total[...], dec_mixed[...]))
    if last:
        _, total, mixed = state
        for sub in range(GROUP):
            outs[1][:, sub * HEAD_DIM : (sub + 1) * HEAD_DIM] = (mixed[sub] / total[sub]).astype(jnp.bfloat16)
    else:
        outs[3][...], outs[4][...], outs[5][...] = state

    mask = jnp.concatenate([shard_mask(shard, own, limit, tokens, half) for shard in shards], axis=0)
    keys = jnp.concatenate([jnp.concatenate([ref[:half] for ref in shard_refs], axis=0), mask], axis=1)
    values_t = jnp.concatenate([ref[half:] for ref in shard_refs], axis=0).T
    for start in range(0, rows, width):
        cols = slice(start, start + width)
        state = (high_in[:, cols], total_in[:, cols], accum_in[:, cols])
        high, total, accum = attend(qt_ref, cols, keys, values_t, state)
        if last:
            mixed = (accum * (1.0 / total)).astype(jnp.bfloat16)
            for piece in range(width // tokens):
                col = (start // tokens + piece) * HEAD_DIM
                outs[0][:, col : col + HEAD_DIM] = mixed[:, piece * tokens : (piece + 1) * tokens].T
        else:
            outs[0][:, cols] = high
            outs[1][:, cols] = total
            outs[2][:, cols] = accum


def per_device(
    count,
    queries,
    stretch_keys,
    stretch_values,
    cache_keys,
    cache_values,
    prefix_length,
    page_targets,
    pool_keys,
    pool_values,
    decode_queries,
    page_lists,
    context_length,
):
    own = lax.axis_index("ctx")
    own_array = jnp.full((1,), own, jnp.int32)
    tokens, width = queries.shape
    kv_local = stretch_keys.shape[1] // HEAD_DIM
    rows = GROUP * tokens
    dec_rows = decode_queries.shape[0]
    half = tokens + cache_keys.shape[0]
    pool = pool_keys.shape[0]
    f32, bf16 = jnp.float32, jnp.bfloat16
    params = pltpu.CompilerParams(vmem_limit_bytes=VMEM_BYTES)
    up_pairs = [(i, (i + 1) % count) for i in range(count)]
    down_pairs = [(i, (i - 1) % count) for i in range(count)]
    shape = jax.ShapeDtypeStruct

    def cost(keys):
        pairs = rows * keys
        return pl.CostEstimate(
            flops=4 * pairs * HEAD_DIM, bytes_accessed=4 * rows * HEAD_DIM, transcendentals=pairs
        )

    shard = pl.pallas_call(
        pack_kernel,
        out_shape=(shape((2 * half, HEAD_DIM), bf16),) * kv_local,
        in_specs=[HBM] * 4,
        out_specs=(HBM,) * kv_local,
        scratch_shapes=[pltpu.SemaphoreType.DMA((kv_local, 4))],
        name="pack_own_shard",
    )(stretch_keys, cache_keys, stretch_values, cache_values)

    ups = [list(shard), [lax.ppermute(piece, "ctx", up_pairs) for piece in shard]]

    state_shapes = (shape((1, rows), f32), shape((1, rows), f32), shape((HEAD_DIM, rows), f32))
    dec_shapes = (
        shape((GROUP, dec_rows, 1), f32),
        shape((GROUP, dec_rows, 1), f32),
        shape((GROUP, dec_rows, HEAD_DIM), f32),
    )
    results = pl.pallas_call(
        functools.partial(own_kernel, kv_local),
        out_shape=((shape((HEAD_DIM, rows), bf16),) + state_shapes) * kv_local,
        in_specs=[SMEM, SMEM] + [VMEM] * (1 + kv_local),
        out_specs=(VMEM,) * (4 * kv_local),
        compiler_params=params,
        cost_estimate=cost(half * kv_local),
        name="own_shard",
    )(own_array, prefix_length, queries, *shard)
    states = [list(results[4 * head : 4 * head + 4]) for head in range(kv_local)]

    sent_down, states = lax.optimization_barrier((list(shard), states))
    downs = [sent_down, [lax.ppermute(piece, "ctx", down_pairs) for piece in sent_down]]

    results = pl.pallas_call(
        functools.partial(held_kernel, kv_local),
        out_shape=((shape((GROUP * dec_rows, HEAD_DIM), bf16),) + dec_shapes) * kv_local,
        in_specs=[SMEM] * 3 + [VMEM] * 2 + [HBM] * 2 + [VMEM] * kv_local,
        out_specs=(VMEM,) * (4 * kv_local),
        scratch_shapes=[
            pltpu.VMEM(pool_keys.shape, bf16),
            pltpu.VMEM(pool_values.shape, bf16),
            pltpu.SemaphoreType.DMA((2, 2)),
        ],
        compiler_params=params,
        cost_estimate=pl.CostEstimate(
            flops=4 * 128 * 2048 * 256, bytes_accessed=4 * pool_keys.size, transcendentals=128 * 2560
        ),
        name="decode_held_pages",
    )(
        own_array, page_targets, context_length, decode_queries, page_lists, pool_keys, pool_values, *shard
    )
    dec_states = [list(results[4 * head : 4 * head + 4]) for head in range(kv_local)]

    for head in range(kv_local):
        ups[1][head], dec_states[head] = lax.optimization_barrier((ups[1][head], dec_states[head]))
    for hop in range(2, count // 2 + 1):
        ups.append([lax.ppermute(piece, "ctx", up_pairs) for piece in ups[-1]])
        if hop <= (count - 1) // 2:
            downs.append([lax.ppermute(piece, "ctx", down_pairs) for piece in downs[-1]])

    outputs = None
    for hop in range(1, count // 2 + 1):
        last = hop == count // 2
        hops = [-hop] + ([hop] if hop < len(downs) else [])
        for head in range(kv_local):
            operands = [own_array, prefix_length, page_targets, context_length, page_lists, ups[hop][head]]
            if hop < len(downs):
                operands.append(downs[hop][head])
            operands += states[head] + dec_states[head]
            in_specs = [SMEM] * 4 + [VMEM] * (len(operands) - 4)
            options = {}
            if last:
                out_shape = (shape((tokens, width), bf16), shape(decode_queries.shape, bf16))
                out_specs = (
                    pl.BlockSpec((tokens, rows), lambda step, head=head: (0, head)),
                    pl.BlockSpec((dec_rows, GROUP * HEAD_DIM), lambda step, head=head: (0, head)),
                )
                options["grid"] = (1,)
                if outputs is not None:
                    options["input_output_aliases"] = {len(operands): 0, len(operands) + 1: 1}
                    operands += list(outputs)
                    in_specs += [pl.BlockSpec(memory_space=pl.ANY)] * 2
            else:
                out_shape = state_shapes + dec_shapes
                out_specs = (VMEM,) * len(out_shape)
            results = pl.pallas_call(
                functools.partial(hop_kernel, count, hops, pool, last, len(operands)),
                out_shape=out_shape,
                in_specs=in_specs,
                out_specs=out_specs,
                compiler_params=params,
                cost_estimate=cost(half * len(hops)),
                name="head_" + str(head) + "_shards_" + str(hop) + "_away",
                **options,
            )(*operands)
            if last:
                outputs = results
            else:
                states[head][1:] = results[:3]
                dec_states[head][1:] = results[3:]
    return tuple(outputs)


def solution(mesh):
    in_specs = (
        P(("groups", "ctx"), "head"),
        P(("groups", "ctx"), "head"),
        P(("groups", "ctx"), "head"),
        P(("groups", "ctx"), "head"),
        P(("groups", "ctx"), "head"),
        P("groups"),
        P("groups"),
        P(("groups", "ctx"), None, "head"),
        P(("groups", "ctx"), None, "head"),
        P(("groups", "ctx"), "head"),
        P(("groups", "ctx"), None),
        P(("groups", "ctx")),
    )
    out_specs = (P(("groups", "ctx"), "head"), P(("groups", "ctx"), "head"))
    return jax.shard_map(
        functools.partial(per_device, mesh.shape["ctx"]),
        mesh=mesh,
        in_specs=in_specs,
        out_specs=out_specs,
        check_vma=False,
    )
```

time: 38.2 us -> 52.6 us (1.38)
  the two profiles are of different devices: /device:TPU:0 before, /device:TPU:8 now
where the time goes in v3:
time: 52.6 us; the launch traced here: 52.4 us
  Pallas kernels  33.1 us (63%)
  waiting for transfers between devices  8.29 us (16%)
  starting transfers between devices  7.35 us (14%)
  local copies, waits for them, and re-layouts  2.28 us (4%)
  between operations  1.42 us (3%)
    pallas_call x1, Pallas kernels, per_device(): pl.pallas_call(pack_kernel, out_shape=(shape((2 * half, HEAD_DIM), bf16),...  13.1 us
    pallas_call x4, Pallas kernels, per_device(): pl.pallas_call(functools.partial(hop_kernel, count, hops, pool, last, len...  12.9 us
    ppermute x2, waiting for transfers between devices, per_device(): lax.ppermute(piece, 'ctx', down_pairs)  8.28 us
    pallas_call x1, Pallas kernels, per_device(): pl.pallas_call(functools.partial(own_kernel, kv_local), out_shape=((shape...  4.27 us
    ppermute x2, starting transfers between devices, per_device(): lax.ppermute(piece, 'ctx', up_pairs)  3.21 us
    pallas_call x1, Pallas kernels, per_device(): pl.pallas_call(functools.partial(held_kernel, kv_local), out_shape=((shap...  2.79 us
    ppermute x2, starting transfers between devices, per_device(): lax.ppermute(piece, 'ctx', down_pairs)  2.75 us
    unnamed x14, local copies, waits for them, and re-layouts  2.28 us
  transfers between devices with their start and end apart: 6, of which 1 were waited for; matrix products, arithmetic and copies ran while one was open for 0% of the time, Pallas kernels for 32%

profile of v3, /device:TPU:8, one launch (start us, length us, event | category | flops | bytes accessed | tf_op | source)
XLA Modules:
  0.0 52.4 jit_solution(2532315522097625207)
XLA Ops:
  0.6 13.1 %pack_own_shard.1 = (bf16[768,128]{1,0:T(8,128)(2,1)}, bf16[768,128]{1,0:T(8,128)(2,1)}) custom-call(bf16[128,256]{1,0:T(8,128)(2,1)} %sk_ref.1, bf16[256,256]{1,0:T(8,128)(2,1)} %ck_ref.1, bf16[128,256]{1,0:T(8,128)(2,1)} %sv_ref.1, bf16[256,256]{1,0:T(8,128)(2,1)} %cv_ref.1), custom_call_target="tpu_custom_call" | custom-call | tf_op jit(solution)/shard_map/pack_own_shard/pallas_call | solution.py:286
  13.7 1.6 %collective-permute-start.3 = (bf16[768,128]{1,0:T(8,128)(2,1)}, bf16[768,128]{1,0:T(8,128)(2,1)S(1)}, u32[]{:S(2)}, u32[]{:S(2)}) collective-permute-start(bf16[768,128]{1,0:T(8,128)(2,1)} %get-tuple-element.90.refs_0_), channel_id=1, source_target_pairs={{0,4},{4,8},{8,12},{12,0},{1,5},{5,9},{9,13},{13,1},{2,6},{6,10},{... | collective-permute-start | bytes 589832 | tf_op jit(solution)/shard_map/ppermute | solution.py:295
  15.4 1.6 %collective-permute-start = (bf16[768,128]{1,0:T(8,128)(2,1)}, bf16[768,128]{1,0:T(8,128)(2,1)S(1)}, u32[]{:S(2)}, u32[]{:S(2)}) collective-permute-start(bf16[768,128]{1,0:T(8,128)(2,1)} %get-tuple-element.70.refs_1_), channel_id=1, source_target_pairs={{0,4},{4,8},{8,12},{12,0},{1,5},{5,9},{9,13},{13,1},{2,6},{6,10},{... | collective-permute-start | bytes 589832 | tf_op jit(solution)/shard_map/ppermute | solution.py:295
  17.6 0.0 copy-start.6
  17.6 1.0 %copy-done.6 = bf16[128,2048]{1,0:T(8,128)(2,1)S(1)} copy-done((bf16[128,2048]{1,0:T(8,128)(2,1)S(1)}, bf16[128,2048]{1,0:T(8,128)(2,1)}, u32[]{:S(2)}) %copy-start.6) | copy-done | bytes 524312
  18.6 4.3 %own_shard.1 = (bf16[128,1024]{1,0:T(8,128)(2,1)S(1)}, f32[1,1024]{1,0:T(1,128)S(1)}, f32[1,1024]{1,0:T(1,128)S(1)}, f32[128,1024]{1,0:T(8,128)S(1)}, bf16[128,1...) custom-call(s32[1]{0:T(128)} %bitcast.own_ref.refs_0_, ...), custom_call_target="tpu_custom_call" | custom-call | flops 402653184 | bytes 524288 | tf_op jit(solution)/shard_map/own_shard/pallas_call | solution.py:303
  22.9 0.0 copy-start.2
  22.9 0.0 copy-start.4
  22.9 0.0 copy-start.5
  23.0 0.5 collective-permute-start.5
  23.5 2.2 %collective-permute-start.2 = (bf16[768,128]{1,0:T(8,128)(2,1)}, bf16[768,128]{1,0:T(8,128)(2,1)S(1)}, u32[]{:S(2)}, u32[]{:S(2)}) collective-permute-start(bf16[768,128]{1,0:T(8,128)(2,1)} %get-tuple-element.70.refs_1_), channel_id=1, source_target_pairs={{0,12},{4,0},{8,4},{12,8},{1,13},{5,1},{9,5},{13,9},{2,14},{6,2},{... | collective-permute-start | bytes 589832 | tf_op jit(solution)/shard_map/ppermute | solution.py:315
  25.7 0.0 copy-start.1
  25.7 1.2 %copy-done.1 = bf16[128,16,256]{2,1,0:T(8,128)(2,1)S(1)} copy-done((bf16[128,16,256]{2,1,0:T(8,128)(2,1)S(1)}, bf16[128,16,256]{2,1,0:T(8,128)(2,1)}, u32[]{:S(2)}) %copy-start.1) | copy-done | bytes 1048600
  27.0 2.8 %decode_held_pages.1 = (bf16[64,128]{1,0:T(8,128)(2,1)S(1)}, f32[8,8,1]{2,1,0:T(8,128)S(1)}, f32[8,8,1]{2,1,0:T(8,128)S(1)}, f32[8,8,128]{2,1,0:T(8,128)S(1)}, b...) custom-call(s32[1]{0:T(128)} %bitcast.own_ref.refs_0_, ...), custom_call_target="tpu_custom_call" | custom-call | flops 268435456 | bytes 2097152 | tf_op jit(solution)/shard_map/decode_held_pages/pallas_call | solution.py:317
  29.8 0.0 collective-permute-done.3.refs_5_
  29.8 0.1 collective-permute-start.4
  29.8 0.0 collective-permute-done.refs_5_
  29.8 1.3 %collective-permute-start.1 = (bf16[768,128]{1,0:T(8,128)(2,1)S(1)}, bf16[768,128]{1,0:T(8,128)(2,1)S(1)}, u32[]{:S(2)}, u32[]{:S(2)}) collective-permute-start(bf16[768,128]{1,0:T(8,128)(2,1)S(1)} %collective-permute-done.refs_5_), channel_id=1, source_target_pairs={{0,4},{4,8},{8,12},{12,0},{1,5},{5,9},{9,13},{13,1},{2,6},{6,10},{... | collective-permute-start | bytes 589832 | tf_op jit(solution)/shard_map/ppermute | solution.py:340
  31.2 0.0 collective-permute-done.5.refs_6_
  31.2 3.2 %head_0_shards_1_away.1 = (f32[1,1024]{1,0:T(1,128)S(1)}, f32[1,1024]{1,0:T(1,128)S(1)}, f32[128,1024]{1,0:T(8,128)S(1)}, f32[8,8,1]{2,1,0:T(8,128)S(1)}, f32[8,...) custom-call(s32[1]{0:T(128)} %bitcast.own_ref.refs_0_, s32[1]{0:T(128)S(6)} %copy.18.limit_ref.refs_1_, s32[32]{0:T(128)S(1)} %copy-done.4, ...), custom_call_target="tpu_custom_call" | custom-call | flops 402653184 | bytes 524288 | tf_op jit(solution)/shard_map/head_0_shards_1_away/pallas_call | solution.py:369
  34.4 8.3 %collective-permute-done.2.refs_6_ = bf16[768,128]{1,0:T(8,128)(2,1)S(1)} collective-permute-done((bf16[768,128]{1,0:T(8,128)(2,1)}, bf16[768,128]{1,0:T(8,128)(2,1)S(1)}, u32[]{:S(2)}, u32[]{:S(2)}) %collective-permute-start.2) | collective-permute-done | bytes 196640 | tf_op jit(solution)/shard_map/ppermute | solution.py:315
  42.7 3.2 %head_1_shards_1_away.1 = (f32[1,1024]{1,0:T(1,128)S(1)}, f32[1,1024]{1,0:T(1,128)S(1)}, f32[128,1024]{1,0:T(8,128)S(1)}, f32[8,8,1]{2,1,0:T(8,128)S(1)}, f32[8,...) custom-call(s32[1]{0:T(128)} %bitcast.own_ref.refs_0_, s32[1]{0:T(128)S(6)} %copy.18.limit_ref.refs_1_, s32[32]{0:T(128)S(1)} %copy-done.4, ...), custom_call_target="tpu_custom_call" | custom-call | flops 402653184 | bytes 524288 | tf_op jit(solution)/shard_map/head_1_shards_1_away/pallas_call | solution.py:369
  45.9 3.3 %head_0_shards_2_away.1 = (bf16[128,2048]{1,0:T(8,128)(2,1)}, bf16[8,2048]{1,0:T(8,128)(2,1)}) custom-call(s32[1]{0:T(128)} %bitcast.own_ref.refs_0_, s32[1]{0:T(128)S(6)} %copy.18.limit_ref.refs_1_, s32[32]{0:T(128)S(1)} %copy-done.4, s32[8]{0:T(128)S(1)} %copy-done.5, s32[8,32]{1,0:T(8,128)S(1)} %copy-done.2, ...), custom_call_target="tpu_custom_call" | custom-call | flops 201326592 | bytes 524288 | tf_op jit(solution)/shard_map/head_0_shards_2_away/pallas_call | solution.py:369
  49.1 3.2 %head_1_shards_2_away.1 = (bf16[128,2048]{1,0:T(8,128)(2,1)}, bf16[8,2048]{1,0:T(8,128)(2,1)}) custom-call(s32[1]{0:T(128)} %bitcast.own_ref.refs_0_, s32[1]{0:T(128)S(6)} %copy.18.limit_ref.refs_1_, s32[32]{0:T(128)S(1)} %copy-done.4, s32[8]{0:T(128)S(1)} %copy-done.5, s32[8,32]{1,0:T(8,128)S(1)} %copy-done.2, ...), custom_call_target="tpu_custom_call", output_to_operand_aliasing={{0}: (14, {}), {1}: (15, {})} | custom-call | flops 201326592 | bytes 524288 | tf_op jit(solution)/shard_map/head_1_shards_2_away/pallas_call | solution.py:369
  (9 shorter events, 0.0 us)
Async XLA Ops:
  0.6 25.1 %copy-start = (bf16[128,16,256]{2,1,0:T(8,128)(2,1)S(1)}, bf16[128,16,256]{2,1,0:T(8,128)(2,1)}, u32[]{:S(2)}) copy-start(bf16[128,16,256]{2,1,0:T(8,128)(2,1)} %pool_k.1) | copy-start | bytes 3145732
  13.7 16.0 %collective-permute-start.3 = (bf16[768,128]{1,0:T(8,128)(2,1)}, bf16[768,128]{1,0:T(8,128)(2,1)S(1)}, u32[]{:S(2)}, u32[]{:S(2)}) collective-permute-start(bf16[768,128]{1,0:T(8,128)(2,1)} %get-tuple-element.90.refs_0_), channel_id=1, source_target_pairs={{0,4},{4,8},{8,12},{12,0},{1,5},{5,9},{9,13},{13,1},{2,6},{6,10},{... | collective-permute-start | bytes 589832 | tf_op jit(solution)/shard_map/ppermute | solution.py:295
  15.4 14.5 %collective-permute-start = (bf16[768,128]{1,0:T(8,128)(2,1)}, bf16[768,128]{1,0:T(8,128)(2,1)S(1)}, u32[]{:S(2)}, u32[]{:S(2)}) collective-permute-start(bf16[768,128]{1,0:T(8,128)(2,1)} %get-tuple-element.70.refs_1_), channel_id=1, source_target_pairs={{0,4},{4,8},{8,12},{12,0},{1,5},{5,9},{9,13},{13,1},{2,6},{6,10},{... | collective-permute-start | bytes 589832 | tf_op jit(solution)/shard_map/ppermute | solution.py:295
  17.6 1.0 %copy-start.6 = (bf16[128,2048]{1,0:T(8,128)(2,1)S(1)}, bf16[128,2048]{1,0:T(8,128)(2,1)}, u32[]{:S(2)}) copy-start(bf16[128,2048]{1,0:T(8,128)(2,1)} %q_ref.3) | copy-start | bytes 1572868
  18.6 7.1 %copy-start.3 = (bf16[8,2048]{1,0:T(8,128)(2,1)S(1)}, bf16[8,2048]{1,0:T(8,128)(2,1)}, u32[]{:S(2)}) copy-start(bf16[8,2048]{1,0:T(8,128)(2,1)} %q_ref.2) | copy-start | bytes 98308
  22.9 2.8 %copy-start.2 = (s32[8,32]{1,0:T(8,128)S(1)}, s32[8,32]{1,0:T(8,128)}, u32[]{:S(2)}) copy-start(s32[8,32]{1,0:T(8,128)} %refs_4_.7) | copy-start | bytes 3076
  22.9 2.8 %copy-start.4 = (s32[32]{0:T(128)S(1)}, s32[32]{0:T(128)}, u32[]{:S(2)}) copy-start(s32[32]{0:T(128)} %refs_2_.7) | copy-start | bytes 388
  22.9 2.8 %copy-start.5 = (s32[8]{0:T(128)S(1)}, s32[8]{0:T(128)}, u32[]{:S(2)}) copy-start(s32[8]{0:T(128)} %refs_3_.7) | copy-start | bytes 100
  23.0 8.2 %collective-permute-start.5 = (bf16[768,128]{1,0:T(8,128)(2,1)}, bf16[768,128]{1,0:T(8,128)(2,1)S(1)}, u32[]{:S(2)}, u32[]{:S(2)}) collective-permute-start(bf16[768,128]{1,0:T(8,128)(2,1)} %get-tuple-element.90.refs_0_), channel_id=1, source_target_pairs={{0,12},{4,0},{8,4},{12,8},{1,13},{5,1},{9,5},{13,9},{2,14},{6,2},{... | collective-permute-start | bytes 589832 | tf_op jit(solution)/shard_map/ppermute | solution.py:315
  23.5 19.2 %collective-permute-start.2 = (bf16[768,128]{1,0:T(8,128)(2,1)}, bf16[768,128]{1,0:T(8,128)(2,1)S(1)}, u32[]{:S(2)}, u32[]{:S(2)}) collective-permute-start(bf16[768,128]{1,0:T(8,128)(2,1)} %get-tuple-element.70.refs_1_), channel_id=1, source_target_pairs={{0,12},{4,0},{8,4},{12,8},{1,13},{5,1},{9,5},{13,9},{2,14},{6,2},{... | collective-permute-start | bytes 589832 | tf_op jit(solution)/shard_map/ppermute | solution.py:315
  25.7 1.2 %copy-start.1 = (bf16[128,16,256]{2,1,0:T(8,128)(2,1)S(1)}, bf16[128,16,256]{2,1,0:T(8,128)(2,1)}, u32[]{:S(2)}) copy-start(bf16[128,16,256]{2,1,0:T(8,128)(2,1)} %pool_v.1) | copy-start | bytes 3145732
  29.8 16.1 %collective-permute-start.4 = (bf16[768,128]{1,0:T(8,128)(2,1)S(1)}, bf16[768,128]{1,0:T(8,128)(2,1)S(1)}, u32[]{:S(2)}, u32[]{:S(2)}) collective-permute-start(bf16[768,128]{1,0:T(8,128)(2,1)S(1)} %collective-permute-done.3.refs_5_), channel_id=1, source_target_pairs={{0,4},{4,8},{8,12},{12,0},{1,5},{5,9},{9,13},{13,1},{2,6},{6,10},{... | collective-permute-start | bytes 589832 | tf_op jit(solution)/shard_map/ppermute | solution.py:340
  29.8 19.3 %collective-permute-start.1 = (bf16[768,128]{1,0:T(8,128)(2,1)S(1)}, bf16[768,128]{1,0:T(8,128)(2,1)S(1)}, u32[]{:S(2)}, u32[]{:S(2)}) collective-permute-start(bf16[768,128]{1,0:T(8,128)(2,1)S(1)} %collective-permute-done.refs_5_), channel_id=1, source_target_pairs={{0,4},{4,8},{8,12},{12,0},{1,5},{5,9},{9,13},{13,1},{2,6},{6,10},{... | collective-permute-start | bytes 589832 | tf_op jit(solution)/shard_map/ppermute | solution.py:340

commit v4 on v0

v4 whole, which is shorter than its diff:
```python
import functools

import jax
import jax.numpy as jnp
from jax import lax
from jax.experimental import pallas as pl
from jax.experimental.pallas import tpu as pltpu
from jax.sharding import PartitionSpec as P

HEADS = 64
KV_HEADS = 8
HEAD_DIM = 128
GROUP = HEADS // KV_HEADS
PAGE = 16
P_DEV = 8
EXP2_SCALE = HEAD_DIM ** (-0.5) * 1.4426950408889634
HIDDEN = -1e30
VMEM_BYTES = 48 * 1024 * 1024

VMEM = pl.BlockSpec(memory_space=pltpu.VMEM)
SMEM = pl.BlockSpec(memory_space=pltpu.SMEM)
HBM = pl.BlockSpec(memory_space=pltpu.HBM)


def attend(qt_ref, cols, keys, values_t, state):
    tokens = keys.shape[1] - HEAD_DIM
    queries = qt_ref[:, cols]
    place = lax.broadcasted_iota(jnp.int32, (tokens, queries.shape[1]), 0)
    token = lax.rem(lax.broadcasted_iota(jnp.int32, (tokens, queries.shape[1]), 1), tokens)
    pick = jnp.where(place == token, jnp.float32(1.0), jnp.float32(0.0)).astype(jnp.bfloat16)
    queries = jnp.concatenate([queries, pick], axis=0)
    scores = jnp.dot(keys, queries, preferred_element_type=jnp.float32)
    high = jnp.max(scores, axis=0, keepdims=True)
    if state is not None:
        old_high, old_total, old_accum = state
        high = jnp.maximum(high, old_high)
    weights = jnp.exp2((scores - high) * EXP2_SCALE)
    total = jnp.sum(weights, axis=0, keepdims=True)
    accum = jnp.dot(values_t, weights.astype(jnp.bfloat16), preferred_element_type=jnp.float32)
    if state is not None:
        decay = jnp.exp2((old_high - high) * EXP2_SCALE)
        total = total + old_total * decay
        accum = accum + old_accum * decay
    return high, total, accum


def hidden(seen):
    return jnp.where(seen, jnp.float32(0.0), jnp.float32(HIDDEN)).astype(jnp.bfloat16)


def stretch_mask(shard, own, tokens):
    place = lax.broadcasted_iota(jnp.int32, (tokens, tokens), 0)
    token = lax.broadcasted_iota(jnp.int32, (tokens, tokens), 1)
    return hidden(place - token <= (own - shard) * tokens)


def cache_mask(shard, limit, c_rows, tokens):
    place = lax.broadcasted_iota(jnp.int32, (c_rows, tokens), 0)
    return hidden(place < limit - shard * c_rows)


def slot_row(targets_ref, shard, own, tokens, pool):
    page = lax.broadcasted_iota(jnp.int32, (1, tokens), 1) // PAGE
    slots = jnp.full((1, tokens), -1, jnp.int32)
    for index in range(tokens // PAGE):
        target = targets_ref[shard * (tokens // PAGE) + index]
        slot = jnp.where(target // P_DEV == own, pool + target % P_DEV, -1)
        slots = jnp.where(page == index, slot, slots)
    return slots


def length_column(length_ref):
    rows = length_ref.shape[0]
    place = lax.broadcasted_iota(jnp.int32, (rows, 1), 0)
    lengths = jnp.zeros((rows, 1), jnp.int32)
    for row in range(rows):
        lengths = jnp.where(place == row, length_ref[row], lengths)
    return lengths


def tally_of(lists, lengths, slot):
    rows, span = lists.shape
    tokens = slot.shape[1]
    slot = jnp.broadcast_to(slot, (rows, tokens))
    offset = lax.rem(lax.broadcasted_iota(jnp.int32, (rows, tokens), 1), PAGE)
    tally = jnp.zeros((rows, tokens), jnp.float32)
    for entry in range(span):
        hit = (slot == lists[:, entry : entry + 1]) & (offset < lengths - entry * PAGE)
        tally = tally + jnp.where(hit, jnp.float32(1.0), jnp.float32(0.0))
    return tally[None]


def shard_of(own, hop, count):
    return lax.rem(own + hop + count, count)


def own_kernel(own_ref, limit_ref, q_ref, stretch_ref, cache_ref, qt_ref, high_ref, total_ref, accum_ref):
    kv_local, _, rows = qt_ref.shape
    tokens = q_ref.shape[0]
    c_rows = cache_ref.shape[0] // 2
    width = min(2 * tokens, rows)
    own = own_ref[0]
    mask = jnp.concatenate(
        [stretch_mask(own, own, tokens), cache_mask(own, limit_ref[0], c_rows, tokens)], axis=0
    )
    for head in range(kv_local):
        for sub in range(GROUP):
            col = (head * GROUP + sub) * HEAD_DIM
            qt_ref[head, :, sub * tokens : (sub + 1) * tokens] = q_ref[:, col : col + HEAD_DIM].T
        feats = slice(head * HEAD_DIM, (head + 1) * HEAD_DIM)
        keys = jnp.concatenate([stretch_ref[:tokens, feats], cache_ref[:c_rows, feats]], axis=0)
        keys = jnp.concatenate([keys, mask], axis=1)
        values_t = jnp.concatenate([stretch_ref[tokens:, feats], cache_ref[c_rows:, feats]], axis=0).T
        for start in range(0, rows, width):
            cols = slice(start, start + width)
            high, total, accum = attend(qt_ref.at[head], cols, keys, values_t, None)
            high_ref[head, :, cols] = high
            total_ref[head, :, cols] = total
            accum_ref[head, :, cols] = accum


def hop_kernel(count, stretch_hops, hop, last, own_ref, limit_ref, qt_ref, high_in, total_in, accum_in, *refs):
    stretch_refs, refs = refs[: len(stretch_hops)], refs[len(stretch_hops) :]
    cache_ref, outs = refs[0], refs[1:]
    own = own_ref[0]
    kv_local, _, rows = qt_ref.shape
    tokens = rows // GROUP
    c_rows = cache_ref.shape[0] // 2
    width = min(2 * tokens, rows)
    masks = [stretch_mask(shard_of(own, far, count), own, tokens) for far in stretch_hops]
    masks.append(cache_mask(shard_of(own, hop, count), limit_ref[0], c_rows, tokens))
    mask = jnp.concatenate(masks, axis=0)
    for head in range(kv_local):
        feats = slice(head * HEAD_DIM, (head + 1) * HEAD_DIM)
        keys = [ref[:tokens, feats] for ref in stretch_refs] + [cache_ref[:c_rows, feats]]
        values = [ref[tokens:, feats] for ref in stretch_refs] + [cache_ref[c_rows:, feats]]
        keys = jnp.concatenate([jnp.concatenate(keys, axis=0), mask], axis=1)
        values_t = jnp.concatenate(values, axis=0).T
        for start in range(0, rows, width):
            cols = slice(start, start + width)
            state = (high_in[head, :, cols], total_in[head, :, cols], accum_in[head, :, cols])
            high, total, accum = attend(qt_ref.at[head], cols, keys, values_t, state)
            if last:
                mixed = (accum * (1.0 / total)).astype(jnp.bfloat16)
                for piece in range(width // tokens):
                    col = (head * GROUP + start // tokens + piece) * HEAD_DIM
                    outs[0][:, col : col + HEAD_DIM] = mixed[:, piece * tokens : (piece + 1) * tokens].T
            else:
                outs[0][head, :, cols] = high
                outs[1][head, :, cols] = total
                outs[2][head, :, cols] = accum


def decode_kernel(count, hops, own_ref, targets_ref, length_ref, q_ref, lists_ref, pool_k, pool_v, *refs):
    stretch_refs, out_ref = refs[:-1], refs[-1]
    rows, q_width = q_ref.shape
    heads = q_width // HEAD_DIM
    kv_local = heads // GROUP
    pool = pool_k.shape[0]
    held = pool * PAGE
    tokens = stretch_refs[0].shape[0] // 2
    own = own_ref[0]
    lists = lists_ref[...]
    lengths = length_column(length_ref)

    queries = q_ref[...].astype(jnp.float32)
    stacked = []
    for head in range(heads):
        piece = queries[:, head * HEAD_DIM : (head + 1) * HEAD_DIM]
        blank = jnp.zeros_like(piece)
        stacked.append(
            jnp.concatenate([piece if kv == head // GROUP else blank for kv in range(kv_local)], axis=1)
        )
    wide = jnp.concatenate(stacked, axis=0).astype(jnp.bfloat16)

    parts = [(pool_k[...].reshape(held, -1), pool_v[...].reshape(held, -1))]
    slots = [lax.broadcasted_iota(jnp.int32, (1, held), 1) // PAGE]
    for hop, ref in zip(hops, stretch_refs):
        parts.append((ref[:tokens], ref[tokens:]))
        slots.append(slot_row(targets_ref, shard_of(own, hop, count), own, tokens, pool))
    done = []
    for (keys, values), slot in zip(parts, slots):
        scores = lax.dot_general(wide, keys, (((1,), (1,)), ((), ())), preferred_element_type=jnp.float32)
        tally = tally_of(lists, lengths, slot)
        scores = scores.reshape(heads, rows, -1)
        done.append((jnp.where(tally > 0, scores, jnp.float32(HIDDEN)), tally, values))
    high = functools.reduce(
        jnp.maximum, [jnp.max(scores, axis=-1, keepdims=True) for scores, _, _ in done]
    )
    total, mixed = 0.0, 0.0
    for scores, tally, values in done:
        weights = jnp.exp2((scores - high) * EXP2_SCALE) * tally
        total = total + jnp.sum(weights, axis=-1, keepdims=True)
        mixed = mixed + jnp.dot(
            weights.reshape(heads * rows, -1).astype(jnp.bfloat16),
            values,
            preferred_element_type=jnp.float32,
        )
    for head in range(heads):
        kv = head // GROUP
        piece = mixed[head * rows : (head + 1) * rows, kv * HEAD_DIM : (kv + 1) * HEAD_DIM]
        out_ref[:, head * HEAD_DIM : (head + 1) * HEAD_DIM] = (piece / total[head]).astype(jnp.bfloat16)


def per_device(
    count,
    queries,
    stretch_keys,
    stretch_values,
    cache_keys,
    cache_values,
    prefix_length,
    page_targets,
    pool_keys,
    pool_values,
    decode_queries,
    page_lists,
    context_length,
):
    own = lax.axis_index("ctx")
    own_array = jnp.full((1,), own, jnp.int32)
    tokens, width = queries.shape
    kv_local = stretch_keys.shape[1] // HEAD_DIM
    rows = GROUP * tokens
    c_rows = cache_keys.shape[0]
    f32 = jnp.float32
    params = pltpu.CompilerParams(vmem_limit_bytes=VMEM_BYTES)
    up_pairs = [(i, (i + 1) % count) for i in range(count)]
    down_pairs = [(i, (i - 1) % count) for i in range(count)]
    ups, downs = count // 2, (count - 1) // 2

    def send(array, hop):
        return lax.ppermute(array, "ctx", up_pairs if hop < 0 else down_pairs)

    def cost(keys):
        pairs = kv_local * rows * keys
        return pl.CostEstimate(
            flops=4 * pairs * HEAD_DIM, bytes_accessed=4 * rows * kv_local * HEAD_DIM, transcendentals=pairs
        )

    stretch = {0: jnp.concatenate([stretch_keys, stretch_values], axis=0)}
    cache = {0: jnp.concatenate([cache_keys, cache_values], axis=0)}
    stretch[-1] = send(stretch[0], -1)
    stretch[1] = send(stretch[0], 1)
    cache[-1] = send(cache[0], -1)

    state_shapes = (
        jax.ShapeDtypeStruct((kv_local, 1, rows), f32),
        jax.ShapeDtypeStruct((kv_local, 1, rows), f32),
        jax.ShapeDtypeStruct((kv_local, HEAD_DIM, rows), f32),
    )
    qt, *state = pl.pallas_call(
        own_kernel,
        out_shape=(jax.ShapeDtypeStruct((kv_local, HEAD_DIM, rows), jnp.bfloat16),) + state_shapes,
        in_specs=[SMEM, SMEM] + [VMEM] * 3,
        out_specs=(VMEM,) * 4,
        compiler_params=params,
        cost_estimate=cost(tokens + c_rows),
        name="own_shard",
    )(own_array, prefix_length, queries, stretch[0], cache[0])

    stretch[-1], state = lax.optimization_barrier((stretch[-1], state))
    for far in range(2, ups + 1):
        stretch[-far] = send(stretch[1 - far], -1)
        if far <= downs:
            stretch[far] = send(stretch[far - 1], 1)
    later, state = lax.optimization_barrier((cache[0], state))
    cache[1] = send(later, 1)

    hops = sorted(stretch)
    decoded = pl.pallas_call(
        functools.partial(decode_kernel, count, hops),
        out_shape=jax.ShapeDtypeStruct(decode_queries.shape, jnp.bfloat16),
        in_specs=[SMEM] * 3 + [VMEM] * (4 + len(hops)),
        out_specs=VMEM,
        compiler_params=params,
        cost_estimate=pl.CostEstimate(
            flops=4 * 128 * 2560 * 256, bytes_accessed=4 * pool_keys.size, transcendentals=128 * 2560
        ),
        name="decode_rows",
    )(
        own_array, page_targets, context_length, decode_queries, page_lists, pool_keys, pool_values,
        *[stretch[hop] for hop in hops],
    )

    cache[-1], decoded = lax.optimization_barrier((cache[-1], decoded))
    order = [-1, 1]
    for far in range(2, ups + 1):
        cache[-far] = send(cache[1 - far], -1)
        order.append(-far)
        if far <= downs:
            cache[far] = send(cache[far - 1], 1)
            order.append(far)

    for place, hop in enumerate(order):
        last = place == len(order) - 1
        stretch_hops = [far for far in hops if far != 0] if place == 0 else []
        out_shape = (jax.ShapeDtypeStruct((tokens, width), jnp.bfloat16),) if last else state_shapes
        state = pl.pallas_call(
            functools.partial(hop_kernel, count, stretch_hops, hop, last),
            out_shape=out_shape,
            in_specs=[SMEM, SMEM] + [VMEM] * (5 + len(stretch_hops)),
            out_specs=(VMEM,) * len(out_shape),
            compiler_params=params,
            cost_estimate=cost(c_rows + tokens * len(stretch_hops)),
            name="hop_kernel_" + str(place),
        )(own_array, prefix_length, qt, *state, *[stretch[far] for far in stretch_hops], cache[hop])
    return (state[0], decoded)


def solution(mesh):
    in_specs = (
        P(("groups", "ctx"), "head"),
        P(("groups", "ctx"), "head"),
        P(("groups", "ctx"), "head"),
        P(("groups", "ctx"), "head"),
        P(("groups", "ctx"), "head"),
        P("groups"),
        P("groups"),
        P(("groups", "ctx"), None, "head"),
        P(("groups", "ctx"), None, "head"),
        P(("groups", "ctx"), "head"),
        P(("groups", "ctx"), None),
        P(("groups", "ctx")),
    )
    out_specs = (P(("groups", "ctx"), "head"), P(("groups", "ctx"), "head"))
    return jax.shard_map(
        functools.partial(per_device, mesh.shape["ctx"]),
        mesh=mesh,
        in_specs=in_specs,
        out_specs=out_specs,
        check_vma=False,
    )
```

time: 58.3 us -> 40 us (0.69)
  blocking collectives: 22.2 us -> 0 us
  between operations: 14.8 us -> 1.41 us
  starting transfers between devices: 0.04 us -> 10.8 us
  waiting for transfers between devices: 3.08 us -> 7.66 us
  Pallas kernels: 12.1 us -> 16.1 us
  local copies, waits for them, and re-layouts: 5.1 us -> 3.81 us
  other arithmetic: 0.68 us -> 0 us
    all_gather x1 -> x0, blocking collectives: 22.2 us -> none  [per_device(): lax.all_gather(own_s, 'ctx', axis=0, tiled=True)]
    ppermute x0 -> x6, starting transfers between devices: none -> 10.8 us  [send(): return lax.ppermute(array, 'ctx', up_pairs if hop < 0 else down_pairs)]
    ppermute x0 -> x6, waiting for transfers between devices: none -> 7.66 us  [send(): return lax.ppermute(array, 'ctx', up_pairs if hop < 0 else down_pairs)]
    pallas_call x3 -> x5, Pallas kernels: 12.1 us -> 16.1 us  [the longest x3 9.98 us: per_device(): pl.pallas_call(functools.partial(hop_kernel, count, stretch_hops, hop, la...]
    all_gather x1 -> x0, waiting for transfers between devices: 3.07 us -> none  [per_device(): lax.all_gather(own_c, 'ctx', axis=0, tiled=True)]
    unnamed x23 -> x18, local copies, waits for them, and re-layouts: 4.21 us -> 1.96 us
    concatenate x1 -> x2, local copies, waits for them, and re-layouts: 0.01 us -> 1.85 us  [the longest x1 0.93 us: per_device(): stretch = {0: jnp.concatenate([stretch_keys, stretch_values], axis=0)}]
    reshape x1 -> x0, local copies, waits for them, and re-layouts: 0.73 us -> none  [per_device(): context_length.reshape(-1, 1)]
  transfers between devices with their start and end apart: 1 -> 6, of which waited for: 1 -> 3; matrix products, arithmetic and copies ran while one was open for 3% -> 2% of each run, Pallas kernels for 12% -> 32%
where the time goes in v4:
time: 40 us; the launch traced here: 39.8 us
  Pallas kernels  16.1 us (40%)
  starting transfers between devices  10.8 us (27%)
  waiting for transfers between devices  7.66 us (19%)
  local copies, waits for them, and re-layouts  3.81 us (10%)
  between operations  1.41 us (4%)
    ppermute x6, starting transfers between devices, send(): return lax.ppermute(array, 'ctx', up_pairs if hop < 0 else down_pairs)  10.8 us
    pallas_call x3, Pallas kernels, per_device(): pl.pallas_call(functools.partial(hop_kernel, count, stretch_hops, hop, la...  9.98 us
    ppermute x6, waiting for transfers between devices, send(): return lax.ppermute(array, 'ctx', up_pairs if hop < 0 else down_pairs)  7.66 us
    pallas_call x1, Pallas kernels, per_device(): pl.pallas_call(own_kernel, out_shape=(jax.ShapeDtypeStruct((kv_local, HEA...  3.25 us
    pallas_call x1, Pallas kernels, per_device(): pl.pallas_call(functools.partial(decode_kernel, count, hops), out_shape=j...  2.92 us
    unnamed x18, local copies, waits for them, and re-layouts  1.96 us
    concatenate x1, local copies, waits for them, and re-layouts, per_device(): stretch = {0: jnp.concatenate([stretch_keys, stretch_values], axis=0)}  0.93 us
    concatenate x1, local copies, waits for them, and re-layouts, per_device(): cache = {0: jnp.concatenate([cache_keys, cache_values], axis=0)}  0.92 us
  transfers between devices with their start and end apart: 6, of which 3 were waited for; matrix products, arithmetic and copies ran while one was open for 2% of the time, Pallas kernels for 32%

profile of v4, /device:TPU:0, one launch (start us, length us, event | category | flops | bytes accessed | tf_op | source)
XLA Modules:
  0.0 39.8 jit_solution(12260125577890496257)
XLA Ops:
  0.6 0.9 %constant_dynamic-update-slice_fusion.1 = bf16[256,256]{1,0:T(8,128)(2,1)S(1)} fusion(bf16[128,256]{1,0:T(8,128)(2,1)} %param.13), kind=kLoop, calls=%fused_computation.1 | loop fusion | bytes 131072
  1.5 0.9 %constant_dynamic-update-slice_fusion.stretch_ref.refs_2_ = bf16[256,256]{1,0:T(8,128)(2,1)S(1)} fusion(bf16[256,256]{1,0:T(8,128)(2,1)S(1)} %constant_dynamic-update-slice_fusion.1, bf16[128,256]{1,0:T(8,128)(2,1)} %param.14), kind=kLoop, calls=%fused_computation | loop fusion | bytes 131072 | tf_op jit(solution)/shard_map/concatenate | solution.py:241
  2.5 3.0 %collective-permute-start = (bf16[256,256]{1,0:T(8,128)(2,1)S(1)}, bf16[256,256]{1,0:T(8,128)(2,1)S(1)}, u32[]{:S(2)}, u32[]{:S(2)}) collective-permute-start(bf16[256,256]{1,0:T(8,128)(2,1)S(1)} %constant_dynamic-update-slice_fusion.stretch_ref.refs_2_), channel_id=1, source_target_pairs={{0,4},{4,8},{8,12},{12,0},{1,5},{5,9},{9,13},{13,1},{2,6},{6,10},{... | collective-permute-start | bytes 393224 | tf_op jit(solution)/shard_map/ppermute | solution.py:233
  5.5 0.9 %constant_dynamic-update-slice_fusion.2.cache_ref = bf16[512,256]{1,0:T(8,128)(2,1)S(1)} fusion(bf16[512,256]{1,0:T(8,128)(2,1)S(1)} %constant_dynamic-update-slice_fusion.3, bf16[256,256]{1,0:T(8,128)(2,1)} %param.16), kind=kLoop, calls=%fused_computation.2 | loop fusion | bytes 262144 | tf_op jit(solution)/shard_map/concatenate | solution.py:242
  6.4 1.6 %collective-permute-start.3 = (bf16[512,256]{1,0:T(8,128)(2,1)S(1)}, bf16[512,256]{1,0:T(8,128)(2,1)S(1)}, u32[]{:S(2)}, u32[]{:S(2)}) collective-permute-start(bf16[512,256]{1,0:T(8,128)(2,1)S(1)} %constant_dynamic-update-slice_fusion.2.cache_ref), channel_id=1, source_target_pairs={{0,4},{4,8},{8,12},{12,0},{1,5},{5,9},{9,13},{13,1},{2,6},{6,10},{... | collective-permute-start | bytes 786440 | tf_op jit(solution)/shard_map/ppermute | solution.py:233
  8.0 2.2 %collective-permute-start.2 = (bf16[256,256]{1,0:T(8,128)(2,1)S(1)}, bf16[256,256]{1,0:T(8,128)(2,1)S(1)}, u32[]{:S(2)}, u32[]{:S(2)}) collective-permute-start(bf16[256,256]{1,0:T(8,128)(2,1)S(1)} %constant_dynamic-update-slice_fusion.stretch_ref.refs_2_), channel_id=1, source_target_pairs={{0,12},{4,0},{8,4},{12,8},{1,13},{5,1},{9,5},{13,9},{2,14},{6,2},{... | collective-permute-start | bytes 393224 | tf_op jit(solution)/shard_map/ppermute | solution.py:233
  10.9 0.0 copy-start.6
  11.0 1.0 %copy-done.6 = bf16[128,2048]{1,0:T(8,128)(2,1)S(1)} copy-done((bf16[128,2048]{1,0:T(8,128)(2,1)S(1)}, bf16[128,2048]{1,0:T(8,128)(2,1)}, u32[]{:S(2)}) %copy-start.6) | copy-done | bytes 524312
  12.0 3.2 %own_shard.1 = (bf16[2,128,1024]{2,1,0:T(8,128)(2,1)S(1)}, f32[2,1,1024]{2,1,0:T(1,128)S(1)}, f32[2,1,1024]{2,1,0:T(1,128)S(1)}, f32[2,128,1024]{2,1,0:T(8,128)S(1)}) custom-call(s32[1]{0:T(128)} %bitcast.own_ref, s32[1]{0:T(128)S(6)} %copy.16.limit_ref, bf16[128,2048]{1,0:T(8,128)(2,1)S(1)} %copy-done.6, ...), custom_call_target="tpu_custom_call" | custom-call | flops 402653184 | bytes 1048576 | tf_op jit(solution)/shard_map/own_shard/pallas_call | solution.py:252
  15.2 0.0 copy-start.3
  15.3 0.0 collective-permute-done.refs_1_
  15.3 0.0 copy-start.4
  15.3 0.0 copy-start.5
  15.3 0.1 collective-permute-start.1
  15.4 3.8 %collective-permute-start.4 = (bf16[512,256]{1,0:T(8,128)(2,1)S(1)}, bf16[512,256]{1,0:T(8,128)(2,1)S(1)}, u32[]{:S(2)}, u32[]{:S(2)}) collective-permute-start(bf16[512,256]{1,0:T(8,128)(2,1)S(1)} %constant_dynamic-update-slice_fusion.2.cache_ref), channel_id=1, source_target_pairs={{0,12},{4,0},{8,4},{12,8},{1,13},{5,1},{9,5},{13,9},{2,14},{6,2},{... | collective-permute-start | bytes 786440 | tf_op jit(solution)/shard_map/ppermute | solution.py:233
  19.2 1.0 %collective-permute-done.2.refs_3_.refs_2_ = bf16[256,256]{1,0:T(8,128)(2,1)S(1)} collective-permute-done((bf16[256,256]{1,0:T(8,128)(2,1)S(1)}, bf16[256,256]{1,0:T(8,128)(2,1)S(1)}, u32[]{:S(2)}, u32[]{:S(2)}) %collective-permute-start.2) | collective-permute-done | bytes 131104 | tf_op jit(solution)/shard_map/ppermute | solution.py:233
  20.2 3.4 %collective-permute-done.1.refs_0_ = bf16[256,256]{1,0:T(8,128)(2,1)S(1)} collective-permute-done((bf16[256,256]{1,0:T(8,128)(2,1)S(1)}, bf16[256,256]{1,0:T(8,128)(2,1)S(1)}, u32[]{:S(2)}, u32[]{:S(2)}) %collective-permute-start.1) | collective-permute-done | bytes 131104 | tf_op jit(solution)/shard_map/ppermute | solution.py:233
  23.6 2.9 %decode_rows.1 = bf16[8,2048]{1,0:T(8,128)(2,1)} custom-call(s32[1]{0:T(128)} %bitcast.own_ref, s32[32]{0:T(128)S(1)} %copy-done.4, s32[8]{0:T(128)S(1)} %copy-done.5, bf16[8,2048]{1,0:T(8,128)(2,1)S(1)} %copy-done.2, s32[8,32]{1,0:T(8,128)S(1)} %copy-done.3, bf16[128,16,256]{2,1,0:T(8,128)(2,1)S(1)} %copy-done, bf16[128,16,256]{2,1,0:T(8,128)(2,1)S(1)} %copy-done.1, ...), custom_call_target="tpu_custom_call" | custom-call | flops 335544320 | bytes 2097152 | tf_op jit(solution)/shard_map/decode_rows/pallas_call | solution.py:271
  26.5 0.0 collective-permute-done.3.refs_3_
  26.5 0.0 collective-permute-start.5
  26.5 4.2 %hop_kernel_0.1 = (f32[2,1,1024]{2,1,0:T(1,128)S(1)}, f32[2,1,1024]{2,1,0:T(1,128)S(1)}, f32[2,128,1024]{2,1,0:T(8,128)S(1)}) custom-call(s32[1]{0:T(128)} %bitcast.own_ref, s32[1]{0:T(128)S(6)} %copy.16.limit_ref, bf16[2,128,1024]{2,1,0:T(8,128)(2,1)S(1)} %get-tuple-element.22.qt_ref, f32[2,1,1024]{2,1,0:T(1,128)S(1)} %get-tuple-element.29.high_in, ...), custom_call_target="tpu_custom_call" | custom-call | flops 671088640 | bytes 1048576 | tf_op jit(solution)/shard_map/hop_kernel_0/pallas_call | solution.py:299
  30.7 2.5 %hop_kernel_1.1 = (f32[2,1,1024]{2,1,0:T(1,128)S(1)}, f32[2,1,1024]{2,1,0:T(1,128)S(1)}, f32[2,128,1024]{2,1,0:T(8,128)S(1)}) custom-call(s32[1]{0:T(128)} %bitcast.own_ref, s32[1]{0:T(128)S(6)} %copy.16.limit_ref, bf16[2,128,1024]{2,1,0:T(8,128)(2,1)S(1)} %get-tuple-element.22.qt_ref, f32[2,1,1024]{2,1,0:T(1,128)S(1)} %get-tuple-element.34.high_in, ...), custom_call_target="tpu_custom_call" | custom-call | flops 268435456 | bytes 1048576 | tf_op jit(solution)/shard_map/hop_kernel_1/pallas_call | solution.py:299
  33.2 3.2 %collective-permute-done.5.refs_0_ = bf16[512,256]{1,0:T(8,128)(2,1)S(1)} collective-permute-done((bf16[512,256]{1,0:T(8,128)(2,1)S(1)}, bf16[512,256]{1,0:T(8,128)(2,1)S(1)}, u32[]{:S(2)}, u32[]{:S(2)}) %collective-permute-start.5) | collective-permute-done | bytes 262176 | tf_op jit(solution)/shard_map/ppermute | solution.py:233
  36.5 3.3 %hop_kernel_2.1 = bf16[128,2048]{1,0:T(8,128)(2,1)} custom-call(s32[1]{0:T(128)} %bitcast.own_ref, s32[1]{0:T(128)S(6)} %copy.16.limit_ref, bf16[2,128,1024]{2,1,0:T(8,128)(2,1)S(1)} %get-tuple-element.22.qt_ref, f32[2,1,1024]{2,1,0:T(1,128)S(1)} %get-tuple-element.38.high_in, f32[2,1,1024]{2,1,0:T(1,128)S(1)} %get-tuple-element.39.total_in, ...), custom_call_target="tpu_custom_call" | custom-call | flops 268435456 | bytes 1048576 | tf_op jit(solution)/shard_map/hop_kernel_2/pallas_call | solution.py:299
  (13 shorter events, 0.0 us)
Async XLA Ops:
  0.6 4.9 %copy-start.7 = (bf16[256,256]{1,0:T(8,128)(2,1)S(1)}, bf16[256,256]{1,0:T(8,128)(2,1)}, u32[]{:S(2)}) copy-start(bf16[256,256]{1,0:T(8,128)(2,1)} %param.15) | copy-start | bytes 393220
  1.5 22.1 %copy-start.1 = (bf16[128,16,256]{2,1,0:T(8,128)(2,1)S(1)}, bf16[128,16,256]{2,1,0:T(8,128)(2,1)}, u32[]{:S(2)}) copy-start(bf16[128,16,256]{2,1,0:T(8,128)(2,1)} %pool_v.1) | copy-start | bytes 3145732
  2.5 21.1 %copy-start = (bf16[128,16,256]{2,1,0:T(8,128)(2,1)S(1)}, bf16[128,16,256]{2,1,0:T(8,128)(2,1)}, u32[]{:S(2)}) copy-start(bf16[128,16,256]{2,1,0:T(8,128)(2,1)} %pool_k.1) | copy-start | bytes 3145732
  2.5 12.8 %collective-permute-start = (bf16[256,256]{1,0:T(8,128)(2,1)S(1)}, bf16[256,256]{1,0:T(8,128)(2,1)S(1)}, u32[]{:S(2)}, u32[]{:S(2)}) collective-permute-start(bf16[256,256]{1,0:T(8,128)(2,1)S(1)} %constant_dynamic-update-slice_fusion.stretch_ref.refs_2_), channel_id=1, source_target_pairs={{0,4},{4,8},{8,12},{12,0},{1,5},{5,9},{9,13},{13,1},{2,6},{6,10},{... | collective-permute-start | bytes 393224 | tf_op jit(solution)/shard_map/ppermute | solution.py:233
  6.4 20.1 %collective-permute-start.3 = (bf16[512,256]{1,0:T(8,128)(2,1)S(1)}, bf16[512,256]{1,0:T(8,128)(2,1)S(1)}, u32[]{:S(2)}, u32[]{:S(2)}) collective-permute-start(bf16[512,256]{1,0:T(8,128)(2,1)S(1)} %constant_dynamic-update-slice_fusion.2.cache_ref), channel_id=1, source_target_pairs={{0,4},{4,8},{8,12},{12,0},{1,5},{5,9},{9,13},{13,1},{2,6},{6,10},{... | collective-permute-start | bytes 786440 | tf_op jit(solution)/shard_map/ppermute | solution.py:233
  8.0 12.2 %collective-permute-start.2 = (bf16[256,256]{1,0:T(8,128)(2,1)S(1)}, bf16[256,256]{1,0:T(8,128)(2,1)S(1)}, u32[]{:S(2)}, u32[]{:S(2)}) collective-permute-start(bf16[256,256]{1,0:T(8,128)(2,1)S(1)} %constant_dynamic-update-slice_fusion.stretch_ref.refs_2_), channel_id=1, source_target_pairs={{0,12},{4,0},{8,4},{12,8},{1,13},{5,1},{9,5},{13,9},{2,14},{6,2},{... | collective-permute-start | bytes 393224 | tf_op jit(solution)/shard_map/ppermute | solution.py:233
  10.9 1.0 %copy-start.6 = (bf16[128,2048]{1,0:T(8,128)(2,1)S(1)}, bf16[128,2048]{1,0:T(8,128)(2,1)}, u32[]{:S(2)}) copy-start(bf16[128,2048]{1,0:T(8,128)(2,1)} %q_ref.2) | copy-start | bytes 1572868
  12.0 11.6 %copy-start.2 = (bf16[8,2048]{1,0:T(8,128)(2,1)S(1)}, bf16[8,2048]{1,0:T(8,128)(2,1)}, u32[]{:S(2)}) copy-start(bf16[8,2048]{1,0:T(8,128)(2,1)} %q_ref.3) | copy-start | bytes 98308
  15.2 8.3 %copy-start.3 = (s32[8,32]{1,0:T(8,128)S(1)}, s32[8,32]{1,0:T(8,128)}, u32[]{:S(2)}) copy-start(s32[8,32]{1,0:T(8,128)} %lists_ref.1) | copy-start | bytes 3076
  15.3 8.3 %copy-start.4 = (s32[32]{0:T(128)S(1)}, s32[32]{0:T(128)}, u32[]{:S(2)}) copy-start(s32[32]{0:T(128)} %targets_ref.1) | copy-start | bytes 388
  15.3 8.3 %copy-start.5 = (s32[8]{0:T(128)S(1)}, s32[8]{0:T(128)}, u32[]{:S(2)}) copy-start(s32[8]{0:T(128)} %length_ref.1) | copy-start | bytes 100
  15.3 8.3 %collective-permute-start.1 = (bf16[256,256]{1,0:T(8,128)(2,1)S(1)}, bf16[256,256]{1,0:T(8,128)(2,1)S(1)}, u32[]{:S(2)}, u32[]{:S(2)}) collective-permute-start(bf16[256,256]{1,0:T(8,128)(2,1)S(1)} %collective-permute-done.refs_1_), channel_id=1, source_target_pairs={{0,4},{4,8},{8,12},{12,0},{1,5},{5,9},{9,13},{13,1},{2,6},{6,10},{... | collective-permute-start | bytes 393224 | tf_op jit(solution)/shard_map/ppermute | solution.py:233
  15.4 15.4 %collective-permute-start.4 = (bf16[512,256]{1,0:T(8,128)(2,1)S(1)}, bf16[512,256]{1,0:T(8,128)(2,1)S(1)}, u32[]{:S(2)}, u32[]{:S(2)}) collective-permute-start(bf16[512,256]{1,0:T(8,128)(2,1)S(1)} %constant_dynamic-update-slice_fusion.2.cache_ref), channel_id=1, source_target_pairs={{0,12},{4,0},{8,4},{12,8},{1,13},{5,1},{9,5},{13,9},{2,14},{6,2},{... | collective-permute-start | bytes 786440 | tf_op jit(solution)/shard_map/ppermute | solution.py:233
  26.5 9.9 %collective-permute-start.5 = (bf16[512,256]{1,0:T(8,128)(2,1)S(1)}, bf16[512,256]{1,0:T(8,128)(2,1)S(1)}, u32[]{:S(2)}, u32[]{:S(2)}) collective-permute-start(bf16[512,256]{1,0:T(8,128)(2,1)S(1)} %collective-permute-done.3.refs_3_), channel_id=1, source_target_pairs={{0,4},{4,8},{8,12},{12,0},{1,5},{5,9},{9,13},{13,1},{2,6},{6,10},{... | collective-permute-start | bytes 786440 | tf_op jit(solution)/shard_map/ppermute | solution.py:233

commit v5 on v4

v5 whole, which is shorter than its diff:
```python
import functools

import jax
import jax.numpy as jnp
from jax import lax
from jax.experimental import pallas as pl
from jax.experimental.pallas import tpu as pltpu
from jax.sharding import PartitionSpec as P

HEADS = 64
KV_HEADS = 8
HEAD_DIM = 128
GROUP = HEADS // KV_HEADS
PAGE = 16
P_DEV = 8
EXP2_SCALE = HEAD_DIM ** (-0.5) * 1.4426950408889634
HIDDEN = -1e30
VMEM_BYTES = 48 * 1024 * 1024

VMEM = pl.BlockSpec(memory_space=pltpu.VMEM)
SMEM = pl.BlockSpec(memory_space=pltpu.SMEM)
HBM = pl.BlockSpec(memory_space=pltpu.HBM)


def attend(qt_ref, cols, keys, values_t, state):
    tokens = keys.shape[1] - HEAD_DIM
    queries = qt_ref[:, cols]
    place = lax.broadcasted_iota(jnp.int32, (tokens, queries.shape[1]), 0)
    token = lax.rem(lax.broadcasted_iota(jnp.int32, (tokens, queries.shape[1]), 1), tokens)
    pick = jnp.where(place == token, jnp.float32(1.0), jnp.float32(0.0)).astype(jnp.bfloat16)
    queries = jnp.concatenate([queries, pick], axis=0)
    scores = jnp.dot(keys, queries, preferred_element_type=jnp.float32)
    high = jnp.max(scores, axis=0, keepdims=True)
    if state is not None:
        old_high, old_total, old_accum = state
        high = jnp.maximum(high, old_high)
    weights = jnp.exp2((scores - high) * EXP2_SCALE)
    total = jnp.sum(weights, axis=0, keepdims=True)
    accum = jnp.dot(values_t, weights.astype(jnp.bfloat16), preferred_element_type=jnp.float32)
    if state is not None:
        decay = jnp.exp2((old_high - high) * EXP2_SCALE)
        total = total + old_total * decay
        accum = accum + old_accum * decay
    return high, total, accum


def hidden(seen):
    return jnp.where(seen, jnp.float32(0.0), jnp.float32(HIDDEN)).astype(jnp.bfloat16)


def stretch_mask(shard, own, tokens):
    place = lax.broadcasted_iota(jnp.int32, (tokens, tokens), 0)
    token = lax.broadcasted_iota(jnp.int32, (tokens, tokens), 1)
    return hidden(place - token <= (own - shard) * tokens)


def cache_mask(shard, limit, c_rows, tokens):
    place = lax.broadcasted_iota(jnp.int32, (c_rows, tokens), 0)
    return hidden(place < limit - shard * c_rows)


def slot_row(targets_ref, shard, own, tokens, pool):
    page = lax.broadcasted_iota(jnp.int32, (1, tokens), 1) // PAGE
    slots = jnp.full((1, tokens), -1, jnp.int32)
    for index in range(tokens // PAGE):
        target = targets_ref[shard * (tokens // PAGE) + index]
        slot = jnp.where(target // P_DEV == own, pool + target % P_DEV, -1)
        slots = jnp.where(page == index, slot, slots)
    return slots


def length_column(length_ref):
    rows = length_ref.shape[0]
    place = lax.broadcasted_iota(jnp.int32, (rows, 1), 0)
    lengths = jnp.zeros((rows, 1), jnp.int32)
    for row in range(rows):
        lengths = jnp.where(place == row, length_ref[row], lengths)
    return lengths


def tally_of(lists, lengths, slot):
    rows, span = lists.shape
    tokens = slot.shape[1]
    slot = jnp.broadcast_to(slot, (rows, tokens))
    offset = lax.rem(lax.broadcasted_iota(jnp.int32, (rows, tokens), 1), PAGE)
    tally = jnp.zeros((rows, tokens), jnp.float32)
    for entry in range(span):
        hit = (slot == lists[:, entry : entry + 1]) & (offset < lengths - entry * PAGE)
        tally = tally + jnp.where(hit, jnp.float32(1.0), jnp.float32(0.0))
    return tally[None]


def shard_of(own, hop, count):
    return lax.rem(own + hop + count, count)


def wide_queries(q_ref, kv_local):
    heads = q_ref.shape[1] // HEAD_DIM
    queries = q_ref[...].astype(jnp.float32)
    stacked = []
    for head in range(heads):
        piece = queries[:, head * HEAD_DIM : (head + 1) * HEAD_DIM]
        blank = jnp.zeros_like(piece)
        stacked.append(
            jnp.concatenate([piece if kv == head // GROUP else blank for kv in range(kv_local)], axis=1)
        )
    return jnp.concatenate(stacked, axis=0).astype(jnp.bfloat16)


def decode_attend(queries, parts, state):
    done = []
    for keys, values, tally in parts:
        scores = lax.dot_general(
            queries, keys, (((1,), (1,)), ((), ())), preferred_element_type=jnp.float32
        ).reshape(-1, tally.shape[1], tally.shape[2])
        done.append((jnp.where(tally > 0, scores, jnp.float32(HIDDEN)), tally, values))
    highs = [jnp.max(scores, axis=-1, keepdims=True) for scores, _, _ in done]
    if state is not None:
        old_high, old_total, old_mixed = state
        highs.append(old_high)
    high = functools.reduce(jnp.maximum, highs)
    total, mixed = 0.0, 0.0
    if state is not None:
        decay = jnp.exp2((old_high - high) * EXP2_SCALE)
        total = old_total * decay
        mixed = old_mixed * decay
    for scores, tally, values in done:
        weights = jnp.exp2((scores - high) * EXP2_SCALE) * tally
        total = total + jnp.sum(weights, axis=-1, keepdims=True)
        mixed = mixed + jnp.dot(
            weights.reshape(queries.shape[0], -1).astype(jnp.bfloat16),
            values,
            preferred_element_type=jnp.float32,
        ).reshape(high.shape[0], high.shape[1], -1)
    return high, total, mixed


def pack_kernel(sk_ref, sv_ref, cv_ref, ck_ref, out_ref, sems):
    copies, start = [], 0
    for place, ref in enumerate((sk_ref, sv_ref, cv_ref, ck_ref)):
        span = pl.ds(start, ref.shape[0])
        copies.append(pltpu.make_async_copy(ref, out_ref.at[span], sems.at[place]))
        start += ref.shape[0]
    for copy in copies:
        copy.start()
    for copy in copies:
        copy.wait()


def own_kernel(
    count, hops, own_ref, limit_ref, q_ref, shard_ref,
    qt_ref, near_ref, far_ref, high_ref, total_ref, accum_ref,
):
    kv_local, _, rows = qt_ref.shape
    tokens = q_ref.shape[0]
    c_rows = far_ref.shape[1]
    cached = 2 * tokens + c_rows
    width = min(2 * tokens, rows)
    own = own_ref[0]
    limit = limit_ref[0]
    for place, hop in enumerate(hops):
        shard = shard_of(own, hop, count)
        near_ref[place] = stretch_mask(shard, own, tokens)
        far_ref[place] = cache_mask(shard, limit, c_rows, tokens)
    mask = jnp.concatenate([stretch_mask(own, own, tokens), cache_mask(own, limit, c_rows, tokens)], axis=0)
    for head in range(kv_local):
        for sub in range(GROUP):
            col = (head * GROUP + sub) * HEAD_DIM
            qt_ref[head, :, sub * tokens : (sub + 1) * tokens] = q_ref[:, col : col + HEAD_DIM].T
        feats = slice(head * HEAD_DIM, (head + 1) * HEAD_DIM)
        keys = jnp.concatenate([shard_ref[:tokens, feats], shard_ref[cached:, feats]], axis=0)
        keys = jnp.concatenate([keys, mask], axis=1)
        values_t = shard_ref[tokens:cached, feats].T
        for start in range(0, rows, width):
            cols = slice(start, start + width)
            high, total, accum = attend(qt_ref.at[head], cols, keys, values_t, None)
            high_ref[head, :, cols] = high
            total_ref[head, :, cols] = total
            accum_ref[head, :, cols] = accum


def held_kernel(
    own_ref, targets_ref, length_ref, q_ref, lists_ref, pool_k, pool_v, rest_ref,
    wide_ref, high_ref, total_ref, mixed_ref,
):
    kv_width = rest_ref.shape[1]
    pool = pool_k.shape[0]
    held = pool * PAGE
    tokens = PAGE * P_DEV
    own = own_ref[0]
    lists = lists_ref[...]
    lengths = length_column(length_ref)
    wide_ref[...] = wide_queries(q_ref, kv_width // HEAD_DIM)
    held_slot = lax.broadcasted_iota(jnp.int32, (1, held), 1) // PAGE
    own_slot = slot_row(targets_ref, own, own, tokens, pool)
    parts = [
        (
            pool_k[...].reshape(held, kv_width),
            pool_v[...].reshape(held, kv_width),
            tally_of(lists, lengths, held_slot),
        ),
        (rest_ref[:tokens], rest_ref[tokens : 2 * tokens], tally_of(lists, lengths, own_slot)),
    ]
    high_ref[...], total_ref[...], mixed_ref[...] = decode_attend(wide_ref[...], parts, None)


def hop_kernel(places, qt_ref, near_ref, far_ref, high_in, total_in, accum_in, *refs):
    shard_refs, outs = refs[: len(places)], refs[len(places) :]
    kv_local, _, rows = qt_ref.shape
    tokens = rows // GROUP
    cached = 2 * tokens + far_ref.shape[1]
    width = min(2 * tokens, rows)
    for head in range(kv_local):
        feats = slice(head * HEAD_DIM, (head + 1) * HEAD_DIM)
        keys, values, masks = [], [], []
        for place, shard_ref in zip(places, shard_refs):
            keys += [shard_ref[:tokens, feats], shard_ref[cached:, feats]]
            masks += [near_ref[place], far_ref[place]]
            values.append(shard_ref[tokens:cached, feats])
        keys = jnp.concatenate([jnp.concatenate(keys, axis=0), jnp.concatenate(masks, axis=0)], axis=1)
        values_t = jnp.concatenate(values, axis=0).T
        for start in range(0, rows, width):
            cols = slice(start, start + width)
            state = (high_in[head, :, cols], total_in[head, :, cols], accum_in[head, :, cols])
            high, total, accum = attend(qt_ref.at[head], cols, keys, values_t, state)
            outs[0][head, :, cols] = high
            outs[1][head, :, cols] = total
            outs[2][head, :, cols] = accum


def fresh_kernel(count, hops, pool, place, own_ref, targets_ref, length_ref, lists_ref, *refs):
    rest_refs, refs = refs[: len(hops)], refs[len(hops) :]
    wide_ref, dec_high, dec_total, dec_mixed, qt_ref, near_ref, high_in, total_in, accum_in = refs[:9]
    dec_out, high_ref, total_ref, accum_ref = refs[9:]
    kv_local, _, rows = qt_ref.shape
    tokens = rows // GROUP
    width = min(2 * tokens, rows)
    own = own_ref[0]
    lists = lists_ref[...]
    lengths = length_column(length_ref)
    parts = []
    for hop, ref in zip(hops, rest_refs):
        slot = slot_row(targets_ref, shard_of(own, hop, count), own, tokens, pool)
        parts.append((ref[:tokens], ref[tokens : 2 * tokens], tally_of(lists, lengths, slot)))
    _, total, mixed = decode_attend(wide_ref[...], parts, (dec_high[...], dec_total[...], dec_mixed[...]))
    for head in range(kv_local * GROUP):
        kv = head // GROUP
        piece = mixed[head, :, kv * HEAD_DIM : (kv + 1) * HEAD_DIM] / total[head]
        dec_out[:, head * HEAD_DIM : (head + 1) * HEAD_DIM] = piece.astype(jnp.bfloat16)
    for head in range(kv_local):
        feats = slice(head * HEAD_DIM, (head + 1) * HEAD_DIM)
        keys = jnp.concatenate([rest_refs[place][:tokens, feats], near_ref[place]], axis=1)
        values_t = rest_refs[place][tokens : 2 * tokens, feats].T
        for start in range(0, rows, width):
            cols = slice(start, start + width)
            state = (high_in[head, :, cols], total_in[head, :, cols], accum_in[head, :, cols])
            high, total, accum = attend(qt_ref.at[head], cols, keys, values_t, state)
            high_ref[head, :, cols] = high
            total_ref[head, :, cols] = total
            accum_ref[head, :, cols] = accum


def last_kernel(
    place, qt_ref, far_ref, high_in, total_in, accum_in, ck_ref, rest_ref, out_ref, result_ref, sems
):
    kv_local, _, rows = qt_ref.shape
    tokens = rows // GROUP
    width = min(2 * tokens, rows)
    copies = []
    for head in range(kv_local):
        feats = slice(head * HEAD_DIM, (head + 1) * HEAD_DIM)
        keys = jnp.concatenate([ck_ref[:, feats], far_ref[place]], axis=1)
        values_t = rest_ref[2 * tokens :, feats].T
        for start in range(0, rows, width):
            cols = slice(start, start + width)
            state = (high_in[head, :, cols], total_in[head, :, cols], accum_in[head, :, cols])
            _, total, accum = attend(qt_ref.at[head], cols, keys, values_t, state)
            mixed = (accum * (1.0 / total)).astype(jnp.bfloat16)
            first = (head * GROUP + start // tokens) * HEAD_DIM
            for piece in range(width // tokens):
                col = first + piece * HEAD_DIM
                result_ref[:, col : col + HEAD_DIM] = mixed[:, piece * tokens : (piece + 1) * tokens].T
            span = pl.ds(first, width // tokens * HEAD_DIM)
            copy = pltpu.make_async_copy(result_ref.at[:, span], out_ref.at[:, span], sems.at[len(copies)])
            copy.start()
            copies.append(copy)
    for copy in copies:
        copy.wait()


def per_device(
    count,
    queries,
    stretch_keys,
    stretch_values,
    cache_keys,
    cache_values,
    prefix_length,
    page_targets,
    pool_keys,
    pool_values,
    decode_queries,
    page_lists,
    context_length,
):
    own = lax.axis_index("ctx")
    own_array = jnp.full((1,), own, jnp.int32)
    tokens, width = queries.shape
    kv_width = stretch_keys.shape[1]
    kv_local = kv_width // HEAD_DIM
    rows = GROUP * tokens
    heads = kv_local * GROUP
    dec_rows = decode_queries.shape[0]
    c_rows = cache_keys.shape[0]
    pool = pool_keys.shape[0]
    f32, bf16 = jnp.float32, jnp.bfloat16
    shape = jax.ShapeDtypeStruct
    params = pltpu.CompilerParams(vmem_limit_bytes=VMEM_BYTES)
    up_pairs = [(i, (i + 1) % count) for i in range(count)]
    down_pairs = [(i, (i - 1) % count) for i in range(count)]
    hops = []
    for far in range(1, count // 2 + 1):
        hops += [-far, far] if far <= (count - 1) // 2 else [-far]

    def send(array, hop):
        return lax.ppermute(array, "ctx", up_pairs if hop < 0 else down_pairs)

    def cost(keys):
        pairs = kv_local * rows * keys
        return pl.CostEstimate(
            flops=4 * pairs * HEAD_DIM, bytes_accessed=4 * rows * kv_local * HEAD_DIM, transcendentals=pairs
        )

    parts = (stretch_keys, stretch_values, cache_values, cache_keys)
    packed = pl.pallas_call(
        pack_kernel,
        out_shape=shape((2 * tokens + 2 * c_rows, kv_width), bf16),
        in_specs=[HBM] * 4,
        out_specs=HBM,
        scratch_shapes=[pltpu.SemaphoreType.DMA((4,))],
        name="pack_own_shard",
    )(*parts)
    shard = {0: packed}
    for hop in hops[:2]:
        shard[hop] = send(shard[0], hop)

    state_shapes = (
        shape((kv_local, 1, rows), f32),
        shape((kv_local, 1, rows), f32),
        shape((kv_local, HEAD_DIM, rows), f32),
    )
    qt, near, far, *state = pl.pallas_call(
        functools.partial(own_kernel, count, hops),
        out_shape=(
            shape((kv_local, HEAD_DIM, rows), bf16),
            shape((count - 1, tokens, tokens), bf16),
            shape((count - 1, c_rows, tokens), bf16),
        )
        + state_shapes,
        in_specs=[SMEM, SMEM] + [VMEM] * 2,
        out_specs=(VMEM,) * 6,
        compiler_params=params,
        cost_estimate=cost(tokens + c_rows),
        name="own_shard",
    )(own_array, prefix_length, queries, shard[0])

    wide, *dec_state = pl.pallas_call(
        held_kernel,
        out_shape=(
            shape((heads * dec_rows, kv_width), bf16),
            shape((heads, dec_rows, 1), f32),
            shape((heads, dec_rows, 1), f32),
            shape((heads, dec_rows, kv_width), f32),
        ),
        in_specs=[SMEM] * 3 + [VMEM] * 5,
        out_specs=(VMEM,) * 4,
        compiler_params=params,
        cost_estimate=pl.CostEstimate(
            flops=4 * 128 * 2048 * 256, bytes_accessed=4 * pool_keys.size, transcendentals=128 * 2048
        ),
        name="decode_held_pages",
    )(own_array, page_targets, context_length, decode_queries, page_lists, pool_keys, pool_values, shard[0])

    shard[-1], state, dec_state = lax.optimization_barrier((shard[-1], state, dec_state))
    for hop in hops[2:-1]:
        shard[hop] = send(shard[hop + 1 if hop < 0 else hop - 1], hop)
    hop = hops[-1]
    nearer = shard[hop + 1 if hop < 0 else hop - 1]
    last_rest = send(nearer[: 2 * tokens + c_rows], hop)
    last_keys = send(nearer[2 * tokens + c_rows :], hop)

    for first in range(0, len(hops) - 1, 2):
        places = list(range(first, min(first + 2, len(hops) - 1)))
        state = pl.pallas_call(
            functools.partial(hop_kernel, places),
            out_shape=state_shapes,
            in_specs=[VMEM] * (6 + len(places)),
            out_specs=(VMEM,) * 3,
            compiler_params=params,
            cost_estimate=cost((c_rows + tokens) * len(places)),
            name="whole_shards_" + str(first),
        )(qt, near, far, *state, *[shard[hops[place]] for place in places])

    final = len(hops) - 1
    decoded, *state = pl.pallas_call(
        functools.partial(fresh_kernel, count, hops, pool, final),
        out_shape=(shape(decode_queries.shape, bf16),) + state_shapes,
        in_specs=[SMEM] * 3 + [VMEM] * (10 + len(hops)),
        out_specs=(VMEM,) * 4,
        compiler_params=params,
        cost_estimate=cost(tokens),
        name="new_pages_and_last_stretch",
    )(
        own_array, page_targets, context_length, page_lists, *[shard[hop] for hop in hops[:-1]], last_rest,
        wide, *dec_state, qt, near, *state,
    )

    prefill = pl.pallas_call(
        functools.partial(last_kernel, final),
        out_shape=shape((tokens, width), bf16),
        in_specs=[VMEM] * 7,
        out_specs=HBM,
        scratch_shapes=[
            pltpu.VMEM((tokens, width), bf16),
            pltpu.SemaphoreType.DMA((kv_local * max(GROUP // 2, 1),)),
        ],
        compiler_params=params,
        cost_estimate=cost(c_rows),
        name="last_cached_keys",
    )(qt, far, *state, last_keys, last_rest)
    return (prefill, decoded)


def solution(mesh):
    in_specs = (
        P(("groups", "ctx"), "head"),
        P(("groups", "ctx"), "head"),
        P(("groups", "ctx"), "head"),
        P(("groups", "ctx"), "head"),
        P(("groups", "ctx"), "head"),
        P("groups"),
        P("groups"),
        P(("groups", "ctx"), None, "head"),
        P(("groups", "ctx"), None, "head"),
        P(("groups", "ctx"), "head"),
        P(("groups", "ctx"), None),
        P(("groups", "ctx")),
    )
    out_specs = (P(("groups", "ctx"), "head"), P(("groups", "ctx"), "head"))
    return jax.shard_map(
        functools.partial(per_device, mesh.shape["ctx"]),
        mesh=mesh,
        in_specs=in_specs,
        out_specs=out_specs,
        check_vma=False,
    )
```

time: 40 us -> 48.9 us (1.22)
  Pallas kernels: 16.1 us -> 27.7 us
  waiting for transfers between devices: 7.66 us -> 2.42 us
  starting transfers between devices: 10.8 us -> 13 us
    pallas_call x5 -> x6, Pallas kernels: 16.1 us -> 27.7 us  [the longest x1 13.1 us: per_device(): pl.pallas_call(pack_kernel, out_shape=shape((2 * tokens + 2 * c_rows, kv_...]
    ppermute x6 -> x4, waiting for transfers between devices: 7.66 us -> 2.42 us  [send(): return lax.ppermute(array, 'ctx', up_pairs if hop < 0 else down_pairs)]
    ppermute x6 -> x4, starting transfers between devices: 10.8 us -> 13 us  [send(): return lax.ppermute(array, 'ctx', up_pairs if hop < 0 else down_pairs)]
    unnamed x18, local copies, waits for them, and re-layouts: 1.96 us -> 4.1 us
    concatenate x2 -> x0, local copies, waits for them, and re-layouts: 1.85 us -> none  [the longest x1 0.93 us: per_device(): stretch = {0: jnp.concatenate([stretch_keys, stretch_values], axis=0)}]
  transfers between devices with their start and end apart: 6 -> 4, of which waited for: 3 -> 2; matrix products, arithmetic and copies ran while one was open for 2% -> 0% of each run, Pallas kernels for 32% -> 23%
where the time goes in v5:
time: 48.9 us; the launch traced here: 48.7 us
  Pallas kernels  27.7 us (57%)
  starting transfers between devices  13 us (27%)
  local copies, waits for them, and re-layouts  4.13 us (8%)
  waiting for transfers between devices  2.42 us (5%)
  between operations  1.41 us (3%)
    pallas_call x1, Pallas kernels, per_device(): pl.pallas_call(pack_kernel, out_shape=shape((2 * tokens + 2 * c_rows, kv_...  13.1 us
    ppermute x4, starting transfers between devices, send(): return lax.ppermute(array, 'ctx', up_pairs if hop < 0 else down_pairs)  13 us
    pallas_call x1, Pallas kernels, per_device(): pl.pallas_call(functools.partial(hop_kernel, places), out_shape=state_sha...  4.5 us
    unnamed x18, local copies, waits for them, and re-layouts  4.1 us
    pallas_call x1, Pallas kernels, per_device(): pl.pallas_call(functools.partial(own_kernel, count, hops), out_shape=(sha...  3.24 us
    pallas_call x1, Pallas kernels, per_device(): pl.pallas_call(functools.partial(last_kernel, final), out_shape=shape((to...  3.23 us
    ppermute x4, waiting for transfers between devices, send(): return lax.ppermute(array, 'ctx', up_pairs if hop < 0 else down_pairs)  2.42 us
    pallas_call x1, Pallas kernels, per_device(): pl.pallas_call(held_kernel, out_shape=(shape((heads * dec_rows, kv_width)...  1.87 us
  transfers between devices with their start and end apart: 4, of which 2 were waited for; matrix products, arithmetic and copies ran while one was open for 0% of the time, Pallas kernels for 23%

profile of v5, /device:TPU:0, one launch (start us, length us, event | category | flops | bytes accessed | tf_op | source)
XLA Modules:
  0.0 48.7 jit_solution(6012961849289541417)
XLA Ops:
  0.6 0.0 copy-start.4
  0.6 13.1 %pack_own_shard.1.shard_ref.rest_ref = bf16[768,256]{1,0:T(8,128)(2,1)} custom-call(bf16[128,256]{1,0:T(8,128)(2,1)} %sk_ref.1, bf16[128,256]{1,0:T(8,128)(2,1)} %sv_ref.1, bf16[256,256]{1,0:T(8,128)(2,1)} %cv_ref.1, bf16[256,256]{1,0:T(8,128)(2,1)} %ck_ref.1), custom_call_target="tpu_custom_call" | custom-call | tf_op jit(solution)/shard_map/pack_own_shard/pallas_call | solution.py:335
  13.7 3.1 %collective-permute-start = (bf16[768,256]{1,0:T(8,128)(2,1)}, bf16[768,256]{1,0:T(8,128)(2,1)S(1)}, u32[]{:S(2)}, u32[]{:S(2)}) collective-permute-start(bf16[768,256]{1,0:T(8,128)(2,1)} %pack_own_shard.1.shard_ref.rest_ref), channel_id=1, source_target_pairs={{0,4},{4,8},{8,12},{12,0},{1,5},{5,9},{9,13},{13,1},{2,6},{6,10},{... | collective-permute-start | bytes 1179656 | tf_op jit(solution)/shard_map/ppermute | solution.py:326
  16.8 2.1 %collective-permute-start.1 = (bf16[768,256]{1,0:T(8,128)(2,1)}, bf16[768,256]{1,0:T(8,128)(2,1)S(1)}, u32[]{:S(2)}, u32[]{:S(2)}) collective-permute-start(bf16[768,256]{1,0:T(8,128)(2,1)} %pack_own_shard.1.shard_ref.rest_ref), channel_id=1, source_target_pairs={{0,12},{4,0},{8,4},{12,8},{1,13},{5,1},{9,5},{13,9},{2,14},{6,2},{... | collective-permute-start | bytes 1179656 | tf_op jit(solution)/shard_map/ppermute | solution.py:326
  19.5 0.0 copy-start.6
  19.5 0.0 copy-start.7
  19.6 0.0 copy-done.4
  19.6 0.0 copy-done.5
  19.6 0.6 %copy-done.6 = s32[32]{0:T(128)S(1)} copy-done((s32[32]{0:T(128)S(1)}, s32[32]{0:T(128)}, u32[]{:S(2)}) %copy-start.6) | copy-done | bytes 152
  20.2 0.0 copy-done.7
  20.2 1.0 %copy-done = bf16[768,256]{1,0:T(8,128)(2,1)S(1)} copy-done((bf16[768,256]{1,0:T(8,128)(2,1)S(1)}, bf16[768,256]{1,0:T(8,128)(2,1)}, u32[]{:S(2)}) %copy-start) | copy-done | bytes 393240
  21.2 1.2 %copy-done.2 = bf16[128,16,256]{2,1,0:T(8,128)(2,1)S(1)} copy-done((bf16[128,16,256]{2,1,0:T(8,128)(2,1)S(1)}, bf16[128,16,256]{2,1,0:T(8,128)(2,1)}, u32[]{:S(2)}) %copy-start.2) | copy-done | bytes 1048600
  22.4 1.2 %copy-done.3 = bf16[128,16,256]{2,1,0:T(8,128)(2,1)S(1)} copy-done((bf16[128,16,256]{2,1,0:T(8,128)(2,1)S(1)}, bf16[128,16,256]{2,1,0:T(8,128)(2,1)}, u32[]{:S(2)}) %copy-start.3) | copy-done | bytes 1048600
  23.7 1.9 %decode_held_pages.1 = (bf16[128,256]{1,0:T(8,128)(2,1)S(1)}, f32[16,8,1]{2,1,0:T(8,128)S(1)}, f32[16,8,1]{2,1,0:T(8,128)S(1)}, f32[16,8,256]{2,1,0:T(8,128)S(1)}) custom-call(s32[1]{0:T(128)} %bitcast.own_ref, s32[32]{0:T(128)S(1)} %copy-done.6, s32[8]{0:T(128)S(1)} %copy-done.7, bf16[8,2048]{1,0:T(8,128)(2,1)S(1)} %copy-done.4, s32[8,32]{1,0:T(8,128)S(1)} %copy-done.5, ...), custom_call_target="tpu_custom_call" | custom-call | flops 268435456 | bytes 2097152 | tf_op jit(solution)/shard_map/decode_held_pages/pallas_call | solution.py:367
  25.6 3.2 %own_shard.1 = (bf16[2,128,1024]{2,1,0:T(8,128)(2,1)S(1)}, bf16[3,128,128]{2,1,0:T(8,128)(2,1)S(1)}, bf16[3,256,128]{2,1,0:T(8,128)(2,1)S(1)}, f32[2,1,1024]{2,1...) custom-call(s32[1]{0:T(128)} %bitcast.own_ref, s32[1]{0:T(128)S(6)} %copy.14.limit_ref, ...), custom_call_target="tpu_custom_call" | custom-call | flops 402653184 | bytes 1048576 | tf_op jit(solution)/shard_map/own_shard/pallas_call | solution.py:352
  28.8 0.2 collective-permute-done.refs_0_
  29.0 0.1 collective-permute-start.2
  29.1 7.8 %collective-permute-start.3 = (bf16[256,256]{1,0:T(8,128)(2,1)S(1)}, bf16[256,256]{1,0:T(8,128)(2,1)S(1)}, u32[]{:S(2)}, u32[]{:S(2)}) collective-permute-start(bf16[256,256]{1,0:T(8,128)(2,1)S(1)} %slice.7), channel_id=1, source_target_pairs={{0,4},{4,8},{8,12},{12,0},{1,5},{5,9},{9,13},{13,1},{2,6},{6,10},{... | collective-permute-start | bytes 393224 | tf_op jit(solution)/shard_map/ppermute | solution.py:326
  36.9 0.0 collective-permute-done.1.refs_1_
  36.9 4.5 %whole_shards_0.1 = (f32[2,1,1024]{2,1,0:T(1,128)S(1)}, f32[2,1,1024]{2,1,0:T(1,128)S(1)}, f32[2,128,1024]{2,1,0:T(8,128)S(1)}) custom-call(bf16[2,128,1024]{2,1,0:T(8,128)(2,1)S(1)} %get-tuple-element.26.qt_ref.refs_7_, bf16[3,128,128]{2,1,0:T(8,128)(2,1)S(1)} %get-tuple-element.39.near_ref.refs_8_, bf16[3,256,128]{2,1,0:T(8,128)(2,1)S(1)} %get-tuple-element.27.far_ref, ...), custom_call_target="tpu_custom_call" | custom-call | flops 805306368 | bytes 1048576 | tf_op jit(solution)/shard_map/whole_shards_0/pallas_call | solution.py:394
  41.4 2.2 %collective-permute-done.2.refs_2_.rest_ref = bf16[512,256]{1,0:T(8,128)(2,1)S(1)} collective-permute-done((bf16[512,256]{1,0:T(8,128)(2,1)S(1)}, bf16[512,256]{1,0:T(8,128)(2,1)S(1)}, u32[]{:S(2)}, u32[]{:S(2)}) %collective-permute-start.2) | collective-permute-done | bytes 262176 | tf_op jit(solution)/shard_map/ppermute | solution.py:326
  43.6 1.8 %new_pages_and_last_stretch.1 = (bf16[8,2048]{1,0:T(8,128)(2,1)}, f32[2,1,1024]{2,1,0:T(1,128)S(1)}, f32[2,1,1024]{2,1,0:T(1,128)S(1)}, f32[2,128,1024]{2,1,0:T(8,128)S(1)}) custom-call(s32[1]{0:T(128)} %bitcast.own_ref, s32[32]{0:T(128)S(1)} %copy-done.6, s32[8]{0:T(128)S(1)} %copy-done.7, s32[8,32]{1,0:T(8,128)S(1)} %copy-done.5, ...), custom_call_target="tpu_custom_call" | custom-call | flops 134217728 | bytes 1048576 | tf_op jit(solution)/shard_map/new_pages_and_last_stretch/pallas_call | solution.py:405
  45.4 0.0 collective-permute-done.3.ck_ref
  45.4 3.2 %last_cached_keys.1 = bf16[128,2048]{1,0:T(8,128)(2,1)} custom-call(bf16[2,128,1024]{2,1,0:T(8,128)(2,1)S(1)} %get-tuple-element.26.qt_ref.refs_7_, bf16[3,256,128]{2,1,0:T(8,128)(2,1)S(1)} %get-tuple-element.27.far_ref, f32[2,1,1024]{2,1,0:T(1,128)S(1)} %get-tuple-element.46.high_in, f32[2,1,1024]{2,1,0:T(1,128)S(1)} %get-tuple-element.47.total_in, ...), custom_call_target="tpu_custom_call" | custom-call | flops 268435456 | bytes 1048576 | tf_op jit(solution)/shard_map/last_cached_keys/pallas_call | solution.py:418
  (10 shorter events, 0.0 us)
Async XLA Ops:
  0.6 18.9 %copy-start.4 = (bf16[8,2048]{1,0:T(8,128)(2,1)S(1)}, bf16[8,2048]{1,0:T(8,128)(2,1)}, u32[]{:S(2)}) copy-start(bf16[8,2048]{1,0:T(8,128)(2,1)} %q_ref.3) | copy-start | bytes 98308
  13.7 15.3 %collective-permute-start = (bf16[768,256]{1,0:T(8,128)(2,1)}, bf16[768,256]{1,0:T(8,128)(2,1)S(1)}, u32[]{:S(2)}, u32[]{:S(2)}) collective-permute-start(bf16[768,256]{1,0:T(8,128)(2,1)} %pack_own_shard.1.shard_ref.rest_ref), channel_id=1, source_target_pairs={{0,4},{4,8},{8,12},{12,0},{1,5},{5,9},{9,13},{13,1},{2,6},{6,10},{... | collective-permute-start | bytes 1179656 | tf_op jit(solution)/shard_map/ppermute | solution.py:326
  16.8 20.1 %collective-permute-start.1 = (bf16[768,256]{1,0:T(8,128)(2,1)}, bf16[768,256]{1,0:T(8,128)(2,1)S(1)}, u32[]{:S(2)}, u32[]{:S(2)}) collective-permute-start(bf16[768,256]{1,0:T(8,128)(2,1)} %pack_own_shard.1.shard_ref.rest_ref), channel_id=1, source_target_pairs={{0,12},{4,0},{8,4},{12,8},{1,13},{5,1},{9,5},{13,9},{2,14},{6,2},{... | collective-permute-start | bytes 1179656 | tf_op jit(solution)/shard_map/ppermute | solution.py:326
  18.9 0.7 %copy-start.5 = (s32[8,32]{1,0:T(8,128)S(1)}, s32[8,32]{1,0:T(8,128)}, u32[]{:S(2)}) copy-start(s32[8,32]{1,0:T(8,128)} %lists_ref.3) | copy-start | bytes 3076
  19.5 0.7 %copy-start.6 = (s32[32]{0:T(128)S(1)}, s32[32]{0:T(128)}, u32[]{:S(2)}) copy-start(s32[32]{0:T(128)} %targets_ref.3) | copy-start | bytes 388
  19.5 0.7 %copy-start.7 = (s32[8]{0:T(128)S(1)}, s32[8]{0:T(128)}, u32[]{:S(2)}) copy-start(s32[8]{0:T(128)} %length_ref.3) | copy-start | bytes 100
  20.2 1.0 %copy-start = (bf16[768,256]{1,0:T(8,128)(2,1)S(1)}, bf16[768,256]{1,0:T(8,128)(2,1)}, u32[]{:S(2)}) copy-start(bf16[768,256]{1,0:T(8,128)(2,1)} %pack_own_shard.1.shard_ref.rest_ref) | copy-start | bytes 1179652
  21.2 1.2 %copy-start.2 = (bf16[128,16,256]{2,1,0:T(8,128)(2,1)S(1)}, bf16[128,16,256]{2,1,0:T(8,128)(2,1)}, u32[]{:S(2)}) copy-start(bf16[128,16,256]{2,1,0:T(8,128)(2,1)} %pool_k.1) | copy-start | bytes 3145732
  22.4 1.2 %copy-start.3 = (bf16[128,16,256]{2,1,0:T(8,128)(2,1)S(1)}, bf16[128,16,256]{2,1,0:T(8,128)(2,1)}, u32[]{:S(2)}) copy-start(bf16[128,16,256]{2,1,0:T(8,128)(2,1)} %pool_v.1) | copy-start | bytes 3145732
  23.7 1.9 %copy-start.1 = (bf16[768,256]{1,0:T(8,128)(2,1)S(1)}, bf16[768,256]{1,0:T(8,128)(2,1)}, u32[]{:S(2)}) copy-start(bf16[768,256]{1,0:T(8,128)(2,1)} %pack_own_shard.1.shard_ref.rest_ref) | copy-start | bytes 1179652
  23.7 1.9 %copy-start.8 = (bf16[128,2048]{1,0:T(8,128)(2,1)S(1)}, bf16[128,2048]{1,0:T(8,128)(2,1)}, u32[]{:S(2)}) copy-start(bf16[128,2048]{1,0:T(8,128)(2,1)} %q_ref.2) | copy-start | bytes 1572868
  29.0 14.6 %collective-permute-start.2 = (bf16[512,256]{1,0:T(8,128)(2,1)S(1)}, bf16[512,256]{1,0:T(8,128)(2,1)S(1)}, u32[]{:S(2)}, u32[]{:S(2)}) collective-permute-start(bf16[512,256]{1,0:T(8,128)(2,1)S(1)} %slice.6), channel_id=1, source_target_pairs={{0,4},{4,8},{8,12},{12,0},{1,5},{5,9},{9,13},{13,1},{2,6},{6,10},{... | collective-permute-start | bytes 786440 | tf_op jit(solution)/shard_map/ppermute | solution.py:326
  29.1 16.3 %collective-permute-start.3 = (bf16[256,256]{1,0:T(8,128)(2,1)S(1)}, bf16[256,256]{1,0:T(8,128)(2,1)S(1)}, u32[]{:S(2)}, u32[]{:S(2)}) collective-permute-start(bf16[256,256]{1,0:T(8,128)(2,1)S(1)} %slice.7), channel_id=1, source_target_pairs={{0,4},{4,8},{8,12},{12,0},{1,5},{5,9},{9,13},{13,1},{2,6},{6,10},{... | collective-permute-start | bytes 393224 | tf_op jit(solution)/shard_map/ppermute | solution.py:326

commit v6 on v5

--- a/solution.py
+++ b/solution.py
@@ -22,26 +22,53 @@
 HBM = pl.BlockSpec(memory_space=pltpu.HBM)
 
 
-def attend(qt_ref, cols, keys, values_t, state):
-    tokens = keys.shape[1] - HEAD_DIM
-    queries = qt_ref[:, cols]
-    place = lax.broadcasted_iota(jnp.int32, (tokens, queries.shape[1]), 0)
-    token = lax.rem(lax.broadcasted_iota(jnp.int32, (tokens, queries.shape[1]), 1), tokens)
-    pick = jnp.where(place == token, jnp.float32(1.0), jnp.float32(0.0)).astype(jnp.bfloat16)
-    queries = jnp.concatenate([queries, pick], axis=0)
-    scores = jnp.dot(keys, queries, preferred_element_type=jnp.float32)
+def scores_of(qt_ref, head, cols, keys):
+    return jnp.dot(keys, qt_ref[head, :, cols], preferred_element_type=jnp.float32)
+
+
+def soften(scores, old):
     high = jnp.max(scores, axis=0, keepdims=True)
-    if state is not None:
-        old_high, old_total, old_accum = state
-        high = jnp.maximum(high, old_high)
+    if old is None:
+        weights = jnp.exp2((scores - high) * EXP2_SCALE)
+        return weights.astype(jnp.bfloat16), high, jnp.sum(weights, axis=0, keepdims=True), None
+    old_high, old_total = old
+    high = jnp.maximum(high, old_high)
+    decay = jnp.exp2((old_high - high) * EXP2_SCALE)
     weights = jnp.exp2((scores - high) * EXP2_SCALE)
-    total = jnp.sum(weights, axis=0, keepdims=True)
-    accum = jnp.dot(values_t, weights.astype(jnp.bfloat16), preferred_element_type=jnp.float32)
-    if state is not None:
-        decay = jnp.exp2((old_high - high) * EXP2_SCALE)
-        total = total + old_total * decay
-        accum = accum + old_accum * decay
-    return high, total, accum
+    total = old_total * decay + jnp.sum(weights, axis=0, keepdims=True)
+    return weights.astype(jnp.bfloat16), high, total, decay
+
+
+def walk(blocks, first, second):
+    ahead = first(blocks[0])
+    for place, block in enumerate(blocks):
+        current = ahead
+        if place + 1 < len(blocks):
+            ahead = first(blocks[place + 1])
+        second(block, current)
+
+
+def blocks_of(qt_ref):
+    kv_local, _, rows = qt_ref.shape
+    width = min(2 * (rows // GROUP), rows)
+    return [(head, slice(start, start + width)) for head in range(kv_local) for start in range(0, rows, width)]
+
+
+def attend(qt_ref, keys, values_t, old, new):
+    high_ref, total_ref, accum_ref = new
+
+    def second(block, scores):
+        head, cols = block
+        before = None if old is None else (old[0][head, :, cols], old[1][head, :, cols])
+        weights, high, total, decay = soften(scores, before)
+        accum = jnp.dot(values_t[head], weights, preferred_element_type=jnp.float32)
+        if old is not None:
+            accum = accum + old[2][head, :, cols] * decay
+        high_ref[head, :, cols] = high
+        total_ref[head, :, cols] = total
+        accum_ref[head, :, cols] = accum
+
+    walk(blocks_of(qt_ref), lambda block: scores_of(qt_ref, block[0], block[1], keys[block[0]]), second)
 
 
 def hidden(seen):
@@ -135,16 +162,12 @@
     return high, total, mixed
 
 
-def pack_kernel(sk_ref, sv_ref, cv_ref, ck_ref, out_ref, sems):
-    copies, start = [], 0
-    for place, ref in enumerate((sk_ref, sv_ref, cv_ref, ck_ref)):
-        span = pl.ds(start, ref.shape[0])
-        copies.append(pltpu.make_async_copy(ref, out_ref.at[span], sems.at[place]))
-        start += ref.shape[0]
-    for copy in copies:
-        copy.start()
-    for copy in copies:
-        copy.wait()
+def features(head):
+    return slice(head * HEAD_DIM, (head + 1) * HEAD_DIM)
+
+
+def shard_parts(ref, tokens, c_rows):
+    return slice(0, tokens + c_rows), slice(tokens + c_rows, 2 * (tokens + c_rows))
 
 
 def own_kernel(
@@ -154,29 +177,25 @@
     kv_local, _, rows = qt_ref.shape
     tokens = q_ref.shape[0]
     c_rows = far_ref.shape[1]
-    cached = 2 * tokens + c_rows
-    width = min(2 * tokens, rows)
     own = own_ref[0]
     limit = limit_ref[0]
+    place = lax.broadcasted_iota(jnp.int32, (tokens, tokens), 0)
+    token = lax.broadcasted_iota(jnp.int32, (tokens, tokens), 1)
+    pick = jnp.where(place == token, jnp.float32(1.0), jnp.float32(0.0)).astype(jnp.bfloat16)
+    for head in range(kv_local):
+        for sub in range(GROUP):
+            cols = slice(sub * tokens, (sub + 1) * tokens)
+            qt_ref[head, :HEAD_DIM, cols] = q_ref[:, features(head * GROUP + sub)].T
+            qt_ref[head, HEAD_DIM:, cols] = pick
     for place, hop in enumerate(hops):
         shard = shard_of(own, hop, count)
         near_ref[place] = stretch_mask(shard, own, tokens)
         far_ref[place] = cache_mask(shard, limit, c_rows, tokens)
     mask = jnp.concatenate([stretch_mask(own, own, tokens), cache_mask(own, limit, c_rows, tokens)], axis=0)
-    for head in range(kv_local):
-        for sub in range(GROUP):
-            col = (head * GROUP + sub) * HEAD_DIM
-            qt_ref[head, :, sub * tokens : (sub + 1) * tokens] = q_ref[:, col : col + HEAD_DIM].T
-        feats = slice(head * HEAD_DIM, (head + 1) * HEAD_DIM)
-        keys = jnp.concatenate([shard_ref[:tokens, feats], shard_ref[cached:, feats]], axis=0)
-        keys = jnp.concatenate([keys, mask], axis=1)
-        values_t = shard_ref[tokens:cached, feats].T
-        for start in range(0, rows, width):
-            cols = slice(start, start + width)
-            high, total, accum = attend(qt_ref.at[head], cols, keys, values_t, None)
-            high_ref[head, :, cols] = high
-            total_ref[head, :, cols] = total
-            accum_ref[head, :, cols] = accum
+    key_rows, value_rows = shard_parts(shard_ref, tokens, c_rows)
+    keys = [jnp.concatenate([shard_ref[key_rows, features(head)], mask], axis=1) for head in range(kv_local)]
+    values_t = [shard_ref[value_rows, features(head)].T for head in range(kv_local)]
+    attend(qt_ref, keys, values_t, None, (high_ref, total_ref, accum_ref))
 
 
 def held_kernel(
@@ -187,6 +206,7 @@
     pool = pool_k.shape[0]
     held = pool * PAGE
     tokens = PAGE * P_DEV
+    half = rest_ref.shape[0] // 2
     own = own_ref[0]
     lists = lists_ref[...]
     lengths = length_column(length_ref)
@@ -199,91 +219,88 @@
             pool_v[...].reshape(held, kv_width),
             tally_of(lists, lengths, held_slot),
         ),
-        (rest_ref[:tokens], rest_ref[tokens : 2 * tokens], tally_of(lists, lengths, own_slot)),
+        (rest_ref[:tokens], rest_ref[half : half + tokens], tally_of(lists, lengths, own_slot)),
     ]
     high_ref[...], total_ref[...], mixed_ref[...] = decode_attend(wide_ref[...], parts, None)
 
 
 def hop_kernel(places, qt_ref, near_ref, far_ref, high_in, total_in, accum_in, *refs):
     shard_refs, outs = refs[: len(places)], refs[len(places) :]
-    kv_local, _, rows = qt_ref.shape
-    tokens = rows // GROUP
-    cached = 2 * tokens + far_ref.shape[1]
-    width = min(2 * tokens, rows)
-    for head in range(kv_local):
-        feats = slice(head * HEAD_DIM, (head + 1) * HEAD_DIM)
-        keys, values, masks = [], [], []
-        for place, shard_ref in zip(places, shard_refs):
-            keys += [shard_ref[:tokens, feats], shard_ref[cached:, feats]]
-            masks += [near_ref[place], far_ref[place]]
-            values.append(shard_ref[tokens:cached, feats])
-        keys = jnp.concatenate([jnp.concatenate(keys, axis=0), jnp.concatenate(masks, axis=0)], axis=1)
-        values_t = jnp.concatenate(values, axis=0).T
-        for start in range(0, rows, width):
-            cols = slice(start, start + width)
-            state = (high_in[head, :, cols], total_in[head, :, cols], accum_in[head, :, cols])
-            high, total, accum = attend(qt_ref.at[head], cols, keys, values_t, state)
-            outs[0][head, :, cols] = high
-            outs[1][head, :, cols] = total
-            outs[2][head, :, cols] = accum
-
-
-def fresh_kernel(count, hops, pool, place, own_ref, targets_ref, length_ref, lists_ref, *refs):
-    rest_refs, refs = refs[: len(hops)], refs[len(hops) :]
-    wide_ref, dec_high, dec_total, dec_mixed, qt_ref, near_ref, high_in, total_in, accum_in = refs[:9]
-    dec_out, high_ref, total_ref, accum_ref = refs[9:]
-    kv_local, _, rows = qt_ref.shape
-    tokens = rows // GROUP
-    width = min(2 * tokens, rows)
+    tokens, c_rows = near_ref.shape[1], far_ref.shape[1]
+    mask = jnp.concatenate([ref[place] for place in places for ref in (near_ref, far_ref)], axis=0)
+    keys, values_t = [], []
+    for head in range(qt_ref.shape[0]):
+        pieces, values = [], []
+        for ref in shard_refs:
+            key_rows, value_rows = shard_parts(ref, tokens, c_rows)
+            pieces.append(ref[key_rows, features(head)])
+            values.append(ref[value_rows, features(head)])
+        keys.append(jnp.concatenate([jnp.concatenate(pieces, axis=0), mask], axis=1))
+        values_t.append(jnp.concatenate(values, axis=0).T)
+    attend(qt_ref, keys, values_t, (high_in, total_in, accum_in), outs)
+
+
+def fresh_kernel(count, hops, pool, final, own_ref, targets_ref, length_ref, lists_ref, *refs):
+    shard_refs, refs = refs[: len(hops)], refs[len(hops) :]
+    wide_ref, dec_high, dec_total, dec_mixed, qt_ref, near_ref, far_ref, high_in, total_in, accum_in = refs[:10]
+    dec_out, weights_ref, total_ref, accum_ref = refs[10:]
+    kv_local = qt_ref.shape[0]
+    tokens, c_rows = near_ref.shape[1], far_ref.shape[1]
+    half = tokens + c_rows
+    last_ref = shard_refs[final]
+    mask = jnp.concatenate([near_ref[final], far_ref[final]], axis=0)
+    keys = [jnp.concatenate([last_ref[:half, features(head)], mask], axis=1) for head in range(kv_local)]
+    values_t = [last_ref[half : half + tokens, features(head)].T for head in range(kv_local)]
+
+    def second(block, scores):
+        head, cols = block
+        before = (high_in[head, :, cols], total_in[head, :, cols])
+        weights, _, total, decay = soften(scores, before)
+        weights_ref[head, :, cols] = weights[tokens:]
+        total_ref[head, :, cols] = total
+        accum_ref[head, :, cols] = accum_in[head, :, cols] * decay + jnp.dot(
+            values_t[head], weights[:tokens], preferred_element_type=jnp.float32
+        )
+
+    walk(blocks_of(qt_ref), lambda block: scores_of(qt_ref, block[0], block[1], keys[block[0]]), second)
+
     own = own_ref[0]
     lists = lists_ref[...]
     lengths = length_column(length_ref)
     parts = []
-    for hop, ref in zip(hops, rest_refs):
+    for hop, ref in zip(hops, shard_refs):
         slot = slot_row(targets_ref, shard_of(own, hop, count), own, tokens, pool)
-        parts.append((ref[:tokens], ref[tokens : 2 * tokens], tally_of(lists, lengths, slot)))
+        parts.append((ref[:tokens], ref[half : half + tokens], tally_of(lists, lengths, slot)))
     _, total, mixed = decode_attend(wide_ref[...], parts, (dec_high[...], dec_total[...], dec_mixed[...]))
     for head in range(kv_local * GROUP):
-        kv = head // GROUP
-        piece = mixed[head, :, kv * HEAD_DIM : (kv + 1) * HEAD_DIM] / total[head]
-        dec_out[:, head * HEAD_DIM : (head + 1) * HEAD_DIM] = piece.astype(jnp.bfloat16)
-    for head in range(kv_local):
-        feats = slice(head * HEAD_DIM, (head + 1) * HEAD_DIM)
-        keys = jnp.concatenate([rest_refs[place][:tokens, feats], near_ref[place]], axis=1)
-        values_t = rest_refs[place][tokens : 2 * tokens, feats].T
-        for start in range(0, rows, width):
-            cols = slice(start, start + width)
-            state = (high_in[head, :, cols], total_in[head, :, cols], accum_in[head, :, cols])
-            high, total, accum = attend(qt_ref.at[head], cols, keys, values_t, state)
-            high_ref[head, :, cols] = high
-            total_ref[head, :, cols] = total
-            accum_ref[head, :, cols] = accum
-
-
-def last_kernel(
-    place, qt_ref, far_ref, high_in, total_in, accum_in, ck_ref, rest_ref, out_ref, result_ref, sems
-):
-    kv_local, _, rows = qt_ref.shape
-    tokens = rows // GROUP
-    width = min(2 * tokens, rows)
+        piece = mixed[head, :, features(head // GROUP)] / total[head]
+        dec_out[:, features(head)] = piece.astype(jnp.bfloat16)
+
+
+def last_kernel(weights_ref, total_ref, accum_ref, values_ref, out_ref, result_ref, sems):
+    tokens = result_ref.shape[0]
+    values_t = [values_ref[:, features(head)].T for head in range(weights_ref.shape[0])]
     copies = []
-    for head in range(kv_local):
-        feats = slice(head * HEAD_DIM, (head + 1) * HEAD_DIM)
-        keys = jnp.concatenate([ck_ref[:, feats], far_ref[place]], axis=1)
-        values_t = rest_ref[2 * tokens :, feats].T
-        for start in range(0, rows, width):
-            cols = slice(start, start + width)
-            state = (high_in[head, :, cols], total_in[head, :, cols], accum_in[head, :, cols])
-            _, total, accum = attend(qt_ref.at[head], cols, keys, values_t, state)
-            mixed = (accum * (1.0 / total)).astype(jnp.bfloat16)
-            first = (head * GROUP + start // tokens) * HEAD_DIM
-            for piece in range(width // tokens):
-                col = first + piece * HEAD_DIM
-                result_ref[:, col : col + HEAD_DIM] = mixed[:, piece * tokens : (piece + 1) * tokens].T
-            span = pl.ds(first, width // tokens * HEAD_DIM)
-            copy = pltpu.make_async_copy(result_ref.at[:, span], out_ref.at[:, span], sems.at[len(copies)])
-            copy.start()
-            copies.append(copy)
+
+    def first(block):
+        head, cols = block
+        return jnp.dot(values_t[head], weights_ref[head, :, cols], preferred_element_type=jnp.float32)
+
+    def second(block, mixed):
+        head, cols = block
+        mixed = mixed + accum_ref[head, :, cols]
+        mixed = (mixed * (1.0 / total_ref[head, :, cols])).astype(jnp.bfloat16)
+        start = (head * GROUP + cols.start // tokens) * HEAD_DIM
+        pieces = (cols.stop - cols.start) // tokens
+        for piece in range(pieces):
+            col = start + piece * HEAD_DIM
+            result_ref[:, col : col + HEAD_DIM] = mixed[:, piece * tokens : (piece + 1) * tokens].T
+        span = pl.ds(start, pieces * HEAD_DIM)
+        copy = pltpu.make_async_copy(result_ref.at[:, span], out_ref.at[:, span], sems.at[len(copies)])
+        copy.start()
+        copies.append(copy)
+
+    walk(blocks_of(weights_ref), first, second)
     for copy in copies:
         copy.wait()
 
@@ -331,16 +348,8 @@
             flops=4 * pairs * HEAD_DIM, bytes_accessed=4 * rows * kv_local * HEAD_DIM, transcendentals=pairs
         )
 
-    parts = (stretch_keys, stretch_values, cache_values, cache_keys)
-    packed = pl.pallas_call(
-        pack_kernel,
-        out_shape=shape((2 * tokens + 2 * c_rows, kv_width), bf16),
-        in_specs=[HBM] * 4,
-        out_specs=HBM,
-        scratch_shapes=[pltpu.SemaphoreType.DMA((4,))],
-        name="pack_own_shard",
-    )(*parts)
-    shard = {0: packed}
+    half = tokens + c_rows
+    shard = {0: jnp.concatenate([stretch_keys, cache_keys, stretch_values, cache_values], axis=0)}
     for hop in hops[:2]:
         shard[hop] = send(shard[0], hop)
 
@@ -352,7 +361,7 @@
     qt, near, far, *state = pl.pallas_call(
         functools.partial(own_kernel, count, hops),
         out_shape=(
-            shape((kv_local, HEAD_DIM, rows), bf16),
+            shape((kv_local, HEAD_DIM + tokens, rows), bf16),
             shape((count - 1, tokens, tokens), bf16),
             shape((count - 1, c_rows, tokens), bf16),
         )
@@ -386,8 +395,8 @@
         shard[hop] = send(shard[hop + 1 if hop < 0 else hop - 1], hop)
     hop = hops[-1]
     nearer = shard[hop + 1 if hop < 0 else hop - 1]
-    last_rest = send(nearer[: 2 * tokens + c_rows], hop)
-    last_keys = send(nearer[2 * tokens + c_rows :], hop)
+    last_rest = send(nearer[: half + tokens], hop)
+    last_values = send(nearer[half + tokens :], hop)
 
     for first in range(0, len(hops) - 1, 2):
         places = list(range(first, min(first + 2, len(hops) - 1)))
@@ -402,32 +411,37 @@
         )(qt, near, far, *state, *[shard[hops[place]] for place in places])
 
     final = len(hops) - 1
-    decoded, *state = pl.pallas_call(
+    decoded, weights, total, accum = pl.pallas_call(
         functools.partial(fresh_kernel, count, hops, pool, final),
-        out_shape=(shape(decode_queries.shape, bf16),) + state_shapes,
-        in_specs=[SMEM] * 3 + [VMEM] * (10 + len(hops)),
+        out_shape=(
+            shape(decode_queries.shape, bf16),
+            shape((kv_local, c_rows, rows), bf16),
+            shape((kv_local, 1, rows), f32),
+            shape((kv_local, HEAD_DIM, rows), f32),
+        ),
+        in_specs=[SMEM] * 3 + [VMEM] * (11 + len(hops)),
         out_specs=(VMEM,) * 4,
         compiler_params=params,
-        cost_estimate=cost(tokens),
-        name="new_pages_and_last_stretch",
+        cost_estimate=cost(half),
+        name="new_pages_and_last_scores",
     )(
         own_array, page_targets, context_length, page_lists, *[shard[hop] for hop in hops[:-1]], last_rest,
-        wide, *dec_state, qt, near, *state,
+        wide, *dec_state, qt, near, far, *state,
     )
 
     prefill = pl.pallas_call(
-        functools.partial(last_kernel, final),
+        last_kernel,
         out_shape=shape((tokens, width), bf16),
-        in_specs=[VMEM] * 7,
+        in_specs=[VMEM] * 4,
         out_specs=HBM,
         scratch_shapes=[
             pltpu.VMEM((tokens, width), bf16),
             pltpu.SemaphoreType.DMA((kv_local * max(GROUP // 2, 1),)),
         ],
         compiler_params=params,
-        cost_estimate=cost(c_rows),
-        name="last_cached_keys",
-    )(qt, far, *state, last_keys, last_rest)
+        cost_estimate=cost(c_rows // 2),
+        name="last_values",
+    )(weights, total, accum, last_values)
     return (prefill, decoded)
 
 

time: 48.9 us -> 36.9 us (0.75)
  Pallas kernels: 27.7 us -> 10.9 us
  waiting for transfers between devices: 2.42 us -> 6.3 us
  local copies, waits for them, and re-layouts: 4.13 us -> 5 us
    pallas_call x2 -> x1, Pallas kernels: 16.3 us -> 1.14 us  [per_device(): pl.pallas_call(last_kernel, out_shape=shape((tokens, width), bf16), in_sp...]
    ppermute x4, waiting for transfers between devices: 2.42 us -> 6.3 us  [send(): return lax.ppermute(array, 'ctx', up_pairs if hop < 0 else down_pairs)]
    pallas_call x1, Pallas kernels: 4.5 us -> 2.86 us  [per_device(): pl.pallas_call(functools.partial(hop_kernel, places), out_shape=state_sha...]
    pallas_call x1, Pallas kernels: 1.81 us -> 3.25 us  [per_device(): pl.pallas_call(functools.partial(fresh_kernel, count, hops, pool, final),...]
    pallas_call x1, Pallas kernels: 3.24 us -> 1.8 us  [per_device(): pl.pallas_call(functools.partial(own_kernel, count, hops), out_shape=(sha...]
    unnamed x18 -> x23, local copies, waits for them, and re-layouts: 4.1 us -> 4.96 us
  transfers between devices with their start and end apart: 4 -> 4, of which waited for: 2 -> 2; matrix products, arithmetic and copies ran while one was open for 0% -> 0% of each run, Pallas kernels for 23% -> 27%
where the time goes in v6:
time: 36.9 us; the launch traced here: 36.6 us
  starting transfers between devices  13 us (35%)
  Pallas kernels  10.9 us (30%)
  waiting for transfers between devices  6.3 us (17%)
  local copies, waits for them, and re-layouts  5 us (14%)
  between operations  1.4 us (4%)
    ppermute x4, starting transfers between devices, send(): return lax.ppermute(array, 'ctx', up_pairs if hop < 0 else down_pairs)  13 us
    ppermute x4, waiting for transfers between devices, send(): return lax.ppermute(array, 'ctx', up_pairs if hop < 0 else down_pairs)  6.3 us
    unnamed x23, local copies, waits for them, and re-layouts  4.96 us
    pallas_call x1, Pallas kernels, per_device(): pl.pallas_call(functools.partial(fresh_kernel, count, hops, pool, final),...  3.25 us
    pallas_call x1, Pallas kernels, per_device(): pl.pallas_call(functools.partial(hop_kernel, places), out_shape=state_sha...  2.86 us
    pallas_call x1, Pallas kernels, per_device(): pl.pallas_call(held_kernel, out_shape=(shape((heads * dec_rows, kv_width)...  1.87 us
    pallas_call x1, Pallas kernels, per_device(): pl.pallas_call(functools.partial(own_kernel, count, hops), out_shape=(sha...  1.8 us
    pallas_call x1, Pallas kernels, per_device(): pl.pallas_call(last_kernel, out_shape=shape((tokens, width), bf16), in_sp...  1.14 us
  transfers between devices with their start and end apart: 4, of which 2 were waited for; matrix products, arithmetic and copies ran while one was open for 0% of the time, Pallas kernels for 27%

profile of v6, /device:TPU:0, one launch (start us, length us, event | category | flops | bytes accessed | tf_op | source)
XLA Modules:
  0.0 36.6 jit_solution(14808375893424350153)
XLA Ops:
  0.6 0.0 copy-start.7
  0.6 0.9 %constant_dynamic-update-slice_fusion.3 = bf16[768,256]{1,0:T(8,128)(2,1)S(1)} fusion(bf16[128,256]{1,0:T(8,128)(2,1)} %param.13), kind=kLoop, calls=%fused_computation.3 | loop fusion | bytes 131072
  1.5 0.0 copy-done.7
  1.6 0.8 %copy-done.9 = bf16[128,256]{1,0:T(8,128)(2,1)S(1)} copy-done((bf16[128,256]{1,0:T(8,128)(2,1)S(1)}, bf16[128,256]{1,0:T(8,128)(2,1)}, u32[]{:S(2)}) %copy-start.9) | copy-done | bytes 65560
  2.4 0.1 copy-done.8
  2.5 3.1 %collective-permute-start = (bf16[768,256]{1,0:T(8,128)(2,1)S(1)}, bf16[768,256]{1,0:T(8,128)(2,1)S(1)}, u32[]{:S(2)}, u32[]{:S(2)}) collective-permute-start(bf16[768,256]{1,0:T(8,128)(2,1)S(1)} %constant_dynamic-update-slice_fusion.shard_ref.rest_ref), channel_id=1, source_target_pairs={{0,4},{4,8},{8,12},{12,0},{1,5},{5,9},{9,13},{13,1},{2,6},{6,10},{... | collective-permute-start | bytes 1179656 | tf_op jit(solution)/shard_map/ppermute | solution.py:343
  5.6 2.1 %collective-permute-start.1 = (bf16[768,256]{1,0:T(8,128)(2,1)S(1)}, bf16[768,256]{1,0:T(8,128)(2,1)S(1)}, u32[]{:S(2)}, u32[]{:S(2)}) collective-permute-start(bf16[768,256]{1,0:T(8,128)(2,1)S(1)} %constant_dynamic-update-slice_fusion.shard_ref.rest_ref), channel_id=1, source_target_pairs={{0,12},{4,0},{8,4},{12,8},{1,13},{5,1},{9,5},{13,9},{2,14},{6,2},{... | collective-permute-start | bytes 1179656 | tf_op jit(solution)/shard_map/ppermute | solution.py:343
  8.4 0.0 copy-start.4
  8.4 0.0 copy-start.5
  8.4 0.6 %copy-done.4 = s32[32]{0:T(128)S(1)} copy-done((s32[32]{0:T(128)S(1)}, s32[32]{0:T(128)}, u32[]{:S(2)}) %copy-start.4) | copy-done | bytes 152
  9.0 0.0 copy-done.5
  9.0 1.2 %copy-done = bf16[128,16,256]{2,1,0:T(8,128)(2,1)S(1)} copy-done((bf16[128,16,256]{2,1,0:T(8,128)(2,1)S(1)}, bf16[128,16,256]{2,1,0:T(8,128)(2,1)}, u32[]{:S(2)}) %copy-start) | copy-done | bytes 1048600
  10.3 1.2 %copy-done.1 = bf16[128,16,256]{2,1,0:T(8,128)(2,1)S(1)} copy-done((bf16[128,16,256]{2,1,0:T(8,128)(2,1)S(1)}, bf16[128,16,256]{2,1,0:T(8,128)(2,1)}, u32[]{:S(2)}) %copy-start.1) | copy-done | bytes 1048600
  11.5 1.9 %decode_held_pages.1 = (bf16[128,256]{1,0:T(8,128)(2,1)S(1)}, f32[16,8,1]{2,1,0:T(8,128)S(1)}, f32[16,8,1]{2,1,0:T(8,128)S(1)}, f32[16,8,256]{2,1,0:T(8,128)S(1)}) custom-call(s32[1]{0:T(128)} %bitcast.own_ref, s32[32]{0:T(128)S(1)} %copy-done.4, s32[8]{0:T(128)S(1)} %copy-done.5, bf16[8,2048]{1,0:T(8,128)(2,1)S(1)} %copy-done.2, s32[8,32]{1,0:T(8,128)S(1)} %copy-done.3, ...), custom_call_target="tpu_custom_call" | custom-call | flops 268435456 | bytes 2097152 | tf_op jit(solution)/shard_map/decode_held_pages/pallas_call | solution.py:376
  13.4 1.8 %own_shard.1 = (bf16[2,256,1024]{2,1,0:T(8,128)(2,1)S(1)}, bf16[3,128,128]{2,1,0:T(8,128)(2,1)S(1)}, bf16[3,256,128]{2,1,0:T(8,128)(2,1)S(1)}, f32[2,1,1024]{2,1...) custom-call(s32[1]{0:T(128)} %bitcast.own_ref, s32[1]{0:T(128)S(6)} %copy.17.limit_ref, ...), custom_call_target="tpu_custom_call" | custom-call | flops 402653184 | bytes 1048576 | tf_op jit(solution)/shard_map/own_shard/pallas_call | solution.py:361
  15.2 2.4 %collective-permute-done.refs_0_ = bf16[768,256]{1,0:T(8,128)(2,1)S(1)} collective-permute-done((bf16[768,256]{1,0:T(8,128)(2,1)S(1)}, bf16[768,256]{1,0:T(8,128)(2,1)S(1)}, u32[]{:S(2)}, u32[]{:S(2)}) %collective-permute-start) | collective-permute-done | bytes 393248 | tf_op jit(solution)/shard_map/ppermute | solution.py:343
  17.6 0.1 collective-permute-start.2
  17.7 7.8 %collective-permute-start.3 = (bf16[256,256]{1,0:T(8,128)(2,1)S(1)}, bf16[256,256]{1,0:T(8,128)(2,1)S(1)}, u32[]{:S(2)}, u32[]{:S(2)}) collective-permute-start(bf16[256,256]{1,0:T(8,128)(2,1)S(1)} %slice.7), channel_id=1, source_target_pairs={{0,4},{4,8},{8,12},{12,0},{1,5},{5,9},{9,13},{13,1},{2,6},{6,10},{... | collective-permute-start | bytes 393224 | tf_op jit(solution)/shard_map/ppermute | solution.py:343
  25.5 0.0 collective-permute-done.1.refs_1_
  25.5 2.9 %whole_shards_0.1 = (f32[2,1,1024]{2,1,0:T(1,128)S(1)}, f32[2,1,1024]{2,1,0:T(1,128)S(1)}, f32[2,128,1024]{2,1,0:T(8,128)S(1)}) custom-call(bf16[2,256,1024]{2,1,0:T(8,128)(2,1)S(1)} %get-tuple-element.37.qt_ref.refs_7_, bf16[3,128,128]{2,1,0:T(8,128)(2,1)S(1)} %get-tuple-element.38.near_ref.refs_8_, ...), custom_call_target="tpu_custom_call" | custom-call | flops 805306368 | bytes 1048576 | tf_op jit(solution)/shard_map/whole_shards_0/pallas_call | solution.py:403
  28.4 3.9 %collective-permute-done.2.refs_2_ = bf16[512,256]{1,0:T(8,128)(2,1)S(1)} collective-permute-done((bf16[512,256]{1,0:T(8,128)(2,1)S(1)}, bf16[512,256]{1,0:T(8,128)(2,1)S(1)}, u32[]{:S(2)}, u32[]{:S(2)}) %collective-permute-start.2) | collective-permute-done | bytes 262176 | tf_op jit(solution)/shard_map/ppermute | solution.py:343
  32.2 3.3 %new_pages_and_last_scores.1 = (bf16[8,2048]{1,0:T(8,128)(2,1)}, bf16[2,256,1024]{2,1,0:T(8,128)(2,1)S(1)}, f32[2,1,1024]{2,1,0:T(1,128)S(1)}, f32[2,128,1024]{2,1,0:T(8,128)S(1)}) custom-call(s32[1]{0:T(128)} %bitcast.own_ref, s32[32]{0:T(128)S(1)} %copy-done.4, s32[8]{0:T(128)S(1)} %copy-done.5, s32[8,32]{1,0:T(8,128)S(1)} %copy-done.3, ...), custom_call_target="tpu_custom_call" | custom-call | flops 402653184 | bytes 1048576 | tf_op jit(solution)/shard_map/new_pages_and_last_scores/pallas_call | solution.py:414
  35.5 0.0 collective-permute-done.3.values_ref
  35.5 1.1 %last_values.1 = bf16[128,2048]{1,0:T(8,128)(2,1)} custom-call(bf16[2,256,1024]{2,1,0:T(8,128)(2,1)S(1)} %get-tuple-element.46.weights_ref, f32[2,1,1024]{2,1,0:T(1,128)S(1)} %get-tuple-element.47.total_ref, f32[2,128,1024]{2,1,0:T(8,128)S(1)} %get-tuple-element.48.accum_ref, bf16[256,256]{1,0:T(8,128)(2,1)S(1)} %collective-permute-done.3.values_ref), custom_call_target="tpu_custom_call" | custom-call | flops 134217728 | bytes 1048576 | tf_op jit(solution)/shard_map/last_values/pallas_call | solution.py:432
  (15 shorter events, 0.1 us)
Async XLA Ops:
  0.6 0.9 %copy-start.7 = (bf16[256,256]{1,0:T(8,128)(2,1)S(1)}, bf16[256,256]{1,0:T(8,128)(2,1)}, u32[]{:S(2)}) copy-start(bf16[256,256]{1,0:T(8,128)(2,1)} %param.15) | copy-start | bytes 393220
  1.6 0.8 %copy-start.9 = (bf16[128,256]{1,0:T(8,128)(2,1)S(1)}, bf16[128,256]{1,0:T(8,128)(2,1)}, u32[]{:S(2)}) copy-start(bf16[128,256]{1,0:T(8,128)(2,1)} %param.14) | copy-start | bytes 196612
  1.6 0.9 %copy-start.8 = (bf16[256,256]{1,0:T(8,128)(2,1)S(1)}, bf16[256,256]{1,0:T(8,128)(2,1)}, u32[]{:S(2)}) copy-start(bf16[256,256]{1,0:T(8,128)(2,1)} %param.16) | copy-start | bytes 393220
  2.5 5.9 %copy-start.2 = (bf16[8,2048]{1,0:T(8,128)(2,1)S(1)}, bf16[8,2048]{1,0:T(8,128)(2,1)}, u32[]{:S(2)}) copy-start(bf16[8,2048]{1,0:T(8,128)(2,1)} %q_ref.3) | copy-start | bytes 98308
  2.5 15.1 %collective-permute-start = (bf16[768,256]{1,0:T(8,128)(2,1)S(1)}, bf16[768,256]{1,0:T(8,128)(2,1)S(1)}, u32[]{:S(2)}, u32[]{:S(2)}) collective-permute-start(bf16[768,256]{1,0:T(8,128)(2,1)S(1)} %constant_dynamic-update-slice_fusion.shard_ref.rest_ref), channel_id=1, source_target_pairs={{0,4},{4,8},{8,12},{12,0},{1,5},{5,9},{9,13},{13,1},{2,6},{6,10},{... | collective-permute-start | bytes 1179656 | tf_op jit(solution)/shard_map/ppermute | solution.py:343
  5.6 19.9 %collective-permute-start.1 = (bf16[768,256]{1,0:T(8,128)(2,1)S(1)}, bf16[768,256]{1,0:T(8,128)(2,1)S(1)}, u32[]{:S(2)}, u32[]{:S(2)}) collective-permute-start(bf16[768,256]{1,0:T(8,128)(2,1)S(1)} %constant_dynamic-update-slice_fusion.shard_ref.rest_ref), channel_id=1, source_target_pairs={{0,12},{4,0},{8,4},{12,8},{1,13},{5,1},{9,5},{13,9},{2,14},{6,2},{... | collective-permute-start | bytes 1179656 | tf_op jit(solution)/shard_map/ppermute | solution.py:343
  7.7 0.7 %copy-start.3 = (s32[8,32]{1,0:T(8,128)S(1)}, s32[8,32]{1,0:T(8,128)}, u32[]{:S(2)}) copy-start(s32[8,32]{1,0:T(8,128)} %lists_ref.3) | copy-start | bytes 3076
  8.4 0.7 %copy-start.4 = (s32[32]{0:T(128)S(1)}, s32[32]{0:T(128)}, u32[]{:S(2)}) copy-start(s32[32]{0:T(128)} %targets_ref.3) | copy-start | bytes 388
  8.4 0.7 %copy-start.5 = (s32[8]{0:T(128)S(1)}, s32[8]{0:T(128)}, u32[]{:S(2)}) copy-start(s32[8]{0:T(128)} %length_ref.3) | copy-start | bytes 100
  9.0 1.2 %copy-start = (bf16[128,16,256]{2,1,0:T(8,128)(2,1)S(1)}, bf16[128,16,256]{2,1,0:T(8,128)(2,1)}, u32[]{:S(2)}) copy-start(bf16[128,16,256]{2,1,0:T(8,128)(2,1)} %pool_k.1) | copy-start | bytes 3145732
  10.3 1.2 %copy-start.1 = (bf16[128,16,256]{2,1,0:T(8,128)(2,1)S(1)}, bf16[128,16,256]{2,1,0:T(8,128)(2,1)}, u32[]{:S(2)}) copy-start(bf16[128,16,256]{2,1,0:T(8,128)(2,1)} %pool_v.1) | copy-start | bytes 3145732
  11.5 1.9 %copy-start.6 = (bf16[128,2048]{1,0:T(8,128)(2,1)S(1)}, bf16[128,2048]{1,0:T(8,128)(2,1)}, u32[]{:S(2)}) copy-start(bf16[128,2048]{1,0:T(8,128)(2,1)} %q_ref.2) | copy-start | bytes 1572868
  17.6 14.6 %collective-permute-start.2 = (bf16[512,256]{1,0:T(8,128)(2,1)S(1)}, bf16[512,256]{1,0:T(8,128)(2,1)S(1)}, u32[]{:S(2)}, u32[]{:S(2)}) collective-permute-start(bf16[512,256]{1,0:T(8,128)(2,1)S(1)} %slice.6), channel_id=1, source_target_pairs={{0,4},{4,8},{8,12},{12,0},{1,5},{5,9},{9,13},{13,1},{2,6},{6,10},{... | collective-permute-start | bytes 786440 | tf_op jit(solution)/shard_map/ppermute | solution.py:343
  17.7 17.8 %collective-permute-start.3 = (bf16[256,256]{1,0:T(8,128)(2,1)S(1)}, bf16[256,256]{1,0:T(8,128)(2,1)S(1)}, u32[]{:S(2)}, u32[]{:S(2)}) collective-permute-start(bf16[256,256]{1,0:T(8,128)(2,1)S(1)} %slice.7), channel_id=1, source_target_pairs={{0,4},{4,8},{8,12},{12,0},{1,5},{5,9},{9,13},{13,1},{2,6},{6,10},{... | collective-permute-start | bytes 393224 | tf_op jit(solution)/shard_map/ppermute | solution.py:343

commit v7 on v6

--- a/solution.py
+++ b/solution.py
@@ -13,6 +13,7 @@
 GROUP = HEADS // KV_HEADS
 PAGE = 16
 P_DEV = 8
+SEND_CAP = 2
 EXP2_SCALE = HEAD_DIM ** (-0.5) * 1.4426950408889634
 HIDDEN = -1e30
 VMEM_BYTES = 48 * 1024 * 1024
@@ -91,9 +92,27 @@
     slots = jnp.full((1, tokens), -1, jnp.int32)
     for index in range(tokens // PAGE):
         target = targets_ref[shard * (tokens // PAGE) + index]
-        slot = jnp.where(target // P_DEV == own, pool + target % P_DEV, -1)
+        slot = jnp.where(lax.div(target, P_DEV) == own, pool + lax.rem(target, P_DEV), -1)
         slots = jnp.where(page == index, slot, slots)
     return slots
+
+
+def sent_pages(targets_ref, shard, owner, pages):
+    one, two = jnp.int32(-1), jnp.int32(-1)
+    for index in range(pages):
+        hit = lax.div(targets_ref[shard * pages + index], P_DEV) == owner
+        two = jnp.where(hit & (one >= 0) & (two < 0), index, two)
+        one = jnp.where(hit & (one < 0), index, one)
+    return one, two
+
+
+def sent_slots(targets_ref, shard, owner, pages, pool):
+    place = lax.broadcasted_iota(jnp.int32, (1, SEND_CAP * PAGE), 1)
+    slots = []
+    for index in sent_pages(targets_ref, shard, owner, pages):
+        target = targets_ref[shard * pages + jnp.maximum(index, 0)]
+        slots.append(jnp.where(index >= 0, pool + lax.rem(target, P_DEV), -1))
+    return jnp.where(place < PAGE, slots[0], slots[1])
 
 
 def length_column(length_ref):
@@ -171,8 +190,8 @@
 
 
 def own_kernel(
-    count, hops, own_ref, limit_ref, q_ref, shard_ref,
-    qt_ref, near_ref, far_ref, high_ref, total_ref, accum_ref,
+    count, hops, own_ref, limit_ref, targets_ref, q_ref, shard_ref,
+    qt_ref, near_ref, far_ref, pick_ref, high_ref, total_ref, accum_ref,
 ):
     kv_local, _, rows = qt_ref.shape
     tokens = q_ref.shape[0]
@@ -191,6 +210,17 @@
         shard = shard_of(own, hop, count)
         near_ref[place] = stretch_mask(shard, own, tokens)
         far_ref[place] = cache_mask(shard, limit, c_rows, tokens)
+    onward = 1 if hops[-1] < 0 else -1
+    pages = tokens // PAGE
+    one, two = sent_pages(
+        targets_ref, shard_of(own, hops[-1] + onward, count), shard_of(own, onward, count), pages
+    )
+    row = lax.broadcasted_iota(jnp.int32, pick_ref.shape, 0)
+    token = lax.broadcasted_iota(jnp.int32, pick_ref.shape, 1)
+    sent = ((row < PAGE) & (one >= 0) & (token == row + one * PAGE)) | (
+        (row >= PAGE) & (two >= 0) & (token == row + (two - 1) * PAGE)
+    )
+    pick_ref[...] = jnp.where(sent, jnp.float32(1.0), jnp.float32(0.0)).astype(jnp.bfloat16)
     mask = jnp.concatenate([stretch_mask(own, own, tokens), cache_mask(own, limit, c_rows, tokens)], axis=0)
     key_rows, value_rows = shard_parts(shard_ref, tokens, c_rows)
     keys = [jnp.concatenate([shard_ref[key_rows, features(head)], mask], axis=1) for head in range(kv_local)]
@@ -240,17 +270,54 @@
     attend(qt_ref, keys, values_t, (high_in, total_in, accum_in), outs)
 
 
-def fresh_kernel(count, hops, pool, final, own_ref, targets_ref, length_ref, lists_ref, *refs):
+def split_kernel(pick_ref, shard_ref, first_ref, stretch_ref, values_ref):
+    tokens = pick_ref.shape[1]
+    half = shard_ref.shape[0] // 2
+    c_rows = half - tokens
+    first_ref[:c_rows] = shard_ref[tokens:half]
+    sent = pick_ref.shape[0]
+    for place, start in enumerate((0, half)):
+        rows = jnp.dot(pick_ref[...], shard_ref[start : start + tokens], preferred_element_type=jnp.float32)
+        first_ref[c_rows + place * sent : c_rows + (place + 1) * sent] = rows.astype(jnp.bfloat16)
+        stretch_ref[place * tokens : (place + 1) * tokens] = shard_ref[start : start + tokens]
+    values_ref[...] = shard_ref[half + tokens :]
+
+
+def pages_kernel(count, hops, tokens, pool, own_ref, targets_ref, length_ref, lists_ref, *refs):
     shard_refs, refs = refs[: len(hops)], refs[len(hops) :]
-    wide_ref, dec_high, dec_total, dec_mixed, qt_ref, near_ref, far_ref, high_in, total_in, accum_in = refs[:10]
-    dec_out, weights_ref, total_ref, accum_ref = refs[10:]
+    wide_ref, dec_high, dec_total, dec_mixed, dec_out = refs
+    own = own_ref[0]
+    pages = tokens // PAGE
+    lists = lists_ref[...]
+    lengths = length_column(length_ref)
+    parts = []
+    for hop, ref in zip(hops[:-1], shard_refs):
+        half = ref.shape[0] // 2
+        slot = slot_row(targets_ref, shard_of(own, hop, count), own, tokens, pool)
+        parts.append((ref[:tokens], ref[half : half + tokens], tally_of(lists, lengths, slot)))
+    ref = shard_refs[-1]
+    sent = SEND_CAP * PAGE
+    start = ref.shape[0] - 2 * sent
+    slot = sent_slots(targets_ref, shard_of(own, hops[-1], count), own, pages, pool)
+    parts.append((ref[start : start + sent], ref[start + sent :], tally_of(lists, lengths, slot)))
+    _, total, mixed = decode_attend(wide_ref[...], parts, (dec_high[...], dec_total[...], dec_mixed[...]))
+    for head in range(dec_high.shape[0]):
+        piece = mixed[head, :, features(head // GROUP)] / total[head]
+        dec_out[:, features(head)] = piece.astype(jnp.bfloat16)
+
+
+def score_kernel(
+    final, qt_ref, near_ref, far_ref, high_in, total_in, accum_in, first_ref, stretch_ref,
+    weights_ref, total_ref, accum_ref,
+):
     kv_local = qt_ref.shape[0]
     tokens, c_rows = near_ref.shape[1], far_ref.shape[1]
-    half = tokens + c_rows
-    last_ref = shard_refs[final]
     mask = jnp.concatenate([near_ref[final], far_ref[final]], axis=0)
-    keys = [jnp.concatenate([last_ref[:half, features(head)], mask], axis=1) for head in range(kv_local)]
-    values_t = [last_ref[half : half + tokens, features(head)].T for head in range(kv_local)]
+    keys, values_t = [], []
+    for head in range(kv_local):
+        pieces = [stretch_ref[:tokens, features(head)], first_ref[:c_rows, features(head)]]
+        keys.append(jnp.concatenate([jnp.concatenate(pieces, axis=0), mask], axis=1))
+        values_t.append(stretch_ref[tokens:, features(head)].T)
 
     def second(block, scores):
         head, cols = block
@@ -263,18 +330,6 @@
         )
 
     walk(blocks_of(qt_ref), lambda block: scores_of(qt_ref, block[0], block[1], keys[block[0]]), second)
-
-    own = own_ref[0]
-    lists = lists_ref[...]
-    lengths = length_column(length_ref)
-    parts = []
-    for hop, ref in zip(hops, shard_refs):
-        slot = slot_row(targets_ref, shard_of(own, hop, count), own, tokens, pool)
-        parts.append((ref[:tokens], ref[half : half + tokens], tally_of(lists, lengths, slot)))
-    _, total, mixed = decode_attend(wide_ref[...], parts, (dec_high[...], dec_total[...], dec_mixed[...]))
-    for head in range(kv_local * GROUP):
-        piece = mixed[head, :, features(head // GROUP)] / total[head]
-        dec_out[:, features(head)] = piece.astype(jnp.bfloat16)
 
 
 def last_kernel(weights_ref, total_ref, accum_ref, values_ref, out_ref, result_ref, sems):
@@ -349,7 +404,13 @@
         )
 
     half = tokens + c_rows
-    shard = {0: jnp.concatenate([stretch_keys, cache_keys, stretch_values, cache_values], axis=0)}
+    low = jnp.array(-jnp.inf, bf16)
+    spread, start = [], 0
+    for part in (stretch_keys, cache_keys, stretch_values, cache_values):
+        end = 2 * half - start - part.shape[0]
+        spread.append(lax.pad(part, low, ((start, end, 0), (0, 0, 0))))
+        start += part.shape[0]
+    shard = {0: functools.reduce(jnp.maximum, spread)}
     for hop in hops[:2]:
         shard[hop] = send(shard[0], hop)
 
@@ -358,20 +419,21 @@
         shape((kv_local, 1, rows), f32),
         shape((kv_local, HEAD_DIM, rows), f32),
     )
-    qt, near, far, *state = pl.pallas_call(
+    qt, near, far, pick, *state = pl.pallas_call(
         functools.partial(own_kernel, count, hops),
         out_shape=(
             shape((kv_local, HEAD_DIM + tokens, rows), bf16),
             shape((count - 1, tokens, tokens), bf16),
             shape((count - 1, c_rows, tokens), bf16),
+            shape((SEND_CAP * PAGE, tokens), bf16),
         )
         + state_shapes,
-        in_specs=[SMEM, SMEM] + [VMEM] * 2,
-        out_specs=(VMEM,) * 6,
+        in_specs=[SMEM] * 3 + [VMEM] * 2,
+        out_specs=(VMEM,) * 7,
         compiler_params=params,
         cost_estimate=cost(tokens + c_rows),
         name="own_shard",
-    )(own_array, prefix_length, queries, shard[0])
+    )(own_array, prefix_length, page_targets, queries, shard[0])
 
     wide, *dec_state = pl.pallas_call(
         held_kernel,
@@ -395,8 +457,26 @@
         shard[hop] = send(shard[hop + 1 if hop < 0 else hop - 1], hop)
     hop = hops[-1]
     nearer = shard[hop + 1 if hop < 0 else hop - 1]
-    last_rest = send(nearer[: half + tokens], hop)
-    last_values = send(nearer[half + tokens :], hop)
+    pieces = pl.pallas_call(
+        split_kernel,
+        out_shape=(
+            shape((c_rows + 2 * SEND_CAP * PAGE, kv_width), bf16),
+            shape((2 * tokens, kv_width), bf16),
+            shape((c_rows, kv_width), bf16),
+        ),
+        in_specs=[VMEM] * 2,
+        out_specs=(VMEM,) * 3,
+        compiler_params=params,
+        name="pieces_to_send_on",
+    )(pick, nearer)
+    last_keys = send(pieces[0], hop)
+    if 2 * hop == -count:
+        pairs = [(i - 1, i) for i in range(count // 2, count)]
+        pairs += [(i, i) for i in range(count // 2 - 1)] + [(count - 1, count // 2 - 1)]
+        last_stretch = lax.ppermute(pieces[1], "ctx", pairs)
+    else:
+        last_stretch = send(pieces[1], hop)
+    last_values = send(pieces[2], hop)
 
     for first in range(0, len(hops) - 1, 2):
         places = list(range(first, min(first + 2, len(hops) - 1)))
@@ -411,23 +491,28 @@
         )(qt, near, far, *state, *[shard[hops[place]] for place in places])
 
     final = len(hops) - 1
-    decoded, weights, total, accum = pl.pallas_call(
-        functools.partial(fresh_kernel, count, hops, pool, final),
-        out_shape=(
-            shape(decode_queries.shape, bf16),
-            shape((kv_local, c_rows, rows), bf16),
-            shape((kv_local, 1, rows), f32),
-            shape((kv_local, HEAD_DIM, rows), f32),
-        ),
-        in_specs=[SMEM] * 3 + [VMEM] * (11 + len(hops)),
-        out_specs=(VMEM,) * 4,
+    decoded = pl.pallas_call(
+        functools.partial(pages_kernel, count, hops, tokens, pool),
+        out_shape=shape(decode_queries.shape, bf16),
+        in_specs=[SMEM] * 3 + [VMEM] * (5 + len(hops)),
+        out_specs=VMEM,
+        compiler_params=params,
+        cost_estimate=cost(tokens),
+        name="decode_new_pages",
+    )(
+        own_array, page_targets, context_length, page_lists, *[shard[hop] for hop in hops[:-1]], last_keys,
+        wide, *dec_state,
+    )
+
+    weights, total, accum = pl.pallas_call(
+        functools.partial(score_kernel, final),
+        out_shape=(shape((kv_local, c_rows, rows), bf16),) + state_shapes[1:],
+        in_specs=[VMEM] * 8,
+        out_specs=(VMEM,) * 3,
         compiler_params=params,
         cost_estimate=cost(half),
-        name="new_pages_and_last_scores",
-    )(
-        own_array, page_targets, context_length, page_lists, *[shard[hop] for hop in hops[:-1]], last_rest,
-        wide, *dec_state, qt, near, far, *state,
-    )
+        name="last_scores",
+    )(qt, near, far, *state, last_keys, last_stretch)
 
     prefill = pl.pallas_call(
         last_kernel,

time: 36.9 us -> 36.1 us (0.978)
  waiting for transfers between devices: 6.3 us -> 1.87 us
  starting transfers between devices: 13 us -> 16.6 us
  local copies, waits for them, and re-layouts: 5 us -> 3.1 us
  other arithmetic: 0 us -> 1.03 us
  Pallas kernels: 10.9 us -> 11.8 us
    ppermute x4, waiting for transfers between devices: 6.3 us -> 1.87 us  [send(): return lax.ppermute(array, 'ctx', up_pairs if hop < 0 else down_pairs)]
    ppermute x4, starting transfers between devices: 13 us -> 15.9 us  [send(): return lax.ppermute(array, 'ctx', up_pairs if hop < 0 else down_pairs)]
    unnamed x23 -> x14, local copies, waits for them, and re-layouts: 4.96 us -> 3.1 us
    max x0 -> x1, other arithmetic: none -> 1.03 us  [per_device(): shard = {0: functools.reduce(jnp.maximum, spread)}]
    ppermute x0 -> x1, starting transfers between devices: none -> 0.67 us  [per_device(): last_stretch = lax.ppermute(pieces[1], 'ctx', pairs)]
    pallas_call x1, Pallas kernels: 1.8 us -> 2.37 us  [per_device(): pl.pallas_call(functools.partial(own_kernel, count, hops), out_shape=(sha...]
    pallas_call x1 -> x3, Pallas kernels: 3.25 us -> 3.51 us  [the longest x1 1.76 us: per_device(): pl.pallas_call(functools.partial(pages_kernel, count, hops, tokens, pool)...]
  transfers between devices with their start and end apart: 4 -> 5, of which waited for: 2 -> 1; matrix products, arithmetic and copies ran while one was open for 0% -> 0% of each run, Pallas kernels for 27% -> 30%
where the time goes in v7:
time: 36.1 us; the launch traced here: 35.8 us
  starting transfers between devices  16.6 us (46%)
  Pallas kernels  11.8 us (33%)
  local copies, waits for them, and re-layouts  3.1 us (9%)
  waiting for transfers between devices  1.87 us (5%)
  between operations  1.42 us (4%)
  other arithmetic  1.03 us (3%)
    ppermute x4, starting transfers between devices, send(): return lax.ppermute(array, 'ctx', up_pairs if hop < 0 else down_pairs)  15.9 us
    unnamed x14, local copies, waits for them, and re-layouts  3.1 us
    pallas_call x1, Pallas kernels, per_device(): pl.pallas_call(functools.partial(hop_kernel, places), out_shape=state_sha...  2.88 us
    pallas_call x1, Pallas kernels, per_device(): pl.pallas_call(functools.partial(own_kernel, count, hops), out_shape=(sha...  2.37 us
    ppermute x4, waiting for transfers between devices, send(): return lax.ppermute(array, 'ctx', up_pairs if hop < 0 else down_pairs)  1.87 us
    pallas_call x1, Pallas kernels, per_device(): pl.pallas_call(held_kernel, out_shape=(shape((heads * dec_rows, kv_width)...  1.86 us
    pallas_call x1, Pallas kernels, per_device(): pl.pallas_call(functools.partial(pages_kernel, count, hops, tokens, pool)...  1.76 us
    pallas_call x1, Pallas kernels, per_device(): pl.pallas_call(functools.partial(score_kernel, final), out_shape=(shape((...  1.61 us
  transfers between devices with their start and end apart: 5, of which 1 were waited for; matrix products, arithmetic and copies ran while one was open for 0% of the time, Pallas kernels for 30%

profile of v7, /device:TPU:0, one launch (start us, length us, event | category | flops | bytes accessed | tf_op | source)
XLA Modules:
  0.0 35.8 jit_solution(14253580727143885975)
XLA Ops:
  0.6 1.0 %pad_maximum_fusion.shard_ref.rest_ref = bf16[768,256]{1,0:T(8,128)(2,1)S(1)} fusion(bf16[256,256]{1,0:T(8,128)(2,1)} %param.16, bf16[128,256]{1,0:T(8,128)(2,1)} %param.14, bf16[256,256]{1,0:T(8,128)(2,1)} %param.15, bf16[128,256]{1,0:T(8,128)(2,1)} %param.13), kind=kLoop, calls=%fused_computation | loop fusion | flops 1572864 | bytes 786432 | tf_op jit(solution)/shard_map/max | solution.py:413
  1.7 3.1 %collective-permute-start = (bf16[768,256]{1,0:T(8,128)(2,1)S(1)}, bf16[768,256]{1,0:T(8,128)(2,1)S(1)}, u32[]{:S(2)}, u32[]{:S(2)}) collective-permute-start(bf16[768,256]{1,0:T(8,128)(2,1)S(1)} %pad_maximum_fusion.shard_ref.rest_ref), channel_id=1, source_target_pairs={{0,4},{4,8},{8,12},{12,0},{1,5},{5,9},{9,13},{13,1},{2,6},{6,10},{... | collective-permute-start | bytes 1179656 | tf_op jit(solution)/shard_map/ppermute | solution.py:398
  4.8 2.1 %collective-permute-start.1 = (bf16[768,256]{1,0:T(8,128)(2,1)S(1)}, bf16[768,256]{1,0:T(8,128)(2,1)S(1)}, u32[]{:S(2)}, u32[]{:S(2)}) collective-permute-start(bf16[768,256]{1,0:T(8,128)(2,1)S(1)} %pad_maximum_fusion.shard_ref.rest_ref), channel_id=1, source_target_pairs={{0,12},{4,0},{8,4},{12,8},{1,13},{5,1},{9,5},{13,9},{2,14},{6,2},{... | collective-permute-start | bytes 1179656 | tf_op jit(solution)/shard_map/ppermute | solution.py:398
  7.5 0.0 copy-start.4
  7.5 0.0 copy-start.5
  7.6 0.6 %copy-done.4 = s32[32]{0:T(128)S(1)} copy-done((s32[32]{0:T(128)S(1)}, s32[32]{0:T(128)}, u32[]{:S(2)}) %copy-start.4) | copy-done | bytes 152
  8.2 0.0 copy-done.5
  8.2 1.2 %copy-done = bf16[128,16,256]{2,1,0:T(8,128)(2,1)S(1)} copy-done((bf16[128,16,256]{2,1,0:T(8,128)(2,1)S(1)}, bf16[128,16,256]{2,1,0:T(8,128)(2,1)}, u32[]{:S(2)}) %copy-start) | copy-done | bytes 1048600
  9.4 1.2 %copy-done.1 = bf16[128,16,256]{2,1,0:T(8,128)(2,1)S(1)} copy-done((bf16[128,16,256]{2,1,0:T(8,128)(2,1)S(1)}, bf16[128,16,256]{2,1,0:T(8,128)(2,1)}, u32[]{:S(2)}) %copy-start.1) | copy-done | bytes 1048600
  10.6 1.9 %decode_held_pages.1 = (bf16[128,256]{1,0:T(8,128)(2,1)S(1)}, f32[16,8,1]{2,1,0:T(8,128)S(1)}, f32[16,8,1]{2,1,0:T(8,128)S(1)}, f32[16,8,256]{2,1,0:T(8,128)S(1)}) custom-call(s32[1]{0:T(128)} %bitcast.own_ref, s32[32]{0:T(128)S(1)} %copy-done.4, s32[8]{0:T(128)S(1)} %copy-done.5, bf16[8,2048]{1,0:T(8,128)(2,1)S(1)} %copy-done.2, s32[8,32]{1,0:T(8,128)S(1)} %copy-done.3, ...), custom_call_target="tpu_custom_call" | custom-call | flops 268435456 | bytes 2097152 | tf_op jit(solution)/shard_map/decode_held_pages/pallas_call | solution.py:438
  12.5 2.4 %own_shard.1 = (bf16[2,256,1024]{2,1,0:T(8,128)(2,1)S(1)}, bf16[3,128,128]{2,1,0:T(8,128)(2,1)S(1)}, bf16[3,256,128]{2,1,0:T(8,128)(2,1)S(1)}, bf16[32,128]{1,0:...) custom-call(s32[1]{0:T(128)} %bitcast.own_ref, ...), custom_call_target="tpu_custom_call" | custom-call | flops 402653184 | bytes 1048576 | tf_op jit(solution)/shard_map/own_shard/pallas_call | solution.py:422
  14.9 1.9 %collective-permute-done.refs_0_.shard_ref = bf16[768,256]{1,0:T(8,128)(2,1)S(1)} collective-permute-done((bf16[768,256]{1,0:T(8,128)(2,1)S(1)}, bf16[768,256]{1,0:T(8,128)(2,1)S(1)}, u32[]{:S(2)}, u32[]{:S(2)}) %collective-permute-start) | collective-permute-done | bytes 393248 | tf_op jit(solution)/shard_map/ppermute | solution.py:398
  16.8 0.1 pieces_to_send_on.1
  16.9 0.1 collective-permute-start.2
  17.0 0.7 %collective-permute-start.3 = (bf16[256,256]{1,0:T(8,128)(2,1)S(1)}, bf16[256,256]{1,0:T(8,128)(2,1)S(1)}, u32[]{:S(2)}, u32[]{:S(2)}) collective-permute-start(bf16[256,256]{1,0:T(8,128)(2,1)S(1)} %get-tuple-element.47), channel_id=1, source_target_pairs={{4,8},{8,12},{0,0},{12,4},{5,9},{9,13},{1,1},{13,5},{6,10},{10,14}... | collective-permute-start | bytes 393224 | tf_op jit(solution)/shard_map/ppermute | solution.py:476
  17.7 10.7 %collective-permute-start.4 = (bf16[256,256]{1,0:T(8,128)(2,1)S(1)}, bf16[256,256]{1,0:T(8,128)(2,1)S(1)}, u32[]{:S(2)}, u32[]{:S(2)}) collective-permute-start(bf16[256,256]{1,0:T(8,128)(2,1)S(1)} %get-tuple-element.51), channel_id=1, source_target_pairs={{0,4},{4,8},{8,12},{12,0},{1,5},{5,9},{9,13},{13,1},{2,6},{6,10},{... | collective-permute-start | bytes 393224 | tf_op jit(solution)/shard_map/ppermute | solution.py:398
  28.4 0.0 collective-permute-done.1.refs_1_
  28.4 2.9 %whole_shards_0.1 = (f32[2,1,1024]{2,1,0:T(1,128)S(1)}, f32[2,1,1024]{2,1,0:T(1,128)S(1)}, f32[2,128,1024]{2,1,0:T(8,128)S(1)}) custom-call(bf16[2,256,1024]{2,1,0:T(8,128)(2,1)S(1)} %get-tuple-element.29.qt_ref, bf16[3,128,128]{2,1,0:T(8,128)(2,1)S(1)} %get-tuple-element.30.near_ref, bf16[3,256,128]{2,1,0:T(8,128)(2,1)S(1)} %get-tuple-element.31.far_ref, ...), custom_call_target="tpu_custom_call" | custom-call | flops 805306368 | bytes 1048576 | tf_op jit(solution)/shard_map/whole_shards_0/pallas_call | solution.py:483
  31.3 0.0 collective-permute-done.2.first_ref.refs_2_
  31.3 1.8 %decode_new_pages.1 = bf16[8,2048]{1,0:T(8,128)(2,1)} custom-call(s32[1]{0:T(128)} %bitcast.own_ref, s32[32]{0:T(128)S(1)} %copy-done.4, s32[8]{0:T(128)S(1)} %copy-done.5, s32[8,32]{1,0:T(8,128)S(1)} %copy-done.3, bf16[768,256]{1,0:T(8,128)(2,1)S(1)} %collective-permute-done.refs_0_.shard_ref, bf16[768,256]{1,0:T(8,128)(2,1)S(1)} %collective-permute-done.1.refs_1_, ...), custom_call_target="tpu_custom_call" | custom-call | flops 134217728 | bytes 1048576 | tf_op jit(solution)/shard_map/decode_new_pages/pallas_call | solution.py:494
  33.0 0.0 collective-permute-done.3.stretch_ref
  33.0 1.6 %last_scores.1 = (bf16[2,256,1024]{2,1,0:T(8,128)(2,1)S(1)}, f32[2,1,1024]{2,1,0:T(1,128)S(1)}, f32[2,128,1024]{2,1,0:T(8,128)S(1)}) custom-call(bf16[2,256,1024]{2,1,0:T(8,128)(2,1)S(1)} %get-tuple-element.29.qt_ref, bf16[3,128,128]{2,1,0:T(8,128)(2,1)S(1)} %get-tuple-element.30.near_ref, bf16[3,256,128]{2,1,0:T(8,128)(2,1)S(1)} %get-tuple-element.31.far_ref, ...), custom_call_target="tpu_custom_call" | custom-call | flops 402653184 | bytes 1048576 | tf_op jit(solution)/shard_map/last_scores/pallas_call | solution.py:507
  34.7 0.0 collective-permute-done.4.values_ref
  34.7 1.1 %last_values.1 = bf16[128,2048]{1,0:T(8,128)(2,1)} custom-call(bf16[2,256,1024]{2,1,0:T(8,128)(2,1)S(1)} %get-tuple-element.48.weights_ref, f32[2,1,1024]{2,1,0:T(1,128)S(1)} %get-tuple-element.49.total_ref, f32[2,128,1024]{2,1,0:T(8,128)S(1)} %get-tuple-element.50.accum_ref, bf16[256,256]{1,0:T(8,128)(2,1)S(1)} %collective-permute-done.4.values_ref), custom_call_target="tpu_custom_call" | custom-call | flops 134217728 | bytes 1048576 | tf_op jit(solution)/shard_map/last_values/pallas_call | solution.py:517
  (8 shorter events, 0.0 us)
Async XLA Ops:
  0.6 6.9 %copy-start.2 = (bf16[8,2048]{1,0:T(8,128)(2,1)S(1)}, bf16[8,2048]{1,0:T(8,128)(2,1)}, u32[]{:S(2)}) copy-start(bf16[8,2048]{1,0:T(8,128)(2,1)} %q_ref.3) | copy-start | bytes 98308
  1.7 15.1 %collective-permute-start = (bf16[768,256]{1,0:T(8,128)(2,1)S(1)}, bf16[768,256]{1,0:T(8,128)(2,1)S(1)}, u32[]{:S(2)}, u32[]{:S(2)}) collective-permute-start(bf16[768,256]{1,0:T(8,128)(2,1)S(1)} %pad_maximum_fusion.shard_ref.rest_ref), channel_id=1, source_target_pairs={{0,4},{4,8},{8,12},{12,0},{1,5},{5,9},{9,13},{13,1},{2,6},{6,10},{... | collective-permute-start | bytes 1179656 | tf_op jit(solution)/shard_map/ppermute | solution.py:398
  4.8 23.6 %collective-permute-start.1 = (bf16[768,256]{1,0:T(8,128)(2,1)S(1)}, bf16[768,256]{1,0:T(8,128)(2,1)S(1)}, u32[]{:S(2)}, u32[]{:S(2)}) collective-permute-start(bf16[768,256]{1,0:T(8,128)(2,1)S(1)} %pad_maximum_fusion.shard_ref.rest_ref), channel_id=1, source_target_pairs={{0,12},{4,0},{8,4},{12,8},{1,13},{5,1},{9,5},{13,9},{2,14},{6,2},{... | collective-permute-start | bytes 1179656 | tf_op jit(solution)/shard_map/ppermute | solution.py:398
  6.8 0.7 %copy-start.3 = (s32[8,32]{1,0:T(8,128)S(1)}, s32[8,32]{1,0:T(8,128)}, u32[]{:S(2)}) copy-start(s32[8,32]{1,0:T(8,128)} %lists_ref.3) | copy-start | bytes 3076
  7.5 0.7 %copy-start.4 = (s32[32]{0:T(128)S(1)}, s32[32]{0:T(128)}, u32[]{:S(2)}) copy-start(s32[32]{0:T(128)} %targets_ref.5) | copy-start | bytes 388
  7.5 0.7 %copy-start.5 = (s32[8]{0:T(128)S(1)}, s32[8]{0:T(128)}, u32[]{:S(2)}) copy-start(s32[8]{0:T(128)} %length_ref.3) | copy-start | bytes 100
  8.2 1.2 %copy-start = (bf16[128,16,256]{2,1,0:T(8,128)(2,1)S(1)}, bf16[128,16,256]{2,1,0:T(8,128)(2,1)}, u32[]{:S(2)}) copy-start(bf16[128,16,256]{2,1,0:T(8,128)(2,1)} %pool_k.1) | copy-start | bytes 3145732
  9.4 1.2 %copy-start.1 = (bf16[128,16,256]{2,1,0:T(8,128)(2,1)S(1)}, bf16[128,16,256]{2,1,0:T(8,128)(2,1)}, u32[]{:S(2)}) copy-start(bf16[128,16,256]{2,1,0:T(8,128)(2,1)} %pool_v.1) | copy-start | bytes 3145732
  10.6 1.9 %copy-start.6 = (bf16[128,2048]{1,0:T(8,128)(2,1)S(1)}, bf16[128,2048]{1,0:T(8,128)(2,1)}, u32[]{:S(2)}) copy-start(bf16[128,2048]{1,0:T(8,128)(2,1)} %q_ref.2) | copy-start | bytes 1572868
  16.9 14.4 %collective-permute-start.2 = (bf16[320,256]{1,0:T(8,128)(2,1)S(1)}, bf16[320,256]{1,0:T(8,128)(2,1)S(1)}, u32[]{:S(2)}, u32[]{:S(2)}) collective-permute-start(bf16[320,256]{1,0:T(8,128)(2,1)S(1)} %get-tuple-element.46), channel_id=1, source_target_pairs={{0,4},{4,8},{8,12},{12,0},{1,5},{5,9},{9,13},{13,1},{2,6},{6,10},{... | collective-permute-start | bytes 491528 | tf_op jit(solution)/shard_map/ppermute | solution.py:398
  17.0 16.1 %collective-permute-start.3 = (bf16[256,256]{1,0:T(8,128)(2,1)S(1)}, bf16[256,256]{1,0:T(8,128)(2,1)S(1)}, u32[]{:S(2)}, u32[]{:S(2)}) collective-permute-start(bf16[256,256]{1,0:T(8,128)(2,1)S(1)} %get-tuple-element.47), channel_id=1, source_target_pairs={{4,8},{8,12},{0,0},{12,4},{5,9},{9,13},{1,1},{13,5},{6,10},{10,14}... | collective-permute-start | bytes 393224 | tf_op jit(solution)/shard_map/ppermute | solution.py:476
  17.7 17.0 %collective-permute-start.4 = (bf16[256,256]{1,0:T(8,128)(2,1)S(1)}, bf16[256,256]{1,0:T(8,128)(2,1)S(1)}, u32[]{:S(2)}, u32[]{:S(2)}) collective-permute-start(bf16[256,256]{1,0:T(8,128)(2,1)S(1)} %get-tuple-element.51), channel_id=1, source_target_pairs={{0,4},{4,8},{8,12},{12,0},{1,5},{5,9},{9,13},{13,1},{2,6},{6,10},{... | collective-permute-start | bytes 393224 | tf_op jit(solution)/shard_map/ppermute | solution.py:398

commit v8 on v7

--- a/solution.py
+++ b/solution.py
@@ -411,8 +411,7 @@
         spread.append(lax.pad(part, low, ((start, end, 0), (0, 0, 0))))
         start += part.shape[0]
     shard = {0: functools.reduce(jnp.maximum, spread)}
-    for hop in hops[:2]:
-        shard[hop] = send(shard[0], hop)
+    shard[-1] = send(shard[0], -1)
 
     state_shapes = (
         shape((kv_local, 1, rows), f32),
@@ -434,6 +433,10 @@
         cost_estimate=cost(tokens + c_rows),
         name="own_shard",
     )(own_array, prefix_length, page_targets, queries, shard[0])
+
+    if 1 in hops:
+        sent_down, state = lax.optimization_barrier((shard[0], state))
+        shard[1] = send(sent_down, 1)
 
     wide, *dec_state = pl.pallas_call(
         held_kernel,
@@ -478,8 +481,8 @@
         last_stretch = send(pieces[1], hop)
     last_values = send(pieces[2], hop)
 
-    for first in range(0, len(hops) - 1, 2):
-        places = list(range(first, min(first + 2, len(hops) - 1)))
+    for first in range(len(hops) - 1):
+        places = [first]
         state = pl.pallas_call(
             functools.partial(hop_kernel, places),
             out_shape=state_shapes,

time: 36.1 us -> 37.4 us (1.036)
  waiting for transfers between devices: 1.87 us -> 3.26 us
  local copies, waits for them, and re-layouts: 3.1 us -> 2.36 us
  Pallas kernels: 11.8 us -> 12.3 us
    ppermute x4, waiting for transfers between devices: 1.87 us -> 3.26 us  [send(): return lax.ppermute(array, 'ctx', up_pairs if hop < 0 else down_pairs)]
    unnamed x14 -> x16, local copies, waits for them, and re-layouts: 3.1 us -> 2.36 us
    pallas_call x1 -> x2, Pallas kernels: 2.88 us -> 3.46 us  [per_device(): pl.pallas_call(functools.partial(hop_kernel, places), out_shape=state_sha...]
where the time goes in v8:
time: 37.4 us; the launch traced here: 37.2 us
  starting transfers between devices  16.6 us (44%)
  Pallas kernels  12.3 us (33%)
  waiting for transfers between devices  3.26 us (9%)
  local copies, waits for them, and re-layouts  2.36 us (6%)
  between operations  1.43 us (4%)
  other arithmetic  1.17 us (3%)
    ppermute x4, starting transfers between devices, send(): return lax.ppermute(array, 'ctx', up_pairs if hop < 0 else down_pairs)  15.9 us
    pallas_call x2, Pallas kernels, per_device(): pl.pallas_call(functools.partial(hop_kernel, places), out_shape=state_sha...  3.46 us
    ppermute x4, waiting for transfers between devices, send(): return lax.ppermute(array, 'ctx', up_pairs if hop < 0 else down_pairs)  3.26 us
    pallas_call x1, Pallas kernels, per_device(): pl.pallas_call(functools.partial(own_kernel, count, hops), out_shape=(sha...  2.38 us
    unnamed x16, local copies, waits for them, and re-layouts  2.36 us
    pallas_call x1, Pallas kernels, per_device(): pl.pallas_call(held_kernel, out_shape=(shape((heads * dec_rows, kv_width)...  1.87 us
    pallas_call x1, Pallas kernels, per_device(): pl.pallas_call(functools.partial(pages_kernel, count, hops, tokens, pool)...  1.75 us
    pallas_call x1, Pallas kernels, per_device(): pl.pallas_call(functools.partial(score_kernel, final), out_shape=(shape((...  1.61 us
  transfers between devices with their start and end apart: 5, of which 1 were waited for; matrix products, arithmetic and copies ran while one was open for 0% of the time, Pallas kernels for 30%

profile of v8, /device:TPU:0, one launch (start us, length us, event | category | flops | bytes accessed | tf_op | source)
XLA Modules:
  0.0 37.2 jit_solution(1020490763368476514)
XLA Ops:
  0.7 1.2 %pad_maximum_fusion.shard_ref.rest_ref = bf16[768,256]{1,0:T(8,128)(2,1)S(1)} fusion(bf16[256,256]{1,0:T(8,128)(2,1)} %param.16, bf16[128,256]{1,0:T(8,128)(2,1)} %param.14, bf16[256,256]{1,0:T(8,128)(2,1)} %param.15, bf16[128,256]{1,0:T(8,128)(2,1)} %param.13), kind=kLoop, calls=%fused_computation | loop fusion | flops 1572864 | bytes 786432 | tf_op jit(solution)/shard_map/max | solution.py:413
  1.8 3.1 %collective-permute-start = (bf16[768,256]{1,0:T(8,128)(2,1)S(1)}, bf16[768,256]{1,0:T(8,128)(2,1)S(1)}, u32[]{:S(2)}, u32[]{:S(2)}) collective-permute-start(bf16[768,256]{1,0:T(8,128)(2,1)S(1)} %pad_maximum_fusion.shard_ref.rest_ref), channel_id=1, source_target_pairs={{0,4},{4,8},{8,12},{12,0},{1,5},{5,9},{9,13},{13,1},{2,6},{6,10},{... | collective-permute-start | bytes 1179656 | tf_op jit(solution)/shard_map/ppermute | solution.py:398
  5.6 0.0 copy-start.4
  5.6 0.6 %copy-done.4 = s32[32]{0:T(128)S(1)} copy-done((s32[32]{0:T(128)S(1)}, s32[32]{0:T(128)}, u32[]{:S(2)}) %copy-start.4) | copy-done | bytes 152
  6.2 1.0 %copy-done.7 = bf16[128,2048]{1,0:T(8,128)(2,1)S(1)} copy-done((bf16[128,2048]{1,0:T(8,128)(2,1)S(1)}, bf16[128,2048]{1,0:T(8,128)(2,1)}, u32[]{:S(2)}) %copy-start.7) | copy-done | bytes 524312
  7.3 2.4 %own_shard.1 = (bf16[2,256,1024]{2,1,0:T(8,128)(2,1)S(1)}, bf16[3,128,128]{2,1,0:T(8,128)(2,1)S(1)}, bf16[3,256,128]{2,1,0:T(8,128)(2,1)S(1)}, bf16[32,128]{1,0:...) custom-call(s32[1]{0:T(128)} %bitcast.own_ref, ...), custom_call_target="tpu_custom_call" | custom-call | flops 402653184 | bytes 1048576 | tf_op jit(solution)/shard_map/own_shard/pallas_call | solution.py:421
  9.6 0.0 copy-start.3
  9.7 0.0 copy-start.6
  9.7 2.1 %collective-permute-start.1 = (bf16[768,256]{1,0:T(8,128)(2,1)S(1)}, bf16[768,256]{1,0:T(8,128)(2,1)S(1)}, u32[]{:S(2)}, u32[]{:S(2)}) collective-permute-start(bf16[768,256]{1,0:T(8,128)(2,1)S(1)} %pad_maximum_fusion.shard_ref.rest_ref), channel_id=1, source_target_pairs={{0,12},{4,0},{8,4},{12,8},{1,13},{5,1},{9,5},{13,9},{2,14},{6,2},{... | collective-permute-start | bytes 1179656 | tf_op jit(solution)/shard_map/ppermute | solution.py:398
  11.8 1.9 %decode_held_pages.1 = (bf16[128,256]{1,0:T(8,128)(2,1)S(1)}, f32[16,8,1]{2,1,0:T(8,128)S(1)}, f32[16,8,1]{2,1,0:T(8,128)S(1)}, f32[16,8,256]{2,1,0:T(8,128)S(1)}) custom-call(s32[1]{0:T(128)} %bitcast.own_ref, s32[32]{0:T(128)S(1)} %copy-done.4, s32[8]{0:T(128)S(1)} %copy-done.6, bf16[8,2048]{1,0:T(8,128)(2,1)S(1)} %copy-done.2, s32[8,32]{1,0:T(8,128)S(1)} %copy-done.3, ...), custom_call_target="tpu_custom_call" | custom-call | flops 268435456 | bytes 2097152 | tf_op jit(solution)/shard_map/decode_held_pages/pallas_call | solution.py:441
  13.7 3.3 %collective-permute-done.refs_0_.shard_ref = bf16[768,256]{1,0:T(8,128)(2,1)S(1)} collective-permute-done((bf16[768,256]{1,0:T(8,128)(2,1)S(1)}, bf16[768,256]{1,0:T(8,128)(2,1)S(1)}, u32[]{:S(2)}, u32[]{:S(2)}) %collective-permute-start) | collective-permute-done | bytes 393248 | tf_op jit(solution)/shard_map/ppermute | solution.py:398
  16.9 0.1 pieces_to_send_on.1
  17.1 0.1 collective-permute-start.2
  17.1 0.7 %collective-permute-start.3 = (bf16[256,256]{1,0:T(8,128)(2,1)S(1)}, bf16[256,256]{1,0:T(8,128)(2,1)S(1)}, u32[]{:S(2)}, u32[]{:S(2)}) collective-permute-start(bf16[256,256]{1,0:T(8,128)(2,1)S(1)} %get-tuple-element.61), channel_id=1, source_target_pairs={{4,8},{8,12},{0,0},{12,4},{5,9},{9,13},{1,1},{13,5},{6,10},{10,14}... | collective-permute-start | bytes 393224 | tf_op jit(solution)/shard_map/ppermute | solution.py:479
  17.8 10.7 %collective-permute-start.4 = (bf16[256,256]{1,0:T(8,128)(2,1)S(1)}, bf16[256,256]{1,0:T(8,128)(2,1)S(1)}, u32[]{:S(2)}, u32[]{:S(2)}) collective-permute-start(bf16[256,256]{1,0:T(8,128)(2,1)S(1)} %get-tuple-element.65), channel_id=1, source_target_pairs={{0,4},{4,8},{8,12},{12,0},{1,5},{5,9},{9,13},{13,1},{2,6},{6,10},{... | collective-permute-start | bytes 393224 | tf_op jit(solution)/shard_map/ppermute | solution.py:398
  28.5 1.7 %whole_shards_0.1 = (f32[2,1,1024]{2,1,0:T(1,128)S(1)}, f32[2,1,1024]{2,1,0:T(1,128)S(1)}, f32[2,128,1024]{2,1,0:T(8,128)S(1)}) custom-call(bf16[2,256,1024]{2,1,0:T(8,128)(2,1)S(1)} %get-tuple-element.36.qt_ref, bf16[3,128,128]{2,1,0:T(8,128)(2,1)S(1)} %get-tuple-element.37.near_ref, bf16[3,256,128]{2,1,0:T(8,128)(2,1)S(1)} %get-tuple-element.38.far_ref, ...), custom_call_target="tpu_custom_call" | custom-call | flops 402653184 | bytes 1048576 | tf_op jit(solution)/shard_map/whole_shards_0/pallas_call | solution.py:486
  30.3 1.7 %whole_shards_1.1 = (f32[2,1,1024]{2,1,0:T(1,128)S(1)}, f32[2,1,1024]{2,1,0:T(1,128)S(1)}, f32[2,128,1024]{2,1,0:T(8,128)S(1)}) custom-call(bf16[2,256,1024]{2,1,0:T(8,128)(2,1)S(1)} %get-tuple-element.36.qt_ref, bf16[3,128,128]{2,1,0:T(8,128)(2,1)S(1)} %get-tuple-element.37.near_ref, bf16[3,256,128]{2,1,0:T(8,128)(2,1)S(1)} %get-tuple-element.38.far_ref, ...), custom_call_target="tpu_custom_call" | custom-call | flops 402653184 | bytes 1048576 | tf_op jit(solution)/shard_map/whole_shards_1/pallas_call | solution.py:486
  32.0 0.0 copy-start.5
  32.0 0.0 collective-permute-done.2.first_ref.refs_2_
  32.0 0.6 %copy-done.5 = s32[32]{0:T(128)S(1)} copy-done((s32[32]{0:T(128)S(1)}, s32[32]{0:T(128)}, u32[]{:S(2)}) %copy-start.5) | copy-done | bytes 152
  32.7 1.8 %decode_new_pages.1 = bf16[8,2048]{1,0:T(8,128)(2,1)} custom-call(s32[1]{0:T(128)} %bitcast.own_ref, s32[32]{0:T(128)S(1)} %copy-done.5, s32[8]{0:T(128)S(1)} %copy-done.6, s32[8,32]{1,0:T(8,128)S(1)} %copy-done.3, bf16[768,256]{1,0:T(8,128)(2,1)S(1)} %collective-permute-done.refs_0_.shard_ref, bf16[768,256]{1,0:T(8,128)(2,1)S(1)} %collective-permute-done.1.refs_0_.refs_1_, ...), custom_call_target="tpu_custom_call" | custom-call | flops 134217728 | bytes 1048576 | tf_op jit(solution)/shard_map/decode_new_pages/pallas_call | solution.py:497
  34.4 0.0 collective-permute-done.3.stretch_ref
  34.4 1.6 %last_scores.1 = (bf16[2,256,1024]{2,1,0:T(8,128)(2,1)S(1)}, f32[2,1,1024]{2,1,0:T(1,128)S(1)}, f32[2,128,1024]{2,1,0:T(8,128)S(1)}) custom-call(bf16[2,256,1024]{2,1,0:T(8,128)(2,1)S(1)} %get-tuple-element.36.qt_ref, bf16[3,128,128]{2,1,0:T(8,128)(2,1)S(1)} %get-tuple-element.37.near_ref, bf16[3,256,128]{2,1,0:T(8,128)(2,1)S(1)} %get-tuple-element.38.far_ref, ...), custom_call_target="tpu_custom_call" | custom-call | flops 402653184 | bytes 1048576 | tf_op jit(solution)/shard_map/last_scores/pallas_call | solution.py:510
  36.0 1.1 %last_values.1 = bf16[128,2048]{1,0:T(8,128)(2,1)} custom-call(bf16[2,256,1024]{2,1,0:T(8,128)(2,1)S(1)} %get-tuple-element.62.weights_ref, f32[2,1,1024]{2,1,0:T(1,128)S(1)} %get-tuple-element.63.total_ref, f32[2,128,1024]{2,1,0:T(8,128)S(1)} %get-tuple-element.64.accum_ref, bf16[256,256]{1,0:T(8,128)(2,1)S(1)} %collective-permute-done.4.values_ref), custom_call_target="tpu_custom_call" | custom-call | flops 134217728 | bytes 1048576 | tf_op jit(solution)/shard_map/last_values/pallas_call | solution.py:520
  (11 shorter events, 0.0 us)
Async XLA Ops:
  0.6 11.1 %copy-start.1 = (bf16[128,16,256]{2,1,0:T(8,128)(2,1)S(1)}, bf16[128,16,256]{2,1,0:T(8,128)(2,1)}, u32[]{:S(2)}) copy-start(bf16[128,16,256]{2,1,0:T(8,128)(2,1)} %pool_v.1) | copy-start | bytes 3145732
  0.6 11.1 %copy-start = (bf16[128,16,256]{2,1,0:T(8,128)(2,1)S(1)}, bf16[128,16,256]{2,1,0:T(8,128)(2,1)}, u32[]{:S(2)}) copy-start(bf16[128,16,256]{2,1,0:T(8,128)(2,1)} %pool_k.1) | copy-start | bytes 3145732
  1.8 15.1 %collective-permute-start = (bf16[768,256]{1,0:T(8,128)(2,1)S(1)}, bf16[768,256]{1,0:T(8,128)(2,1)S(1)}, u32[]{:S(2)}, u32[]{:S(2)}) collective-permute-start(bf16[768,256]{1,0:T(8,128)(2,1)S(1)} %pad_maximum_fusion.shard_ref.rest_ref), channel_id=1, source_target_pairs={{0,4},{4,8},{8,12},{12,0},{1,5},{5,9},{9,13},{13,1},{2,6},{6,10},{... | collective-permute-start | bytes 1179656 | tf_op jit(solution)/shard_map/ppermute | solution.py:398
  5.6 0.7 %copy-start.4 = (s32[32]{0:T(128)S(1)}, s32[32]{0:T(128)}, u32[]{:S(2)}) copy-start(s32[32]{0:T(128)} %targets_ref.5) | copy-start | bytes 388
  6.2 1.0 %copy-start.7 = (bf16[128,2048]{1,0:T(8,128)(2,1)S(1)}, bf16[128,2048]{1,0:T(8,128)(2,1)}, u32[]{:S(2)}) copy-start(bf16[128,2048]{1,0:T(8,128)(2,1)} %q_ref.2) | copy-start | bytes 1572868
  7.3 4.5 %copy-start.2 = (bf16[8,2048]{1,0:T(8,128)(2,1)S(1)}, bf16[8,2048]{1,0:T(8,128)(2,1)}, u32[]{:S(2)}) copy-start(bf16[8,2048]{1,0:T(8,128)(2,1)} %q_ref.3) | copy-start | bytes 98308
  9.6 2.1 %copy-start.3 = (s32[8,32]{1,0:T(8,128)S(1)}, s32[8,32]{1,0:T(8,128)}, u32[]{:S(2)}) copy-start(s32[8,32]{1,0:T(8,128)} %lists_ref.3) | copy-start | bytes 3076
  9.7 2.1 %copy-start.6 = (s32[8]{0:T(128)S(1)}, s32[8]{0:T(128)}, u32[]{:S(2)}) copy-start(s32[8]{0:T(128)} %length_ref.3) | copy-start | bytes 100
  9.7 20.6 %collective-permute-start.1 = (bf16[768,256]{1,0:T(8,128)(2,1)S(1)}, bf16[768,256]{1,0:T(8,128)(2,1)S(1)}, u32[]{:S(2)}, u32[]{:S(2)}) collective-permute-start(bf16[768,256]{1,0:T(8,128)(2,1)S(1)} %pad_maximum_fusion.shard_ref.rest_ref), channel_id=1, source_target_pairs={{0,12},{4,0},{8,4},{12,8},{1,13},{5,1},{9,5},{13,9},{2,14},{6,2},{... | collective-permute-start | bytes 1179656 | tf_op jit(solution)/shard_map/ppermute | solution.py:398
  17.1 15.0 %collective-permute-start.2 = (bf16[320,256]{1,0:T(8,128)(2,1)S(1)}, bf16[320,256]{1,0:T(8,128)(2,1)S(1)}, u32[]{:S(2)}, u32[]{:S(2)}) collective-permute-start(bf16[320,256]{1,0:T(8,128)(2,1)S(1)} %get-tuple-element.60), channel_id=1, source_target_pairs={{0,4},{4,8},{8,12},{12,0},{1,5},{5,9},{9,13},{13,1},{2,6},{6,10},{... | collective-permute-start | bytes 491528 | tf_op jit(solution)/shard_map/ppermute | solution.py:398
  17.1 17.3 %collective-permute-start.3 = (bf16[256,256]{1,0:T(8,128)(2,1)S(1)}, bf16[256,256]{1,0:T(8,128)(2,1)S(1)}, u32[]{:S(2)}, u32[]{:S(2)}) collective-permute-start(bf16[256,256]{1,0:T(8,128)(2,1)S(1)} %get-tuple-element.61), channel_id=1, source_target_pairs={{4,8},{8,12},{0,0},{12,4},{5,9},{9,13},{1,1},{13,5},{6,10},{10,14}... | collective-permute-start | bytes 393224 | tf_op jit(solution)/shard_map/ppermute | solution.py:479
  17.8 18.2 %collective-permute-start.4 = (bf16[256,256]{1,0:T(8,128)(2,1)S(1)}, bf16[256,256]{1,0:T(8,128)(2,1)S(1)}, u32[]{:S(2)}, u32[]{:S(2)}) collective-permute-start(bf16[256,256]{1,0:T(8,128)(2,1)S(1)} %get-tuple-element.65), channel_id=1, source_target_pairs={{0,4},{4,8},{8,12},{12,0},{1,5},{5,9},{9,13},{13,1},{2,6},{6,10},{... | collective-permute-start | bytes 393224 | tf_op jit(solution)/shard_map/ppermute | solution.py:398
  32.0 0.7 %copy-start.5 = (s32[32]{0:T(128)S(1)}, s32[32]{0:T(128)}, u32[]{:S(2)}) copy-start(s32[32]{0:T(128)} %targets_ref.5) | copy-start | bytes 388

commit v9 on v8

--- a/solution.py
+++ b/solution.py
@@ -434,10 +434,6 @@
         name="own_shard",
     )(own_array, prefix_length, page_targets, queries, shard[0])
 
-    if 1 in hops:
-        sent_down, state = lax.optimization_barrier((shard[0], state))
-        shard[1] = send(sent_down, 1)
-
     wide, *dec_state = pl.pallas_call(
         held_kernel,
         out_shape=(
@@ -455,6 +451,9 @@
         name="decode_held_pages",
     )(own_array, page_targets, context_length, decode_queries, page_lists, pool_keys, pool_values, shard[0])
 
+    if 1 in hops:
+        sent_down, state, dec_state = lax.optimization_barrier((shard[0], state, dec_state))
+        shard[1] = send(sent_down, 1)
     shard[-1], state, dec_state = lax.optimization_barrier((shard[-1], state, dec_state))
     for hop in hops[2:-1]:
         shard[hop] = send(shard[hop + 1 if hop < 0 else hop - 1], hop)

time: 37.4 us -> 36 us (0.963)
  starting transfers between devices: 16.6 us -> 9.94 us
  waiting for transfers between devices: 3.26 us -> 7.93 us
  local copies, waits for them, and re-layouts: 2.36 us -> 3.1 us
    ppermute x4, starting transfers between devices: 15.9 us -> 9.28 us  [send(): return lax.ppermute(array, 'ctx', up_pairs if hop < 0 else down_pairs)]
    ppermute x4, waiting for transfers between devices: 3.26 us -> 7.93 us  [send(): return lax.ppermute(array, 'ctx', up_pairs if hop < 0 else down_pairs)]
    unnamed x16 -> x14, local copies, waits for them, and re-layouts: 2.36 us -> 3.1 us
  transfers between devices with their start and end apart: 5 -> 5, of which waited for: 1 -> 4; matrix products, arithmetic and copies ran while one was open for 0% -> 0% of each run, Pallas kernels for 30% -> 31%
where the time goes in v9:
time: 36 us; the launch traced here: 35.7 us
  Pallas kernels  12.3 us (34%)
  starting transfers between devices  9.94 us (28%)
  waiting for transfers between devices  7.93 us (22%)
  local copies, waits for them, and re-layouts  3.1 us (9%)
  between operations  1.41 us (4%)
  other arithmetic  1.03 us (3%)
    ppermute x4, starting transfers between devices, send(): return lax.ppermute(array, 'ctx', up_pairs if hop < 0 else down_pairs)  9.28 us
    ppermute x4, waiting for transfers between devices, send(): return lax.ppermute(array, 'ctx', up_pairs if hop < 0 else down_pairs)  7.93 us
    pallas_call x2, Pallas kernels, per_device(): pl.pallas_call(functools.partial(hop_kernel, places), out_shape=state_sha...  3.45 us
    unnamed x14, local copies, waits for them, and re-layouts  3.1 us
    pallas_call x1, Pallas kernels, per_device(): pl.pallas_call(functools.partial(own_kernel, count, hops), out_shape=(sha...  2.36 us
    pallas_call x1, Pallas kernels, per_device(): pl.pallas_call(held_kernel, out_shape=(shape((heads * dec_rows, kv_width)...  1.86 us
    pallas_call x1, Pallas kernels, per_device(): pl.pallas_call(functools.partial(pages_kernel, count, hops, tokens, pool)...  1.75 us
    pallas_call x1, Pallas kernels, per_device(): pl.pallas_call(functools.partial(score_kernel, final), out_shape=(shape((...  1.6 us
  transfers between devices with their start and end apart: 5, of which 4 were waited for; matrix products, arithmetic and copies ran while one was open for 0% of the time, Pallas kernels for 31%

profile of v9, /device:TPU:0, one launch (start us, length us, event | category | flops | bytes accessed | tf_op | source)
XLA Modules:
  0.0 35.7 jit_solution(7876139207618305355)
XLA Ops:
  0.6 1.0 %pad_maximum_fusion.shard_ref.rest_ref = bf16[768,256]{1,0:T(8,128)(2,1)S(1)} fusion(bf16[256,256]{1,0:T(8,128)(2,1)} %param.16, bf16[128,256]{1,0:T(8,128)(2,1)} %param.14, bf16[256,256]{1,0:T(8,128)(2,1)} %param.15, bf16[128,256]{1,0:T(8,128)(2,1)} %param.13), kind=kLoop, calls=%fused_computation | loop fusion | flops 1572864 | bytes 786432 | tf_op jit(solution)/shard_map/max | solution.py:413
  1.7 3.1 %collective-permute-start = (bf16[768,256]{1,0:T(8,128)(2,1)S(1)}, bf16[768,256]{1,0:T(8,128)(2,1)S(1)}, u32[]{:S(2)}, u32[]{:S(2)}) collective-permute-start(bf16[768,256]{1,0:T(8,128)(2,1)S(1)} %pad_maximum_fusion.shard_ref.rest_ref), channel_id=1, source_target_pairs={{0,4},{4,8},{8,12},{12,0},{1,5},{5,9},{9,13},{13,1},{2,6},{6,10},{... | collective-permute-start | bytes 1179656 | tf_op jit(solution)/shard_map/ppermute | solution.py:398
  5.4 0.0 copy-start.4
  5.4 0.0 copy-start.5
  5.5 0.6 %copy-done.4 = s32[32]{0:T(128)S(1)} copy-done((s32[32]{0:T(128)S(1)}, s32[32]{0:T(128)}, u32[]{:S(2)}) %copy-start.4) | copy-done | bytes 152
  6.1 0.0 copy-done.5
  6.1 1.2 %copy-done = bf16[128,16,256]{2,1,0:T(8,128)(2,1)S(1)} copy-done((bf16[128,16,256]{2,1,0:T(8,128)(2,1)S(1)}, bf16[128,16,256]{2,1,0:T(8,128)(2,1)}, u32[]{:S(2)}) %copy-start) | copy-done | bytes 1048600
  7.3 1.2 %copy-done.1 = bf16[128,16,256]{2,1,0:T(8,128)(2,1)S(1)} copy-done((bf16[128,16,256]{2,1,0:T(8,128)(2,1)S(1)}, bf16[128,16,256]{2,1,0:T(8,128)(2,1)}, u32[]{:S(2)}) %copy-start.1) | copy-done | bytes 1048600
  8.5 1.9 %decode_held_pages.1 = (bf16[128,256]{1,0:T(8,128)(2,1)S(1)}, f32[16,8,1]{2,1,0:T(8,128)S(1)}, f32[16,8,1]{2,1,0:T(8,128)S(1)}, f32[16,8,256]{2,1,0:T(8,128)S(1)}) custom-call(s32[1]{0:T(128)} %bitcast.own_ref, s32[32]{0:T(128)S(1)} %copy-done.4, s32[8]{0:T(128)S(1)} %copy-done.5, bf16[8,2048]{1,0:T(8,128)(2,1)S(1)} %copy-done.2, s32[8,32]{1,0:T(8,128)S(1)} %copy-done.3, ...), custom_call_target="tpu_custom_call" | custom-call | flops 268435456 | bytes 2097152 | tf_op jit(solution)/shard_map/decode_held_pages/pallas_call | solution.py:437
  10.4 2.4 %own_shard.1 = (bf16[2,256,1024]{2,1,0:T(8,128)(2,1)S(1)}, bf16[3,128,128]{2,1,0:T(8,128)(2,1)S(1)}, bf16[3,256,128]{2,1,0:T(8,128)(2,1)S(1)}, bf16[32,128]{1,0:...) custom-call(s32[1]{0:T(128)} %bitcast.own_ref, ...), custom_call_target="tpu_custom_call" | custom-call | flops 402653184 | bytes 1048576 | tf_op jit(solution)/shard_map/own_shard/pallas_call | solution.py:421
  12.8 2.1 %collective-permute-start.1 = (bf16[768,256]{1,0:T(8,128)(2,1)S(1)}, bf16[768,256]{1,0:T(8,128)(2,1)S(1)}, u32[]{:S(2)}, u32[]{:S(2)}) collective-permute-start(bf16[768,256]{1,0:T(8,128)(2,1)S(1)} %pad_maximum_fusion.shard_ref.rest_ref), channel_id=1, source_target_pairs={{0,12},{4,0},{8,4},{12,8},{1,13},{5,1},{9,5},{13,9},{2,14},{6,2},{... | collective-permute-start | bytes 1179656 | tf_op jit(solution)/shard_map/ppermute | solution.py:398
  14.9 1.1 %collective-permute-done.refs_0_.shard_ref = bf16[768,256]{1,0:T(8,128)(2,1)S(1)} collective-permute-done((bf16[768,256]{1,0:T(8,128)(2,1)S(1)}, bf16[768,256]{1,0:T(8,128)(2,1)S(1)}, u32[]{:S(2)}, u32[]{:S(2)}) %collective-permute-start) | collective-permute-done | bytes 393248 | tf_op jit(solution)/shard_map/ppermute | solution.py:398
  16.0 0.1 pieces_to_send_on.1
  16.1 0.1 collective-permute-start.2
  16.2 0.7 %collective-permute-start.3 = (bf16[256,256]{1,0:T(8,128)(2,1)S(1)}, bf16[256,256]{1,0:T(8,128)(2,1)S(1)}, u32[]{:S(2)}, u32[]{:S(2)}) collective-permute-start(bf16[256,256]{1,0:T(8,128)(2,1)S(1)} %get-tuple-element.67), channel_id=1, source_target_pairs={{4,8},{8,12},{0,0},{12,4},{5,9},{9,13},{1,1},{13,5},{6,10},{10,14}... | collective-permute-start | bytes 393224 | tf_op jit(solution)/shard_map/ppermute | solution.py:478
  16.9 4.0 %collective-permute-start.4 = (bf16[256,256]{1,0:T(8,128)(2,1)S(1)}, bf16[256,256]{1,0:T(8,128)(2,1)S(1)}, u32[]{:S(2)}, u32[]{:S(2)}) collective-permute-start(bf16[256,256]{1,0:T(8,128)(2,1)S(1)} %get-tuple-element.71), channel_id=1, source_target_pairs={{0,4},{4,8},{8,12},{12,0},{1,5},{5,9},{9,13},{13,1},{2,6},{6,10},{... | collective-permute-start | bytes 393224 | tf_op jit(solution)/shard_map/ppermute | solution.py:398
  20.9 1.7 %whole_shards_0.1 = (f32[2,1,1024]{2,1,0:T(1,128)S(1)}, f32[2,1,1024]{2,1,0:T(1,128)S(1)}, f32[2,128,1024]{2,1,0:T(8,128)S(1)}) custom-call(bf16[2,256,1024]{2,1,0:T(8,128)(2,1)S(1)} %get-tuple-element.39.qt_ref, bf16[3,128,128]{2,1,0:T(8,128)(2,1)S(1)} %get-tuple-element.40.near_ref, bf16[3,256,128]{2,1,0:T(8,128)(2,1)S(1)} %get-tuple-element.41.far_ref, ...), custom_call_target="tpu_custom_call" | custom-call | flops 402653184 | bytes 1048576 | tf_op jit(solution)/shard_map/whole_shards_0/pallas_call | solution.py:485
  22.6 2.0 %collective-permute-done.1.refs_0_.refs_1_ = bf16[768,256]{1,0:T(8,128)(2,1)S(1)} collective-permute-done((bf16[768,256]{1,0:T(8,128)(2,1)S(1)}, bf16[768,256]{1,0:T(8,128)(2,1)S(1)}, u32[]{:S(2)}, u32[]{:S(2)}) %collective-permute-start.1) | collective-permute-done | bytes 393248 | tf_op jit(solution)/shard_map/ppermute | solution.py:398
  24.6 1.7 %whole_shards_1.1 = (f32[2,1,1024]{2,1,0:T(1,128)S(1)}, f32[2,1,1024]{2,1,0:T(1,128)S(1)}, f32[2,128,1024]{2,1,0:T(8,128)S(1)}) custom-call(bf16[2,256,1024]{2,1,0:T(8,128)(2,1)S(1)} %get-tuple-element.39.qt_ref, bf16[3,128,128]{2,1,0:T(8,128)(2,1)S(1)} %get-tuple-element.40.near_ref, bf16[3,256,128]{2,1,0:T(8,128)(2,1)S(1)} %get-tuple-element.41.far_ref, ...), custom_call_target="tpu_custom_call" | custom-call | flops 402653184 | bytes 1048576 | tf_op jit(solution)/shard_map/whole_shards_1/pallas_call | solution.py:485
  26.4 4.1 %collective-permute-done.2.first_ref.refs_2_ = bf16[320,256]{1,0:T(8,128)(2,1)S(1)} collective-permute-done((bf16[320,256]{1,0:T(8,128)(2,1)S(1)}, bf16[320,256]{1,0:T(8,128)(2,1)S(1)}, u32[]{:S(2)}, u32[]{:S(2)}) %collective-permute-start.2) | collective-permute-done | bytes 163872 | tf_op jit(solution)/shard_map/ppermute | solution.py:398
  30.4 1.8 %decode_new_pages.1 = bf16[8,2048]{1,0:T(8,128)(2,1)} custom-call(s32[1]{0:T(128)} %bitcast.own_ref, s32[32]{0:T(128)S(1)} %copy-done.4, s32[8]{0:T(128)S(1)} %copy-done.5, s32[8,32]{1,0:T(8,128)S(1)} %copy-done.3, bf16[768,256]{1,0:T(8,128)(2,1)S(1)} %collective-permute-done.refs_0_.shard_ref, bf16[768,256]{1,0:T(8,128)(2,1)S(1)} %collective-permute-done.1.refs_0_.refs_1_, ...), custom_call_target="tpu_custom_call" | custom-call | flops 134217728 | bytes 1048576 | tf_op jit(solution)/shard_map/decode_new_pages/pallas_call | solution.py:496
  32.2 1.6 %last_scores.1 = (bf16[2,256,1024]{2,1,0:T(8,128)(2,1)S(1)}, f32[2,1,1024]{2,1,0:T(1,128)S(1)}, f32[2,128,1024]{2,1,0:T(8,128)S(1)}) custom-call(bf16[2,256,1024]{2,1,0:T(8,128)(2,1)S(1)} %get-tuple-element.39.qt_ref, bf16[3,128,128]{2,1,0:T(8,128)(2,1)S(1)} %get-tuple-element.40.near_ref, bf16[3,256,128]{2,1,0:T(8,128)(2,1)S(1)} %get-tuple-element.41.far_ref, ...), custom_call_target="tpu_custom_call" | custom-call | flops 402653184 | bytes 1048576 | tf_op jit(solution)/shard_map/last_scores/pallas_call | solution.py:509
  33.8 0.8 %collective-permute-done.4.values_ref = bf16[256,256]{1,0:T(8,128)(2,1)S(1)} collective-permute-done((bf16[256,256]{1,0:T(8,128)(2,1)S(1)}, bf16[256,256]{1,0:T(8,128)(2,1)S(1)}, u32[]{:S(2)}, u32[]{:S(2)}) %collective-permute-start.4) | collective-permute-done | bytes 131104 | tf_op jit(solution)/shard_map/ppermute | solution.py:398
  34.6 1.1 %last_values.1 = bf16[128,2048]{1,0:T(8,128)(2,1)} custom-call(bf16[2,256,1024]{2,1,0:T(8,128)(2,1)S(1)} %get-tuple-element.68.weights_ref, f32[2,1,1024]{2,1,0:T(1,128)S(1)} %get-tuple-element.69.total_ref, f32[2,128,1024]{2,1,0:T(8,128)S(1)} %get-tuple-element.70.accum_ref, bf16[256,256]{1,0:T(8,128)(2,1)S(1)} %collective-permute-done.4.values_ref), custom_call_target="tpu_custom_call" | custom-call | flops 134217728 | bytes 1048576 | tf_op jit(solution)/shard_map/last_values/pallas_call | solution.py:519
  (9 shorter events, 0.0 us)
Async XLA Ops:
  0.6 4.8 %copy-start.2 = (bf16[8,2048]{1,0:T(8,128)(2,1)S(1)}, bf16[8,2048]{1,0:T(8,128)(2,1)}, u32[]{:S(2)}) copy-start(bf16[8,2048]{1,0:T(8,128)(2,1)} %q_ref.3) | copy-start | bytes 98308
  1.7 14.3 %collective-permute-start = (bf16[768,256]{1,0:T(8,128)(2,1)S(1)}, bf16[768,256]{1,0:T(8,128)(2,1)S(1)}, u32[]{:S(2)}, u32[]{:S(2)}) collective-permute-start(bf16[768,256]{1,0:T(8,128)(2,1)S(1)} %pad_maximum_fusion.shard_ref.rest_ref), channel_id=1, source_target_pairs={{0,4},{4,8},{8,12},{12,0},{1,5},{5,9},{9,13},{13,1},{2,6},{6,10},{... | collective-permute-start | bytes 1179656 | tf_op jit(solution)/shard_map/ppermute | solution.py:398
  4.8 0.7 %copy-start.3 = (s32[8,32]{1,0:T(8,128)S(1)}, s32[8,32]{1,0:T(8,128)}, u32[]{:S(2)}) copy-start(s32[8,32]{1,0:T(8,128)} %lists_ref.3) | copy-start | bytes 3076
  5.4 0.7 %copy-start.4 = (s32[32]{0:T(128)S(1)}, s32[32]{0:T(128)}, u32[]{:S(2)}) copy-start(s32[32]{0:T(128)} %targets_ref.5) | copy-start | bytes 388
  5.4 0.7 %copy-start.5 = (s32[8]{0:T(128)S(1)}, s32[8]{0:T(128)}, u32[]{:S(2)}) copy-start(s32[8]{0:T(128)} %length_ref.3) | copy-start | bytes 100
  6.1 1.2 %copy-start = (bf16[128,16,256]{2,1,0:T(8,128)(2,1)S(1)}, bf16[128,16,256]{2,1,0:T(8,128)(2,1)}, u32[]{:S(2)}) copy-start(bf16[128,16,256]{2,1,0:T(8,128)(2,1)} %pool_k.1) | copy-start | bytes 3145732
  7.3 1.2 %copy-start.1 = (bf16[128,16,256]{2,1,0:T(8,128)(2,1)S(1)}, bf16[128,16,256]{2,1,0:T(8,128)(2,1)}, u32[]{:S(2)}) copy-start(bf16[128,16,256]{2,1,0:T(8,128)(2,1)} %pool_v.1) | copy-start | bytes 3145732
  8.5 1.9 %copy-start.6 = (bf16[128,2048]{1,0:T(8,128)(2,1)S(1)}, bf16[128,2048]{1,0:T(8,128)(2,1)}, u32[]{:S(2)}) copy-start(bf16[128,2048]{1,0:T(8,128)(2,1)} %q_ref.2) | copy-start | bytes 1572868
  12.8 11.8 %collective-permute-start.1 = (bf16[768,256]{1,0:T(8,128)(2,1)S(1)}, bf16[768,256]{1,0:T(8,128)(2,1)S(1)}, u32[]{:S(2)}, u32[]{:S(2)}) collective-permute-start(bf16[768,256]{1,0:T(8,128)(2,1)S(1)} %pad_maximum_fusion.shard_ref.rest_ref), channel_id=1, source_target_pairs={{0,12},{4,0},{8,4},{12,8},{1,13},{5,1},{9,5},{13,9},{2,14},{6,2},{... | collective-permute-start | bytes 1179656 | tf_op jit(solution)/shard_map/ppermute | solution.py:398
  16.1 14.3 %collective-permute-start.2 = (bf16[320,256]{1,0:T(8,128)(2,1)S(1)}, bf16[320,256]{1,0:T(8,128)(2,1)S(1)}, u32[]{:S(2)}, u32[]{:S(2)}) collective-permute-start(bf16[320,256]{1,0:T(8,128)(2,1)S(1)} %get-tuple-element.66), channel_id=1, source_target_pairs={{0,4},{4,8},{8,12},{12,0},{1,5},{5,9},{9,13},{13,1},{2,6},{6,10},{... | collective-permute-start | bytes 491528 | tf_op jit(solution)/shard_map/ppermute | solution.py:398
  16.2 16.0 %collective-permute-start.3 = (bf16[256,256]{1,0:T(8,128)(2,1)S(1)}, bf16[256,256]{1,0:T(8,128)(2,1)S(1)}, u32[]{:S(2)}, u32[]{:S(2)}) collective-permute-start(bf16[256,256]{1,0:T(8,128)(2,1)S(1)} %get-tuple-element.67), channel_id=1, source_target_pairs={{4,8},{8,12},{0,0},{12,4},{5,9},{9,13},{1,1},{13,5},{6,10},{10,14}... | collective-permute-start | bytes 393224 | tf_op jit(solution)/shard_map/ppermute | solution.py:478
  16.9 17.7 %collective-permute-start.4 = (bf16[256,256]{1,0:T(8,128)(2,1)S(1)}, bf16[256,256]{1,0:T(8,128)(2,1)S(1)}, u32[]{:S(2)}, u32[]{:S(2)}) collective-permute-start(bf16[256,256]{1,0:T(8,128)(2,1)S(1)} %get-tuple-element.71), channel_id=1, source_target_pairs={{0,4},{4,8},{8,12},{12,0},{1,5},{5,9},{9,13},{13,1},{2,6},{6,10},{... | collective-permute-start | bytes 393224 | tf_op jit(solution)/shard_map/ppermute | solution.py:398

commit v10 on v9

--- a/solution.py
+++ b/solution.py
@@ -270,21 +270,20 @@
     attend(qt_ref, keys, values_t, (high_in, total_in, accum_in), outs)
 
 
-def split_kernel(pick_ref, shard_ref, first_ref, stretch_ref, values_ref):
+def split_kernel(pick_ref, shard_ref, keys_ref, stretch_ref, values_ref, pages_ref):
     tokens = pick_ref.shape[1]
     half = shard_ref.shape[0] // 2
-    c_rows = half - tokens
-    first_ref[:c_rows] = shard_ref[tokens:half]
     sent = pick_ref.shape[0]
     for place, start in enumerate((0, half)):
+        stretch_ref[place * tokens : (place + 1) * tokens] = shard_ref[start : start + tokens]
         rows = jnp.dot(pick_ref[...], shard_ref[start : start + tokens], preferred_element_type=jnp.float32)
-        first_ref[c_rows + place * sent : c_rows + (place + 1) * sent] = rows.astype(jnp.bfloat16)
-        stretch_ref[place * tokens : (place + 1) * tokens] = shard_ref[start : start + tokens]
+        pages_ref[place * sent : (place + 1) * sent] = rows.astype(jnp.bfloat16)
+    keys_ref[...] = shard_ref[tokens:half]
     values_ref[...] = shard_ref[half + tokens :]
 
 
 def pages_kernel(count, hops, tokens, pool, own_ref, targets_ref, length_ref, lists_ref, *refs):
-    shard_refs, refs = refs[: len(hops)], refs[len(hops) :]
+    shard_refs, refs = refs[: len(hops) + 1], refs[len(hops) + 1 :]
     wide_ref, dec_high, dec_total, dec_mixed, dec_out = refs
     own = own_ref[0]
     pages = tokens // PAGE
@@ -295,11 +294,14 @@
         half = ref.shape[0] // 2
         slot = slot_row(targets_ref, shard_of(own, hop, count), own, tokens, pool)
         parts.append((ref[:tokens], ref[half : half + tokens], tally_of(lists, lengths, slot)))
-    ref = shard_refs[-1]
-    sent = SEND_CAP * PAGE
-    start = ref.shape[0] - 2 * sent
-    slot = sent_slots(targets_ref, shard_of(own, hops[-1], count), own, pages, pool)
-    parts.append((ref[start : start + sent], ref[start + sent :], tally_of(lists, lengths, slot)))
+    stretch_ref, pages_ref = shard_refs[-2:]
+    shard = shard_of(own, hops[-1], count)
+    attended = shard < own
+    slot = jnp.where(attended, slot_row(targets_ref, shard, own, tokens, pool), -1)
+    parts.append((stretch_ref[:tokens], stretch_ref[tokens:], tally_of(lists, lengths, slot)))
+    sent = pages_ref.shape[0] // 2
+    slot = jnp.where(attended, -1, sent_slots(targets_ref, shard, own, pages, pool))
+    parts.append((pages_ref[:sent], pages_ref[sent:], tally_of(lists, lengths, slot)))
     _, total, mixed = decode_attend(wide_ref[...], parts, (dec_high[...], dec_total[...], dec_mixed[...]))
     for head in range(dec_high.shape[0]):
         piece = mixed[head, :, features(head // GROUP)] / total[head]
@@ -307,7 +309,7 @@
 
 
 def score_kernel(
-    final, qt_ref, near_ref, far_ref, high_in, total_in, accum_in, first_ref, stretch_ref,
+    final, qt_ref, near_ref, far_ref, high_in, total_in, accum_in, keys_ref, stretch_ref,
     weights_ref, total_ref, accum_ref,
 ):
     kv_local = qt_ref.shape[0]
@@ -315,7 +317,7 @@
     mask = jnp.concatenate([near_ref[final], far_ref[final]], axis=0)
     keys, values_t = [], []
     for head in range(kv_local):
-        pieces = [stretch_ref[:tokens, features(head)], first_ref[:c_rows, features(head)]]
+        pieces = [stretch_ref[:tokens, features(head)], keys_ref[:, features(head)]]
         keys.append(jnp.concatenate([jnp.concatenate(pieces, axis=0), mask], axis=1))
         values_t.append(stretch_ref[tokens:, features(head)].T)
 
@@ -462,22 +464,22 @@
     pieces = pl.pallas_call(
         split_kernel,
         out_shape=(
-            shape((c_rows + 2 * SEND_CAP * PAGE, kv_width), bf16),
+            shape((c_rows, kv_width), bf16),
             shape((2 * tokens, kv_width), bf16),
             shape((c_rows, kv_width), bf16),
+            shape((2 * SEND_CAP * PAGE, kv_width), bf16),
         ),
         in_specs=[VMEM] * 2,
-        out_specs=(VMEM,) * 3,
+        out_specs=(VMEM,) * 4,
         compiler_params=params,
         name="pieces_to_send_on",
     )(pick, nearer)
     last_keys = send(pieces[0], hop)
-    if 2 * hop == -count:
-        pairs = [(i - 1, i) for i in range(count // 2, count)]
-        pairs += [(i, i) for i in range(count // 2 - 1)] + [(count - 1, count // 2 - 1)]
-        last_stretch = lax.ppermute(pieces[1], "ctx", pairs)
-    else:
-        last_stretch = send(pieces[1], hop)
+    attending, others = [], []
+    for pair in up_pairs if hop < 0 else down_pairs:
+        (attending if (pair[1] + hop) % count < pair[1] else others).append(pair)
+    last_stretch = lax.ppermute(pieces[1], "ctx", attending)
+    last_pages = lax.ppermute(pieces[3], "ctx", others)
     last_values = send(pieces[2], hop)
 
     for first in range(len(hops) - 1):
@@ -496,16 +498,17 @@
     decoded = pl.pallas_call(
         functools.partial(pages_kernel, count, hops, tokens, pool),
         out_shape=shape(decode_queries.shape, bf16),
-        in_specs=[SMEM] * 3 + [VMEM] * (5 + len(hops)),
+        in_specs=[SMEM] * 3 + [VMEM] * (6 + len(hops)),
         out_specs=VMEM,
         compiler_params=params,
         cost_estimate=cost(tokens),
         name="decode_new_pages",
     )(
-        own_array, page_targets, context_length, page_lists, *[shard[hop] for hop in hops[:-1]], last_keys,
+        own_array, page_targets, context_length, page_lists, *[shard[hop] for hop in hops[:-1]], last_stretch, last_pages,
         wide, *dec_state,
     )
 
+    decoded, state = lax.optimization_barrier((decoded, state))
     weights, total, accum = pl.pallas_call(
         functools.partial(score_kernel, final),
         out_shape=(shape((kv_local, c_rows, rows), bf16),) + state_shapes[1:],

time: 36 us -> 36.7 us (1.019)
  starting transfers between devices: 9.94 us -> 11.9 us
  waiting for transfers between devices: 7.93 us -> 6.56 us
    ppermute x4, waiting for transfers between devices: 7.93 us -> 1.16 us  [send(): return lax.ppermute(array, 'ctx', up_pairs if hop < 0 else down_pairs)]
    ppermute x1 -> x2, waiting for transfers between devices: 0.01 us -> 5.4 us  [the longest x1 5.4 us: per_device(): last_pages = lax.ppermute(pieces[3], 'ctx', others)]
    ppermute x1 -> x2, starting transfers between devices: 0.67 us -> 2.63 us  [the longest x1 1.96 us: per_device(): last_pages = lax.ppermute(pieces[3], 'ctx', others)]
  transfers between devices with their start and end apart: 5 -> 6, of which waited for: 4 -> 3; matrix products, arithmetic and copies ran while one was open for 0% -> 0% of each run, Pallas kernels for 31% -> 31%
where the time goes in v10:
time: 36.7 us; the launch traced here: 36.4 us
  Pallas kernels  12.4 us (34%)
  starting transfers between devices  11.9 us (32%)
  waiting for transfers between devices  6.56 us (18%)
  local copies, waits for them, and re-layouts  3.1 us (8%)
  between operations  1.42 us (4%)
  other arithmetic  1.03 us (3%)
    ppermute x4, starting transfers between devices, send(): return lax.ppermute(array, 'ctx', up_pairs if hop < 0 else down_pairs)  9.24 us
    ppermute x1, waiting for transfers between devices, per_device(): last_pages = lax.ppermute(pieces[3], 'ctx', others)  5.4 us
    pallas_call x2, Pallas kernels, per_device(): pl.pallas_call(functools.partial(hop_kernel, places), out_shape=state_sha...  3.45 us
    unnamed x14, local copies, waits for them, and re-layouts  3.1 us
    pallas_call x1, Pallas kernels, per_device(): pl.pallas_call(functools.partial(own_kernel, count, hops), out_shape=(sha...  2.36 us
    ppermute x1, starting transfers between devices, per_device(): last_pages = lax.ppermute(pieces[3], 'ctx', others)  1.96 us
    pallas_call x1, Pallas kernels, per_device(): pl.pallas_call(held_kernel, out_shape=(shape((heads * dec_rows, kv_width)...  1.86 us
    pallas_call x1, Pallas kernels, per_device(): pl.pallas_call(functools.partial(pages_kernel, count, hops, tokens, pool)...  1.82 us
  transfers between devices with their start and end apart: 6, of which 3 were waited for; matrix products, arithmetic and copies ran while one was open for 0% of the time, Pallas kernels for 31%

profile of v10, /device:TPU:0, one launch (start us, length us, event | category | flops | bytes accessed | tf_op | source)
XLA Modules:
  0.0 36.4 jit_solution(16491837385056543668)
XLA Ops:
  0.6 1.0 %pad_maximum_fusion.shard_ref.rest_ref = bf16[768,256]{1,0:T(8,128)(2,1)S(1)} fusion(bf16[256,256]{1,0:T(8,128)(2,1)} %param.16, bf16[128,256]{1,0:T(8,128)(2,1)} %param.14, bf16[256,256]{1,0:T(8,128)(2,1)} %param.15, bf16[128,256]{1,0:T(8,128)(2,1)} %param.13), kind=kLoop, calls=%fused_computation | loop fusion | flops 1572864 | bytes 786432 | tf_op jit(solution)/shard_map/max | solution.py:415
  1.7 3.1 %collective-permute-start = (bf16[768,256]{1,0:T(8,128)(2,1)S(1)}, bf16[768,256]{1,0:T(8,128)(2,1)S(1)}, u32[]{:S(2)}, u32[]{:S(2)}) collective-permute-start(bf16[768,256]{1,0:T(8,128)(2,1)S(1)} %pad_maximum_fusion.shard_ref.rest_ref), channel_id=1, source_target_pairs={{0,4},{4,8},{8,12},{12,0},{1,5},{5,9},{9,13},{13,1},{2,6},{6,10},{... | collective-permute-start | bytes 1179656 | tf_op jit(solution)/shard_map/ppermute | solution.py:400
  5.4 0.0 copy-start.4
  5.4 0.0 copy-start.5
  5.5 0.6 %copy-done.4 = s32[32]{0:T(128)S(1)} copy-done((s32[32]{0:T(128)S(1)}, s32[32]{0:T(128)}, u32[]{:S(2)}) %copy-start.4) | copy-done | bytes 152
  6.1 0.0 copy-done.5
  6.1 1.2 %copy-done = bf16[128,16,256]{2,1,0:T(8,128)(2,1)S(1)} copy-done((bf16[128,16,256]{2,1,0:T(8,128)(2,1)S(1)}, bf16[128,16,256]{2,1,0:T(8,128)(2,1)}, u32[]{:S(2)}) %copy-start) | copy-done | bytes 1048600
  7.3 1.2 %copy-done.1 = bf16[128,16,256]{2,1,0:T(8,128)(2,1)S(1)} copy-done((bf16[128,16,256]{2,1,0:T(8,128)(2,1)S(1)}, bf16[128,16,256]{2,1,0:T(8,128)(2,1)}, u32[]{:S(2)}) %copy-start.1) | copy-done | bytes 1048600
  8.5 1.9 %decode_held_pages.1 = (bf16[128,256]{1,0:T(8,128)(2,1)S(1)}, f32[16,8,1]{2,1,0:T(8,128)S(1)}, f32[16,8,1]{2,1,0:T(8,128)S(1)}, f32[16,8,256]{2,1,0:T(8,128)S(1)}) custom-call(s32[1]{0:T(128)} %bitcast.own_ref, s32[32]{0:T(128)S(1)} %copy-done.4, s32[8]{0:T(128)S(1)} %copy-done.5, bf16[8,2048]{1,0:T(8,128)(2,1)S(1)} %copy-done.2, s32[8,32]{1,0:T(8,128)S(1)} %copy-done.3, ...), custom_call_target="tpu_custom_call" | custom-call | flops 268435456 | bytes 2097152 | tf_op jit(solution)/shard_map/decode_held_pages/pallas_call | solution.py:439
  10.4 2.4 %own_shard.1 = (bf16[2,256,1024]{2,1,0:T(8,128)(2,1)S(1)}, bf16[3,128,128]{2,1,0:T(8,128)(2,1)S(1)}, bf16[3,256,128]{2,1,0:T(8,128)(2,1)S(1)}, bf16[32,128]{1,0:...) custom-call(s32[1]{0:T(128)} %bitcast.own_ref, ...), custom_call_target="tpu_custom_call" | custom-call | flops 402653184 | bytes 1048576 | tf_op jit(solution)/shard_map/own_shard/pallas_call | solution.py:423
  12.8 2.1 %collective-permute-start.1 = (bf16[768,256]{1,0:T(8,128)(2,1)S(1)}, bf16[768,256]{1,0:T(8,128)(2,1)S(1)}, u32[]{:S(2)}, u32[]{:S(2)}) collective-permute-start(bf16[768,256]{1,0:T(8,128)(2,1)S(1)} %pad_maximum_fusion.shard_ref.rest_ref), channel_id=1, source_target_pairs={{0,12},{4,0},{8,4},{12,8},{1,13},{5,1},{9,5},{13,9},{2,14},{6,2},{... | collective-permute-start | bytes 1179656 | tf_op jit(solution)/shard_map/ppermute | solution.py:400
  14.9 1.1 %collective-permute-done.shard_ref.refs_0_ = bf16[768,256]{1,0:T(8,128)(2,1)S(1)} collective-permute-done((bf16[768,256]{1,0:T(8,128)(2,1)S(1)}, bf16[768,256]{1,0:T(8,128)(2,1)S(1)}, u32[]{:S(2)}, u32[]{:S(2)}) %collective-permute-start) | collective-permute-done | bytes 393248 | tf_op jit(solution)/shard_map/ppermute | solution.py:400
  16.0 0.1 pieces_to_send_on.1
  16.1 0.7 %collective-permute-start.2 = (bf16[256,256]{1,0:T(8,128)(2,1)S(1)}, bf16[256,256]{1,0:T(8,128)(2,1)S(1)}, u32[]{:S(2)}, u32[]{:S(2)}) collective-permute-start(bf16[256,256]{1,0:T(8,128)(2,1)S(1)} %get-tuple-element.62), channel_id=1, source_target_pairs={{4,8},{8,12},{5,9},{9,13},{6,10},{10,14},{7,11},{11,15},{20,24},{2... | collective-permute-start | bytes 393224 | tf_op jit(solution)/shard_map/ppermute | solution.py:481
  16.8 2.5 %collective-permute-start.4 = (bf16[256,256]{1,0:T(8,128)(2,1)S(1)}, bf16[256,256]{1,0:T(8,128)(2,1)S(1)}, u32[]{:S(2)}, u32[]{:S(2)}) collective-permute-start(bf16[256,256]{1,0:T(8,128)(2,1)S(1)} %get-tuple-element.80), channel_id=1, source_target_pairs={{0,4},{4,8},{8,12},{12,0},{1,5},{5,9},{9,13},{13,1},{2,6},{6,10},{... | collective-permute-start | bytes 393224 | tf_op jit(solution)/shard_map/ppermute | solution.py:400
  19.3 1.6 %collective-permute-start.5 = (bf16[256,256]{1,0:T(8,128)(2,1)S(1)}, bf16[256,256]{1,0:T(8,128)(2,1)S(1)}, u32[]{:S(2)}, u32[]{:S(2)}) collective-permute-start(bf16[256,256]{1,0:T(8,128)(2,1)S(1)} %get-tuple-element.84), channel_id=1, source_target_pairs={{0,4},{4,8},{8,12},{12,0},{1,5},{5,9},{9,13},{13,1},{2,6},{6,10},{... | collective-permute-start | bytes 393224 | tf_op jit(solution)/shard_map/ppermute | solution.py:400
  20.9 2.0 %collective-permute-start.3 = (bf16[64,256]{1,0:T(8,128)(2,1)S(1)}, bf16[64,256]{1,0:T(8,128)(2,1)S(1)}, u32[]{:S(2)}, u32[]{:S(2)}) collective-permute-start(bf16[64,256]{1,0:T(8,128)(2,1)S(1)} %get-tuple-element.63), channel_id=1, source_target_pairs={{0,4},{12,0},{1,5},{13,1},{2,6},{14,2},{3,7},{15,3},{16,20},{28,16... | collective-permute-start | bytes 98312 | tf_op jit(solution)/shard_map/ppermute | solution.py:482
  22.8 1.7 %whole_shards_0.1 = (f32[2,1,1024]{2,1,0:T(1,128)S(1)}, f32[2,1,1024]{2,1,0:T(1,128)S(1)}, f32[2,128,1024]{2,1,0:T(8,128)S(1)}) custom-call(bf16[2,256,1024]{2,1,0:T(8,128)(2,1)S(1)} %get-tuple-element.44.qt_ref, bf16[3,128,128]{2,1,0:T(8,128)(2,1)S(1)} %get-tuple-element.45.near_ref, bf16[3,256,128]{2,1,0:T(8,128)(2,1)S(1)} %get-tuple-element.46.far_ref, ...), custom_call_target="tpu_custom_call" | custom-call | flops 402653184 | bytes 1048576 | tf_op jit(solution)/shard_map/whole_shards_0/pallas_call | solution.py:487
  24.6 0.1 collective-permute-done.1.refs_1_.refs_0_
  24.6 1.7 %whole_shards_1.1 = (f32[2,1,1024]{2,1,0:T(1,128)S(1)}, f32[2,1,1024]{2,1,0:T(1,128)S(1)}, f32[2,128,1024]{2,1,0:T(8,128)S(1)}) custom-call(bf16[2,256,1024]{2,1,0:T(8,128)(2,1)S(1)} %get-tuple-element.44.qt_ref, bf16[3,128,128]{2,1,0:T(8,128)(2,1)S(1)} %get-tuple-element.45.near_ref, bf16[3,256,128]{2,1,0:T(8,128)(2,1)S(1)} %get-tuple-element.46.far_ref, ...), custom_call_target="tpu_custom_call" | custom-call | flops 402653184 | bytes 1048576 | tf_op jit(solution)/shard_map/whole_shards_1/pallas_call | solution.py:487
  26.4 5.4 %collective-permute-done.3.refs_3_ = bf16[64,256]{1,0:T(8,128)(2,1)S(1)} collective-permute-done((bf16[64,256]{1,0:T(8,128)(2,1)S(1)}, bf16[64,256]{1,0:T(8,128)(2,1)S(1)}, u32[]{:S(2)}, u32[]{:S(2)}) %collective-permute-start.3) | collective-permute-done | bytes 32800 | tf_op jit(solution)/shard_map/ppermute | solution.py:482
  31.8 1.8 %decode_new_pages.1 = bf16[8,2048]{1,0:T(8,128)(2,1)} custom-call(s32[1]{0:T(128)} %bitcast.own_ref, s32[32]{0:T(128)S(1)} %copy-done.4, s32[8]{0:T(128)S(1)} %copy-done.5, s32[8,32]{1,0:T(8,128)S(1)} %copy-done.3, bf16[768,256]{1,0:T(8,128)(2,1)S(1)} %collective-permute-done.shard_ref.refs_0_, bf16[768,256]{1,0:T(8,128)(2,1)S(1)} %collective-permute-done.1.refs_1_.refs_0_, ...), custom_call_target="tpu_custom_call" | custom-call | flops 134217728 | bytes 1048576 | tf_op jit(solution)/shard_map/decode_new_pages/pallas_call | solution.py:498
  33.6 1.6 %last_scores.1 = (bf16[2,256,1024]{2,1,0:T(8,128)(2,1)S(1)}, f32[2,1,1024]{2,1,0:T(1,128)S(1)}, f32[2,128,1024]{2,1,0:T(8,128)S(1)}) custom-call(bf16[2,256,1024]{2,1,0:T(8,128)(2,1)S(1)} %get-tuple-element.44.qt_ref, bf16[3,128,128]{2,1,0:T(8,128)(2,1)S(1)} %get-tuple-element.45.near_ref, bf16[3,256,128]{2,1,0:T(8,128)(2,1)S(1)} %get-tuple-element.46.far_ref, ...), custom_call_target="tpu_custom_call" | custom-call | flops 402653184 | bytes 1048576 | tf_op jit(solution)/shard_map/last_scores/pallas_call | solution.py:512
  35.2 1.1 %last_values.1 = bf16[128,2048]{1,0:T(8,128)(2,1)} custom-call(bf16[2,256,1024]{2,1,0:T(8,128)(2,1)S(1)} %get-tuple-element.81.weights_ref, f32[2,1,1024]{2,1,0:T(1,128)S(1)} %get-tuple-element.82.total_ref, f32[2,128,1024]{2,1,0:T(8,128)S(1)} %get-tuple-element.83.accum_ref, bf16[256,256]{1,0:T(8,128)(2,1)S(1)} %collective-permute-done.5.values_ref), custom_call_target="tpu_custom_call" | custom-call | flops 134217728 | bytes 1048576 | tf_op jit(solution)/shard_map/last_values/pallas_call | solution.py:522
  (11 shorter events, 0.0 us)
Async XLA Ops:
  0.6 4.8 %copy-start.2 = (bf16[8,2048]{1,0:T(8,128)(2,1)S(1)}, bf16[8,2048]{1,0:T(8,128)(2,1)}, u32[]{:S(2)}) copy-start(bf16[8,2048]{1,0:T(8,128)(2,1)} %q_ref.3) | copy-start | bytes 98308
  1.7 14.3 %collective-permute-start = (bf16[768,256]{1,0:T(8,128)(2,1)S(1)}, bf16[768,256]{1,0:T(8,128)(2,1)S(1)}, u32[]{:S(2)}, u32[]{:S(2)}) collective-permute-start(bf16[768,256]{1,0:T(8,128)(2,1)S(1)} %pad_maximum_fusion.shard_ref.rest_ref), channel_id=1, source_target_pairs={{0,4},{4,8},{8,12},{12,0},{1,5},{5,9},{9,13},{13,1},{2,6},{6,10},{... | collective-permute-start | bytes 1179656 | tf_op jit(solution)/shard_map/ppermute | solution.py:400
  4.8 0.7 %copy-start.3 = (s32[8,32]{1,0:T(8,128)S(1)}, s32[8,32]{1,0:T(8,128)}, u32[]{:S(2)}) copy-start(s32[8,32]{1,0:T(8,128)} %lists_ref.3) | copy-start | bytes 3076
  5.4 0.7 %copy-start.4 = (s32[32]{0:T(128)S(1)}, s32[32]{0:T(128)}, u32[]{:S(2)}) copy-start(s32[32]{0:T(128)} %targets_ref.5) | copy-start | bytes 388
  5.4 0.7 %copy-start.5 = (s32[8]{0:T(128)S(1)}, s32[8]{0:T(128)}, u32[]{:S(2)}) copy-start(s32[8]{0:T(128)} %length_ref.3) | copy-start | bytes 100
  6.1 1.2 %copy-start = (bf16[128,16,256]{2,1,0:T(8,128)(2,1)S(1)}, bf16[128,16,256]{2,1,0:T(8,128)(2,1)}, u32[]{:S(2)}) copy-start(bf16[128,16,256]{2,1,0:T(8,128)(2,1)} %pool_k.1) | copy-start | bytes 3145732
  7.3 1.2 %copy-start.1 = (bf16[128,16,256]{2,1,0:T(8,128)(2,1)S(1)}, bf16[128,16,256]{2,1,0:T(8,128)(2,1)}, u32[]{:S(2)}) copy-start(bf16[128,16,256]{2,1,0:T(8,128)(2,1)} %pool_v.1) | copy-start | bytes 3145732
  8.5 1.9 %copy-start.6 = (bf16[128,2048]{1,0:T(8,128)(2,1)S(1)}, bf16[128,2048]{1,0:T(8,128)(2,1)}, u32[]{:S(2)}) copy-start(bf16[128,2048]{1,0:T(8,128)(2,1)} %q_ref.2) | copy-start | bytes 1572868
  12.8 11.8 %collective-permute-start.1 = (bf16[768,256]{1,0:T(8,128)(2,1)S(1)}, bf16[768,256]{1,0:T(8,128)(2,1)S(1)}, u32[]{:S(2)}, u32[]{:S(2)}) collective-permute-start(bf16[768,256]{1,0:T(8,128)(2,1)S(1)} %pad_maximum_fusion.shard_ref.rest_ref), channel_id=1, source_target_pairs={{0,12},{4,0},{8,4},{12,8},{1,13},{5,1},{9,5},{13,9},{2,14},{6,2},{... | collective-permute-start | bytes 1179656 | tf_op jit(solution)/shard_map/ppermute | solution.py:400
  16.1 15.6 %collective-permute-start.2 = (bf16[256,256]{1,0:T(8,128)(2,1)S(1)}, bf16[256,256]{1,0:T(8,128)(2,1)S(1)}, u32[]{:S(2)}, u32[]{:S(2)}) collective-permute-start(bf16[256,256]{1,0:T(8,128)(2,1)S(1)} %get-tuple-element.62), channel_id=1, source_target_pairs={{4,8},{8,12},{5,9},{9,13},{6,10},{10,14},{7,11},{11,15},{20,24},{2... | collective-permute-start | bytes 393224 | tf_op jit(solution)/shard_map/ppermute | solution.py:481
  16.8 16.8 %collective-permute-start.4 = (bf16[256,256]{1,0:T(8,128)(2,1)S(1)}, bf16[256,256]{1,0:T(8,128)(2,1)S(1)}, u32[]{:S(2)}, u32[]{:S(2)}) collective-permute-start(bf16[256,256]{1,0:T(8,128)(2,1)S(1)} %get-tuple-element.80), channel_id=1, source_target_pairs={{0,4},{4,8},{8,12},{12,0},{1,5},{5,9},{9,13},{13,1},{2,6},{6,10},{... | collective-permute-start | bytes 393224 | tf_op jit(solution)/shard_map/ppermute | solution.py:400
  19.3 15.9 %collective-permute-start.5 = (bf16[256,256]{1,0:T(8,128)(2,1)S(1)}, bf16[256,256]{1,0:T(8,128)(2,1)S(1)}, u32[]{:S(2)}, u32[]{:S(2)}) collective-permute-start(bf16[256,256]{1,0:T(8,128)(2,1)S(1)} %get-tuple-element.84), channel_id=1, source_target_pairs={{0,4},{4,8},{8,12},{12,0},{1,5},{5,9},{9,13},{13,1},{2,6},{6,10},{... | collective-permute-start | bytes 393224 | tf_op jit(solution)/shard_map/ppermute | solution.py:400
  20.9 10.9 %collective-permute-start.3 = (bf16[64,256]{1,0:T(8,128)(2,1)S(1)}, bf16[64,256]{1,0:T(8,128)(2,1)S(1)}, u32[]{:S(2)}, u32[]{:S(2)}) collective-permute-start(bf16[64,256]{1,0:T(8,128)(2,1)S(1)} %get-tuple-element.63), channel_id=1, source_target_pairs={{0,4},{12,0},{1,5},{13,1},{2,6},{14,2},{3,7},{15,3},{16,20},{28,16... | collective-permute-start | bytes 98312 | tf_op jit(solution)/shard_map/ppermute | solution.py:482

commit v11 on v7

--- a/solution.py
+++ b/solution.py
@@ -87,14 +87,20 @@
     return hidden(place < limit - shard * c_rows)
 
 
-def slot_row(targets_ref, shard, own, tokens, pool):
-    page = lax.broadcasted_iota(jnp.int32, (1, tokens), 1) // PAGE
-    slots = jnp.full((1, tokens), -1, jnp.int32)
-    for index in range(tokens // PAGE):
-        target = targets_ref[shard * (tokens // PAGE) + index]
-        slot = jnp.where(lax.div(target, P_DEV) == own, pool + lax.rem(target, P_DEV), -1)
-        slots = jnp.where(page == index, slot, slots)
-    return slots
+def entries_of(count):
+    entries = [(kind, hop) for hop in range(1, count - 2) for kind in "ud"]
+    return entries + [("f", count - 2), ("x", count - 1)]
+
+
+def source_of(entry, own, count):
+    kind, hop = entry
+    nothing = 2 * count
+    below, above = own - hop, own + hop
+    if kind == "u":
+        return jnp.where(below >= 0, below, nothing)
+    if kind == "d":
+        return jnp.where(above < count, above, nothing)
+    return jnp.where(below >= 0, below, jnp.where(above < count, above, nothing))
 
 
 def sent_pages(targets_ref, shard, owner, pages):
@@ -106,13 +112,31 @@
     return one, two
 
 
-def sent_slots(targets_ref, shard, owner, pages, pool):
-    place = lax.broadcasted_iota(jnp.int32, (1, SEND_CAP * PAGE), 1)
+def shard_slots(targets_ref, shard, own, count, pages, pool):
+    first = jnp.minimum(shard, count - 1) * pages
     slots = []
-    for index in sent_pages(targets_ref, shard, owner, pages):
-        target = targets_ref[shard * pages + jnp.maximum(index, 0)]
-        slots.append(jnp.where(index >= 0, pool + lax.rem(target, P_DEV), -1))
-    return jnp.where(place < PAGE, slots[0], slots[1])
+    for index in range(pages):
+        target = targets_ref[first + index]
+        mine = (shard < count) & (lax.div(target, P_DEV) == own)
+        slots.append(jnp.where(mine, pool + lax.rem(target, P_DEV), -1))
+    return slots
+
+
+def sent_slots(targets_ref, shard, own, count, pages, pool):
+    held = jnp.minimum(shard, count - 1)
+    slots = []
+    for index in sent_pages(targets_ref, held, own, pages):
+        target = targets_ref[held * pages + jnp.maximum(index, 0)]
+        slots.append(jnp.where((shard < count) & (index >= 0), pool + lax.rem(target, P_DEV), -1))
+    return slots
+
+
+def slot_row(slots):
+    page = lax.broadcasted_iota(jnp.int32, (1, len(slots) * PAGE), 1) // PAGE
+    row = jnp.full(page.shape, -1, jnp.int32)
+    for index, slot in enumerate(slots):
+        row = jnp.where(page == index, slot, row)
+    return row
 
 
 def length_column(length_ref):
@@ -134,10 +158,6 @@
         hit = (slot == lists[:, entry : entry + 1]) & (offset < lengths - entry * PAGE)
         tally = tally + jnp.where(hit, jnp.float32(1.0), jnp.float32(0.0))
     return tally[None]
-
-
-def shard_of(own, hop, count):
-    return lax.rem(own + hop + count, count)
 
 
 def wide_queries(q_ref, kv_local):
@@ -189,9 +209,33 @@
     return slice(0, tokens + c_rows), slice(tokens + c_rows, 2 * (tokens + c_rows))
 
 
+def page_kernel(count, own_ref, targets_ref, shard_ref, *outs):
+    tokens = P_DEV * PAGE
+    half = shard_ref.shape[0] // 2
+    c_rows = half - tokens
+    own = own_ref[0]
+    sent = SEND_CAP * PAGE
+    row = lax.broadcasted_iota(jnp.int32, (sent, tokens), 0)
+    token = lax.broadcasted_iota(jnp.int32, (sent, tokens), 1)
+    for index, out_ref in enumerate(outs):
+        hop = index + 1
+        one, two = sent_pages(targets_ref, own, own - hop, P_DEV)
+        picked = ((row < PAGE) & (one >= 0) & (token == row + one * PAGE)) | (
+            (row >= PAGE) & (two >= 0) & (token == row + (two - 1) * PAGE)
+        )
+        pick = jnp.where(picked, jnp.float32(1.0), jnp.float32(0.0)).astype(jnp.bfloat16)
+        first = out_ref.shape[0] - 2 * sent
+        if first:
+            out_ref[:c_rows] = shard_ref[tokens:half]
+            out_ref[c_rows:first] = shard_ref[half + tokens :]
+        for place, start in enumerate((0, half)):
+            rows = jnp.dot(pick, shard_ref[start : start + tokens], preferred_element_type=jnp.float32)
+            out_ref[first + place * sent : first + (place + 1) * sent] = rows.astype(jnp.bfloat16)
+
+
 def own_kernel(
-    count, hops, own_ref, limit_ref, targets_ref, q_ref, shard_ref,
-    qt_ref, near_ref, far_ref, pick_ref, high_ref, total_ref, accum_ref,
+    count, own_ref, limit_ref, q_ref, shard_ref,
+    qt_ref, near_ref, far_ref, high_ref, total_ref, accum_ref,
 ):
     kv_local, _, rows = qt_ref.shape
     tokens = q_ref.shape[0]
@@ -206,21 +250,10 @@
             cols = slice(sub * tokens, (sub + 1) * tokens)
             qt_ref[head, :HEAD_DIM, cols] = q_ref[:, features(head * GROUP + sub)].T
             qt_ref[head, HEAD_DIM:, cols] = pick
-    for place, hop in enumerate(hops):
-        shard = shard_of(own, hop, count)
-        near_ref[place] = stretch_mask(shard, own, tokens)
-        far_ref[place] = cache_mask(shard, limit, c_rows, tokens)
-    onward = 1 if hops[-1] < 0 else -1
-    pages = tokens // PAGE
-    one, two = sent_pages(
-        targets_ref, shard_of(own, hops[-1] + onward, count), shard_of(own, onward, count), pages
-    )
-    row = lax.broadcasted_iota(jnp.int32, pick_ref.shape, 0)
-    token = lax.broadcasted_iota(jnp.int32, pick_ref.shape, 1)
-    sent = ((row < PAGE) & (one >= 0) & (token == row + one * PAGE)) | (
-        (row >= PAGE) & (two >= 0) & (token == row + (two - 1) * PAGE)
-    )
-    pick_ref[...] = jnp.where(sent, jnp.float32(1.0), jnp.float32(0.0)).astype(jnp.bfloat16)
+    for index, entry in enumerate(entries_of(count)):
+        shard = source_of(entry, own, count)
+        near_ref[index] = stretch_mask(shard, own, tokens)
+        far_ref[index] = cache_mask(shard, limit, c_rows, tokens)
     mask = jnp.concatenate([stretch_mask(own, own, tokens), cache_mask(own, limit, c_rows, tokens)], axis=0)
     key_rows, value_rows = shard_parts(shard_ref, tokens, c_rows)
     keys = [jnp.concatenate([shard_ref[key_rows, features(head)], mask], axis=1) for head in range(kv_local)]
@@ -242,7 +275,8 @@
     lengths = length_column(length_ref)
     wide_ref[...] = wide_queries(q_ref, kv_width // HEAD_DIM)
     held_slot = lax.broadcasted_iota(jnp.int32, (1, held), 1) // PAGE
-    own_slot = slot_row(targets_ref, own, own, tokens, pool)
+    count = targets_ref.shape[0] // P_DEV
+    own_slot = slot_row(shard_slots(targets_ref, own, own, count, P_DEV, pool))
     parts = [
         (
             pool_k[...].reshape(held, kv_width),
@@ -254,52 +288,62 @@
     high_ref[...], total_ref[...], mixed_ref[...] = decode_attend(wide_ref[...], parts, None)
 
 
-def hop_kernel(places, qt_ref, near_ref, far_ref, high_in, total_in, accum_in, *refs):
-    shard_refs, outs = refs[: len(places)], refs[len(places) :]
+def hop_kernel(index, kind, qt_ref, near_ref, far_ref, high_in, total_in, accum_in, ref, *outs):
     tokens, c_rows = near_ref.shape[1], far_ref.shape[1]
-    mask = jnp.concatenate([ref[place] for place in places for ref in (near_ref, far_ref)], axis=0)
+    mask = far_ref[index] if kind == "d" else jnp.concatenate([near_ref[index], far_ref[index]], axis=0)
     keys, values_t = [], []
+    rows = c_rows if kind == "d" else tokens + c_rows
     for head in range(qt_ref.shape[0]):
-        pieces, values = [], []
-        for ref in shard_refs:
-            key_rows, value_rows = shard_parts(ref, tokens, c_rows)
-            pieces.append(ref[key_rows, features(head)])
-            values.append(ref[value_rows, features(head)])
-        keys.append(jnp.concatenate([jnp.concatenate(pieces, axis=0), mask], axis=1))
-        values_t.append(jnp.concatenate(values, axis=0).T)
+        keys.append(jnp.concatenate([ref[:rows, features(head)], mask], axis=1))
+        values_t.append(ref[rows : 2 * rows, features(head)].T)
     attend(qt_ref, keys, values_t, (high_in, total_in, accum_in), outs)
 
 
-def split_kernel(pick_ref, shard_ref, first_ref, stretch_ref, values_ref):
-    tokens = pick_ref.shape[1]
-    half = shard_ref.shape[0] // 2
-    c_rows = half - tokens
-    first_ref[:c_rows] = shard_ref[tokens:half]
-    sent = pick_ref.shape[0]
+def split_kernel(shard_ref, keys_ref, stretch_ref, values_ref):
+    c_rows = keys_ref.shape[0]
+    tokens = stretch_ref.shape[0] // 2
+    half = tokens + c_rows
     for place, start in enumerate((0, half)):
-        rows = jnp.dot(pick_ref[...], shard_ref[start : start + tokens], preferred_element_type=jnp.float32)
-        first_ref[c_rows + place * sent : c_rows + (place + 1) * sent] = rows.astype(jnp.bfloat16)
         stretch_ref[place * tokens : (place + 1) * tokens] = shard_ref[start : start + tokens]
+    keys_ref[...] = shard_ref[tokens:half]
     values_ref[...] = shard_ref[half + tokens :]
 
 
-def pages_kernel(count, hops, tokens, pool, own_ref, targets_ref, length_ref, lists_ref, *refs):
-    shard_refs, refs = refs[: len(hops)], refs[len(hops) :]
+def pages_kernel(count, pool, own_ref, targets_ref, length_ref, lists_ref, *refs):
+    whole_refs, refs = refs[: count - 2], refs[count - 2 :]
+    last_ref, refs = refs[0], refs[1:]
+    page_refs, refs = refs[: count - 2], refs[count - 2 :]
     wide_ref, dec_high, dec_total, dec_mixed, dec_out = refs
+    tokens = P_DEV * PAGE
     own = own_ref[0]
-    pages = tokens // PAGE
     lists = lists_ref[...]
     lengths = length_column(length_ref)
-    parts = []
-    for hop, ref in zip(hops[:-1], shard_refs):
+    whole = [("u", hop) for hop in range(1, count - 2)] + [("x", count - 1), ("u", count - 2)]
+    keys, values, slots = [], [], []
+    for entry, ref in zip(whole, (*whole_refs, last_ref)):
         half = ref.shape[0] // 2
-        slot = slot_row(targets_ref, shard_of(own, hop, count), own, tokens, pool)
-        parts.append((ref[:tokens], ref[half : half + tokens], tally_of(lists, lengths, slot)))
-    ref = shard_refs[-1]
+        keys.append(ref[:tokens])
+        values.append(ref[half : half + tokens])
+        shard = source_of(entry, own, count)
+        slots += shard_slots(targets_ref, shard, own, count, P_DEV, pool)
+    parts = [(keys, values, slots)]
+    keys, values, slots = [], [], []
     sent = SEND_CAP * PAGE
-    start = ref.shape[0] - 2 * sent
-    slot = sent_slots(targets_ref, shard_of(own, hops[-1], count), own, pages, pool)
-    parts.append((ref[start : start + sent], ref[start + sent :], tally_of(lists, lengths, slot)))
+    for hop, ref in enumerate(page_refs, 1):
+        first = ref.shape[0] - 2 * sent
+        keys.append(ref[first : first + sent])
+        values.append(ref[first + sent :])
+        shard = source_of(("d", hop), own, count)
+        slots += sent_slots(targets_ref, shard, own, count, P_DEV, pool)
+    parts.append((keys, values, slots))
+    parts = [
+        (
+            jnp.concatenate(keys, axis=0),
+            jnp.concatenate(values, axis=0),
+            tally_of(lists, lengths, slot_row(slots)),
+        )
+        for keys, values, slots in parts
+    ]
     _, total, mixed = decode_attend(wide_ref[...], parts, (dec_high[...], dec_total[...], dec_mixed[...]))
     for head in range(dec_high.shape[0]):
         piece = mixed[head, :, features(head // GROUP)] / total[head]
@@ -307,16 +351,17 @@
 
 
 def score_kernel(
-    final, qt_ref, near_ref, far_ref, high_in, total_in, accum_in, first_ref, stretch_ref,
+    index, qt_ref, near_ref, far_ref, high_in, total_in, accum_in, keys_ref, stretch_ref, down_ref,
     weights_ref, total_ref, accum_ref,
 ):
     kv_local = qt_ref.shape[0]
     tokens, c_rows = near_ref.shape[1], far_ref.shape[1]
-    mask = jnp.concatenate([near_ref[final], far_ref[final]], axis=0)
+    mask = jnp.concatenate([near_ref[index], far_ref[index]], axis=0)
     keys, values_t = [], []
     for head in range(kv_local):
-        pieces = [stretch_ref[:tokens, features(head)], first_ref[:c_rows, features(head)]]
-        keys.append(jnp.concatenate([jnp.concatenate(pieces, axis=0), mask], axis=1))
+        cached = keys_ref[:, features(head)] + down_ref[:c_rows, features(head)]
+        pieces = jnp.concatenate([stretch_ref[:tokens, features(head)], cached], axis=0)
+        keys.append(jnp.concatenate([pieces, mask], axis=1))
         values_t.append(stretch_ref[tokens:, features(head)].T)
 
     def second(block, scores):
@@ -332,9 +377,13 @@
     walk(blocks_of(qt_ref), lambda block: scores_of(qt_ref, block[0], block[1], keys[block[0]]), second)
 
 
-def last_kernel(weights_ref, total_ref, accum_ref, values_ref, out_ref, result_ref, sems):
+def last_kernel(weights_ref, total_ref, accum_ref, values_ref, down_ref, out_ref, result_ref, sems):
     tokens = result_ref.shape[0]
-    values_t = [values_ref[:, features(head)].T for head in range(weights_ref.shape[0])]
+    c_rows = values_ref.shape[0]
+    values_t = [
+        (values_ref[:, features(head)] + down_ref[c_rows : 2 * c_rows, features(head)]).T
+        for head in range(weights_ref.shape[0])
+    ]
     copies = []
 
     def first(block):
@@ -388,14 +437,19 @@
     f32, bf16 = jnp.float32, jnp.bfloat16
     shape = jax.ShapeDtypeStruct
     params = pltpu.CompilerParams(vmem_limit_bytes=VMEM_BYTES)
-    up_pairs = [(i, (i + 1) % count) for i in range(count)]
-    down_pairs = [(i, (i - 1) % count) for i in range(count)]
-    hops = []
-    for far in range(1, count // 2 + 1):
-        hops += [-far, far] if far <= (count - 1) // 2 else [-far]
-
-    def send(array, hop):
-        return lax.ppermute(array, "ctx", up_pairs if hop < 0 else down_pairs)
+    half = tokens + c_rows
+    page_rows = 2 * SEND_CAP * PAGE
+    entries = entries_of(count)
+    final = count - 2
+
+    def send(array, pairs):
+        return lax.ppermute(array, "ctx", pairs)
+
+    def rising(hop):
+        return [(i, i + 1) for i in range(hop - 1, count - 1)]
+
+    def falling(hop):
+        return [(i, i - 1) for i in range(1, count - hop + 1)]
 
     def cost(keys):
         pairs = kv_local * rows * keys
@@ -403,37 +457,50 @@
             flops=4 * pairs * HEAD_DIM, bytes_accessed=4 * rows * kv_local * HEAD_DIM, transcendentals=pairs
         )
 
-    half = tokens + c_rows
     low = jnp.array(-jnp.inf, bf16)
     spread, start = [], 0
     for part in (stretch_keys, cache_keys, stretch_values, cache_values):
         end = 2 * half - start - part.shape[0]
         spread.append(lax.pad(part, low, ((start, end, 0), (0, 0, 0))))
         start += part.shape[0]
-    shard = {0: functools.reduce(jnp.maximum, spread)}
-    for hop in hops[:2]:
-        shard[hop] = send(shard[0], hop)
+    shard = functools.reduce(jnp.maximum, spread)
+    ups = {1: send(shard, rising(1))}
+
+    wide_rows = 2 * c_rows + page_rows
+    going = pl.pallas_call(
+        functools.partial(page_kernel, count),
+        out_shape=tuple(
+            shape((wide_rows if hop == 1 else page_rows, kv_width), bf16) for hop in range(1, count - 1)
+        ),
+        in_specs=[SMEM] * 2 + [VMEM],
+        out_specs=(VMEM,) * (count - 2),
+        compiler_params=params,
+        name="pages_to_send_down",
+    )(own_array, page_targets, shard)
+    downs = {1: send(going[0], falling(1))}
+    pages = {
+        hop: send(going[hop - 1], [(i, i - hop) for i in range(hop, count)]) for hop in range(2, count - 1)
+    }
 
     state_shapes = (
         shape((kv_local, 1, rows), f32),
         shape((kv_local, 1, rows), f32),
         shape((kv_local, HEAD_DIM, rows), f32),
     )
-    qt, near, far, pick, *state = pl.pallas_call(
-        functools.partial(own_kernel, count, hops),
+    qt, near, far, *state = pl.pallas_call(
+        functools.partial(own_kernel, count),
         out_shape=(
             shape((kv_local, HEAD_DIM + tokens, rows), bf16),
-            shape((count - 1, tokens, tokens), bf16),
-            shape((count - 1, c_rows, tokens), bf16),
-            shape((SEND_CAP * PAGE, tokens), bf16),
+            shape((len(entries), tokens, tokens), bf16),
+            shape((len(entries), c_rows, tokens), bf16),
         )
         + state_shapes,
-        in_specs=[SMEM] * 3 + [VMEM] * 2,
-        out_specs=(VMEM,) * 7,
+        in_specs=[SMEM] * 2 + [VMEM] * 2,
+        out_specs=(VMEM,) * 6,
         compiler_params=params,
         cost_estimate=cost(tokens + c_rows),
         name="own_shard",
-    )(own_array, prefix_length, page_targets, queries, shard[0])
+    )(own_array, prefix_length, queries, shard)
 
     wide, *dec_state = pl.pallas_call(
         held_kernel,
@@ -450,74 +517,78 @@
             flops=4 * 128 * 2048 * 256, bytes_accessed=4 * pool_keys.size, transcendentals=128 * 2048
         ),
         name="decode_held_pages",
-    )(own_array, page_targets, context_length, decode_queries, page_lists, pool_keys, pool_values, shard[0])
-
-    shard[-1], state, dec_state = lax.optimization_barrier((shard[-1], state, dec_state))
-    for hop in hops[2:-1]:
-        shard[hop] = send(shard[hop + 1 if hop < 0 else hop - 1], hop)
-    hop = hops[-1]
-    nearer = shard[hop + 1 if hop < 0 else hop - 1]
+    )(own_array, page_targets, context_length, decode_queries, page_lists, pool_keys, pool_values, shard)
+
+    pages, state, dec_state = lax.optimization_barrier((pages, state, dec_state))
+    later, state, dec_state = lax.optimization_barrier((shard, state, dec_state))
+    across = send(later, [(0, count - 1), (count - 1, 0)])
+    ups[1], state = lax.optimization_barrier((ups[1], state))
+    pages[1] = downs[1]
+    for hop in range(2, final):
+        ups[hop] = send(ups[hop - 1], rising(hop))
+        downs[hop] = send(downs[hop - 1][: 2 * c_rows], falling(hop))
+
     pieces = pl.pallas_call(
         split_kernel,
         out_shape=(
-            shape((c_rows + 2 * SEND_CAP * PAGE, kv_width), bf16),
+            shape((c_rows, kv_width), bf16),
             shape((2 * tokens, kv_width), bf16),
             shape((c_rows, kv_width), bf16),
         ),
-        in_specs=[VMEM] * 2,
+        in_specs=[VMEM],
         out_specs=(VMEM,) * 3,
         compiler_params=params,
         name="pieces_to_send_on",
-    )(pick, nearer)
-    last_keys = send(pieces[0], hop)
-    if 2 * hop == -count:
-        pairs = [(i - 1, i) for i in range(count // 2, count)]
-        pairs += [(i, i) for i in range(count // 2 - 1)] + [(count - 1, count // 2 - 1)]
-        last_stretch = lax.ppermute(pieces[1], "ctx", pairs)
-    else:
-        last_stretch = send(pieces[1], hop)
-    last_values = send(pieces[2], hop)
-
-    for first in range(0, len(hops) - 1, 2):
-        places = list(range(first, min(first + 2, len(hops) - 1)))
+    )(ups[final - 1])
+    pieces, downs[final - 1] = lax.optimization_barrier((pieces, downs[final - 1]))
+    last_keys, last_stretch, last_values = [send(piece, rising(final)) for piece in pieces]
+    last_down = send(downs[final - 1][: 2 * c_rows], falling(final))
+
+    for index, entry in enumerate(entries):
+        kind, hop = entry
+        if kind == "f":
+            continue
+        received = {"u": ups.get(hop), "d": downs.get(hop), "x": across}[kind]
         state = pl.pallas_call(
-            functools.partial(hop_kernel, places),
+            functools.partial(hop_kernel, index, kind),
             out_shape=state_shapes,
-            in_specs=[VMEM] * (6 + len(places)),
+            in_specs=[VMEM] * 7,
             out_specs=(VMEM,) * 3,
             compiler_params=params,
-            cost_estimate=cost((c_rows + tokens) * len(places)),
-            name="whole_shards_" + str(first),
-        )(qt, near, far, *state, *[shard[hops[place]] for place in places])
-
-    final = len(hops) - 1
+            cost_estimate=cost(c_rows if kind == "d" else half),
+            name="entry_" + kind + str(hop),
+        )(qt, near, far, *state, received)
+
     decoded = pl.pallas_call(
-        functools.partial(pages_kernel, count, hops, tokens, pool),
+        functools.partial(pages_kernel, count, pool),
         out_shape=shape(decode_queries.shape, bf16),
-        in_specs=[SMEM] * 3 + [VMEM] * (5 + len(hops)),
+        in_specs=[SMEM] * 3 + [VMEM] * (5 + (count - 1) + (count - 2)),
         out_specs=VMEM,
         compiler_params=params,
         cost_estimate=cost(tokens),
         name="decode_new_pages",
     )(
-        own_array, page_targets, context_length, page_lists, *[shard[hop] for hop in hops[:-1]], last_keys,
+        own_array, page_targets, context_length, page_lists,
+        *[ups[hop] for hop in range(1, final)], across, last_stretch,
+        *[pages[hop] for hop in range(1, count - 1)],
         wide, *dec_state,
     )
 
+    decoded, state = lax.optimization_barrier((decoded, state))
     weights, total, accum = pl.pallas_call(
-        functools.partial(score_kernel, final),
+        functools.partial(score_kernel, len(entries) - 2),
         out_shape=(shape((kv_local, c_rows, rows), bf16),) + state_shapes[1:],
-        in_specs=[VMEM] * 8,
+        in_specs=[VMEM] * 9,
         out_specs=(VMEM,) * 3,
         compiler_params=params,
         cost_estimate=cost(half),
         name="last_scores",
-    )(qt, near, far, *state, last_keys, last_stretch)
+    )(qt, near, far, *state, last_keys, last_stretch, last_down)
 
     prefill = pl.pallas_call(
         last_kernel,
         out_shape=shape((tokens, width), bf16),
-        in_specs=[VMEM] * 4,
+        in_specs=[VMEM] * 5,
         out_specs=HBM,
         scratch_shapes=[
             pltpu.VMEM((tokens, width), bf16),
@@ -526,7 +597,7 @@
         compiler_params=params,
         cost_estimate=cost(c_rows // 2),
         name="last_values",
-    )(weights, total, accum, last_values)
+    )(weights, total, accum, last_values, last_down)
     return (prefill, decoded)
 
 

time: 36.1 us -> 42.2 us (1.17)
  waiting for transfers between devices: 1.87 us -> 8.22 us
  Pallas kernels: 11.8 us -> 14.1 us
  starting transfers between devices: 16.6 us -> 14.4 us
  local copies, waits for them, and re-layouts: 3.1 us -> 2.55 us
    ppermute x5 -> x8, waiting for transfers between devices: 1.87 us -> 8.22 us  [send(): return lax.ppermute(array, 'ctx', pairs)]
    pallas_call x5 -> x8, Pallas kernels: 8.76 us -> 11.1 us  [the longest x3 4.93 us: per_device(): pl.pallas_call(functools.partial(hop_kernel, index, kind), out_shape=stat...]
    ppermute x5 -> x8, starting transfers between devices: 16.6 us -> 14.4 us  [send(): return lax.ppermute(array, 'ctx', pairs)]
    unnamed x14 -> x16, local copies, waits for them, and re-layouts: 3.1 us -> 2.53 us
  transfers between devices with their start and end apart: 5 -> 8, of which waited for: 1 -> 3; matrix products, arithmetic and copies ran while one was open for 0% -> 0% of each run, Pallas kernels for 30% -> 31%
where the time goes in v11:
time: 42.2 us; the launch traced here: 41.8 us
  starting transfers between devices  14.4 us (34%)
  Pallas kernels  14.1 us (33%)
  waiting for transfers between devices  8.22 us (19%)
  local copies, waits for them, and re-layouts  2.55 us (6%)
  between operations  1.53 us (4%)
  other arithmetic  1.12 us (3%)
    ppermute x8, starting transfers between devices, send(): return lax.ppermute(array, 'ctx', pairs)  14.4 us
    ppermute x8, waiting for transfers between devices, send(): return lax.ppermute(array, 'ctx', pairs)  8.22 us
    pallas_call x3, Pallas kernels, per_device(): pl.pallas_call(functools.partial(hop_kernel, index, kind), out_shape=stat...  4.93 us
    unnamed x16, local copies, waits for them, and re-layouts  2.53 us
    pallas_call x1, Pallas kernels, per_device(): pl.pallas_call(functools.partial(pages_kernel, count, pool), out_shape=sh...  1.89 us
    pallas_call x1, Pallas kernels, per_device(): pl.pallas_call(held_kernel, out_shape=(shape((heads * dec_rows, kv_width)...  1.86 us
    pallas_call x1, Pallas kernels, per_device(): pl.pallas_call(functools.partial(own_kernel, count), out_shape=(shape((kv...  1.86 us
    pallas_call x1, Pallas kernels, per_device(): pl.pallas_call(functools.partial(score_kernel, len(entries) - 2), out_sha...  1.6 us
  transfers between devices with their start and end apart: 8, of which 3 were waited for; matrix products, arithmetic and copies ran while one was open for 0% of the time, Pallas kernels for 31%

profile of v11, /device:TPU:0, one launch (start us, length us, event | category | flops | bytes accessed | tf_op | source)
XLA Modules:
  0.0 41.8 jit_solution(16031386966434698260)
XLA Ops:
  0.6 1.1 %pad_maximum_fusion.shard_ref.rest_ref = bf16[768,256]{1,0:T(8,128)(2,1)S(1)} fusion(bf16[256,256]{1,0:T(8,128)(2,1)} %param.16, bf16[128,256]{1,0:T(8,128)(2,1)} %param.14, bf16[256,256]{1,0:T(8,128)(2,1)} %param.15, bf16[128,256]{1,0:T(8,128)(2,1)} %param.13), kind=kLoop, calls=%fused_computation | loop fusion | flops 1572864 | bytes 786432 | tf_op jit(solution)/shard_map/max | solution.py:466
  1.8 5.0 %collective-permute-start = (bf16[768,256]{1,0:T(8,128)(2,1)S(1)}, bf16[768,256]{1,0:T(8,128)(2,1)S(1)}, u32[]{:S(2)}, u32[]{:S(2)}) collective-permute-start(bf16[768,256]{1,0:T(8,128)(2,1)S(1)} %pad_maximum_fusion.shard_ref.rest_ref), channel_id=1, source_target_pairs={{0,4},{4,8},{8,12},{1,5},{5,9},{9,13},{2,6},{6,10},{10,14},{3,7},{... | collective-permute-start | bytes 1179656 | tf_op jit(solution)/shard_map/ppermute | solution.py:446
  6.7 0.6 %copy-done.4 = s32[32]{0:T(128)S(1)} copy-done((s32[32]{0:T(128)S(1)}, s32[32]{0:T(128)}, u32[]{:S(2)}) %copy-start.4) | copy-done | bytes 152
  7.4 0.7 %pages_to_send_down.1 = (bf16[576,256]{1,0:T(8,128)(2,1)S(1)}, bf16[64,256]{1,0:T(8,128)(2,1)S(1)}) custom-call(s32[1]{0:T(128)} %bitcast.own_ref, s32[32]{0:T(128)S(1)} %copy-done.4, bf16[768,256]{1,0:T(8,128)(2,1)S(1)} %pad_maximum_fusion.shard_ref.rest_ref), custom_call_target="tpu_custom_call" | custom-call | tf_op jit(solution)/shard_map/pages_to_send_down/pallas_call | solution.py:470
  8.1 1.4 %collective-permute-start.3 = (bf16[576,256]{1,0:T(8,128)(2,1)S(1)}, bf16[576,256]{1,0:T(8,128)(2,1)S(1)}, u32[]{:S(2)}, u32[]{:S(2)}) collective-permute-start(bf16[576,256]{1,0:T(8,128)(2,1)S(1)} %get-tuple-element.79), channel_id=1, source_target_pairs={{4,0},{8,4},{12,8},{5,1},{9,5},{13,9},{6,2},{10,6},{14,10},{7,3},{... | collective-permute-start | bytes 884744 | tf_op jit(solution)/shard_map/ppermute | solution.py:446
  9.6 1.3 %collective-permute-start.1 = (bf16[64,256]{1,0:T(8,128)(2,1)S(1)}, bf16[64,256]{1,0:T(8,128)(2,1)S(1)}, u32[]{:S(2)}, u32[]{:S(2)}) collective-permute-start(bf16[64,256]{1,0:T(8,128)(2,1)S(1)} %get-tuple-element.58), channel_id=1, source_target_pairs={{8,0},{12,4},{9,1},{13,5},{10,2},{14,6},{11,3},{15,7},{24,16},{28,... | collective-permute-start | bytes 98312 | tf_op jit(solution)/shard_map/ppermute | solution.py:446
  11.6 1.2 %copy-done.1 = bf16[128,16,256]{2,1,0:T(8,128)(2,1)S(1)} copy-done((bf16[128,16,256]{2,1,0:T(8,128)(2,1)S(1)}, bf16[128,16,256]{2,1,0:T(8,128)(2,1)}, u32[]{:S(2)}) %copy-start.1) | copy-done | bytes 1048600
  12.8 1.9 %decode_held_pages.1 = (bf16[128,256]{1,0:T(8,128)(2,1)S(1)}, f32[16,8,1]{2,1,0:T(8,128)S(1)}, f32[16,8,1]{2,1,0:T(8,128)S(1)}, f32[16,8,256]{2,1,0:T(8,128)S(1)}) custom-call(s32[1]{0:T(128)} %bitcast.own_ref, s32[32]{0:T(128)S(1)} %copy-done.4, s32[8]{0:T(128)S(1)} %copy-done.6, bf16[8,2048]{1,0:T(8,128)(2,1)S(1)} %copy-done.2, s32[8,32]{1,0:T(8,128)S(1)} %copy-done.3, ...), custom_call_target="tpu_custom_call" | custom-call | flops 268435456 | bytes 2097152 | tf_op jit(solution)/shard_map/decode_held_pages/pallas_call | solution.py:505
  14.7 1.9 %own_shard.1 = (bf16[2,256,1024]{2,1,0:T(8,128)(2,1)S(1)}, bf16[4,128,128]{2,1,0:T(8,128)(2,1)S(1)}, bf16[4,256,128]{2,1,0:T(8,128)(2,1)S(1)}, f32[2,1,1024]{2,1...) custom-call(s32[1]{0:T(128)} %bitcast.own_ref, s32[1]{0:T(128)S(6)} %copy.14.limit_ref, ...), custom_call_target="tpu_custom_call" | custom-call | flops 402653184 | bytes 1048576 | tf_op jit(solution)/shard_map/own_shard/pallas_call | solution.py:490
  16.5 4.1 %collective-permute-done.1.refs_4_ = bf16[64,256]{1,0:T(8,128)(2,1)S(1)} collective-permute-done((bf16[64,256]{1,0:T(8,128)(2,1)S(1)}, bf16[64,256]{1,0:T(8,128)(2,1)S(1)}, u32[]{:S(2)}, u32[]{:S(2)}) %collective-permute-start.1) | collective-permute-done | bytes 32800 | tf_op jit(solution)/shard_map/ppermute | solution.py:446
  20.7 3.4 %collective-permute-start.2 = (bf16[768,256]{1,0:T(8,128)(2,1)S(1)}, bf16[768,256]{1,0:T(8,128)(2,1)S(1)}, u32[]{:S(2)}, u32[]{:S(2)}) collective-permute-start(bf16[768,256]{1,0:T(8,128)(2,1)S(1)} %pad_maximum_fusion.shard_ref.rest_ref), channel_id=1, source_target_pairs={{0,12},{12,0},{1,13},{13,1},{2,14},{14,2},{3,15},{15,3},{16,28},{2... | collective-permute-start | bytes 1179656 | tf_op jit(solution)/shard_map/ppermute | solution.py:446
  24.2 1.3 %collective-permute-start.6 = (bf16[512,256]{1,0:T(8,128)(2,1)S(1)}, bf16[512,256]{1,0:T(8,128)(2,1)S(1)}, u32[]{:S(2)}, u32[]{:S(2)}) collective-permute-start(bf16[512,256]{1,0:T(8,128)(2,1)S(1)} %slice.3), channel_id=1, source_target_pairs={{4,0},{8,4},{5,1},{9,5},{6,2},{10,6},{7,3},{11,7},{20,16},{24,20},... | collective-permute-start | bytes 786440 | tf_op jit(solution)/shard_map/ppermute | solution.py:446
  25.5 0.7 %collective-permute-start.4 = (bf16[256,256]{1,0:T(8,128)(2,1)S(1)}, bf16[256,256]{1,0:T(8,128)(2,1)S(1)}, u32[]{:S(2)}, u32[]{:S(2)}) collective-permute-start(bf16[256,256]{1,0:T(8,128)(2,1)S(1)} %get-tuple-element.80), channel_id=1, source_target_pairs={{4,8},{8,12},{5,9},{9,13},{6,10},{10,14},{7,11},{11,15},{20,24},{2... | collective-permute-start | bytes 393224 | tf_op jit(solution)/shard_map/ppermute | solution.py:446
  26.1 0.7 %collective-permute-start.5 = (bf16[256,256]{1,0:T(8,128)(2,1)S(1)}, bf16[256,256]{1,0:T(8,128)(2,1)S(1)}, u32[]{:S(2)}, u32[]{:S(2)}) collective-permute-start(bf16[256,256]{1,0:T(8,128)(2,1)S(1)} %get-tuple-element.102), channel_id=1, source_target_pairs={{4,8},{8,12},{5,9},{9,13},{6,10},{10,14},{7,11},{11,15},{20,24},{2... | collective-permute-start | bytes 393224 | tf_op jit(solution)/shard_map/ppermute | solution.py:446
  26.8 0.7 %collective-permute-start.7 = (bf16[256,256]{1,0:T(8,128)(2,1)S(1)}, bf16[256,256]{1,0:T(8,128)(2,1)S(1)}, u32[]{:S(2)}, u32[]{:S(2)}) collective-permute-start(bf16[256,256]{1,0:T(8,128)(2,1)S(1)} %get-tuple-element.106), channel_id=1, source_target_pairs={{4,8},{8,12},{5,9},{9,13},{6,10},{10,14},{7,11},{11,15},{20,24},{2... | collective-permute-start | bytes 393224 | tf_op jit(solution)/shard_map/ppermute | solution.py:446
  27.5 1.7 %entry_u1.1 = (f32[2,1,1024]{2,1,0:T(1,128)S(1)}, f32[2,1,1024]{2,1,0:T(1,128)S(1)}, f32[2,128,1024]{2,1,0:T(8,128)S(1)}) custom-call(bf16[2,256,1024]{2,1,0:T(8,128)(2,1)S(1)} %get-tuple-element.55.qt_ref, bf16[4,128,128]{2,1,0:T(8,128)(2,1)S(1)} %get-tuple-element.56.near_ref, bf16[4,256,128]{2,1,0:T(8,128)(2,1)S(1)} %get-tuple-element.57.far_ref, ...), custom_call_target="tpu_custom_call" | custom-call | flops 402653184 | bytes 1048576 | tf_op jit(solution)/shard_map/entry_u1/pallas_call | solution.py:552
  29.2 1.5 %entry_d1.1 = (f32[2,1,1024]{2,1,0:T(1,128)S(1)}, f32[2,1,1024]{2,1,0:T(1,128)S(1)}, f32[2,128,1024]{2,1,0:T(8,128)S(1)}) custom-call(bf16[2,256,1024]{2,1,0:T(8,128)(2,1)S(1)} %get-tuple-element.55.qt_ref, bf16[4,128,128]{2,1,0:T(8,128)(2,1)S(1)} %get-tuple-element.56.near_ref, bf16[4,256,128]{2,1,0:T(8,128)(2,1)S(1)} %get-tuple-element.57.far_ref, ...), custom_call_target="tpu_custom_call" | custom-call | flops 268435456 | bytes 1048576 | tf_op jit(solution)/shard_map/entry_d1/pallas_call | solution.py:552
  30.7 2.8 %collective-permute-done.2.refs_1_.ref = bf16[768,256]{1,0:T(8,128)(2,1)S(1)} collective-permute-done((bf16[768,256]{1,0:T(8,128)(2,1)S(1)}, bf16[768,256]{1,0:T(8,128)(2,1)S(1)}, u32[]{:S(2)}, u32[]{:S(2)}) %collective-permute-start.2) | collective-permute-done | bytes 393248 | tf_op jit(solution)/shard_map/ppermute | solution.py:446
  33.6 1.7 %entry_x3.1 = (f32[2,1,1024]{2,1,0:T(1,128)S(1)}, f32[2,1,1024]{2,1,0:T(1,128)S(1)}, f32[2,128,1024]{2,1,0:T(8,128)S(1)}) custom-call(bf16[2,256,1024]{2,1,0:T(8,128)(2,1)S(1)} %get-tuple-element.55.qt_ref, bf16[4,128,128]{2,1,0:T(8,128)(2,1)S(1)} %get-tuple-element.56.near_ref, bf16[4,256,128]{2,1,0:T(8,128)(2,1)S(1)} %get-tuple-element.57.far_ref, ...), custom_call_target="tpu_custom_call" | custom-call | flops 402653184 | bytes 1048576 | tf_op jit(solution)/shard_map/entry_x3/pallas_call | solution.py:552
  35.3 0.6 %copy-done.5 = s32[32]{0:T(128)S(1)} copy-done((s32[32]{0:T(128)S(1)}, s32[32]{0:T(128)}, u32[]{:S(2)}) %copy-start.5) | copy-done | bytes 152
  36.0 1.9 %decode_new_pages.1 = bf16[8,2048]{1,0:T(8,128)(2,1)} custom-call(s32[1]{0:T(128)} %bitcast.own_ref, s32[32]{0:T(128)S(1)} %copy-done.5, s32[8]{0:T(128)S(1)} %copy-done.6, s32[8,32]{1,0:T(8,128)S(1)} %copy-done.3, bf16[768,256]{1,0:T(8,128)(2,1)S(1)} %collective-permute-done.shard_ref.refs_0_.ref, bf16[768,256]{1,0:T(8,128)(2,1)S(1)} %collective-permute-done.2.refs_1_.ref, ...), custom_call_target="tpu_custom_call" | custom-call | flops 134217728 | bytes 1048576 | tf_op jit(solution)/shard_map/decode_new_pages/pallas_call | solution.py:562
  37.9 1.2 %collective-permute-done.6.down_ref = bf16[512,256]{1,0:T(8,128)(2,1)S(1)} collective-permute-done((bf16[512,256]{1,0:T(8,128)(2,1)S(1)}, bf16[512,256]{1,0:T(8,128)(2,1)S(1)}, u32[]{:S(2)}, u32[]{:S(2)}) %collective-permute-start.6) | collective-permute-done | bytes 262176 | tf_op jit(solution)/shard_map/ppermute | solution.py:446
  39.1 1.6 %last_scores.1 = (bf16[2,256,1024]{2,1,0:T(8,128)(2,1)S(1)}, f32[2,1,1024]{2,1,0:T(1,128)S(1)}, f32[2,128,1024]{2,1,0:T(8,128)S(1)}) custom-call(bf16[2,256,1024]{2,1,0:T(8,128)(2,1)S(1)} %get-tuple-element.55.qt_ref, bf16[4,128,128]{2,1,0:T(8,128)(2,1)S(1)} %get-tuple-element.56.near_ref, bf16[4,256,128]{2,1,0:T(8,128)(2,1)S(1)} %get-tuple-element.57.far_ref, ...), custom_call_target="tpu_custom_call" | custom-call | flops 402653184 | bytes 1048576 | tf_op jit(solution)/shard_map/last_scores/pallas_call | solution.py:578
  40.7 1.1 %last_values.1 = bf16[128,2048]{1,0:T(8,128)(2,1)} custom-call(bf16[2,256,1024]{2,1,0:T(8,128)(2,1)S(1)} %get-tuple-element.103.weights_ref, f32[2,1,1024]{2,1,0:T(1,128)S(1)} %get-tuple-element.104.total_ref, f32[2,128,1024]{2,1,0:T(8,128)S(1)} %get-tuple-element.105.accum_ref, bf16[256,256]{1,0:T(8,128)(2,1)S(1)} %collective-permute-done.7.values_ref, ...), custom_call_target="tpu_custom_call" | custom-call | flops 134217728 | bytes 1048576 | tf_op jit(solution)/shard_map/last_values/pallas_call | solution.py:588
  (20 shorter events, 0.1 us)
Async XLA Ops:
  0.6 10.9 %copy-start = (bf16[128,16,256]{2,1,0:T(8,128)(2,1)S(1)}, bf16[128,16,256]{2,1,0:T(8,128)(2,1)}, u32[]{:S(2)}) copy-start(bf16[128,16,256]{2,1,0:T(8,128)(2,1)} %pool_k.1) | copy-start | bytes 3145732
  1.8 22.3 %collective-permute-start = (bf16[768,256]{1,0:T(8,128)(2,1)S(1)}, bf16[768,256]{1,0:T(8,128)(2,1)S(1)}, u32[]{:S(2)}, u32[]{:S(2)}) collective-permute-start(bf16[768,256]{1,0:T(8,128)(2,1)S(1)} %pad_maximum_fusion.shard_ref.rest_ref), channel_id=1, source_target_pairs={{0,4},{4,8},{8,12},{1,5},{5,9},{9,13},{2,6},{6,10},{10,14},{3,7},{... | collective-permute-start | bytes 1179656 | tf_op jit(solution)/shard_map/ppermute | solution.py:446
  6.7 0.7 %copy-start.4 = (s32[32]{0:T(128)S(1)}, s32[32]{0:T(128)}, u32[]{:S(2)}) copy-start(s32[32]{0:T(128)} %targets_ref.5) | copy-start | bytes 388
  7.4 4.1 %copy-start.2 = (bf16[8,2048]{1,0:T(8,128)(2,1)S(1)}, bf16[8,2048]{1,0:T(8,128)(2,1)}, u32[]{:S(2)}) copy-start(bf16[8,2048]{1,0:T(8,128)(2,1)} %q_ref.3) | copy-start | bytes 98308
  8.1 3.4 %copy-start.3 = (s32[8,32]{1,0:T(8,128)S(1)}, s32[8,32]{1,0:T(8,128)}, u32[]{:S(2)}) copy-start(s32[8,32]{1,0:T(8,128)} %lists_ref.3) | copy-start | bytes 3076
  8.1 16.0 %collective-permute-start.3 = (bf16[576,256]{1,0:T(8,128)(2,1)S(1)}, bf16[576,256]{1,0:T(8,128)(2,1)S(1)}, u32[]{:S(2)}, u32[]{:S(2)}) collective-permute-start(bf16[576,256]{1,0:T(8,128)(2,1)S(1)} %get-tuple-element.79), channel_id=1, source_target_pairs={{4,0},{8,4},{12,8},{5,1},{9,5},{13,9},{6,2},{10,6},{14,10},{7,3},{... | collective-permute-start | bytes 884744 | tf_op jit(solution)/shard_map/ppermute | solution.py:446
  9.6 2.0 %copy-start.6 = (s32[8]{0:T(128)S(1)}, s32[8]{0:T(128)}, u32[]{:S(2)}) copy-start(s32[8]{0:T(128)} %length_ref.3) | copy-start | bytes 100
  9.6 11.1 %collective-permute-start.1 = (bf16[64,256]{1,0:T(8,128)(2,1)S(1)}, bf16[64,256]{1,0:T(8,128)(2,1)S(1)}, u32[]{:S(2)}, u32[]{:S(2)}) collective-permute-start(bf16[64,256]{1,0:T(8,128)(2,1)S(1)} %get-tuple-element.58), channel_id=1, source_target_pairs={{8,0},{12,4},{9,1},{13,5},{10,2},{14,6},{11,3},{15,7},{24,16},{28,... | collective-permute-start | bytes 98312 | tf_op jit(solution)/shard_map/ppermute | solution.py:446
  11.6 1.2 %copy-start.1 = (bf16[128,16,256]{2,1,0:T(8,128)(2,1)S(1)}, bf16[128,16,256]{2,1,0:T(8,128)(2,1)}, u32[]{:S(2)}) copy-start(bf16[128,16,256]{2,1,0:T(8,128)(2,1)} %pool_v.1) | copy-start | bytes 3145732
  12.8 1.9 %copy-start.7 = (bf16[128,2048]{1,0:T(8,128)(2,1)S(1)}, bf16[128,2048]{1,0:T(8,128)(2,1)}, u32[]{:S(2)}) copy-start(bf16[128,2048]{1,0:T(8,128)(2,1)} %q_ref.2) | copy-start | bytes 1572868
  20.7 12.9 %collective-permute-start.2 = (bf16[768,256]{1,0:T(8,128)(2,1)S(1)}, bf16[768,256]{1,0:T(8,128)(2,1)S(1)}, u32[]{:S(2)}, u32[]{:S(2)}) collective-permute-start(bf16[768,256]{1,0:T(8,128)(2,1)S(1)} %pad_maximum_fusion.shard_ref.rest_ref), channel_id=1, source_target_pairs={{0,12},{12,0},{1,13},{13,1},{2,14},{14,2},{3,15},{15,3},{16,28},{2... | collective-permute-start | bytes 1179656 | tf_op jit(solution)/shard_map/ppermute | solution.py:446
  24.2 14.9 %collective-permute-start.6 = (bf16[512,256]{1,0:T(8,128)(2,1)S(1)}, bf16[512,256]{1,0:T(8,128)(2,1)S(1)}, u32[]{:S(2)}, u32[]{:S(2)}) collective-permute-start(bf16[512,256]{1,0:T(8,128)(2,1)S(1)} %slice.3), channel_id=1, source_target_pairs={{4,0},{8,4},{5,1},{9,5},{6,2},{10,6},{7,3},{11,7},{20,16},{24,20},... | collective-permute-start | bytes 786440 | tf_op jit(solution)/shard_map/ppermute | solution.py:446
  25.5 9.8 %collective-permute-start.4 = (bf16[256,256]{1,0:T(8,128)(2,1)S(1)}, bf16[256,256]{1,0:T(8,128)(2,1)S(1)}, u32[]{:S(2)}, u32[]{:S(2)}) collective-permute-start(bf16[256,256]{1,0:T(8,128)(2,1)S(1)} %get-tuple-element.80), channel_id=1, source_target_pairs={{4,8},{8,12},{5,9},{9,13},{6,10},{10,14},{7,11},{11,15},{20,24},{2... | collective-permute-start | bytes 393224 | tf_op jit(solution)/shard_map/ppermute | solution.py:446
  26.1 11.7 %collective-permute-start.5 = (bf16[256,256]{1,0:T(8,128)(2,1)S(1)}, bf16[256,256]{1,0:T(8,128)(2,1)S(1)}, u32[]{:S(2)}, u32[]{:S(2)}) collective-permute-start(bf16[256,256]{1,0:T(8,128)(2,1)S(1)} %get-tuple-element.102), channel_id=1, source_target_pairs={{4,8},{8,12},{5,9},{9,13},{6,10},{10,14},{7,11},{11,15},{20,24},{2... | collective-permute-start | bytes 393224 | tf_op jit(solution)/shard_map/ppermute | solution.py:446
  26.8 13.9 %collective-permute-start.7 = (bf16[256,256]{1,0:T(8,128)(2,1)S(1)}, bf16[256,256]{1,0:T(8,128)(2,1)S(1)}, u32[]{:S(2)}, u32[]{:S(2)}) collective-permute-start(bf16[256,256]{1,0:T(8,128)(2,1)S(1)} %get-tuple-element.106), channel_id=1, source_target_pairs={{4,8},{8,12},{5,9},{9,13},{6,10},{10,14},{7,11},{11,15},{20,24},{2... | collective-permute-start | bytes 393224 | tf_op jit(solution)/shard_map/ppermute | solution.py:446
  35.3 0.7 %copy-start.5 = (s32[32]{0:T(128)S(1)}, s32[32]{0:T(128)}, u32[]{:S(2)}) copy-start(s32[32]{0:T(128)} %targets_ref.5) | copy-start | bytes 388

commit v12 on v10

--- a/solution.py
+++ b/solution.py
@@ -482,6 +482,7 @@
     last_pages = lax.ppermute(pieces[3], "ctx", others)
     last_values = send(pieces[2], hop)
 
+    last_pages, state = lax.optimization_barrier((last_pages, state))
     for first in range(len(hops) - 1):
         places = [first]
         state = pl.pallas_call(

time: 36.7 us -> 38.7 us (1.054)
  waiting for transfers between devices: 6.56 us -> 8.62 us
    ppermute x1, waiting for transfers between devices: 5.4 us -> 7.53 us  [per_device(): last_pages = lax.ppermute(pieces[3], 'ctx', others)]
    ppermute x4, starting transfers between devices: 9.24 us -> 7.73 us  [send(): return lax.ppermute(array, 'ctx', up_pairs if hop < 0 else down_pairs)]
    ppermute x1, starting transfers between devices: 1.96 us -> 3.47 us  [per_device(): last_pages = lax.ppermute(pieces[3], 'ctx', others)]
  transfers between devices with their start and end apart: 6 -> 6, of which waited for: 3 -> 2; matrix products, arithmetic and copies ran while one was open for 0% -> 0% of each run, Pallas kernels for 31% -> 29%
where the time goes in v12:
time: 38.7 us; the launch traced here: 38.5 us
  Pallas kernels  12.4 us (32%)
  starting transfers between devices  11.9 us (31%)
  waiting for transfers between devices  8.62 us (22%)
  local copies, waits for them, and re-layouts  3.1 us (8%)
  between operations  1.44 us (4%)
  other arithmetic  1.03 us (3%)
    ppermute x4, starting transfers between devices, send(): return lax.ppermute(array, 'ctx', up_pairs if hop < 0 else down_pairs)  7.73 us
    ppermute x1, waiting for transfers between devices, per_device(): last_pages = lax.ppermute(pieces[3], 'ctx', others)  7.53 us
    ppermute x1, starting transfers between devices, per_device(): last_pages = lax.ppermute(pieces[3], 'ctx', others)  3.47 us
    pallas_call x2, Pallas kernels, per_device(): pl.pallas_call(functools.partial(hop_kernel, places), out_shape=state_sha...  3.45 us
    unnamed x14, local copies, waits for them, and re-layouts  3.1 us
    pallas_call x1, Pallas kernels, per_device(): pl.pallas_call(functools.partial(own_kernel, count, hops), out_shape=(sha...  2.36 us
    pallas_call x1, Pallas kernels, per_device(): pl.pallas_call(held_kernel, out_shape=(shape((heads * dec_rows, kv_width)...  1.86 us
    pallas_call x1, Pallas kernels, per_device(): pl.pallas_call(functools.partial(pages_kernel, count, hops, tokens, pool)...  1.83 us
  transfers between devices with their start and end apart: 6, of which 2 were waited for; matrix products, arithmetic and copies ran while one was open for 0% of the time, Pallas kernels for 29%

profile of v12, /device:TPU:0, one launch (start us, length us, event | category | flops | bytes accessed | tf_op | source)
XLA Modules:
  0.0 38.5 jit_solution(3783455382139122802)
XLA Ops:
  0.6 1.0 %pad_maximum_fusion.shard_ref.rest_ref = bf16[768,256]{1,0:T(8,128)(2,1)S(1)} fusion(bf16[256,256]{1,0:T(8,128)(2,1)} %param.16, bf16[128,256]{1,0:T(8,128)(2,1)} %param.14, bf16[256,256]{1,0:T(8,128)(2,1)} %param.15, bf16[128,256]{1,0:T(8,128)(2,1)} %param.13), kind=kLoop, calls=%fused_computation | loop fusion | flops 1572864 | bytes 786432 | tf_op jit(solution)/shard_map/max | solution.py:415
  1.7 3.1 %collective-permute-start = (bf16[768,256]{1,0:T(8,128)(2,1)S(1)}, bf16[768,256]{1,0:T(8,128)(2,1)S(1)}, u32[]{:S(2)}, u32[]{:S(2)}) collective-permute-start(bf16[768,256]{1,0:T(8,128)(2,1)S(1)} %pad_maximum_fusion.shard_ref.rest_ref), channel_id=1, source_target_pairs={{0,4},{4,8},{8,12},{12,0},{1,5},{5,9},{9,13},{13,1},{2,6},{6,10},{... | collective-permute-start | bytes 1179656 | tf_op jit(solution)/shard_map/ppermute | solution.py:400
  5.4 0.0 copy-start.4
  5.4 0.0 copy-start.5
  5.5 0.6 %copy-done.4 = s32[32]{0:T(128)S(1)} copy-done((s32[32]{0:T(128)S(1)}, s32[32]{0:T(128)}, u32[]{:S(2)}) %copy-start.4) | copy-done | bytes 152
  6.1 0.0 copy-done.5
  6.1 1.2 %copy-done = bf16[128,16,256]{2,1,0:T(8,128)(2,1)S(1)} copy-done((bf16[128,16,256]{2,1,0:T(8,128)(2,1)S(1)}, bf16[128,16,256]{2,1,0:T(8,128)(2,1)}, u32[]{:S(2)}) %copy-start) | copy-done | bytes 1048600
  7.3 1.2 %copy-done.1 = bf16[128,16,256]{2,1,0:T(8,128)(2,1)S(1)} copy-done((bf16[128,16,256]{2,1,0:T(8,128)(2,1)S(1)}, bf16[128,16,256]{2,1,0:T(8,128)(2,1)}, u32[]{:S(2)}) %copy-start.1) | copy-done | bytes 1048600
  8.5 1.9 %decode_held_pages.1 = (bf16[128,256]{1,0:T(8,128)(2,1)S(1)}, f32[16,8,1]{2,1,0:T(8,128)S(1)}, f32[16,8,1]{2,1,0:T(8,128)S(1)}, f32[16,8,256]{2,1,0:T(8,128)S(1)}) custom-call(s32[1]{0:T(128)} %bitcast.own_ref, s32[32]{0:T(128)S(1)} %copy-done.4, s32[8]{0:T(128)S(1)} %copy-done.5, bf16[8,2048]{1,0:T(8,128)(2,1)S(1)} %copy-done.2, s32[8,32]{1,0:T(8,128)S(1)} %copy-done.3, ...), custom_call_target="tpu_custom_call" | custom-call | flops 268435456 | bytes 2097152 | tf_op jit(solution)/shard_map/decode_held_pages/pallas_call | solution.py:439
  10.4 2.4 %own_shard.1 = (bf16[2,256,1024]{2,1,0:T(8,128)(2,1)S(1)}, bf16[3,128,128]{2,1,0:T(8,128)(2,1)S(1)}, bf16[3,256,128]{2,1,0:T(8,128)(2,1)S(1)}, bf16[32,128]{1,0:...) custom-call(s32[1]{0:T(128)} %bitcast.own_ref, ...), custom_call_target="tpu_custom_call" | custom-call | flops 402653184 | bytes 1048576 | tf_op jit(solution)/shard_map/own_shard/pallas_call | solution.py:423
  12.8 2.1 %collective-permute-start.1 = (bf16[768,256]{1,0:T(8,128)(2,1)S(1)}, bf16[768,256]{1,0:T(8,128)(2,1)S(1)}, u32[]{:S(2)}, u32[]{:S(2)}) collective-permute-start(bf16[768,256]{1,0:T(8,128)(2,1)S(1)} %pad_maximum_fusion.shard_ref.rest_ref), channel_id=1, source_target_pairs={{0,12},{4,0},{8,4},{12,8},{1,13},{5,1},{9,5},{13,9},{2,14},{6,2},{... | collective-permute-start | bytes 1179656 | tf_op jit(solution)/shard_map/ppermute | solution.py:400
  14.9 1.1 %collective-permute-done.shard_ref.refs_0_ = bf16[768,256]{1,0:T(8,128)(2,1)S(1)} collective-permute-done((bf16[768,256]{1,0:T(8,128)(2,1)S(1)}, bf16[768,256]{1,0:T(8,128)(2,1)S(1)}, u32[]{:S(2)}, u32[]{:S(2)}) %collective-permute-start) | collective-permute-done | bytes 393248 | tf_op jit(solution)/shard_map/ppermute | solution.py:400
  16.0 0.1 pieces_to_send_on.1
  16.1 0.7 %collective-permute-start.2 = (bf16[256,256]{1,0:T(8,128)(2,1)S(1)}, bf16[256,256]{1,0:T(8,128)(2,1)S(1)}, u32[]{:S(2)}, u32[]{:S(2)}) collective-permute-start(bf16[256,256]{1,0:T(8,128)(2,1)S(1)} %get-tuple-element.66), channel_id=1, source_target_pairs={{4,8},{8,12},{5,9},{9,13},{6,10},{10,14},{7,11},{11,15},{20,24},{2... | collective-permute-start | bytes 393224 | tf_op jit(solution)/shard_map/ppermute | solution.py:481
  16.8 2.5 %collective-permute-start.4 = (bf16[256,256]{1,0:T(8,128)(2,1)S(1)}, bf16[256,256]{1,0:T(8,128)(2,1)S(1)}, u32[]{:S(2)}, u32[]{:S(2)}) collective-permute-start(bf16[256,256]{1,0:T(8,128)(2,1)S(1)} %get-tuple-element.88), channel_id=1, source_target_pairs={{0,4},{4,8},{8,12},{12,0},{1,5},{5,9},{9,13},{13,1},{2,6},{6,10},{... | collective-permute-start | bytes 393224 | tf_op jit(solution)/shard_map/ppermute | solution.py:400
  19.3 3.5 %collective-permute-start.3 = (bf16[64,256]{1,0:T(8,128)(2,1)S(1)}, bf16[64,256]{1,0:T(8,128)(2,1)S(1)}, u32[]{:S(2)}, u32[]{:S(2)}) collective-permute-start(bf16[64,256]{1,0:T(8,128)(2,1)S(1)} %get-tuple-element.67), channel_id=1, source_target_pairs={{0,4},{12,0},{1,5},{13,1},{2,6},{14,2},{3,7},{15,3},{16,20},{28,16... | collective-permute-start | bytes 98312 | tf_op jit(solution)/shard_map/ppermute | solution.py:482
  22.8 0.1 collective-permute-start.5
  22.8 7.5 %collective-permute-done.3.refs_3_ = bf16[64,256]{1,0:T(8,128)(2,1)S(1)} collective-permute-done((bf16[64,256]{1,0:T(8,128)(2,1)S(1)}, bf16[64,256]{1,0:T(8,128)(2,1)S(1)}, u32[]{:S(2)}, u32[]{:S(2)}) %collective-permute-start.3) | collective-permute-done | bytes 32800 | tf_op jit(solution)/shard_map/ppermute | solution.py:482
  30.4 1.7 %whole_shards_0.1 = (f32[2,1,1024]{2,1,0:T(1,128)S(1)}, f32[2,1,1024]{2,1,0:T(1,128)S(1)}, f32[2,128,1024]{2,1,0:T(8,128)S(1)}) custom-call(bf16[2,256,1024]{2,1,0:T(8,128)(2,1)S(1)} %get-tuple-element.48.qt_ref, bf16[3,128,128]{2,1,0:T(8,128)(2,1)S(1)} %get-tuple-element.49.near_ref, bf16[3,256,128]{2,1,0:T(8,128)(2,1)S(1)} %get-tuple-element.50.far_ref, ...), custom_call_target="tpu_custom_call" | custom-call | flops 402653184 | bytes 1048576 | tf_op jit(solution)/shard_map/whole_shards_0/pallas_call | solution.py:488
  32.1 0.0 collective-permute-done.1.refs_1_.refs_0_
  32.1 1.7 %whole_shards_1.1 = (f32[2,1,1024]{2,1,0:T(1,128)S(1)}, f32[2,1,1024]{2,1,0:T(1,128)S(1)}, f32[2,128,1024]{2,1,0:T(8,128)S(1)}) custom-call(bf16[2,256,1024]{2,1,0:T(8,128)(2,1)S(1)} %get-tuple-element.48.qt_ref, bf16[3,128,128]{2,1,0:T(8,128)(2,1)S(1)} %get-tuple-element.49.near_ref, bf16[3,256,128]{2,1,0:T(8,128)(2,1)S(1)} %get-tuple-element.50.far_ref, ...), custom_call_target="tpu_custom_call" | custom-call | flops 402653184 | bytes 1048576 | tf_op jit(solution)/shard_map/whole_shards_1/pallas_call | solution.py:488
  33.9 1.8 %decode_new_pages.1 = bf16[8,2048]{1,0:T(8,128)(2,1)} custom-call(s32[1]{0:T(128)} %bitcast.own_ref, s32[32]{0:T(128)S(1)} %copy-done.4, s32[8]{0:T(128)S(1)} %copy-done.5, s32[8,32]{1,0:T(8,128)S(1)} %copy-done.3, bf16[768,256]{1,0:T(8,128)(2,1)S(1)} %collective-permute-done.shard_ref.refs_0_, bf16[768,256]{1,0:T(8,128)(2,1)S(1)} %collective-permute-done.1.refs_1_.refs_0_, ...), custom_call_target="tpu_custom_call" | custom-call | flops 134217728 | bytes 1048576 | tf_op jit(solution)/shard_map/decode_new_pages/pallas_call | solution.py:499
  35.7 1.6 %last_scores.1 = (bf16[2,256,1024]{2,1,0:T(8,128)(2,1)S(1)}, f32[2,1,1024]{2,1,0:T(1,128)S(1)}, f32[2,128,1024]{2,1,0:T(8,128)S(1)}) custom-call(bf16[2,256,1024]{2,1,0:T(8,128)(2,1)S(1)} %get-tuple-element.48.qt_ref, bf16[3,128,128]{2,1,0:T(8,128)(2,1)S(1)} %get-tuple-element.49.near_ref, bf16[3,256,128]{2,1,0:T(8,128)(2,1)S(1)} %get-tuple-element.50.far_ref, ...), custom_call_target="tpu_custom_call" | custom-call | flops 402653184 | bytes 1048576 | tf_op jit(solution)/shard_map/last_scores/pallas_call | solution.py:513
  37.3 1.1 %last_values.1 = bf16[128,2048]{1,0:T(8,128)(2,1)} custom-call(bf16[2,256,1024]{2,1,0:T(8,128)(2,1)S(1)} %get-tuple-element.89.weights_ref, f32[2,1,1024]{2,1,0:T(1,128)S(1)} %get-tuple-element.90.total_ref, f32[2,128,1024]{2,1,0:T(8,128)S(1)} %get-tuple-element.91.accum_ref, bf16[256,256]{1,0:T(8,128)(2,1)S(1)} %collective-permute-done.5.values_ref), custom_call_target="tpu_custom_call" | custom-call | flops 134217728 | bytes 1048576 | tf_op jit(solution)/shard_map/last_values/pallas_call | solution.py:523
  (11 shorter events, 0.0 us)
Async XLA Ops:
  0.6 4.8 %copy-start.2 = (bf16[8,2048]{1,0:T(8,128)(2,1)S(1)}, bf16[8,2048]{1,0:T(8,128)(2,1)}, u32[]{:S(2)}) copy-start(bf16[8,2048]{1,0:T(8,128)(2,1)} %q_ref.3) | copy-start | bytes 98308
  1.7 14.3 %collective-permute-start = (bf16[768,256]{1,0:T(8,128)(2,1)S(1)}, bf16[768,256]{1,0:T(8,128)(2,1)S(1)}, u32[]{:S(2)}, u32[]{:S(2)}) collective-permute-start(bf16[768,256]{1,0:T(8,128)(2,1)S(1)} %pad_maximum_fusion.shard_ref.rest_ref), channel_id=1, source_target_pairs={{0,4},{4,8},{8,12},{12,0},{1,5},{5,9},{9,13},{13,1},{2,6},{6,10},{... | collective-permute-start | bytes 1179656 | tf_op jit(solution)/shard_map/ppermute | solution.py:400
  4.8 0.7 %copy-start.3 = (s32[8,32]{1,0:T(8,128)S(1)}, s32[8,32]{1,0:T(8,128)}, u32[]{:S(2)}) copy-start(s32[8,32]{1,0:T(8,128)} %lists_ref.3) | copy-start | bytes 3076
  5.4 0.7 %copy-start.4 = (s32[32]{0:T(128)S(1)}, s32[32]{0:T(128)}, u32[]{:S(2)}) copy-start(s32[32]{0:T(128)} %targets_ref.5) | copy-start | bytes 388
  5.4 0.7 %copy-start.5 = (s32[8]{0:T(128)S(1)}, s32[8]{0:T(128)}, u32[]{:S(2)}) copy-start(s32[8]{0:T(128)} %length_ref.3) | copy-start | bytes 100
  6.1 1.2 %copy-start = (bf16[128,16,256]{2,1,0:T(8,128)(2,1)S(1)}, bf16[128,16,256]{2,1,0:T(8,128)(2,1)}, u32[]{:S(2)}) copy-start(bf16[128,16,256]{2,1,0:T(8,128)(2,1)} %pool_k.1) | copy-start | bytes 3145732
  7.3 1.2 %copy-start.1 = (bf16[128,16,256]{2,1,0:T(8,128)(2,1)S(1)}, bf16[128,16,256]{2,1,0:T(8,128)(2,1)}, u32[]{:S(2)}) copy-start(bf16[128,16,256]{2,1,0:T(8,128)(2,1)} %pool_v.1) | copy-start | bytes 3145732
  8.5 1.9 %copy-start.6 = (bf16[128,2048]{1,0:T(8,128)(2,1)S(1)}, bf16[128,2048]{1,0:T(8,128)(2,1)}, u32[]{:S(2)}) copy-start(bf16[128,2048]{1,0:T(8,128)(2,1)} %q_ref.2) | copy-start | bytes 1572868
  12.8 19.3 %collective-permute-start.1 = (bf16[768,256]{1,0:T(8,128)(2,1)S(1)}, bf16[768,256]{1,0:T(8,128)(2,1)S(1)}, u32[]{:S(2)}, u32[]{:S(2)}) collective-permute-start(bf16[768,256]{1,0:T(8,128)(2,1)S(1)} %pad_maximum_fusion.shard_ref.rest_ref), channel_id=1, source_target_pairs={{0,12},{4,0},{8,4},{12,8},{1,13},{5,1},{9,5},{13,9},{2,14},{6,2},{... | collective-permute-start | bytes 1179656 | tf_op jit(solution)/shard_map/ppermute | solution.py:400
  16.1 17.7 %collective-permute-start.2 = (bf16[256,256]{1,0:T(8,128)(2,1)S(1)}, bf16[256,256]{1,0:T(8,128)(2,1)S(1)}, u32[]{:S(2)}, u32[]{:S(2)}) collective-permute-start(bf16[256,256]{1,0:T(8,128)(2,1)S(1)} %get-tuple-element.66), channel_id=1, source_target_pairs={{4,8},{8,12},{5,9},{9,13},{6,10},{10,14},{7,11},{11,15},{20,24},{2... | collective-permute-start | bytes 393224 | tf_op jit(solution)/shard_map/ppermute | solution.py:481
  16.8 18.9 %collective-permute-start.4 = (bf16[256,256]{1,0:T(8,128)(2,1)S(1)}, bf16[256,256]{1,0:T(8,128)(2,1)S(1)}, u32[]{:S(2)}, u32[]{:S(2)}) collective-permute-start(bf16[256,256]{1,0:T(8,128)(2,1)S(1)} %get-tuple-element.88), channel_id=1, source_target_pairs={{0,4},{4,8},{8,12},{12,0},{1,5},{5,9},{9,13},{13,1},{2,6},{6,10},{... | collective-permute-start | bytes 393224 | tf_op jit(solution)/shard_map/ppermute | solution.py:400
  19.3 11.1 %collective-permute-start.3 = (bf16[64,256]{1,0:T(8,128)(2,1)S(1)}, bf16[64,256]{1,0:T(8,128)(2,1)S(1)}, u32[]{:S(2)}, u32[]{:S(2)}) collective-permute-start(bf16[64,256]{1,0:T(8,128)(2,1)S(1)} %get-tuple-element.67), channel_id=1, source_target_pairs={{0,4},{12,0},{1,5},{13,1},{2,6},{14,2},{3,7},{15,3},{16,20},{28,16... | collective-permute-start | bytes 98312 | tf_op jit(solution)/shard_map/ppermute | solution.py:482
  22.8 14.5 %collective-permute-start.5 = (bf16[256,256]{1,0:T(8,128)(2,1)S(1)}, bf16[256,256]{1,0:T(8,128)(2,1)S(1)}, u32[]{:S(2)}, u32[]{:S(2)}) collective-permute-start(bf16[256,256]{1,0:T(8,128)(2,1)S(1)} %get-tuple-element.92), channel_id=1, source_target_pairs={{0,4},{4,8},{8,12},{12,0},{1,5},{5,9},{9,13},{13,1},{2,6},{6,10},{... | collective-permute-start | bytes 393224 | tf_op jit(solution)/shard_map/ppermute | solution.py:400

commit v13 on v10

--- a/solution.py
+++ b/solution.py
@@ -282,26 +282,38 @@
     values_ref[...] = shard_ref[half + tokens :]
 
 
-def pages_kernel(count, hops, tokens, pool, own_ref, targets_ref, length_ref, lists_ref, *refs):
-    shard_refs, refs = refs[: len(hops) + 1], refs[len(hops) + 1 :]
-    wide_ref, dec_high, dec_total, dec_mixed, dec_out = refs
+def near_pages_kernel(count, hops, tokens, pool, own_ref, targets_ref, length_ref, lists_ref, *refs):
+    shard_refs, refs = refs[: len(hops)], refs[len(hops) :]
+    wide_ref, dec_high, dec_total, dec_mixed, high_ref, total_ref, mixed_ref = refs
     own = own_ref[0]
-    pages = tokens // PAGE
     lists = lists_ref[...]
     lengths = length_column(length_ref)
     parts = []
-    for hop, ref in zip(hops[:-1], shard_refs):
+    for hop, ref in zip(hops, shard_refs):
         half = ref.shape[0] // 2
         slot = slot_row(targets_ref, shard_of(own, hop, count), own, tokens, pool)
         parts.append((ref[:tokens], ref[half : half + tokens], tally_of(lists, lengths, slot)))
-    stretch_ref, pages_ref = shard_refs[-2:]
-    shard = shard_of(own, hops[-1], count)
+    state = (dec_high[...], dec_total[...], dec_mixed[...])
+    high_ref[...], total_ref[...], mixed_ref[...] = decode_attend(wide_ref[...], parts, state)
+
+
+def last_pages_kernel(
+    count, hop, pool, own_ref, targets_ref, length_ref, lists_ref, stretch_ref, pages_ref,
+    wide_ref, dec_high, dec_total, dec_mixed, dec_out,
+):
+    own = own_ref[0]
+    tokens = stretch_ref.shape[0] // 2
+    sent = pages_ref.shape[0] // 2
+    lists = lists_ref[...]
+    lengths = length_column(length_ref)
+    shard = shard_of(own, hop, count)
     attended = shard < own
-    slot = jnp.where(attended, slot_row(targets_ref, shard, own, tokens, pool), -1)
-    parts.append((stretch_ref[:tokens], stretch_ref[tokens:], tally_of(lists, lengths, slot)))
-    sent = pages_ref.shape[0] // 2
-    slot = jnp.where(attended, -1, sent_slots(targets_ref, shard, own, pages, pool))
-    parts.append((pages_ref[:sent], pages_ref[sent:], tally_of(lists, lengths, slot)))
+    whole = jnp.where(attended, slot_row(targets_ref, shard, own, tokens, pool), -1)
+    alone = jnp.where(attended, -1, sent_slots(targets_ref, shard, own, tokens // PAGE, pool))
+    parts = [
+        (stretch_ref[:tokens], stretch_ref[tokens:], tally_of(lists, lengths, whole)),
+        (pages_ref[:sent], pages_ref[sent:], tally_of(lists, lengths, alone)),
+    ]
     _, total, mixed = decode_attend(wide_ref[...], parts, (dec_high[...], dec_total[...], dec_mixed[...]))
     for head in range(dec_high.shape[0]):
         piece = mixed[head, :, features(head // GROUP)] / total[head]
@@ -436,14 +448,14 @@
         name="own_shard",
     )(own_array, prefix_length, page_targets, queries, shard[0])
 
+    dec_shapes = (
+        shape((heads, dec_rows, 1), f32),
+        shape((heads, dec_rows, 1), f32),
+        shape((heads, dec_rows, kv_width), f32),
+    )
     wide, *dec_state = pl.pallas_call(
         held_kernel,
-        out_shape=(
-            shape((heads * dec_rows, kv_width), bf16),
-            shape((heads, dec_rows, 1), f32),
-            shape((heads, dec_rows, 1), f32),
-            shape((heads, dec_rows, kv_width), f32),
-        ),
+        out_shape=(shape((heads * dec_rows, kv_width), bf16),) + dec_shapes,
         in_specs=[SMEM] * 3 + [VMEM] * 5,
         out_specs=(VMEM,) * 4,
         compiler_params=params,
@@ -495,20 +507,22 @@
         )(qt, near, far, *state, *[shard[hops[place]] for place in places])
 
     final = len(hops) - 1
-    decoded = pl.pallas_call(
-        functools.partial(pages_kernel, count, hops, tokens, pool),
-        out_shape=shape(decode_queries.shape, bf16),
-        in_specs=[SMEM] * 3 + [VMEM] * (6 + len(hops)),
-        out_specs=VMEM,
+    dec_state, state = lax.optimization_barrier((dec_state, state))
+    near_hops = hops[:-1]
+    dec_state = pl.pallas_call(
+        functools.partial(near_pages_kernel, count, near_hops, tokens, pool),
+        out_shape=dec_shapes,
+        in_specs=[SMEM] * 3 + [VMEM] * (5 + len(near_hops)),
+        out_specs=(VMEM,) * 3,
         compiler_params=params,
         cost_estimate=cost(tokens),
-        name="decode_new_pages",
+        name="decode_near_pages",
     )(
-        own_array, page_targets, context_length, page_lists, *[shard[hop] for hop in hops[:-1]], last_stretch, last_pages,
+        own_array, page_targets, context_length, page_lists, *[shard[hop] for hop in near_hops],
         wide, *dec_state,
     )
-
-    decoded, state = lax.optimization_barrier((decoded, state))
+    dec_state, state = lax.optimization_barrier((dec_state, state))
+
     weights, total, accum = pl.pallas_call(
         functools.partial(score_kernel, final),
         out_shape=(shape((kv_local, c_rows, rows), bf16),) + state_shapes[1:],
@@ -532,6 +546,19 @@
         cost_estimate=cost(c_rows // 2),
         name="last_values",
     )(weights, total, accum, last_values)
+
+    prefill, dec_state = lax.optimization_barrier((prefill, dec_state))
+    decoded = pl.pallas_call(
+        functools.partial(last_pages_kernel, count, hops[-1], pool),
+        out_shape=shape(decode_queries.shape, bf16),
+        in_specs=[SMEM] * 3 + [VMEM] * 7,
+        out_specs=VMEM,
+        compiler_params=params,
+        cost_estimate=cost(tokens // 2),
+        name="decode_last_pages",
+    )(
+        own_array, page_targets, context_length, page_lists, last_stretch, last_pages, wide, *dec_state
+    )
     return (prefill, decoded)
 
 

time: 36.7 us -> 34.6 us (0.943)
  waiting for transfers between devices: 6.56 us -> 1.35 us
  starting transfers between devices: 11.9 us -> 14 us
  Pallas kernels: 12.4 us -> 13.3 us
    ppermute x1, waiting for transfers between devices: 5.4 us -> 0.01 us  [per_device(): last_pages = lax.ppermute(pieces[3], 'ctx', others)]
    ppermute x1, starting transfers between devices: 1.96 us -> 4.07 us  [per_device(): last_pages = lax.ppermute(pieces[3], 'ctx', others)]
    pallas_call x1 -> x2, Pallas kernels: 1.82 us -> 2.76 us  [the longest x1 1.69 us: per_device(): pl.pallas_call(functools.partial(last_pages_kernel, count, hops[-1], pool...]
  transfers between devices with their start and end apart: 6 -> 6, of which waited for: 3 -> 3; matrix products, arithmetic and copies ran while one was open for 0% -> 0% of each run, Pallas kernels for 31% -> 34%
where the time goes in v13:
time: 34.6 us; the launch traced here: 34.3 us
  starting transfers between devices  14 us (40%)
  Pallas kernels  13.3 us (38%)
  local copies, waits for them, and re-layouts  3.1 us (9%)
  between operations  1.45 us (4%)
  waiting for transfers between devices  1.35 us (4%)
  other arithmetic  1.03 us (3%)
    ppermute x4, starting transfers between devices, send(): return lax.ppermute(array, 'ctx', up_pairs if hop < 0 else down_pairs)  9.28 us
    ppermute x1, starting transfers between devices, per_device(): last_pages = lax.ppermute(pieces[3], 'ctx', others)  4.07 us
    pallas_call x2, Pallas kernels, per_device(): pl.pallas_call(functools.partial(hop_kernel, places), out_shape=state_sha...  3.46 us
    unnamed x14, local copies, waits for them, and re-layouts  3.1 us
    pallas_call x1, Pallas kernels, per_device(): pl.pallas_call(functools.partial(own_kernel, count, hops), out_shape=(sha...  2.36 us
    pallas_call x1, Pallas kernels, per_device(): pl.pallas_call(held_kernel, out_shape=(shape((heads * dec_rows, kv_width)...  1.86 us
    pallas_call x1, Pallas kernels, per_device(): pl.pallas_call(functools.partial(last_pages_kernel, count, hops[-1], pool...  1.69 us
    pallas_call x1, Pallas kernels, per_device(): pl.pallas_call(functools.partial(score_kernel, final), out_shape=(shape((...  1.6 us
  transfers between devices with their start and end apart: 6, of which 3 were waited for; matrix products, arithmetic and copies ran while one was open for 0% of the time, Pallas kernels for 34%

profile of v13, /device:TPU:0, one launch (start us, length us, event | category | flops | bytes accessed | tf_op | source)
XLA Modules:
  0.0 34.3 jit_solution(1392883793329481339)
XLA Ops:
  0.6 1.0 %pad_maximum_fusion.shard_ref.rest_ref = bf16[768,256]{1,0:T(8,128)(2,1)S(1)} fusion(bf16[256,256]{1,0:T(8,128)(2,1)} %param.16, bf16[128,256]{1,0:T(8,128)(2,1)} %param.14, bf16[256,256]{1,0:T(8,128)(2,1)} %param.15, bf16[128,256]{1,0:T(8,128)(2,1)} %param.13), kind=kLoop, calls=%fused_computation | loop fusion | flops 1572864 | bytes 786432 | tf_op jit(solution)/shard_map/max | solution.py:427
  1.7 3.1 %collective-permute-start = (bf16[768,256]{1,0:T(8,128)(2,1)S(1)}, bf16[768,256]{1,0:T(8,128)(2,1)S(1)}, u32[]{:S(2)}, u32[]{:S(2)}) collective-permute-start(bf16[768,256]{1,0:T(8,128)(2,1)S(1)} %pad_maximum_fusion.shard_ref.rest_ref), channel_id=1, source_target_pairs={{0,4},{4,8},{8,12},{12,0},{1,5},{5,9},{9,13},{13,1},{2,6},{6,10},{... | collective-permute-start | bytes 1179656 | tf_op jit(solution)/shard_map/ppermute | solution.py:412
  5.4 0.0 copy-start.5
  5.5 0.6 %copy-done.4 = s32[32]{0:T(128)S(1)} copy-done((s32[32]{0:T(128)S(1)}, s32[32]{0:T(128)}, u32[]{:S(2)}) %copy-start.4) | copy-done | bytes 152
  6.1 0.0 copy-done.5
  6.1 1.2 %copy-done = bf16[128,16,256]{2,1,0:T(8,128)(2,1)S(1)} copy-done((bf16[128,16,256]{2,1,0:T(8,128)(2,1)S(1)}, bf16[128,16,256]{2,1,0:T(8,128)(2,1)}, u32[]{:S(2)}) %copy-start) | copy-done | bytes 1048600
  7.3 1.2 %copy-done.1 = bf16[128,16,256]{2,1,0:T(8,128)(2,1)S(1)} copy-done((bf16[128,16,256]{2,1,0:T(8,128)(2,1)S(1)}, bf16[128,16,256]{2,1,0:T(8,128)(2,1)}, u32[]{:S(2)}) %copy-start.1) | copy-done | bytes 1048600
  8.5 1.9 %decode_held_pages.1 = (bf16[128,256]{1,0:T(8,128)(2,1)S(1)}, f32[16,8,1]{2,1,0:T(8,128)S(1)}, f32[16,8,1]{2,1,0:T(8,128)S(1)}, f32[16,8,256]{2,1,0:T(8,128)S(1)}) custom-call(s32[1]{0:T(128)} %bitcast.own_ref, s32[32]{0:T(128)S(1)} %copy-done.4, s32[8]{0:T(128)S(1)} %copy-done.5, bf16[8,2048]{1,0:T(8,128)(2,1)S(1)} %copy-done.3, s32[8,32]{1,0:T(8,128)S(1)} %copy-done.2, ...), custom_call_target="tpu_custom_call" | custom-call | flops 268435456 | bytes 2097152 | tf_op jit(solution)/shard_map/decode_held_pages/pallas_call | solution.py:456
  10.4 2.4 %own_shard.1 = (bf16[2,256,1024]{2,1,0:T(8,128)(2,1)S(1)}, bf16[3,128,128]{2,1,0:T(8,128)(2,1)S(1)}, bf16[3,256,128]{2,1,0:T(8,128)(2,1)S(1)}, bf16[32,128]{1,0:...) custom-call(s32[1]{0:T(128)} %bitcast.own_ref, ...), custom_call_target="tpu_custom_call" | custom-call | flops 402653184 | bytes 1048576 | tf_op jit(solution)/shard_map/own_shard/pallas_call | solution.py:435
  12.8 2.1 %collective-permute-start.1 = (bf16[768,256]{1,0:T(8,128)(2,1)S(1)}, bf16[768,256]{1,0:T(8,128)(2,1)S(1)}, u32[]{:S(2)}, u32[]{:S(2)}) collective-permute-start(bf16[768,256]{1,0:T(8,128)(2,1)S(1)} %pad_maximum_fusion.shard_ref.rest_ref), channel_id=1, source_target_pairs={{0,12},{4,0},{8,4},{12,8},{1,13},{5,1},{9,5},{13,9},{2,14},{6,2},{... | collective-permute-start | bytes 1179656 | tf_op jit(solution)/shard_map/ppermute | solution.py:412
  14.9 1.1 %collective-permute-done.refs_0_.shard_ref = bf16[768,256]{1,0:T(8,128)(2,1)S(1)} collective-permute-done((bf16[768,256]{1,0:T(8,128)(2,1)S(1)}, bf16[768,256]{1,0:T(8,128)(2,1)S(1)}, u32[]{:S(2)}, u32[]{:S(2)}) %collective-permute-start) | collective-permute-done | bytes 393248 | tf_op jit(solution)/shard_map/ppermute | solution.py:412
  16.0 0.1 pieces_to_send_on.1
  16.1 0.1 collective-permute-start.2
  16.2 0.7 %collective-permute-start.3 = (bf16[256,256]{1,0:T(8,128)(2,1)S(1)}, bf16[256,256]{1,0:T(8,128)(2,1)S(1)}, u32[]{:S(2)}, u32[]{:S(2)}) collective-permute-start(bf16[256,256]{1,0:T(8,128)(2,1)S(1)} %get-tuple-element.103), channel_id=1, source_target_pairs={{4,8},{8,12},{5,9},{9,13},{6,10},{10,14},{7,11},{11,15},{20,24},{2... | collective-permute-start | bytes 393224 | tf_op jit(solution)/shard_map/ppermute | solution.py:493
  16.9 4.0 %collective-permute-start.4 = (bf16[256,256]{1,0:T(8,128)(2,1)S(1)}, bf16[256,256]{1,0:T(8,128)(2,1)S(1)}, u32[]{:S(2)}, u32[]{:S(2)}) collective-permute-start(bf16[256,256]{1,0:T(8,128)(2,1)S(1)} %get-tuple-element.107), channel_id=1, source_target_pairs={{0,4},{4,8},{8,12},{12,0},{1,5},{5,9},{9,13},{13,1},{2,6},{6,10},{... | collective-permute-start | bytes 393224 | tf_op jit(solution)/shard_map/ppermute | solution.py:412
  20.9 4.1 %collective-permute-start.5 = (bf16[64,256]{1,0:T(8,128)(2,1)S(1)}, bf16[64,256]{1,0:T(8,128)(2,1)S(1)}, u32[]{:S(2)}, u32[]{:S(2)}) collective-permute-start(bf16[64,256]{1,0:T(8,128)(2,1)S(1)} %get-tuple-element.112), channel_id=1, source_target_pairs={{0,4},{12,0},{1,5},{13,1},{2,6},{14,2},{3,7},{15,3},{16,20},{28,16... | collective-permute-start | bytes 98312 | tf_op jit(solution)/shard_map/ppermute | solution.py:494
  25.0 1.7 %whole_shards_0.1 = (f32[2,1,1024]{2,1,0:T(1,128)S(1)}, f32[2,1,1024]{2,1,0:T(1,128)S(1)}, f32[2,128,1024]{2,1,0:T(8,128)S(1)}) custom-call(bf16[2,256,1024]{2,1,0:T(8,128)(2,1)S(1)} %get-tuple-element.59.qt_ref, bf16[3,128,128]{2,1,0:T(8,128)(2,1)S(1)} %get-tuple-element.60.near_ref, bf16[3,256,128]{2,1,0:T(8,128)(2,1)S(1)} %get-tuple-element.61.far_ref, ...), custom_call_target="tpu_custom_call" | custom-call | flops 402653184 | bytes 1048576 | tf_op jit(solution)/shard_map/whole_shards_0/pallas_call | solution.py:499
  26.7 1.7 %whole_shards_1.1 = (f32[2,1,1024]{2,1,0:T(1,128)S(1)}, f32[2,1,1024]{2,1,0:T(1,128)S(1)}, f32[2,128,1024]{2,1,0:T(8,128)S(1)}) custom-call(bf16[2,256,1024]{2,1,0:T(8,128)(2,1)S(1)} %get-tuple-element.59.qt_ref, bf16[3,128,128]{2,1,0:T(8,128)(2,1)S(1)} %get-tuple-element.60.near_ref, bf16[3,256,128]{2,1,0:T(8,128)(2,1)S(1)} %get-tuple-element.61.far_ref, ...), custom_call_target="tpu_custom_call" | custom-call | flops 402653184 | bytes 1048576 | tf_op jit(solution)/shard_map/whole_shards_1/pallas_call | solution.py:499
  28.5 1.1 %decode_near_pages.1 = (f32[16,8,1]{2,1,0:T(8,128)S(1)}, f32[16,8,1]{2,1,0:T(8,128)S(1)}, f32[16,8,256]{2,1,0:T(8,128)S(1)}) custom-call(s32[1]{0:T(128)} %bitcast.own_ref, s32[32]{0:T(128)S(1)} %copy-done.4, s32[8]{0:T(128)S(1)} %copy-done.5, s32[8,32]{1,0:T(8,128)S(1)} %copy-done.2, bf16[768,256]{1,0:T(8,128)(2,1)S(1)} %collective-permute-done.refs_0_.shard_ref, ...), custom_call_target="tpu_custom_call" | custom-call | flops 134217728 | bytes 1048576 | tf_op jit(solution)/shard_map/decode_near_pages/pallas_call | solution.py:512
  29.6 0.2 collective-permute-done.2.keys_ref
  29.7 1.6 %last_scores.1 = (bf16[2,256,1024]{2,1,0:T(8,128)(2,1)S(1)}, f32[2,1,1024]{2,1,0:T(1,128)S(1)}, f32[2,128,1024]{2,1,0:T(8,128)S(1)}) custom-call(bf16[2,256,1024]{2,1,0:T(8,128)(2,1)S(1)} %get-tuple-element.59.qt_ref, bf16[3,128,128]{2,1,0:T(8,128)(2,1)S(1)} %get-tuple-element.60.near_ref, bf16[3,256,128]{2,1,0:T(8,128)(2,1)S(1)} %get-tuple-element.61.far_ref, ...), custom_call_target="tpu_custom_call" | custom-call | flops 402653184 | bytes 1048576 | tf_op jit(solution)/shard_map/last_scores/pallas_call | solution.py:526
  31.3 0.1 collective-permute-done.4.values_ref
  31.4 1.1 %last_values.1 = bf16[128,2048]{1,0:T(8,128)(2,1)} custom-call(bf16[2,256,1024]{2,1,0:T(8,128)(2,1)S(1)} %get-tuple-element.104.weights_ref, f32[2,1,1024]{2,1,0:T(1,128)S(1)} %get-tuple-element.105.total_ref, f32[2,128,1024]{2,1,0:T(8,128)S(1)} %get-tuple-element.106.accum_ref, bf16[256,256]{1,0:T(8,128)(2,1)S(1)} %collective-permute-done.4.values_ref), custom_call_target="tpu_custom_call" | custom-call | flops 134217728 | bytes 1048576 | tf_op jit(solution)/shard_map/last_values/pallas_call | solution.py:536
  32.6 1.7 %decode_last_pages.1 = bf16[8,2048]{1,0:T(8,128)(2,1)} custom-call(s32[1]{0:T(128)} %bitcast.own_ref, s32[32]{0:T(128)S(1)} %copy-done.4, s32[8]{0:T(128)S(1)} %copy-done.5, s32[8,32]{1,0:T(8,128)S(1)} %copy-done.2, bf16[256,256]{1,0:T(8,128)(2,1)S(1)} %collective-permute-done.3.stretch_ref, bf16[64,256]{1,0:T(8,128)(2,1)S(1)} %collective-permute-done.5.pages_ref, ...), custom_call_target="tpu_custom_call" | custom-call | flops 67108864 | bytes 1048576 | tf_op jit(solution)/shard_map/decode_last_pages/pallas_call | solution.py:551
  (12 shorter events, 0.0 us)
Async XLA Ops:
  0.6 4.8 %copy-start.3 = (bf16[8,2048]{1,0:T(8,128)(2,1)S(1)}, bf16[8,2048]{1,0:T(8,128)(2,1)}, u32[]{:S(2)}) copy-start(bf16[8,2048]{1,0:T(8,128)(2,1)} %q_ref.3) | copy-start | bytes 98308
  1.7 14.3 %collective-permute-start = (bf16[768,256]{1,0:T(8,128)(2,1)S(1)}, bf16[768,256]{1,0:T(8,128)(2,1)S(1)}, u32[]{:S(2)}, u32[]{:S(2)}) collective-permute-start(bf16[768,256]{1,0:T(8,128)(2,1)S(1)} %pad_maximum_fusion.shard_ref.rest_ref), channel_id=1, source_target_pairs={{0,4},{4,8},{8,12},{12,0},{1,5},{5,9},{9,13},{13,1},{2,6},{6,10},{... | collective-permute-start | bytes 1179656 | tf_op jit(solution)/shard_map/ppermute | solution.py:412
  4.8 0.7 %copy-start.2 = (s32[8,32]{1,0:T(8,128)S(1)}, s32[8,32]{1,0:T(8,128)}, u32[]{:S(2)}) copy-start(s32[8,32]{1,0:T(8,128)} %lists_ref.5) | copy-start | bytes 3076
  5.4 0.7 %copy-start.4 = (s32[32]{0:T(128)S(1)}, s32[32]{0:T(128)}, u32[]{:S(2)}) copy-start(s32[32]{0:T(128)} %targets_ref.7) | copy-start | bytes 388
  5.4 0.7 %copy-start.5 = (s32[8]{0:T(128)S(1)}, s32[8]{0:T(128)}, u32[]{:S(2)}) copy-start(s32[8]{0:T(128)} %length_ref.5) | copy-start | bytes 100
  6.1 1.2 %copy-start = (bf16[128,16,256]{2,1,0:T(8,128)(2,1)S(1)}, bf16[128,16,256]{2,1,0:T(8,128)(2,1)}, u32[]{:S(2)}) copy-start(bf16[128,16,256]{2,1,0:T(8,128)(2,1)} %pool_k.1) | copy-start | bytes 3145732
  7.3 1.2 %copy-start.1 = (bf16[128,16,256]{2,1,0:T(8,128)(2,1)S(1)}, bf16[128,16,256]{2,1,0:T(8,128)(2,1)}, u32[]{:S(2)}) copy-start(bf16[128,16,256]{2,1,0:T(8,128)(2,1)} %pool_v.1) | copy-start | bytes 3145732
  8.5 1.9 %copy-start.6 = (bf16[128,2048]{1,0:T(8,128)(2,1)S(1)}, bf16[128,2048]{1,0:T(8,128)(2,1)}, u32[]{:S(2)}) copy-start(bf16[128,2048]{1,0:T(8,128)(2,1)} %q_ref.2) | copy-start | bytes 1572868
  12.8 13.9 %collective-permute-start.1 = (bf16[768,256]{1,0:T(8,128)(2,1)S(1)}, bf16[768,256]{1,0:T(8,128)(2,1)S(1)}, u32[]{:S(2)}, u32[]{:S(2)}) collective-permute-start(bf16[768,256]{1,0:T(8,128)(2,1)S(1)} %pad_maximum_fusion.shard_ref.rest_ref), channel_id=1, source_target_pairs={{0,12},{4,0},{8,4},{12,8},{1,13},{5,1},{9,5},{13,9},{2,14},{6,2},{... | collective-permute-start | bytes 1179656 | tf_op jit(solution)/shard_map/ppermute | solution.py:412
  16.1 13.6 %collective-permute-start.2 = (bf16[256,256]{1,0:T(8,128)(2,1)S(1)}, bf16[256,256]{1,0:T(8,128)(2,1)S(1)}, u32[]{:S(2)}, u32[]{:S(2)}) collective-permute-start(bf16[256,256]{1,0:T(8,128)(2,1)S(1)} %get-tuple-element.102), channel_id=1, source_target_pairs={{0,4},{4,8},{8,12},{12,0},{1,5},{5,9},{9,13},{13,1},{2,6},{6,10},{... | collective-permute-start | bytes 393224 | tf_op jit(solution)/shard_map/ppermute | solution.py:412
  16.2 13.5 %collective-permute-start.3 = (bf16[256,256]{1,0:T(8,128)(2,1)S(1)}, bf16[256,256]{1,0:T(8,128)(2,1)S(1)}, u32[]{:S(2)}, u32[]{:S(2)}) collective-permute-start(bf16[256,256]{1,0:T(8,128)(2,1)S(1)} %get-tuple-element.103), channel_id=1, source_target_pairs={{4,8},{8,12},{5,9},{9,13},{6,10},{10,14},{7,11},{11,15},{20,24},{2... | collective-permute-start | bytes 393224 | tf_op jit(solution)/shard_map/ppermute | solution.py:493
  16.9 14.6 %collective-permute-start.4 = (bf16[256,256]{1,0:T(8,128)(2,1)S(1)}, bf16[256,256]{1,0:T(8,128)(2,1)S(1)}, u32[]{:S(2)}, u32[]{:S(2)}) collective-permute-start(bf16[256,256]{1,0:T(8,128)(2,1)S(1)} %get-tuple-element.107), channel_id=1, source_target_pairs={{0,4},{4,8},{8,12},{12,0},{1,5},{5,9},{9,13},{13,1},{2,6},{6,10},{... | collective-permute-start | bytes 393224 | tf_op jit(solution)/shard_map/ppermute | solution.py:412
  20.9 11.7 %collective-permute-start.5 = (bf16[64,256]{1,0:T(8,128)(2,1)S(1)}, bf16[64,256]{1,0:T(8,128)(2,1)S(1)}, u32[]{:S(2)}, u32[]{:S(2)}) collective-permute-start(bf16[64,256]{1,0:T(8,128)(2,1)S(1)} %get-tuple-element.112), channel_id=1, source_target_pairs={{0,4},{12,0},{1,5},{13,1},{2,6},{14,2},{3,7},{15,3},{16,20},{28,16... | collective-permute-start | bytes 98312 | tf_op jit(solution)/shard_map/ppermute | solution.py:494

commit v14 on v13

--- a/solution.py
+++ b/solution.py
@@ -283,8 +283,8 @@
 
 
 def near_pages_kernel(count, hops, tokens, pool, own_ref, targets_ref, length_ref, lists_ref, *refs):
-    shard_refs, refs = refs[: len(hops)], refs[len(hops) :]
-    wide_ref, dec_high, dec_total, dec_mixed, high_ref, total_ref, mixed_ref = refs
+    shard_refs, refs = refs[: len(hops) - 1], refs[len(hops) - 1 :]
+    wide_ref, dec_high, dec_total, dec_mixed, high_ref, total_ref, mixed_ref, whole_ref, alone_ref = refs
     own = own_ref[0]
     lists = lists_ref[...]
     lengths = length_column(length_ref)
@@ -295,29 +295,12 @@
         parts.append((ref[:tokens], ref[half : half + tokens], tally_of(lists, lengths, slot)))
     state = (dec_high[...], dec_total[...], dec_mixed[...])
     high_ref[...], total_ref[...], mixed_ref[...] = decode_attend(wide_ref[...], parts, state)
-
-
-def last_pages_kernel(
-    count, hop, pool, own_ref, targets_ref, length_ref, lists_ref, stretch_ref, pages_ref,
-    wide_ref, dec_high, dec_total, dec_mixed, dec_out,
-):
-    own = own_ref[0]
-    tokens = stretch_ref.shape[0] // 2
-    sent = pages_ref.shape[0] // 2
-    lists = lists_ref[...]
-    lengths = length_column(length_ref)
-    shard = shard_of(own, hop, count)
+    shard = shard_of(own, hops[-1], count)
     attended = shard < own
     whole = jnp.where(attended, slot_row(targets_ref, shard, own, tokens, pool), -1)
     alone = jnp.where(attended, -1, sent_slots(targets_ref, shard, own, tokens // PAGE, pool))
-    parts = [
-        (stretch_ref[:tokens], stretch_ref[tokens:], tally_of(lists, lengths, whole)),
-        (pages_ref[:sent], pages_ref[sent:], tally_of(lists, lengths, alone)),
-    ]
-    _, total, mixed = decode_attend(wide_ref[...], parts, (dec_high[...], dec_total[...], dec_mixed[...]))
-    for head in range(dec_high.shape[0]):
-        piece = mixed[head, :, features(head // GROUP)] / total[head]
-        dec_out[:, features(head)] = piece.astype(jnp.bfloat16)
+    whole_ref[...] = tally_of(lists, lengths, whole)
+    alone_ref[...] = tally_of(lists, lengths, alone)
 
 
 def score_kernel(
@@ -346,8 +329,20 @@
     walk(blocks_of(qt_ref), lambda block: scores_of(qt_ref, block[0], block[1], keys[block[0]]), second)
 
 
-def last_kernel(weights_ref, total_ref, accum_ref, values_ref, out_ref, result_ref, sems):
+def last_kernel(
+    weights_ref, total_ref, accum_ref, values_ref, stretch_ref, pages_ref, whole_ref, alone_ref,
+    wide_ref, dec_high, dec_total, dec_mixed, out_ref, dec_out, result_ref, sems,
+):
     tokens = result_ref.shape[0]
+    sent = pages_ref.shape[0] // 2
+    parts = [
+        (stretch_ref[:tokens], stretch_ref[tokens:], whole_ref[...]),
+        (pages_ref[:sent], pages_ref[sent:], alone_ref[...]),
+    ]
+    _, total, mixed = decode_attend(wide_ref[...], parts, (dec_high[...], dec_total[...], dec_mixed[...]))
+    for head in range(dec_high.shape[0]):
+        piece = mixed[head, :, features(head // GROUP)] / total[head]
+        dec_out[:, features(head)] = piece.astype(jnp.bfloat16)
     values_t = [values_ref[:, features(head)].T for head in range(weights_ref.shape[0])]
     copies = []
 
@@ -509,11 +504,12 @@
     final = len(hops) - 1
     dec_state, state = lax.optimization_barrier((dec_state, state))
     near_hops = hops[:-1]
-    dec_state = pl.pallas_call(
-        functools.partial(near_pages_kernel, count, near_hops, tokens, pool),
-        out_shape=dec_shapes,
+    *dec_state, whole, alone = pl.pallas_call(
+        functools.partial(near_pages_kernel, count, hops, tokens, pool),
+        out_shape=dec_shapes
+        + (shape((1, dec_rows, tokens), f32), shape((1, dec_rows, SEND_CAP * PAGE), f32)),
         in_specs=[SMEM] * 3 + [VMEM] * (5 + len(near_hops)),
-        out_specs=(VMEM,) * 3,
+        out_specs=(VMEM,) * 5,
         compiler_params=params,
         cost_estimate=cost(tokens),
         name="decode_near_pages",
@@ -533,32 +529,19 @@
         name="last_scores",
     )(qt, near, far, *state, last_keys, last_stretch)
 
-    prefill = pl.pallas_call(
+    prefill, decoded = pl.pallas_call(
         last_kernel,
-        out_shape=shape((tokens, width), bf16),
-        in_specs=[VMEM] * 4,
-        out_specs=HBM,
+        out_shape=(shape((tokens, width), bf16), shape(decode_queries.shape, bf16)),
+        in_specs=[VMEM] * 12,
+        out_specs=(HBM, VMEM),
         scratch_shapes=[
             pltpu.VMEM((tokens, width), bf16),
             pltpu.SemaphoreType.DMA((kv_local * max(GROUP // 2, 1),)),
         ],
         compiler_params=params,
         cost_estimate=cost(c_rows // 2),
-        name="last_values",
-    )(weights, total, accum, last_values)
-
-    prefill, dec_state = lax.optimization_barrier((prefill, dec_state))
-    decoded = pl.pallas_call(
-        functools.partial(last_pages_kernel, count, hops[-1], pool),
-        out_shape=shape(decode_queries.shape, bf16),
-        in_specs=[SMEM] * 3 + [VMEM] * 7,
-        out_specs=VMEM,
-        compiler_params=params,
-        cost_estimate=cost(tokens // 2),
-        name="decode_last_pages",
-    )(
-        own_array, page_targets, context_length, page_lists, last_stretch, last_pages, wide, *dec_state
-    )
+        name="last_values_and_pages",
+    )(weights, total, accum, last_values, last_stretch, last_pages, whole, alone, wide, *dec_state)
     return (prefill, decoded)
 
 

time: 34.6 us -> 34.3 us (level)
  Pallas kernels: 13.3 us -> 12.8 us
  waiting for transfers between devices: 1.35 us -> 1.7 us
    pallas_call x3 -> x2, Pallas kernels: 3.9 us -> 3.33 us  [the longest x1 2.26 us: per_device(): pl.pallas_call(last_kernel, out_shape=(shape((tokens, width), bf16), shap...]
    ppermute x1, waiting for transfers between devices: 0.01 us -> 0.43 us  [per_device(): last_pages = lax.ppermute(pieces[3], 'ctx', others)]
  transfers between devices with their start and end apart: 6 -> 6, of which waited for: 3 -> 3; matrix products, arithmetic and copies ran while one was open for 0% -> 0% of each run, Pallas kernels for 34% -> 31%
where the time goes in v14:
time: 34.3 us; the launch traced here: 34 us
  starting transfers between devices  14 us (41%)
  Pallas kernels  12.8 us (37%)
  local copies, waits for them, and re-layouts  3.1 us (9%)
  waiting for transfers between devices  1.7 us (5%)
  between operations  1.43 us (4%)
  other arithmetic  1.03 us (3%)
    ppermute x4, starting transfers between devices, send(): return lax.ppermute(array, 'ctx', up_pairs if hop < 0 else down_pairs)  9.28 us
    ppermute x1, starting transfers between devices, per_device(): last_pages = lax.ppermute(pieces[3], 'ctx', others)  4.07 us
    pallas_call x2, Pallas kernels, per_device(): pl.pallas_call(functools.partial(hop_kernel, places), out_shape=state_sha...  3.46 us
    unnamed x14, local copies, waits for them, and re-layouts  3.1 us
    pallas_call x1, Pallas kernels, per_device(): pl.pallas_call(functools.partial(own_kernel, count, hops), out_shape=(sha...  2.36 us
    pallas_call x1, Pallas kernels, per_device(): pl.pallas_call(last_kernel, out_shape=(shape((tokens, width), bf16), shap...  2.26 us
    pallas_call x1, Pallas kernels, per_device(): pl.pallas_call(held_kernel, out_shape=(shape((heads * dec_rows, kv_width)...  1.86 us
    pallas_call x1, Pallas kernels, per_device(): pl.pallas_call(functools.partial(score_kernel, final), out_shape=(shape((...  1.6 us
  transfers between devices with their start and end apart: 6, of which 3 were waited for; matrix products, arithmetic and copies ran while one was open for 0% of the time, Pallas kernels for 31%

profile of v14, /device:TPU:0, one launch (start us, length us, event | category | flops | bytes accessed | tf_op | source)
XLA Modules:
  0.0 34.0 jit_solution(2030533259124028655)
XLA Ops:
  0.6 1.0 %pad_maximum_fusion.shard_ref.rest_ref = bf16[768,256]{1,0:T(8,128)(2,1)S(1)} fusion(bf16[256,256]{1,0:T(8,128)(2,1)} %param.16, bf16[128,256]{1,0:T(8,128)(2,1)} %param.14, bf16[256,256]{1,0:T(8,128)(2,1)} %param.15, bf16[128,256]{1,0:T(8,128)(2,1)} %param.13), kind=kLoop, calls=%fused_computation | loop fusion | flops 1572864 | bytes 786432 | tf_op jit(solution)/shard_map/max | solution.py:422
  1.7 3.1 %collective-permute-start = (bf16[768,256]{1,0:T(8,128)(2,1)S(1)}, bf16[768,256]{1,0:T(8,128)(2,1)S(1)}, u32[]{:S(2)}, u32[]{:S(2)}) collective-permute-start(bf16[768,256]{1,0:T(8,128)(2,1)S(1)} %pad_maximum_fusion.shard_ref.rest_ref), channel_id=1, source_target_pairs={{0,4},{4,8},{8,12},{12,0},{1,5},{5,9},{9,13},{13,1},{2,6},{6,10},{... | collective-permute-start | bytes 1179656 | tf_op jit(solution)/shard_map/ppermute | solution.py:407
  5.4 0.0 copy-start.4
  5.4 0.0 copy-start.5
  5.5 0.6 %copy-done.4 = s32[32]{0:T(128)S(1)} copy-done((s32[32]{0:T(128)S(1)}, s32[32]{0:T(128)}, u32[]{:S(2)}) %copy-start.4) | copy-done | bytes 152
  6.1 0.0 copy-done.5
  6.1 1.2 %copy-done = bf16[128,16,256]{2,1,0:T(8,128)(2,1)S(1)} copy-done((bf16[128,16,256]{2,1,0:T(8,128)(2,1)S(1)}, bf16[128,16,256]{2,1,0:T(8,128)(2,1)}, u32[]{:S(2)}) %copy-start) | copy-done | bytes 1048600
  7.3 1.2 %copy-done.1 = bf16[128,16,256]{2,1,0:T(8,128)(2,1)S(1)} copy-done((bf16[128,16,256]{2,1,0:T(8,128)(2,1)S(1)}, bf16[128,16,256]{2,1,0:T(8,128)(2,1)}, u32[]{:S(2)}) %copy-start.1) | copy-done | bytes 1048600
  8.5 1.9 %decode_held_pages.1 = (bf16[128,256]{1,0:T(8,128)(2,1)S(1)}, f32[16,8,1]{2,1,0:T(8,128)S(1)}, f32[16,8,1]{2,1,0:T(8,128)S(1)}, f32[16,8,256]{2,1,0:T(8,128)S(1)}) custom-call(s32[1]{0:T(128)} %bitcast.own_ref, s32[32]{0:T(128)S(1)} %copy-done.4, s32[8]{0:T(128)S(1)} %copy-done.5, bf16[8,2048]{1,0:T(8,128)(2,1)S(1)} %copy-done.2, s32[8,32]{1,0:T(8,128)S(1)} %copy-done.3, ...), custom_call_target="tpu_custom_call" | custom-call | flops 268435456 | bytes 2097152 | tf_op jit(solution)/shard_map/decode_held_pages/pallas_call | solution.py:451
  10.4 2.4 %own_shard.1 = (bf16[2,256,1024]{2,1,0:T(8,128)(2,1)S(1)}, bf16[3,128,128]{2,1,0:T(8,128)(2,1)S(1)}, bf16[3,256,128]{2,1,0:T(8,128)(2,1)S(1)}, bf16[32,128]{1,0:...) custom-call(s32[1]{0:T(128)} %bitcast.own_ref, ...), custom_call_target="tpu_custom_call" | custom-call | flops 402653184 | bytes 1048576 | tf_op jit(solution)/shard_map/own_shard/pallas_call | solution.py:430
  12.8 2.1 %collective-permute-start.1 = (bf16[768,256]{1,0:T(8,128)(2,1)S(1)}, bf16[768,256]{1,0:T(8,128)(2,1)S(1)}, u32[]{:S(2)}, u32[]{:S(2)}) collective-permute-start(bf16[768,256]{1,0:T(8,128)(2,1)S(1)} %pad_maximum_fusion.shard_ref.rest_ref), channel_id=1, source_target_pairs={{0,12},{4,0},{8,4},{12,8},{1,13},{5,1},{9,5},{13,9},{2,14},{6,2},{... | collective-permute-start | bytes 1179656 | tf_op jit(solution)/shard_map/ppermute | solution.py:407
  14.9 1.1 %collective-permute-done.refs_0_.shard_ref = bf16[768,256]{1,0:T(8,128)(2,1)S(1)} collective-permute-done((bf16[768,256]{1,0:T(8,128)(2,1)S(1)}, bf16[768,256]{1,0:T(8,128)(2,1)S(1)}, u32[]{:S(2)}, u32[]{:S(2)}) %collective-permute-start) | collective-permute-done | bytes 393248 | tf_op jit(solution)/shard_map/ppermute | solution.py:407
  16.0 0.1 pieces_to_send_on.1
  16.1 0.1 collective-permute-start.2
  16.2 0.7 %collective-permute-start.3 = (bf16[256,256]{1,0:T(8,128)(2,1)S(1)}, bf16[256,256]{1,0:T(8,128)(2,1)S(1)}, u32[]{:S(2)}, u32[]{:S(2)}) collective-permute-start(bf16[256,256]{1,0:T(8,128)(2,1)S(1)} %get-tuple-element.101), channel_id=1, source_target_pairs={{4,8},{8,12},{5,9},{9,13},{6,10},{10,14},{7,11},{11,15},{20,24},{2... | collective-permute-start | bytes 393224 | tf_op jit(solution)/shard_map/ppermute | solution.py:488
  16.9 4.0 %collective-permute-start.4 = (bf16[256,256]{1,0:T(8,128)(2,1)S(1)}, bf16[256,256]{1,0:T(8,128)(2,1)S(1)}, u32[]{:S(2)}, u32[]{:S(2)}) collective-permute-start(bf16[256,256]{1,0:T(8,128)(2,1)S(1)} %get-tuple-element.105), channel_id=1, source_target_pairs={{0,4},{4,8},{8,12},{12,0},{1,5},{5,9},{9,13},{13,1},{2,6},{6,10},{... | collective-permute-start | bytes 393224 | tf_op jit(solution)/shard_map/ppermute | solution.py:407
  20.9 4.1 %collective-permute-start.5 = (bf16[64,256]{1,0:T(8,128)(2,1)S(1)}, bf16[64,256]{1,0:T(8,128)(2,1)S(1)}, u32[]{:S(2)}, u32[]{:S(2)}) collective-permute-start(bf16[64,256]{1,0:T(8,128)(2,1)S(1)} %get-tuple-element.106), channel_id=1, source_target_pairs={{0,4},{12,0},{1,5},{13,1},{2,6},{14,2},{3,7},{15,3},{16,20},{28,16... | collective-permute-start | bytes 98312 | tf_op jit(solution)/shard_map/ppermute | solution.py:489
  25.0 1.7 %whole_shards_0.1 = (f32[2,1,1024]{2,1,0:T(1,128)S(1)}, f32[2,1,1024]{2,1,0:T(1,128)S(1)}, f32[2,128,1024]{2,1,0:T(8,128)S(1)}) custom-call(bf16[2,256,1024]{2,1,0:T(8,128)(2,1)S(1)} %get-tuple-element.57.qt_ref, bf16[3,128,128]{2,1,0:T(8,128)(2,1)S(1)} %get-tuple-element.58.near_ref, bf16[3,256,128]{2,1,0:T(8,128)(2,1)S(1)} %get-tuple-element.59.far_ref, ...), custom_call_target="tpu_custom_call" | custom-call | flops 402653184 | bytes 1048576 | tf_op jit(solution)/shard_map/whole_shards_0/pallas_call | solution.py:494
  26.7 1.7 %whole_shards_1.1 = (f32[2,1,1024]{2,1,0:T(1,128)S(1)}, f32[2,1,1024]{2,1,0:T(1,128)S(1)}, f32[2,128,1024]{2,1,0:T(8,128)S(1)}) custom-call(bf16[2,256,1024]{2,1,0:T(8,128)(2,1)S(1)} %get-tuple-element.57.qt_ref, bf16[3,128,128]{2,1,0:T(8,128)(2,1)S(1)} %get-tuple-element.58.near_ref, bf16[3,256,128]{2,1,0:T(8,128)(2,1)S(1)} %get-tuple-element.59.far_ref, ...), custom_call_target="tpu_custom_call" | custom-call | flops 402653184 | bytes 1048576 | tf_op jit(solution)/shard_map/whole_shards_1/pallas_call | solution.py:494
  28.5 1.1 %decode_near_pages.1 = (f32[16,8,1]{2,1,0:T(8,128)S(1)}, f32[16,8,1]{2,1,0:T(8,128)S(1)}, f32[16,8,256]{2,1,0:T(8,128)S(1)}, f32[1,8,128]{2,1,0:T(8,128)S(1)}, f32[1,8,32]{2,1,0:T(8,128)S(1)}) custom-call(s32[1]{0:T(128)} %bitcast.own_ref, s32[32]{0:T(128)S(1)} %copy-done.4, s32[8]{0:T(128)S(1)} %copy-done.5, s32[8,32]{1,0:T(8,128)S(1)} %copy-done.3, ...), custom_call_target="tpu_custom_call" | custom-call | flops 134217728 | bytes 1048576 | tf_op jit(solution)/shard_map/decode_near_pages/pallas_call | solution.py:507
  29.6 0.2 collective-permute-done.2.keys_ref
  29.7 1.6 %last_scores.1 = (bf16[2,256,1024]{2,1,0:T(8,128)(2,1)S(1)}, f32[2,1,1024]{2,1,0:T(1,128)S(1)}, f32[2,128,1024]{2,1,0:T(8,128)S(1)}) custom-call(bf16[2,256,1024]{2,1,0:T(8,128)(2,1)S(1)} %get-tuple-element.57.qt_ref, bf16[3,128,128]{2,1,0:T(8,128)(2,1)S(1)} %get-tuple-element.58.near_ref, bf16[3,256,128]{2,1,0:T(8,128)(2,1)S(1)} %get-tuple-element.59.far_ref, ...), custom_call_target="tpu_custom_call" | custom-call | flops 402653184 | bytes 1048576 | tf_op jit(solution)/shard_map/last_scores/pallas_call | solution.py:522
  31.3 0.4 %collective-permute-done.5.pages_ref = bf16[64,256]{1,0:T(8,128)(2,1)S(1)} collective-permute-done((bf16[64,256]{1,0:T(8,128)(2,1)S(1)}, bf16[64,256]{1,0:T(8,128)(2,1)S(1)}, u32[]{:S(2)}, u32[]{:S(2)}) %collective-permute-start.5) | collective-permute-done | bytes 32800 | tf_op jit(solution)/shard_map/ppermute | solution.py:489
  31.8 2.3 %last_values_and_pages.1 = (bf16[128,2048]{1,0:T(8,128)(2,1)}, bf16[8,2048]{1,0:T(8,128)(2,1)}) custom-call(bf16[2,256,1024]{2,1,0:T(8,128)(2,1)S(1)} %get-tuple-element.102.weights_ref, f32[2,1,1024]{2,1,0:T(1,128)S(1)} %get-tuple-element.103.total_ref, f32[2,128,1024]{2,1,0:T(8,128)S(1)} %get-tuple-element.104.accum_ref, ...), custom_call_target="tpu_custom_call" | custom-call | flops 134217728 | bytes 1048576 | tf_op jit(solution)/shard_map/last_values_and_pages/pallas_call | solution.py:532
  (11 shorter events, 0.0 us)
Async XLA Ops:
  0.6 4.8 %copy-start.2 = (bf16[8,2048]{1,0:T(8,128)(2,1)S(1)}, bf16[8,2048]{1,0:T(8,128)(2,1)}, u32[]{:S(2)}) copy-start(bf16[8,2048]{1,0:T(8,128)(2,1)} %q_ref.3) | copy-start | bytes 98308
  1.7 14.3 %collective-permute-start = (bf16[768,256]{1,0:T(8,128)(2,1)S(1)}, bf16[768,256]{1,0:T(8,128)(2,1)S(1)}, u32[]{:S(2)}, u32[]{:S(2)}) collective-permute-start(bf16[768,256]{1,0:T(8,128)(2,1)S(1)} %pad_maximum_fusion.shard_ref.rest_ref), channel_id=1, source_target_pairs={{0,4},{4,8},{8,12},{12,0},{1,5},{5,9},{9,13},{13,1},{2,6},{6,10},{... | collective-permute-start | bytes 1179656 | tf_op jit(solution)/shard_map/ppermute | solution.py:407
  4.8 0.7 %copy-start.3 = (s32[8,32]{1,0:T(8,128)S(1)}, s32[8,32]{1,0:T(8,128)}, u32[]{:S(2)}) copy-start(s32[8,32]{1,0:T(8,128)} %lists_ref.3) | copy-start | bytes 3076
  5.4 0.7 %copy-start.4 = (s32[32]{0:T(128)S(1)}, s32[32]{0:T(128)}, u32[]{:S(2)}) copy-start(s32[32]{0:T(128)} %targets_ref.5) | copy-start | bytes 388
  5.4 0.7 %copy-start.5 = (s32[8]{0:T(128)S(1)}, s32[8]{0:T(128)}, u32[]{:S(2)}) copy-start(s32[8]{0:T(128)} %length_ref.3) | copy-start | bytes 100
  6.1 1.2 %copy-start = (bf16[128,16,256]{2,1,0:T(8,128)(2,1)S(1)}, bf16[128,16,256]{2,1,0:T(8,128)(2,1)}, u32[]{:S(2)}) copy-start(bf16[128,16,256]{2,1,0:T(8,128)(2,1)} %pool_k.1) | copy-start | bytes 3145732
  7.3 1.2 %copy-start.1 = (bf16[128,16,256]{2,1,0:T(8,128)(2,1)S(1)}, bf16[128,16,256]{2,1,0:T(8,128)(2,1)}, u32[]{:S(2)}) copy-start(bf16[128,16,256]{2,1,0:T(8,128)(2,1)} %pool_v.1) | copy-start | bytes 3145732
  8.5 1.9 %copy-start.6 = (bf16[128,2048]{1,0:T(8,128)(2,1)S(1)}, bf16[128,2048]{1,0:T(8,128)(2,1)}, u32[]{:S(2)}) copy-start(bf16[128,2048]{1,0:T(8,128)(2,1)} %q_ref.2) | copy-start | bytes 1572868
  12.8 13.9 %collective-permute-start.1 = (bf16[768,256]{1,0:T(8,128)(2,1)S(1)}, bf16[768,256]{1,0:T(8,128)(2,1)S(1)}, u32[]{:S(2)}, u32[]{:S(2)}) collective-permute-start(bf16[768,256]{1,0:T(8,128)(2,1)S(1)} %pad_maximum_fusion.shard_ref.rest_ref), channel_id=1, source_target_pairs={{0,12},{4,0},{8,4},{12,8},{1,13},{5,1},{9,5},{13,9},{2,14},{6,2},{... | collective-permute-start | bytes 1179656 | tf_op jit(solution)/shard_map/ppermute | solution.py:407
  16.1 13.6 %collective-permute-start.2 = (bf16[256,256]{1,0:T(8,128)(2,1)S(1)}, bf16[256,256]{1,0:T(8,128)(2,1)S(1)}, u32[]{:S(2)}, u32[]{:S(2)}) collective-permute-start(bf16[256,256]{1,0:T(8,128)(2,1)S(1)} %get-tuple-element.100), channel_id=1, source_target_pairs={{0,4},{4,8},{8,12},{12,0},{1,5},{5,9},{9,13},{13,1},{2,6},{6,10},{... | collective-permute-start | bytes 393224 | tf_op jit(solution)/shard_map/ppermute | solution.py:407
  16.2 13.5 %collective-permute-start.3 = (bf16[256,256]{1,0:T(8,128)(2,1)S(1)}, bf16[256,256]{1,0:T(8,128)(2,1)S(1)}, u32[]{:S(2)}, u32[]{:S(2)}) collective-permute-start(bf16[256,256]{1,0:T(8,128)(2,1)S(1)} %get-tuple-element.101), channel_id=1, source_target_pairs={{4,8},{8,12},{5,9},{9,13},{6,10},{10,14},{7,11},{11,15},{20,24},{2... | collective-permute-start | bytes 393224 | tf_op jit(solution)/shard_map/ppermute | solution.py:488
  16.9 14.9 %collective-permute-start.4 = (bf16[256,256]{1,0:T(8,128)(2,1)S(1)}, bf16[256,256]{1,0:T(8,128)(2,1)S(1)}, u32[]{:S(2)}, u32[]{:S(2)}) collective-permute-start(bf16[256,256]{1,0:T(8,128)(2,1)S(1)} %get-tuple-element.105), channel_id=1, source_target_pairs={{0,4},{4,8},{8,12},{12,0},{1,5},{5,9},{9,13},{13,1},{2,6},{6,10},{... | collective-permute-start | bytes 393224 | tf_op jit(solution)/shard_map/ppermute | solution.py:407
  20.9 10.9 %collective-permute-start.5 = (bf16[64,256]{1,0:T(8,128)(2,1)S(1)}, bf16[64,256]{1,0:T(8,128)(2,1)S(1)}, u32[]{:S(2)}, u32[]{:S(2)}) collective-permute-start(bf16[64,256]{1,0:T(8,128)(2,1)S(1)} %get-tuple-element.106), channel_id=1, source_target_pairs={{0,4},{12,0},{1,5},{13,1},{2,6},{14,2},{3,7},{15,3},{16,20},{28,16... | collective-permute-start | bytes 98312 | tf_op jit(solution)/shard_map/ppermute | solution.py:489

commit v15 on v14

--- a/solution.py
+++ b/solution.py
@@ -284,7 +284,7 @@
 
 def near_pages_kernel(count, hops, tokens, pool, own_ref, targets_ref, length_ref, lists_ref, *refs):
     shard_refs, refs = refs[: len(hops) - 1], refs[len(hops) - 1 :]
-    wide_ref, dec_high, dec_total, dec_mixed, high_ref, total_ref, mixed_ref, whole_ref, alone_ref = refs
+    wide_ref, dec_high, dec_total, dec_mixed, high_ref, total_ref, mixed_ref, tally_ref = refs
     own = own_ref[0]
     lists = lists_ref[...]
     lengths = length_column(length_ref)
@@ -299,8 +299,8 @@
     attended = shard < own
     whole = jnp.where(attended, slot_row(targets_ref, shard, own, tokens, pool), -1)
     alone = jnp.where(attended, -1, sent_slots(targets_ref, shard, own, tokens // PAGE, pool))
-    whole_ref[...] = tally_of(lists, lengths, whole)
-    alone_ref[...] = tally_of(lists, lengths, alone)
+    tally_ref[:, :, :tokens] = tally_of(lists, lengths, whole)
+    tally_ref[:, :, tokens:] = tally_of(lists, lengths, alone)
 
 
 def score_kernel(
@@ -330,19 +330,10 @@
 
 
 def last_kernel(
-    weights_ref, total_ref, accum_ref, values_ref, stretch_ref, pages_ref, whole_ref, alone_ref,
+    weights_ref, total_ref, accum_ref, values_ref, stretch_ref, pages_ref, tally_ref,
     wide_ref, dec_high, dec_total, dec_mixed, out_ref, dec_out, result_ref, sems,
 ):
     tokens = result_ref.shape[0]
-    sent = pages_ref.shape[0] // 2
-    parts = [
-        (stretch_ref[:tokens], stretch_ref[tokens:], whole_ref[...]),
-        (pages_ref[:sent], pages_ref[sent:], alone_ref[...]),
-    ]
-    _, total, mixed = decode_attend(wide_ref[...], parts, (dec_high[...], dec_total[...], dec_mixed[...]))
-    for head in range(dec_high.shape[0]):
-        piece = mixed[head, :, features(head // GROUP)] / total[head]
-        dec_out[:, features(head)] = piece.astype(jnp.bfloat16)
     values_t = [values_ref[:, features(head)].T for head in range(weights_ref.shape[0])]
     copies = []
 
@@ -365,6 +356,16 @@
         copies.append(copy)
 
     walk(blocks_of(weights_ref), first, second)
+
+    sent = pages_ref.shape[0] // 2
+    keys = jnp.concatenate([stretch_ref[:tokens], pages_ref[:sent]], axis=0)
+    values = jnp.concatenate([stretch_ref[tokens:], pages_ref[sent:]], axis=0)
+    state = (dec_high[...], dec_total[...], dec_mixed[...])
+    _, total, mixed = decode_attend(wide_ref[...], [(keys, values, tally_ref[...])], state)
+    share = 1.0 / total
+    for head in range(dec_high.shape[0]):
+        piece = mixed[head, :, features(head // GROUP)] * share[head]
+        dec_out[:, features(head)] = piece.astype(jnp.bfloat16)
     for copy in copies:
         copy.wait()
 
@@ -504,12 +505,12 @@
     final = len(hops) - 1
     dec_state, state = lax.optimization_barrier((dec_state, state))
     near_hops = hops[:-1]
-    *dec_state, whole, alone = pl.pallas_call(
+    *dec_state, tally = pl.pallas_call(
         functools.partial(near_pages_kernel, count, hops, tokens, pool),
         out_shape=dec_shapes
-        + (shape((1, dec_rows, tokens), f32), shape((1, dec_rows, SEND_CAP * PAGE), f32)),
+        + (shape((1, dec_rows, tokens + SEND_CAP * PAGE), f32),),
         in_specs=[SMEM] * 3 + [VMEM] * (5 + len(near_hops)),
-        out_specs=(VMEM,) * 5,
+        out_specs=(VMEM,) * 4,
         compiler_params=params,
         cost_estimate=cost(tokens),
         name="decode_near_pages",
@@ -532,7 +533,7 @@
     prefill, decoded = pl.pallas_call(
         last_kernel,
         out_shape=(shape((tokens, width), bf16), shape(decode_queries.shape, bf16)),
-        in_specs=[VMEM] * 12,
+        in_specs=[VMEM] * 11,
         out_specs=(HBM, VMEM),
         scratch_shapes=[
             pltpu.VMEM((tokens, width), bf16),
@@ -541,7 +542,7 @@
         compiler_params=params,
         cost_estimate=cost(c_rows // 2),
         name="last_values_and_pages",
-    )(weights, total, accum, last_values, last_stretch, last_pages, whole, alone, wide, *dec_state)
+    )(weights, total, accum, last_values, last_stretch, last_pages, tally, wide, *dec_state)
     return (prefill, decoded)
 
 

time: 34.3 us -> 34 us (level)
  no operation moved by 1% of the time
where the time goes in v15:
time: 34 us; the launch traced here: 33.8 us
  starting transfers between devices  14 us (41%)
  Pallas kernels  12.5 us (37%)
  local copies, waits for them, and re-layouts  3.1 us (9%)
  waiting for transfers between devices  1.7 us (5%)
  between operations  1.43 us (4%)
  other arithmetic  1.03 us (3%)
    ppermute x4, starting transfers between devices, send(): return lax.ppermute(array, 'ctx', up_pairs if hop < 0 else down_pairs)  9.28 us
    ppermute x1, starting transfers between devices, per_device(): last_pages = lax.ppermute(pieces[3], 'ctx', others)  4.07 us
    pallas_call x2, Pallas kernels, per_device(): pl.pallas_call(functools.partial(hop_kernel, places), out_shape=state_sha...  3.46 us
    unnamed x14, local copies, waits for them, and re-layouts  3.1 us
    pallas_call x1, Pallas kernels, per_device(): pl.pallas_call(functools.partial(own_kernel, count, hops), out_shape=(sha...  2.36 us
    pallas_call x1, Pallas kernels, per_device(): pl.pallas_call(last_kernel, out_shape=(shape((tokens, width), bf16), shap...  1.97 us
    pallas_call x1, Pallas kernels, per_device(): pl.pallas_call(held_kernel, out_shape=(shape((heads * dec_rows, kv_width)...  1.86 us
    pallas_call x1, Pallas kernels, per_device(): pl.pallas_call(functools.partial(score_kernel, final), out_shape=(shape((...  1.6 us
  transfers between devices with their start and end apart: 6, of which 3 were waited for; matrix products, arithmetic and copies ran while one was open for 0% of the time, Pallas kernels for 31%

profile of v15, /device:TPU:0, one launch (start us, length us, event | category | flops | bytes accessed | tf_op | source)
XLA Modules:
  0.0 33.8 jit_solution(10543130081159562981)
XLA Ops:
  0.6 1.0 %pad_maximum_fusion.shard_ref.rest_ref = bf16[768,256]{1,0:T(8,128)(2,1)S(1)} fusion(bf16[256,256]{1,0:T(8,128)(2,1)} %param.16, bf16[128,256]{1,0:T(8,128)(2,1)} %param.14, bf16[256,256]{1,0:T(8,128)(2,1)} %param.15, bf16[128,256]{1,0:T(8,128)(2,1)} %param.13), kind=kLoop, calls=%fused_computation | loop fusion | flops 1572864 | bytes 786432 | tf_op jit(solution)/shard_map/max | solution.py:423
  1.7 3.1 %collective-permute-start = (bf16[768,256]{1,0:T(8,128)(2,1)S(1)}, bf16[768,256]{1,0:T(8,128)(2,1)S(1)}, u32[]{:S(2)}, u32[]{:S(2)}) collective-permute-start(bf16[768,256]{1,0:T(8,128)(2,1)S(1)} %pad_maximum_fusion.shard_ref.rest_ref), channel_id=1, source_target_pairs={{0,4},{4,8},{8,12},{12,0},{1,5},{5,9},{9,13},{13,1},{2,6},{6,10},{... | collective-permute-start | bytes 1179656 | tf_op jit(solution)/shard_map/ppermute | solution.py:408
  5.4 0.0 copy-start.4
  5.4 0.0 copy-start.5
  5.5 0.6 %copy-done.4 = s32[32]{0:T(128)S(1)} copy-done((s32[32]{0:T(128)S(1)}, s32[32]{0:T(128)}, u32[]{:S(2)}) %copy-start.4) | copy-done | bytes 152
  6.1 0.0 copy-done.5
  6.1 1.2 %copy-done = bf16[128,16,256]{2,1,0:T(8,128)(2,1)S(1)} copy-done((bf16[128,16,256]{2,1,0:T(8,128)(2,1)S(1)}, bf16[128,16,256]{2,1,0:T(8,128)(2,1)}, u32[]{:S(2)}) %copy-start) | copy-done | bytes 1048600
  7.3 1.2 %copy-done.1 = bf16[128,16,256]{2,1,0:T(8,128)(2,1)S(1)} copy-done((bf16[128,16,256]{2,1,0:T(8,128)(2,1)S(1)}, bf16[128,16,256]{2,1,0:T(8,128)(2,1)}, u32[]{:S(2)}) %copy-start.1) | copy-done | bytes 1048600
  8.5 1.9 %decode_held_pages.1 = (bf16[128,256]{1,0:T(8,128)(2,1)S(1)}, f32[16,8,1]{2,1,0:T(8,128)S(1)}, f32[16,8,1]{2,1,0:T(8,128)S(1)}, f32[16,8,256]{2,1,0:T(8,128)S(1)}) custom-call(s32[1]{0:T(128)} %bitcast.own_ref, s32[32]{0:T(128)S(1)} %copy-done.4, s32[8]{0:T(128)S(1)} %copy-done.5, bf16[8,2048]{1,0:T(8,128)(2,1)S(1)} %copy-done.2, s32[8,32]{1,0:T(8,128)S(1)} %copy-done.3, ...), custom_call_target="tpu_custom_call" | custom-call | flops 268435456 | bytes 2097152 | tf_op jit(solution)/shard_map/decode_held_pages/pallas_call | solution.py:452
  10.4 2.4 %own_shard.1 = (bf16[2,256,1024]{2,1,0:T(8,128)(2,1)S(1)}, bf16[3,128,128]{2,1,0:T(8,128)(2,1)S(1)}, bf16[3,256,128]{2,1,0:T(8,128)(2,1)S(1)}, bf16[32,128]{1,0:...) custom-call(s32[1]{0:T(128)} %bitcast.own_ref, ...), custom_call_target="tpu_custom_call" | custom-call | flops 402653184 | bytes 1048576 | tf_op jit(solution)/shard_map/own_shard/pallas_call | solution.py:431
  12.8 2.1 %collective-permute-start.1 = (bf16[768,256]{1,0:T(8,128)(2,1)S(1)}, bf16[768,256]{1,0:T(8,128)(2,1)S(1)}, u32[]{:S(2)}, u32[]{:S(2)}) collective-permute-start(bf16[768,256]{1,0:T(8,128)(2,1)S(1)} %pad_maximum_fusion.shard_ref.rest_ref), channel_id=1, source_target_pairs={{0,12},{4,0},{8,4},{12,8},{1,13},{5,1},{9,5},{13,9},{2,14},{6,2},{... | collective-permute-start | bytes 1179656 | tf_op jit(solution)/shard_map/ppermute | solution.py:408
  14.9 1.1 %collective-permute-done.refs_0_.shard_ref = bf16[768,256]{1,0:T(8,128)(2,1)S(1)} collective-permute-done((bf16[768,256]{1,0:T(8,128)(2,1)S(1)}, bf16[768,256]{1,0:T(8,128)(2,1)S(1)}, u32[]{:S(2)}, u32[]{:S(2)}) %collective-permute-start) | collective-permute-done | bytes 393248 | tf_op jit(solution)/shard_map/ppermute | solution.py:408
  16.0 0.1 pieces_to_send_on.1
  16.1 0.1 collective-permute-start.2
  16.2 0.7 %collective-permute-start.3 = (bf16[256,256]{1,0:T(8,128)(2,1)S(1)}, bf16[256,256]{1,0:T(8,128)(2,1)S(1)}, u32[]{:S(2)}, u32[]{:S(2)}) collective-permute-start(bf16[256,256]{1,0:T(8,128)(2,1)S(1)} %get-tuple-element.100), channel_id=1, source_target_pairs={{4,8},{8,12},{5,9},{9,13},{6,10},{10,14},{7,11},{11,15},{20,24},{2... | collective-permute-start | bytes 393224 | tf_op jit(solution)/shard_map/ppermute | solution.py:489
  16.9 4.0 %collective-permute-start.4 = (bf16[256,256]{1,0:T(8,128)(2,1)S(1)}, bf16[256,256]{1,0:T(8,128)(2,1)S(1)}, u32[]{:S(2)}, u32[]{:S(2)}) collective-permute-start(bf16[256,256]{1,0:T(8,128)(2,1)S(1)} %get-tuple-element.104), channel_id=1, source_target_pairs={{0,4},{4,8},{8,12},{12,0},{1,5},{5,9},{9,13},{13,1},{2,6},{6,10},{... | collective-permute-start | bytes 393224 | tf_op jit(solution)/shard_map/ppermute | solution.py:408
  20.9 4.1 %collective-permute-start.5 = (bf16[64,256]{1,0:T(8,128)(2,1)S(1)}, bf16[64,256]{1,0:T(8,128)(2,1)S(1)}, u32[]{:S(2)}, u32[]{:S(2)}) collective-permute-start(bf16[64,256]{1,0:T(8,128)(2,1)S(1)} %get-tuple-element.105), channel_id=1, source_target_pairs={{0,4},{12,0},{1,5},{13,1},{2,6},{14,2},{3,7},{15,3},{16,20},{28,16... | collective-permute-start | bytes 98312 | tf_op jit(solution)/shard_map/ppermute | solution.py:490
  25.0 1.7 %whole_shards_0.1 = (f32[2,1,1024]{2,1,0:T(1,128)S(1)}, f32[2,1,1024]{2,1,0:T(1,128)S(1)}, f32[2,128,1024]{2,1,0:T(8,128)S(1)}) custom-call(bf16[2,256,1024]{2,1,0:T(8,128)(2,1)S(1)} %get-tuple-element.56.qt_ref, bf16[3,128,128]{2,1,0:T(8,128)(2,1)S(1)} %get-tuple-element.57.near_ref, bf16[3,256,128]{2,1,0:T(8,128)(2,1)S(1)} %get-tuple-element.58.far_ref, ...), custom_call_target="tpu_custom_call" | custom-call | flops 402653184 | bytes 1048576 | tf_op jit(solution)/shard_map/whole_shards_0/pallas_call | solution.py:495
  26.7 1.7 %whole_shards_1.1 = (f32[2,1,1024]{2,1,0:T(1,128)S(1)}, f32[2,1,1024]{2,1,0:T(1,128)S(1)}, f32[2,128,1024]{2,1,0:T(8,128)S(1)}) custom-call(bf16[2,256,1024]{2,1,0:T(8,128)(2,1)S(1)} %get-tuple-element.56.qt_ref, bf16[3,128,128]{2,1,0:T(8,128)(2,1)S(1)} %get-tuple-element.57.near_ref, bf16[3,256,128]{2,1,0:T(8,128)(2,1)S(1)} %get-tuple-element.58.far_ref, ...), custom_call_target="tpu_custom_call" | custom-call | flops 402653184 | bytes 1048576 | tf_op jit(solution)/shard_map/whole_shards_1/pallas_call | solution.py:495
  28.5 1.1 %decode_near_pages.1 = (f32[16,8,1]{2,1,0:T(8,128)S(1)}, f32[16,8,1]{2,1,0:T(8,128)S(1)}, f32[16,8,256]{2,1,0:T(8,128)S(1)}, f32[1,8,160]{2,1,0:T(8,128)S(1)}) custom-call(s32[1]{0:T(128)} %bitcast.own_ref, s32[32]{0:T(128)S(1)} %copy-done.4, s32[8]{0:T(128)S(1)} %copy-done.5, s32[8,32]{1,0:T(8,128)S(1)} %copy-done.3, ...), custom_call_target="tpu_custom_call" | custom-call | flops 134217728 | bytes 1048576 | tf_op jit(solution)/shard_map/decode_near_pages/pallas_call | solution.py:508
  29.6 0.2 collective-permute-done.2.keys_ref
  29.7 1.6 %last_scores.1 = (bf16[2,256,1024]{2,1,0:T(8,128)(2,1)S(1)}, f32[2,1,1024]{2,1,0:T(1,128)S(1)}, f32[2,128,1024]{2,1,0:T(8,128)S(1)}) custom-call(bf16[2,256,1024]{2,1,0:T(8,128)(2,1)S(1)} %get-tuple-element.56.qt_ref, bf16[3,128,128]{2,1,0:T(8,128)(2,1)S(1)} %get-tuple-element.57.near_ref, bf16[3,256,128]{2,1,0:T(8,128)(2,1)S(1)} %get-tuple-element.58.far_ref, ...), custom_call_target="tpu_custom_call" | custom-call | flops 402653184 | bytes 1048576 | tf_op jit(solution)/shard_map/last_scores/pallas_call | solution.py:523
  31.3 0.4 %collective-permute-done.5.pages_ref = bf16[64,256]{1,0:T(8,128)(2,1)S(1)} collective-permute-done((bf16[64,256]{1,0:T(8,128)(2,1)S(1)}, bf16[64,256]{1,0:T(8,128)(2,1)S(1)}, u32[]{:S(2)}, u32[]{:S(2)}) %collective-permute-start.5) | collective-permute-done | bytes 32800 | tf_op jit(solution)/shard_map/ppermute | solution.py:490
  31.8 2.0 %last_values_and_pages.1 = (bf16[128,2048]{1,0:T(8,128)(2,1)}, bf16[8,2048]{1,0:T(8,128)(2,1)}) custom-call(bf16[2,256,1024]{2,1,0:T(8,128)(2,1)S(1)} %get-tuple-element.101.weights_ref, f32[2,1,1024]{2,1,0:T(1,128)S(1)} %get-tuple-element.102.total_ref, f32[2,128,1024]{2,1,0:T(8,128)S(1)} %get-tuple-element.103.accum_ref, ...), custom_call_target="tpu_custom_call" | custom-call | flops 134217728 | bytes 1048576 | tf_op jit(solution)/shard_map/last_values_and_pages/pallas_call | solution.py:533
  (11 shorter events, 0.0 us)
Async XLA Ops:
  0.6 4.8 %copy-start.2 = (bf16[8,2048]{1,0:T(8,128)(2,1)S(1)}, bf16[8,2048]{1,0:T(8,128)(2,1)}, u32[]{:S(2)}) copy-start(bf16[8,2048]{1,0:T(8,128)(2,1)} %q_ref.3) | copy-start | bytes 98308
  1.7 14.3 %collective-permute-start = (bf16[768,256]{1,0:T(8,128)(2,1)S(1)}, bf16[768,256]{1,0:T(8,128)(2,1)S(1)}, u32[]{:S(2)}, u32[]{:S(2)}) collective-permute-start(bf16[768,256]{1,0:T(8,128)(2,1)S(1)} %pad_maximum_fusion.shard_ref.rest_ref), channel_id=1, source_target_pairs={{0,4},{4,8},{8,12},{12,0},{1,5},{5,9},{9,13},{13,1},{2,6},{6,10},{... | collective-permute-start | bytes 1179656 | tf_op jit(solution)/shard_map/ppermute | solution.py:408
  4.8 0.7 %copy-start.3 = (s32[8,32]{1,0:T(8,128)S(1)}, s32[8,32]{1,0:T(8,128)}, u32[]{:S(2)}) copy-start(s32[8,32]{1,0:T(8,128)} %lists_ref.3) | copy-start | bytes 3076
  5.4 0.7 %copy-start.4 = (s32[32]{0:T(128)S(1)}, s32[32]{0:T(128)}, u32[]{:S(2)}) copy-start(s32[32]{0:T(128)} %targets_ref.5) | copy-start | bytes 388
  5.4 0.7 %copy-start.5 = (s32[8]{0:T(128)S(1)}, s32[8]{0:T(128)}, u32[]{:S(2)}) copy-start(s32[8]{0:T(128)} %length_ref.3) | copy-start | bytes 100
  6.1 1.2 %copy-start = (bf16[128,16,256]{2,1,0:T(8,128)(2,1)S(1)}, bf16[128,16,256]{2,1,0:T(8,128)(2,1)}, u32[]{:S(2)}) copy-start(bf16[128,16,256]{2,1,0:T(8,128)(2,1)} %pool_k.1) | copy-start | bytes 3145732
  7.3 1.2 %copy-start.1 = (bf16[128,16,256]{2,1,0:T(8,128)(2,1)S(1)}, bf16[128,16,256]{2,1,0:T(8,128)(2,1)}, u32[]{:S(2)}) copy-start(bf16[128,16,256]{2,1,0:T(8,128)(2,1)} %pool_v.1) | copy-start | bytes 3145732
  8.5 1.9 %copy-start.6 = (bf16[128,2048]{1,0:T(8,128)(2,1)S(1)}, bf16[128,2048]{1,0:T(8,128)(2,1)}, u32[]{:S(2)}) copy-start(bf16[128,2048]{1,0:T(8,128)(2,1)} %q_ref.2) | copy-start | bytes 1572868
  12.8 13.9 %collective-permute-start.1 = (bf16[768,256]{1,0:T(8,128)(2,1)S(1)}, bf16[768,256]{1,0:T(8,128)(2,1)S(1)}, u32[]{:S(2)}, u32[]{:S(2)}) collective-permute-start(bf16[768,256]{1,0:T(8,128)(2,1)S(1)} %pad_maximum_fusion.shard_ref.rest_ref), channel_id=1, source_target_pairs={{0,12},{4,0},{8,4},{12,8},{1,13},{5,1},{9,5},{13,9},{2,14},{6,2},{... | collective-permute-start | bytes 1179656 | tf_op jit(solution)/shard_map/ppermute | solution.py:408
  16.1 13.6 %collective-permute-start.2 = (bf16[256,256]{1,0:T(8,128)(2,1)S(1)}, bf16[256,256]{1,0:T(8,128)(2,1)S(1)}, u32[]{:S(2)}, u32[]{:S(2)}) collective-permute-start(bf16[256,256]{1,0:T(8,128)(2,1)S(1)} %get-tuple-element.99), channel_id=1, source_target_pairs={{0,4},{4,8},{8,12},{12,0},{1,5},{5,9},{9,13},{13,1},{2,6},{6,10},{... | collective-permute-start | bytes 393224 | tf_op jit(solution)/shard_map/ppermute | solution.py:408
  16.2 13.5 %collective-permute-start.3 = (bf16[256,256]{1,0:T(8,128)(2,1)S(1)}, bf16[256,256]{1,0:T(8,128)(2,1)S(1)}, u32[]{:S(2)}, u32[]{:S(2)}) collective-permute-start(bf16[256,256]{1,0:T(8,128)(2,1)S(1)} %get-tuple-element.100), channel_id=1, source_target_pairs={{4,8},{8,12},{5,9},{9,13},{6,10},{10,14},{7,11},{11,15},{20,24},{2... | collective-permute-start | bytes 393224 | tf_op jit(solution)/shard_map/ppermute | solution.py:489
  16.9 14.9 %collective-permute-start.4 = (bf16[256,256]{1,0:T(8,128)(2,1)S(1)}, bf16[256,256]{1,0:T(8,128)(2,1)S(1)}, u32[]{:S(2)}, u32[]{:S(2)}) collective-permute-start(bf16[256,256]{1,0:T(8,128)(2,1)S(1)} %get-tuple-element.104), channel_id=1, source_target_pairs={{0,4},{4,8},{8,12},{12,0},{1,5},{5,9},{9,13},{13,1},{2,6},{6,10},{... | collective-permute-start | bytes 393224 | tf_op jit(solution)/shard_map/ppermute | solution.py:408
  20.9 10.9 %collective-permute-start.5 = (bf16[64,256]{1,0:T(8,128)(2,1)S(1)}, bf16[64,256]{1,0:T(8,128)(2,1)S(1)}, u32[]{:S(2)}, u32[]{:S(2)}) collective-permute-start(bf16[64,256]{1,0:T(8,128)(2,1)S(1)} %get-tuple-element.105), channel_id=1, source_target_pairs={{0,4},{12,0},{1,5},{13,1},{2,6},{14,2},{3,7},{15,3},{16,20},{28,16... | collective-permute-start | bytes 98312 | tf_op jit(solution)/shard_map/ppermute | solution.py:490

commit v16 on v15

--- a/solution.py
+++ b/solution.py
@@ -329,10 +329,22 @@
     walk(blocks_of(qt_ref), lambda block: scores_of(qt_ref, block[0], block[1], keys[block[0]]), second)
 
 
-def last_kernel(
-    weights_ref, total_ref, accum_ref, values_ref, stretch_ref, pages_ref, tally_ref,
-    wide_ref, dec_high, dec_total, dec_mixed, out_ref, dec_out, result_ref, sems,
+def last_pages_kernel(
+    stretch_ref, pages_ref, tally_ref, wide_ref, dec_high, dec_total, dec_mixed, dec_out
 ):
+    tokens = stretch_ref.shape[0] // 2
+    sent = pages_ref.shape[0] // 2
+    keys = jnp.concatenate([stretch_ref[:tokens], pages_ref[:sent]], axis=0)
+    values = jnp.concatenate([stretch_ref[tokens:], pages_ref[sent:]], axis=0)
+    state = (dec_high[...], dec_total[...], dec_mixed[...])
+    _, total, mixed = decode_attend(wide_ref[...], [(keys, values, tally_ref[...])], state)
+    share = 1.0 / total
+    for head in range(dec_high.shape[0]):
+        piece = mixed[head, :, features(head // GROUP)] * share[head]
+        dec_out[:, features(head)] = piece.astype(jnp.bfloat16)
+
+
+def last_kernel(weights_ref, total_ref, accum_ref, values_ref, out_ref, result_ref, sems):
     tokens = result_ref.shape[0]
     values_t = [values_ref[:, features(head)].T for head in range(weights_ref.shape[0])]
     copies = []
@@ -357,15 +369,6 @@
 
     walk(blocks_of(weights_ref), first, second)
 
-    sent = pages_ref.shape[0] // 2
-    keys = jnp.concatenate([stretch_ref[:tokens], pages_ref[:sent]], axis=0)
-    values = jnp.concatenate([stretch_ref[tokens:], pages_ref[sent:]], axis=0)
-    state = (dec_high[...], dec_total[...], dec_mixed[...])
-    _, total, mixed = decode_attend(wide_ref[...], [(keys, values, tally_ref[...])], state)
-    share = 1.0 / total
-    for head in range(dec_high.shape[0]):
-        piece = mixed[head, :, features(head // GROUP)] * share[head]
-        dec_out[:, features(head)] = piece.astype(jnp.bfloat16)
     for copy in copies:
         copy.wait()
 
@@ -530,19 +533,31 @@
         name="last_scores",
     )(qt, near, far, *state, last_keys, last_stretch)
 
-    prefill, decoded = pl.pallas_call(
+    dec_state, total = lax.optimization_barrier((dec_state, total))
+    decoded = pl.pallas_call(
+        last_pages_kernel,
+        out_shape=shape(decode_queries.shape, bf16),
+        in_specs=[VMEM] * 7,
+        out_specs=VMEM,
+        compiler_params=params,
+        cost_estimate=cost(tokens // 2),
+        name="decode_last_pages",
+    )(last_stretch, last_pages, tally, wide, *dec_state)
+    decoded, total = lax.optimization_barrier((decoded, total))
+
+    prefill = pl.pallas_call(
         last_kernel,
-        out_shape=(shape((tokens, width), bf16), shape(decode_queries.shape, bf16)),
-        in_specs=[VMEM] * 11,
-        out_specs=(HBM, VMEM),
+        out_shape=shape((tokens, width), bf16),
+        in_specs=[VMEM] * 4,
+        out_specs=HBM,
         scratch_shapes=[
             pltpu.VMEM((tokens, width), bf16),
             pltpu.SemaphoreType.DMA((kv_local * max(GROUP // 2, 1),)),
         ],
         compiler_params=params,
         cost_estimate=cost(c_rows // 2),
-        name="last_values_and_pages",
-    )(weights, total, accum, last_values, last_stretch, last_pages, tally, wide, *dec_state)
+        name="last_values",
+    )(weights, total, accum, last_values)
     return (prefill, decoded)
 
 

time: 34 us -> 33.9 us (level)
  starting transfers between devices: 14 us -> 11.9 us
  waiting for transfers between devices: 1.7 us -> 3.43 us
    ppermute x4, starting transfers between devices: 9.28 us -> 5.29 us  [send(): return lax.ppermute(array, 'ctx', up_pairs if hop < 0 else down_pairs)]
    ppermute x4, waiting for transfers between devices: 1.26 us -> 3.42 us  [send(): return lax.ppermute(array, 'ctx', up_pairs if hop < 0 else down_pairs)]
    ppermute x1, starting transfers between devices: 4.07 us -> 5.9 us  [per_device(): last_pages = lax.ppermute(pieces[3], 'ctx', others)]
    ppermute x1, waiting for transfers between devices: 0.44 us -> 0.01 us  [per_device(): last_pages = lax.ppermute(pieces[3], 'ctx', others)]
    pallas_call x1 -> x2, Pallas kernels: 1.97 us -> 2.26 us  [the longest x1 1.14 us: per_device(): pl.pallas_call(last_kernel, out_shape=shape((tokens, width), bf16), in_sp...]
  transfers between devices with their start and end apart: 6 -> 6, of which waited for: 3 -> 3; matrix products, arithmetic and copies ran while one was open for 0% -> 0% of each run, Pallas kernels for 31% -> 35%
where the time goes in v16:
time: 33.9 us; the launch traced here: 33.6 us
  Pallas kernels  12.8 us (38%)
  starting transfers between devices  11.9 us (35%)
  waiting for transfers between devices  3.43 us (10%)
  local copies, waits for them, and re-layouts  3.1 us (9%)
  between operations  1.44 us (4%)
  other arithmetic  1.03 us (3%)
    ppermute x1, starting transfers between devices, per_device(): last_pages = lax.ppermute(pieces[3], 'ctx', others)  5.9 us
    ppermute x4, starting transfers between devices, send(): return lax.ppermute(array, 'ctx', up_pairs if hop < 0 else down_pairs)  5.29 us
    pallas_call x2, Pallas kernels, per_device(): pl.pallas_call(functools.partial(hop_kernel, places), out_shape=state_sha...  3.45 us
    ppermute x4, waiting for transfers between devices, send(): return lax.ppermute(array, 'ctx', up_pairs if hop < 0 else down_pairs)  3.42 us
    unnamed x14, local copies, waits for them, and re-layouts  3.1 us
    pallas_call x1, Pallas kernels, per_device(): pl.pallas_call(functools.partial(own_kernel, count, hops), out_shape=(sha...  2.36 us
    pallas_call x1, Pallas kernels, per_device(): pl.pallas_call(held_kernel, out_shape=(shape((heads * dec_rows, kv_width)...  1.86 us
    pallas_call x1, Pallas kernels, per_device(): pl.pallas_call(functools.partial(score_kernel, final), out_shape=(shape((...  1.6 us
  transfers between devices with their start and end apart: 6, of which 3 were waited for; matrix products, arithmetic and copies ran while one was open for 0% of the time, Pallas kernels for 35%

profile of v16, /device:TPU:0, one launch (start us, length us, event | category | flops | bytes accessed | tf_op | source)
XLA Modules:
  0.0 33.6 jit_solution(15856622831956321135)
XLA Ops:
  0.6 1.0 %pad_maximum_fusion.shard_ref.rest_ref = bf16[768,256]{1,0:T(8,128)(2,1)S(1)} fusion(bf16[256,256]{1,0:T(8,128)(2,1)} %param.16, bf16[128,256]{1,0:T(8,128)(2,1)} %param.14, bf16[256,256]{1,0:T(8,128)(2,1)} %param.15, bf16[128,256]{1,0:T(8,128)(2,1)} %param.13), kind=kLoop, calls=%fused_computation | loop fusion | flops 1572864 | bytes 786432 | tf_op jit(solution)/shard_map/max | solution.py:426
  1.7 3.1 %collective-permute-start = (bf16[768,256]{1,0:T(8,128)(2,1)S(1)}, bf16[768,256]{1,0:T(8,128)(2,1)S(1)}, u32[]{:S(2)}, u32[]{:S(2)}) collective-permute-start(bf16[768,256]{1,0:T(8,128)(2,1)S(1)} %pad_maximum_fusion.shard_ref.rest_ref), channel_id=1, source_target_pairs={{0,4},{4,8},{8,12},{12,0},{1,5},{5,9},{9,13},{13,1},{2,6},{6,10},{... | collective-permute-start | bytes 1179656 | tf_op jit(solution)/shard_map/ppermute | solution.py:411
  5.4 0.0 copy-start.4
  5.5 0.6 %copy-done.4 = s32[32]{0:T(128)S(1)} copy-done((s32[32]{0:T(128)S(1)}, s32[32]{0:T(128)}, u32[]{:S(2)}) %copy-start.4) | copy-done | bytes 152
  6.1 0.0 copy-done.5
  6.1 1.2 %copy-done = bf16[128,16,256]{2,1,0:T(8,128)(2,1)S(1)} copy-done((bf16[128,16,256]{2,1,0:T(8,128)(2,1)S(1)}, bf16[128,16,256]{2,1,0:T(8,128)(2,1)}, u32[]{:S(2)}) %copy-start) | copy-done | bytes 1048600
  7.3 1.2 %copy-done.1 = bf16[128,16,256]{2,1,0:T(8,128)(2,1)S(1)} copy-done((bf16[128,16,256]{2,1,0:T(8,128)(2,1)S(1)}, bf16[128,16,256]{2,1,0:T(8,128)(2,1)}, u32[]{:S(2)}) %copy-start.1) | copy-done | bytes 1048600
  8.5 1.9 %decode_held_pages.1 = (bf16[128,256]{1,0:T(8,128)(2,1)S(1)}, f32[16,8,1]{2,1,0:T(8,128)S(1)}, f32[16,8,1]{2,1,0:T(8,128)S(1)}, f32[16,8,256]{2,1,0:T(8,128)S(1)}) custom-call(s32[1]{0:T(128)} %bitcast.own_ref, s32[32]{0:T(128)S(1)} %copy-done.4, s32[8]{0:T(128)S(1)} %copy-done.5, bf16[8,2048]{1,0:T(8,128)(2,1)S(1)} %copy-done.2, s32[8,32]{1,0:T(8,128)S(1)} %copy-done.3, ...), custom_call_target="tpu_custom_call" | custom-call | flops 268435456 | bytes 2097152 | tf_op jit(solution)/shard_map/decode_held_pages/pallas_call | solution.py:455
  10.4 2.4 %own_shard.1 = (bf16[2,256,1024]{2,1,0:T(8,128)(2,1)S(1)}, bf16[3,128,128]{2,1,0:T(8,128)(2,1)S(1)}, bf16[3,256,128]{2,1,0:T(8,128)(2,1)S(1)}, bf16[32,128]{1,0:...) custom-call(s32[1]{0:T(128)} %bitcast.own_ref, ...), custom_call_target="tpu_custom_call" | custom-call | flops 402653184 | bytes 1048576 | tf_op jit(solution)/shard_map/own_shard/pallas_call | solution.py:434
  12.8 2.1 %collective-permute-start.1 = (bf16[768,256]{1,0:T(8,128)(2,1)S(1)}, bf16[768,256]{1,0:T(8,128)(2,1)S(1)}, u32[]{:S(2)}, u32[]{:S(2)}) collective-permute-start(bf16[768,256]{1,0:T(8,128)(2,1)S(1)} %pad_maximum_fusion.shard_ref.rest_ref), channel_id=1, source_target_pairs={{0,12},{4,0},{8,4},{12,8},{1,13},{5,1},{9,5},{13,9},{2,14},{6,2},{... | collective-permute-start | bytes 1179656 | tf_op jit(solution)/shard_map/ppermute | solution.py:411
  14.9 1.1 %collective-permute-done.refs_0_.shard_ref = bf16[768,256]{1,0:T(8,128)(2,1)S(1)} collective-permute-done((bf16[768,256]{1,0:T(8,128)(2,1)S(1)}, bf16[768,256]{1,0:T(8,128)(2,1)S(1)}, u32[]{:S(2)}, u32[]{:S(2)}) %collective-permute-start) | collective-permute-done | bytes 393248 | tf_op jit(solution)/shard_map/ppermute | solution.py:411
  16.0 0.1 pieces_to_send_on.1
  16.1 0.1 collective-permute-start.2
  16.2 0.7 %collective-permute-start.3 = (bf16[256,256]{1,0:T(8,128)(2,1)S(1)}, bf16[256,256]{1,0:T(8,128)(2,1)S(1)}, u32[]{:S(2)}, u32[]{:S(2)}) collective-permute-start(bf16[256,256]{1,0:T(8,128)(2,1)S(1)} %get-tuple-element.106), channel_id=1, source_target_pairs={{4,8},{8,12},{5,9},{9,13},{6,10},{10,14},{7,11},{11,15},{20,24},{2... | collective-permute-start | bytes 393224 | tf_op jit(solution)/shard_map/ppermute | solution.py:492
  16.9 5.9 %collective-permute-start.4 = (bf16[64,256]{1,0:T(8,128)(2,1)S(1)}, bf16[64,256]{1,0:T(8,128)(2,1)S(1)}, u32[]{:S(2)}, u32[]{:S(2)}) collective-permute-start(bf16[64,256]{1,0:T(8,128)(2,1)S(1)} %get-tuple-element.108), channel_id=1, source_target_pairs={{0,4},{12,0},{1,5},{13,1},{2,6},{14,2},{3,7},{15,3},{16,20},{28,16... | collective-permute-start | bytes 98312 | tf_op jit(solution)/shard_map/ppermute | solution.py:493
  22.8 0.1 collective-permute-start.5
  22.8 1.7 %whole_shards_0.1 = (f32[2,1,1024]{2,1,0:T(1,128)S(1)}, f32[2,1,1024]{2,1,0:T(1,128)S(1)}, f32[2,128,1024]{2,1,0:T(8,128)S(1)}) custom-call(bf16[2,256,1024]{2,1,0:T(8,128)(2,1)S(1)} %get-tuple-element.62.qt_ref, bf16[3,128,128]{2,1,0:T(8,128)(2,1)S(1)} %get-tuple-element.63.near_ref, bf16[3,256,128]{2,1,0:T(8,128)(2,1)S(1)} %get-tuple-element.64.far_ref, ...), custom_call_target="tpu_custom_call" | custom-call | flops 402653184 | bytes 1048576 | tf_op jit(solution)/shard_map/whole_shards_0/pallas_call | solution.py:498
  24.6 0.1 collective-permute-done.1.refs_0_.refs_1_
  24.6 1.7 %whole_shards_1.1 = (f32[2,1,1024]{2,1,0:T(1,128)S(1)}, f32[2,1,1024]{2,1,0:T(1,128)S(1)}, f32[2,128,1024]{2,1,0:T(8,128)S(1)}) custom-call(bf16[2,256,1024]{2,1,0:T(8,128)(2,1)S(1)} %get-tuple-element.62.qt_ref, bf16[3,128,128]{2,1,0:T(8,128)(2,1)S(1)} %get-tuple-element.63.near_ref, bf16[3,256,128]{2,1,0:T(8,128)(2,1)S(1)} %get-tuple-element.64.far_ref, ...), custom_call_target="tpu_custom_call" | custom-call | flops 402653184 | bytes 1048576 | tf_op jit(solution)/shard_map/whole_shards_1/pallas_call | solution.py:498
  26.4 1.1 %decode_near_pages.1 = (f32[16,8,1]{2,1,0:T(8,128)S(1)}, f32[16,8,1]{2,1,0:T(8,128)S(1)}, f32[16,8,256]{2,1,0:T(8,128)S(1)}, f32[1,8,160]{2,1,0:T(8,128)S(1)}) custom-call(s32[1]{0:T(128)} %bitcast.own_ref, s32[32]{0:T(128)S(1)} %copy-done.4, s32[8]{0:T(128)S(1)} %copy-done.5, s32[8,32]{1,0:T(8,128)S(1)} %copy-done.3, ...), custom_call_target="tpu_custom_call" | custom-call | flops 134217728 | bytes 1048576 | tf_op jit(solution)/shard_map/decode_near_pages/pallas_call | solution.py:511
  27.5 2.3 %collective-permute-done.2.keys_ref = bf16[256,256]{1,0:T(8,128)(2,1)S(1)} collective-permute-done((bf16[256,256]{1,0:T(8,128)(2,1)S(1)}, bf16[256,256]{1,0:T(8,128)(2,1)S(1)}, u32[]{:S(2)}, u32[]{:S(2)}) %collective-permute-start.2) | collective-permute-done | bytes 131104 | tf_op jit(solution)/shard_map/ppermute | solution.py:411
  29.7 1.6 %last_scores.1 = (bf16[2,256,1024]{2,1,0:T(8,128)(2,1)S(1)}, f32[2,1,1024]{2,1,0:T(1,128)S(1)}, f32[2,128,1024]{2,1,0:T(8,128)S(1)}) custom-call(bf16[2,256,1024]{2,1,0:T(8,128)(2,1)S(1)} %get-tuple-element.62.qt_ref, bf16[3,128,128]{2,1,0:T(8,128)(2,1)S(1)} %get-tuple-element.63.near_ref, bf16[3,256,128]{2,1,0:T(8,128)(2,1)S(1)} %get-tuple-element.64.far_ref, ...), custom_call_target="tpu_custom_call" | custom-call | flops 402653184 | bytes 1048576 | tf_op jit(solution)/shard_map/last_scores/pallas_call | solution.py:526
  31.4 1.1 %decode_last_pages.1 = bf16[8,2048]{1,0:T(8,128)(2,1)} custom-call(bf16[256,256]{1,0:T(8,128)(2,1)S(1)} %collective-permute-done.3.stretch_ref, bf16[64,256]{1,0:T(8,128)(2,1)S(1)} %collective-permute-done.4.pages_ref, f32[1,8,160]{2,1,0:T(8,128)S(1)} %get-tuple-element.109.tally_ref, bf16[128,256]{1,0:T(8,128)(2,1)S(1)} %get-tuple-element.79.refs_2_.wide_ref, ...), custom_call_target="tpu_custom_call" | custom-call | flops 67108864 | bytes 1048576 | tf_op jit(solution)/shard_map/decode_last_pages/pallas_call | solution.py:537
  32.5 1.1 %last_values.1 = bf16[128,2048]{1,0:T(8,128)(2,1)} custom-call(bf16[2,256,1024]{2,1,0:T(8,128)(2,1)S(1)} %get-tuple-element.107.weights_ref, f32[2,1,1024]{2,1,0:T(1,128)S(1)} %get-tuple-element.118.total_ref, f32[2,128,1024]{2,1,0:T(8,128)S(1)} %get-tuple-element.119.accum_ref, bf16[256,256]{1,0:T(8,128)(2,1)S(1)} %collective-permute-done.5.values_ref), custom_call_target="tpu_custom_call" | custom-call | flops 134217728 | bytes 1048576 | tf_op jit(solution)/shard_map/last_values/pallas_call | solution.py:548
  (12 shorter events, 0.0 us)
Async XLA Ops:
  0.6 4.8 %copy-start.2 = (bf16[8,2048]{1,0:T(8,128)(2,1)S(1)}, bf16[8,2048]{1,0:T(8,128)(2,1)}, u32[]{:S(2)}) copy-start(bf16[8,2048]{1,0:T(8,128)(2,1)} %q_ref.3) | copy-start | bytes 98308
  1.7 14.3 %collective-permute-start = (bf16[768,256]{1,0:T(8,128)(2,1)S(1)}, bf16[768,256]{1,0:T(8,128)(2,1)S(1)}, u32[]{:S(2)}, u32[]{:S(2)}) collective-permute-start(bf16[768,256]{1,0:T(8,128)(2,1)S(1)} %pad_maximum_fusion.shard_ref.rest_ref), channel_id=1, source_target_pairs={{0,4},{4,8},{8,12},{12,0},{1,5},{5,9},{9,13},{13,1},{2,6},{6,10},{... | collective-permute-start | bytes 1179656 | tf_op jit(solution)/shard_map/ppermute | solution.py:411
  4.8 0.7 %copy-start.3 = (s32[8,32]{1,0:T(8,128)S(1)}, s32[8,32]{1,0:T(8,128)}, u32[]{:S(2)}) copy-start(s32[8,32]{1,0:T(8,128)} %lists_ref.3) | copy-start | bytes 3076
  5.4 0.7 %copy-start.4 = (s32[32]{0:T(128)S(1)}, s32[32]{0:T(128)}, u32[]{:S(2)}) copy-start(s32[32]{0:T(128)} %targets_ref.5) | copy-start | bytes 388
  5.4 0.7 %copy-start.5 = (s32[8]{0:T(128)S(1)}, s32[8]{0:T(128)}, u32[]{:S(2)}) copy-start(s32[8]{0:T(128)} %length_ref.3) | copy-start | bytes 100
  6.1 1.2 %copy-start = (bf16[128,16,256]{2,1,0:T(8,128)(2,1)S(1)}, bf16[128,16,256]{2,1,0:T(8,128)(2,1)}, u32[]{:S(2)}) copy-start(bf16[128,16,256]{2,1,0:T(8,128)(2,1)} %pool_k.1) | copy-start | bytes 3145732
  7.3 1.2 %copy-start.1 = (bf16[128,16,256]{2,1,0:T(8,128)(2,1)S(1)}, bf16[128,16,256]{2,1,0:T(8,128)(2,1)}, u32[]{:S(2)}) copy-start(bf16[128,16,256]{2,1,0:T(8,128)(2,1)} %pool_v.1) | copy-start | bytes 3145732
  8.5 1.9 %copy-start.6 = (bf16[128,2048]{1,0:T(8,128)(2,1)S(1)}, bf16[128,2048]{1,0:T(8,128)(2,1)}, u32[]{:S(2)}) copy-start(bf16[128,2048]{1,0:T(8,128)(2,1)} %q_ref.2) | copy-start | bytes 1572868
  12.8 11.8 %collective-permute-start.1 = (bf16[768,256]{1,0:T(8,128)(2,1)S(1)}, bf16[768,256]{1,0:T(8,128)(2,1)S(1)}, u32[]{:S(2)}, u32[]{:S(2)}) collective-permute-start(bf16[768,256]{1,0:T(8,128)(2,1)S(1)} %pad_maximum_fusion.shard_ref.rest_ref), channel_id=1, source_target_pairs={{0,12},{4,0},{8,4},{12,8},{1,13},{5,1},{9,5},{13,9},{2,14},{6,2},{... | collective-permute-start | bytes 1179656 | tf_op jit(solution)/shard_map/ppermute | solution.py:411
  16.1 13.6 %collective-permute-start.2 = (bf16[256,256]{1,0:T(8,128)(2,1)S(1)}, bf16[256,256]{1,0:T(8,128)(2,1)S(1)}, u32[]{:S(2)}, u32[]{:S(2)}) collective-permute-start(bf16[256,256]{1,0:T(8,128)(2,1)S(1)} %get-tuple-element.105), channel_id=1, source_target_pairs={{0,4},{4,8},{8,12},{12,0},{1,5},{5,9},{9,13},{13,1},{2,6},{6,10},{... | collective-permute-start | bytes 393224 | tf_op jit(solution)/shard_map/ppermute | solution.py:411
  16.2 13.5 %collective-permute-start.3 = (bf16[256,256]{1,0:T(8,128)(2,1)S(1)}, bf16[256,256]{1,0:T(8,128)(2,1)S(1)}, u32[]{:S(2)}, u32[]{:S(2)}) collective-permute-start(bf16[256,256]{1,0:T(8,128)(2,1)S(1)} %get-tuple-element.106), channel_id=1, source_target_pairs={{4,8},{8,12},{5,9},{9,13},{6,10},{10,14},{7,11},{11,15},{20,24},{2... | collective-permute-start | bytes 393224 | tf_op jit(solution)/shard_map/ppermute | solution.py:492
  16.9 14.5 %collective-permute-start.4 = (bf16[64,256]{1,0:T(8,128)(2,1)S(1)}, bf16[64,256]{1,0:T(8,128)(2,1)S(1)}, u32[]{:S(2)}, u32[]{:S(2)}) collective-permute-start(bf16[64,256]{1,0:T(8,128)(2,1)S(1)} %get-tuple-element.108), channel_id=1, source_target_pairs={{0,4},{12,0},{1,5},{13,1},{2,6},{14,2},{3,7},{15,3},{16,20},{28,16... | collective-permute-start | bytes 98312 | tf_op jit(solution)/shard_map/ppermute | solution.py:493
  22.8 9.7 %collective-permute-start.5 = (bf16[256,256]{1,0:T(8,128)(2,1)S(1)}, bf16[256,256]{1,0:T(8,128)(2,1)S(1)}, u32[]{:S(2)}, u32[]{:S(2)}) collective-permute-start(bf16[256,256]{1,0:T(8,128)(2,1)S(1)} %get-tuple-element.120), channel_id=1, source_target_pairs={{0,4},{4,8},{8,12},{12,0},{1,5},{5,9},{9,13},{13,1},{2,6},{6,10},{... | collective-permute-start | bytes 393224 | tf_op jit(solution)/shard_map/ppermute | solution.py:411

commit v17 on v16

--- a/solution.py
+++ b/solution.py
@@ -104,6 +104,16 @@
         two = jnp.where(hit & (one >= 0) & (two < 0), index, two)
         one = jnp.where(hit & (one < 0), index, one)
     return one, two
+
+
+def pick_pages(targets_ref, shard, owner, dims):
+    one, two = sent_pages(targets_ref, shard, owner, dims[1] // PAGE)
+    row = lax.broadcasted_iota(jnp.int32, dims, 0)
+    token = lax.broadcasted_iota(jnp.int32, dims, 1)
+    sent = ((row < PAGE) & (one >= 0) & (token == row + one * PAGE)) | (
+        (row >= PAGE) & (two >= 0) & (token == row + (two - 1) * PAGE)
+    )
+    return jnp.where(sent, jnp.float32(1.0), jnp.float32(0.0)).astype(jnp.bfloat16)
 
 
 def sent_slots(targets_ref, shard, owner, pages, pool):
@@ -191,7 +201,7 @@
 
 def own_kernel(
     count, hops, own_ref, limit_ref, targets_ref, q_ref, shard_ref,
-    qt_ref, near_ref, far_ref, pick_ref, high_ref, total_ref, accum_ref,
+    qt_ref, near_ref, far_ref, pick_ref, below_ref, high_ref, total_ref, accum_ref,
 ):
     kv_local, _, rows = qt_ref.shape
     tokens = q_ref.shape[0]
@@ -211,16 +221,10 @@
         near_ref[place] = stretch_mask(shard, own, tokens)
         far_ref[place] = cache_mask(shard, limit, c_rows, tokens)
     onward = 1 if hops[-1] < 0 else -1
-    pages = tokens // PAGE
-    one, two = sent_pages(
-        targets_ref, shard_of(own, hops[-1] + onward, count), shard_of(own, onward, count), pages
+    pick_ref[...] = pick_pages(
+        targets_ref, shard_of(own, hops[-1] + onward, count), shard_of(own, onward, count), pick_ref.shape
     )
-    row = lax.broadcasted_iota(jnp.int32, pick_ref.shape, 0)
-    token = lax.broadcasted_iota(jnp.int32, pick_ref.shape, 1)
-    sent = ((row < PAGE) & (one >= 0) & (token == row + one * PAGE)) | (
-        (row >= PAGE) & (two >= 0) & (token == row + (two - 1) * PAGE)
-    )
-    pick_ref[...] = jnp.where(sent, jnp.float32(1.0), jnp.float32(0.0)).astype(jnp.bfloat16)
+    below_ref[...] = pick_pages(targets_ref, own, own - 1, below_ref.shape)
     mask = jnp.concatenate([stretch_mask(own, own, tokens), cache_mask(own, limit, c_rows, tokens)], axis=0)
     key_rows, value_rows = shard_parts(shard_ref, tokens, c_rows)
     keys = [jnp.concatenate([shard_ref[key_rows, features(head)], mask], axis=1) for head in range(kv_local)]
@@ -254,20 +258,32 @@
     high_ref[...], total_ref[...], mixed_ref[...] = decode_attend(wide_ref[...], parts, None)
 
 
-def hop_kernel(places, qt_ref, near_ref, far_ref, high_in, total_in, accum_in, *refs):
-    shard_refs, outs = refs[: len(places)], refs[len(places) :]
+def hop_kernel(place, qt_ref, near_ref, far_ref, high_in, total_in, accum_in, shard_ref, *refs):
+    extra, outs = refs[:-3], refs[-3:]
     tokens, c_rows = near_ref.shape[1], far_ref.shape[1]
-    mask = jnp.concatenate([ref[place] for place in places for ref in (near_ref, far_ref)], axis=0)
+    key_rows, value_rows = shard_parts(shard_ref, tokens, c_rows)
+    mask = jnp.concatenate([near_ref[place], far_ref[place]], axis=0)
     keys, values_t = [], []
     for head in range(qt_ref.shape[0]):
-        pieces, values = [], []
-        for ref in shard_refs:
-            key_rows, value_rows = shard_parts(ref, tokens, c_rows)
-            pieces.append(ref[key_rows, features(head)])
-            values.append(ref[value_rows, features(head)])
-        keys.append(jnp.concatenate([jnp.concatenate(pieces, axis=0), mask], axis=1))
-        values_t.append(jnp.concatenate(values, axis=0).T)
+        parts = [shard_ref[key_rows, features(head)], shard_ref[value_rows, features(head)]]
+        for ref in extra:
+            for index in range(2):
+                cached = ref[index * c_rows : (index + 1) * c_rows, features(head)]
+                part = parts[index]
+                parts[index] = jnp.concatenate([part[:tokens], part[tokens:] + cached], axis=0)
+        keys.append(jnp.concatenate([parts[0], mask], axis=1))
+        values_t.append(parts[1].T)
     attend(qt_ref, keys, values_t, (high_in, total_in, accum_in), outs)
+
+
+def down_kernel(pick_ref, shard_ref, out_ref):
+    sent, tokens = pick_ref.shape
+    half = shard_ref.shape[0] // 2
+    c_rows = half - tokens
+    for place, start in enumerate((0, half)):
+        out_ref[place * c_rows : (place + 1) * c_rows] = shard_ref[start + tokens : start + half]
+        rows = jnp.dot(pick_ref[...], shard_ref[start : start + tokens], preferred_element_type=jnp.float32)
+        out_ref[2 * c_rows + place * sent : 2 * c_rows + (place + 1) * sent] = rows.astype(jnp.bfloat16)
 
 
 def split_kernel(pick_ref, shard_ref, keys_ref, stretch_ref, values_ref, pages_ref):
@@ -284,6 +300,7 @@
 
 def near_pages_kernel(count, hops, tokens, pool, own_ref, targets_ref, length_ref, lists_ref, *refs):
     shard_refs, refs = refs[: len(hops) - 1], refs[len(hops) - 1 :]
+    extra, refs = refs[:-8], refs[-8:]
     wide_ref, dec_high, dec_total, dec_mixed, high_ref, total_ref, mixed_ref, tally_ref = refs
     own = own_ref[0]
     lists = lists_ref[...]
@@ -292,7 +309,15 @@
     for hop, ref in zip(hops, shard_refs):
         half = ref.shape[0] // 2
         slot = slot_row(targets_ref, shard_of(own, hop, count), own, tokens, pool)
+        if extra and hop == 1:
+            slot = jnp.where(own + 1 < count, -1, slot)
         parts.append((ref[:tokens], ref[half : half + tokens], tally_of(lists, lengths, slot)))
+    for ref in extra:
+        sent = SEND_CAP * PAGE
+        first = ref.shape[0] - 2 * sent
+        slot = sent_slots(targets_ref, shard_of(own, 1, count), own, tokens // PAGE, pool)
+        slot = jnp.where(own + 1 < count, slot, -1)
+        parts.append((ref[first : first + sent], ref[first + sent :], tally_of(lists, lengths, slot)))
     state = (dec_high[...], dec_total[...], dec_mixed[...])
     high_ref[...], total_ref[...], mixed_ref[...] = decode_attend(wide_ref[...], parts, state)
     shard = shard_of(own, hops[-1], count)
@@ -431,17 +456,18 @@
         shape((kv_local, 1, rows), f32),
         shape((kv_local, HEAD_DIM, rows), f32),
     )
-    qt, near, far, pick, *state = pl.pallas_call(
+    qt, near, far, pick, below, *state = pl.pallas_call(
         functools.partial(own_kernel, count, hops),
         out_shape=(
             shape((kv_local, HEAD_DIM + tokens, rows), bf16),
             shape((count - 1, tokens, tokens), bf16),
             shape((count - 1, c_rows, tokens), bf16),
             shape((SEND_CAP * PAGE, tokens), bf16),
+            shape((SEND_CAP * PAGE, tokens), bf16),
         )
         + state_shapes,
         in_specs=[SMEM] * 3 + [VMEM] * 2,
-        out_specs=(VMEM,) * 7,
+        out_specs=(VMEM,) * 8,
         compiler_params=params,
         cost_estimate=cost(tokens + c_rows),
         name="own_shard",
@@ -464,7 +490,20 @@
         name="decode_held_pages",
     )(own_array, page_targets, context_length, decode_queries, page_lists, pool_keys, pool_values, shard[0])
 
-    if 1 in hops:
+    extra = []
+    if hops == [-1, 1, -2]:
+        down = pl.pallas_call(
+            down_kernel,
+            out_shape=shape((2 * (c_rows + SEND_CAP * PAGE), kv_width), bf16),
+            in_specs=[VMEM] * 2,
+            out_specs=VMEM,
+            compiler_params=params,
+            name="rows_to_send_down",
+        )(below, shard[0])
+        down, straight, state, dec_state = lax.optimization_barrier((down, shard[0], state, dec_state))
+        extra = [lax.ppermute(down, "ctx", down_pairs[1:])]
+        shard[1] = lax.ppermute(straight, "ctx", down_pairs[:1])
+    elif 1 in hops:
         sent_down, state, dec_state = lax.optimization_barrier((shard[0], state, dec_state))
         shard[1] = send(sent_down, 1)
     shard[-1], state, dec_state = lax.optimization_barrier((shard[-1], state, dec_state))
@@ -491,34 +530,37 @@
         (attending if (pair[1] + hop) % count < pair[1] else others).append(pair)
     last_stretch = lax.ppermute(pieces[1], "ctx", attending)
     last_pages = lax.ppermute(pieces[3], "ctx", others)
-    last_values = send(pieces[2], hop)
-
-    for first in range(len(hops) - 1):
-        places = [first]
+
+    for place, hop in enumerate(hops[:-1]):
+        received = [shard[hop]] + (extra if hop == 1 else [])
         state = pl.pallas_call(
-            functools.partial(hop_kernel, places),
+            functools.partial(hop_kernel, place),
             out_shape=state_shapes,
-            in_specs=[VMEM] * (6 + len(places)),
+            in_specs=[VMEM] * (6 + len(received)),
             out_specs=(VMEM,) * 3,
             compiler_params=params,
-            cost_estimate=cost((c_rows + tokens) * len(places)),
-            name="whole_shards_" + str(first),
-        )(qt, near, far, *state, *[shard[hops[place]] for place in places])
+            cost_estimate=cost(half),
+            name="whole_shards_" + str(place),
+        )(qt, near, far, *state, *received)
+        if place == 0:
+            last_piece, shard[1], extra, state = lax.optimization_barrier((pieces[2], shard[1], extra, state))
+            last_values = send(last_piece, hops[-1])
 
     final = len(hops) - 1
     dec_state, state = lax.optimization_barrier((dec_state, state))
+    last_pages, dec_state = lax.optimization_barrier((last_pages, dec_state))
     near_hops = hops[:-1]
     *dec_state, tally = pl.pallas_call(
         functools.partial(near_pages_kernel, count, hops, tokens, pool),
         out_shape=dec_shapes
         + (shape((1, dec_rows, tokens + SEND_CAP * PAGE), f32),),
-        in_specs=[SMEM] * 3 + [VMEM] * (5 + len(near_hops)),
+        in_specs=[SMEM] * 3 + [VMEM] * (5 + len(near_hops) + len(extra)),
         out_specs=(VMEM,) * 4,
         compiler_params=params,
         cost_estimate=cost(tokens),
         name="decode_near_pages",
     )(
-        own_array, page_targets, context_length, page_lists, *[shard[hop] for hop in near_hops],
+        own_array, page_targets, context_length, page_lists, *[shard[hop] for hop in near_hops], *extra,
         wide, *dec_state,
     )
     dec_state, state = lax.optimization_barrier((dec_state, state))

time: 33.9 us -> 41.2 us (1.22)
  waiting for transfers between devices: 3.43 us -> 10.6 us
  local copies, waits for them, and re-layouts: 3.1 us -> 1.24 us
  starting transfers between devices: 11.9 us -> 13.6 us
    ppermute x0 -> x2, waiting for transfers between devices: none -> 6.62 us  [the longest x1 6.62 us: per_device(): extra = [lax.ppermute(down, 'ctx', down_pairs[1:])]]
    ppermute x0 -> x2, starting transfers between devices: none -> 5.26 us  [the longest x1 3.97 us: per_device(): shard[1] = lax.ppermute(straight, 'ctx', down_pairs[:1])]
    ppermute x1, starting transfers between devices: 5.9 us -> 1.91 us  [per_device(): last_pages = lax.ppermute(pieces[3], 'ctx', others)]
    ppermute x1, waiting for transfers between devices: 0.01 us -> 3.93 us  [per_device(): last_pages = lax.ppermute(pieces[3], 'ctx', others)]
    ppermute x4 -> x3, waiting for transfers between devices: 3.42 us -> 0.01 us  [send(): return lax.ppermute(array, 'ctx', up_pairs if hop < 0 else down_pairs)]
    unnamed x14, local copies, waits for them, and re-layouts: 3.1 us -> 1.24 us
    ppermute x4 -> x3, starting transfers between devices: 5.29 us -> 5.77 us  [send(): return lax.ppermute(array, 'ctx', up_pairs if hop < 0 else down_pairs)]
    pallas_call x2 -> x3, Pallas kernels: 3.45 us -> 3.61 us  [the longest x2 3.47 us: per_device(): pl.pallas_call(functools.partial(hop_kernel, place), out_shape=state_shap...]
  transfers between devices with their start and end apart: 6 -> 7, of which waited for: 3 -> 2; matrix products, arithmetic and copies ran while one was open for 0% -> 0% of each run, Pallas kernels for 35% -> 29%
where the time goes in v17:
time: 41.2 us; the launch traced here: 41 us
  starting transfers between devices  13.6 us (33%)
  Pallas kernels  13 us (32%)
  waiting for transfers between devices  10.6 us (26%)
  between operations  1.45 us (4%)
  local copies, waits for them, and re-layouts  1.24 us (3%)
  other arithmetic  1.09 us (3%)
    ppermute x1, waiting for transfers between devices, per_device(): extra = [lax.ppermute(down, 'ctx', down_pairs[1:])]  6.62 us
    ppermute x3, starting transfers between devices, send(): return lax.ppermute(array, 'ctx', up_pairs if hop < 0 else down_pairs)  5.77 us
    ppermute x1, starting transfers between devices, per_device(): shard[1] = lax.ppermute(straight, 'ctx', down_pairs[:1])  3.97 us
    ppermute x1, waiting for transfers between devices, per_device(): last_pages = lax.ppermute(pieces[3], 'ctx', others)  3.93 us
    pallas_call x2, Pallas kernels, per_device(): pl.pallas_call(functools.partial(hop_kernel, place), out_shape=state_shap...  3.47 us
    pallas_call x1, Pallas kernels, per_device(): pl.pallas_call(functools.partial(own_kernel, count, hops), out_shape=(sha...  2.35 us
    ppermute x1, starting transfers between devices, per_device(): last_pages = lax.ppermute(pieces[3], 'ctx', others)  1.91 us
    pallas_call x1, Pallas kernels, per_device(): pl.pallas_call(held_kernel, out_shape=(shape((heads * dec_rows, kv_width)...  1.91 us
  transfers between devices with their start and end apart: 7, of which 2 were waited for; matrix products, arithmetic and copies ran while one was open for 0% of the time, Pallas kernels for 29%

profile of v17, /device:TPU:0, one launch (start us, length us, event | category | flops | bytes accessed | tf_op | source)
XLA Modules:
  0.0 41.0 jit_solution(14728998819285396770)
XLA Ops:
  0.6 1.1 %pad_maximum_fusion.shard_ref.rest_ref = bf16[768,256]{1,0:T(8,128)(2,1)S(1)} fusion(bf16[256,256]{1,0:T(8,128)(2,1)} %param.16, bf16[128,256]{1,0:T(8,128)(2,1)} %param.14, bf16[256,256]{1,0:T(8,128)(2,1)} %param.15, bf16[128,256]{1,0:T(8,128)(2,1)} %param.13), kind=kLoop, calls=%fused_computation | loop fusion | flops 1572864 | bytes 786432 | tf_op jit(solution)/shard_map/max | solution.py:451
  1.7 3.1 %collective-permute-start = (bf16[768,256]{1,0:T(8,128)(2,1)S(1)}, bf16[768,256]{1,0:T(8,128)(2,1)S(1)}, u32[]{:S(2)}, u32[]{:S(2)}) collective-permute-start(bf16[768,256]{1,0:T(8,128)(2,1)S(1)} %pad_maximum_fusion.shard_ref.rest_ref), channel_id=1, source_target_pairs={{0,4},{4,8},{8,12},{12,0},{1,5},{5,9},{9,13},{13,1},{2,6},{6,10},{... | collective-permute-start | bytes 1179656 | tf_op jit(solution)/shard_map/ppermute | solution.py:436
  5.5 0.0 copy-start.4
  5.5 0.6 %copy-done.4 = s32[32]{0:T(128)S(1)} copy-done((s32[32]{0:T(128)S(1)}, s32[32]{0:T(128)}, u32[]{:S(2)}) %copy-start.4) | copy-done | bytes 152
  6.1 2.4 %own_shard.1 = (bf16[2,256,1024]{2,1,0:T(8,128)(2,1)S(1)}, bf16[3,128,128]{2,1,0:T(8,128)(2,1)S(1)}, bf16[3,256,128]{2,1,0:T(8,128)(2,1)S(1)}, bf16[32,128]{1,0:...) custom-call(s32[1]{0:T(128)} %bitcast.own_ref, ...), custom_call_target="tpu_custom_call" | custom-call | flops 402653184 | bytes 1048576 | tf_op jit(solution)/shard_map/own_shard/pallas_call | solution.py:459
  8.5 0.0 copy-start.2
  8.5 0.0 copy-start.3
  8.5 0.1 rows_to_send_down.1
  8.7 0.6 %copy-done.2 = bf16[8,2048]{1,0:T(8,128)(2,1)S(1)} copy-done((bf16[8,2048]{1,0:T(8,128)(2,1)S(1)}, bf16[8,2048]{1,0:T(8,128)(2,1)}, u32[]{:S(2)}) %copy-start.2) | copy-done | bytes 32792
  9.2 1.9 %decode_held_pages.1 = (bf16[128,256]{1,0:T(8,128)(2,1)S(1)}, f32[16,8,1]{2,1,0:T(8,128)S(1)}, f32[16,8,1]{2,1,0:T(8,128)S(1)}, f32[16,8,256]{2,1,0:T(8,128)S(1)}) custom-call(s32[1]{0:T(128)} %bitcast.own_ref, s32[32]{0:T(128)S(1)} %copy-done.4, s32[8]{0:T(128)S(1)} %copy-done.5, bf16[8,2048]{1,0:T(8,128)(2,1)S(1)} %copy-done.2, s32[8,32]{1,0:T(8,128)S(1)} %copy-done.3, ...), custom_call_target="tpu_custom_call" | custom-call | flops 268435456 | bytes 2097152 | tf_op jit(solution)/shard_map/decode_held_pages/pallas_call | solution.py:481
  11.2 4.0 %collective-permute-start.1 = (bf16[768,256]{1,0:T(8,128)(2,1)S(1)}, bf16[768,256]{1,0:T(8,128)(2,1)S(1)}, u32[]{:S(2)}, u32[]{:S(2)}) collective-permute-start(bf16[768,256]{1,0:T(8,128)(2,1)S(1)} %pad_maximum_fusion.shard_ref.rest_ref), channel_id=1, source_target_pairs={{0,12},{1,13},{2,14},{3,15},{16,28},{17,29},{18,30},{19,31}} | collective-permute-start | bytes 1179656 | tf_op jit(solution)/shard_map/ppermute | solution.py:505
  15.1 1.3 %collective-permute-start.2 = (bf16[576,256]{1,0:T(8,128)(2,1)S(1)}, bf16[576,256]{1,0:T(8,128)(2,1)S(1)}, u32[]{:S(2)}, u32[]{:S(2)}) collective-permute-start(bf16[576,256]{1,0:T(8,128)(2,1)S(1)} %rows_to_send_down.1), channel_id=1, source_target_pairs={{4,0},{8,4},{12,8},{5,1},{9,5},{13,9},{6,2},{10,6},{14,10},{7,3},{... | collective-permute-start | bytes 884744 | tf_op jit(solution)/shard_map/ppermute | solution.py:504
  16.5 0.1 pieces_to_send_on.1
  16.6 2.7 %collective-permute-start.4 = (bf16[256,256]{1,0:T(8,128)(2,1)S(1)}, bf16[256,256]{1,0:T(8,128)(2,1)S(1)}, u32[]{:S(2)}, u32[]{:S(2)}) collective-permute-start(bf16[256,256]{1,0:T(8,128)(2,1)S(1)} %get-tuple-element.129), channel_id=1, source_target_pairs={{0,4},{4,8},{8,12},{12,0},{1,5},{5,9},{9,13},{13,1},{2,6},{6,10},{... | collective-permute-start | bytes 393224 | tf_op jit(solution)/shard_map/ppermute | solution.py:436
  19.3 0.7 %collective-permute-start.5 = (bf16[256,256]{1,0:T(8,128)(2,1)S(1)}, bf16[256,256]{1,0:T(8,128)(2,1)S(1)}, u32[]{:S(2)}, u32[]{:S(2)}) collective-permute-start(bf16[256,256]{1,0:T(8,128)(2,1)S(1)} %get-tuple-element.130), channel_id=1, source_target_pairs={{4,8},{8,12},{5,9},{9,13},{6,10},{10,14},{7,11},{11,15},{20,24},{2... | collective-permute-start | bytes 393224 | tf_op jit(solution)/shard_map/ppermute | solution.py:531
  20.0 1.7 %whole_shards_0.1 = (f32[2,1,1024]{2,1,0:T(1,128)S(1)}, f32[2,1,1024]{2,1,0:T(1,128)S(1)}, f32[2,128,1024]{2,1,0:T(8,128)S(1)}) custom-call(bf16[2,256,1024]{2,1,0:T(8,128)(2,1)S(1)} %get-tuple-element.74.qt_ref, bf16[3,128,128]{2,1,0:T(8,128)(2,1)S(1)} %get-tuple-element.75.near_ref, bf16[3,256,128]{2,1,0:T(8,128)(2,1)S(1)} %get-tuple-element.76.far_ref, ...), custom_call_target="tpu_custom_call" | custom-call | flops 402653184 | bytes 1048576 | tf_op jit(solution)/shard_map/whole_shards_0/pallas_call | solution.py:536
  21.7 6.6 %collective-permute-done.2.refs_0_.refs_2_ = bf16[576,256]{1,0:T(8,128)(2,1)S(1)} collective-permute-done((bf16[576,256]{1,0:T(8,128)(2,1)S(1)}, bf16[576,256]{1,0:T(8,128)(2,1)S(1)}, u32[]{:S(2)}, u32[]{:S(2)}) %collective-permute-start.2) | collective-permute-done | bytes 294944 | tf_op jit(solution)/shard_map/ppermute | solution.py:504
  28.3 1.9 %collective-permute-start.3 = (bf16[64,256]{1,0:T(8,128)(2,1)S(1)}, bf16[64,256]{1,0:T(8,128)(2,1)S(1)}, u32[]{:S(2)}, u32[]{:S(2)}) collective-permute-start(bf16[64,256]{1,0:T(8,128)(2,1)S(1)} %get-tuple-element.104), channel_id=1, source_target_pairs={{0,4},{12,0},{1,5},{13,1},{2,6},{14,2},{3,7},{15,3},{16,20},{28,16... | collective-permute-start | bytes 98312 | tf_op jit(solution)/shard_map/ppermute | solution.py:532
  30.2 1.7 %whole_shards_1.1 = (f32[2,1,1024]{2,1,0:T(1,128)S(1)}, f32[2,1,1024]{2,1,0:T(1,128)S(1)}, f32[2,128,1024]{2,1,0:T(8,128)S(1)}) custom-call(bf16[2,256,1024]{2,1,0:T(8,128)(2,1)S(1)} %get-tuple-element.74.qt_ref, bf16[3,128,128]{2,1,0:T(8,128)(2,1)S(1)} %get-tuple-element.75.near_ref, bf16[3,256,128]{2,1,0:T(8,128)(2,1)S(1)} %get-tuple-element.76.far_ref, ...), custom_call_target="tpu_custom_call" | custom-call | flops 402653184 | bytes 1048576 | tf_op jit(solution)/shard_map/whole_shards_1/pallas_call | solution.py:536
  32.0 3.9 %collective-permute-done.3.pages_ref = bf16[64,256]{1,0:T(8,128)(2,1)S(1)} collective-permute-done((bf16[64,256]{1,0:T(8,128)(2,1)S(1)}, bf16[64,256]{1,0:T(8,128)(2,1)S(1)}, u32[]{:S(2)}, u32[]{:S(2)}) %collective-permute-start.3) | collective-permute-done | bytes 32800 | tf_op jit(solution)/shard_map/ppermute | solution.py:532
  35.9 1.1 %decode_near_pages.1 = (f32[16,8,1]{2,1,0:T(8,128)S(1)}, f32[16,8,1]{2,1,0:T(8,128)S(1)}, f32[16,8,256]{2,1,0:T(8,128)S(1)}, f32[1,8,160]{2,1,0:T(8,128)S(1)}) custom-call(s32[1]{0:T(128)} %bitcast.own_ref, s32[32]{0:T(128)S(1)} %copy-done.4, s32[8]{0:T(128)S(1)} %copy-done.5, s32[8,32]{1,0:T(8,128)S(1)} %copy-done.3, ...), custom_call_target="tpu_custom_call" | custom-call | flops 134217728 | bytes 1048576 | tf_op jit(solution)/shard_map/decode_near_pages/pallas_call | solution.py:553
  37.1 1.6 %last_scores.1 = (bf16[2,256,1024]{2,1,0:T(8,128)(2,1)S(1)}, f32[2,1,1024]{2,1,0:T(1,128)S(1)}, f32[2,128,1024]{2,1,0:T(8,128)S(1)}) custom-call(bf16[2,256,1024]{2,1,0:T(8,128)(2,1)S(1)} %get-tuple-element.74.qt_ref, bf16[3,128,128]{2,1,0:T(8,128)(2,1)S(1)} %get-tuple-element.75.near_ref, bf16[3,256,128]{2,1,0:T(8,128)(2,1)S(1)} %get-tuple-element.76.far_ref, ...), custom_call_target="tpu_custom_call" | custom-call | flops 402653184 | bytes 1048576 | tf_op jit(solution)/shard_map/last_scores/pallas_call | solution.py:568
  38.7 1.1 %decode_last_pages.1 = bf16[8,2048]{1,0:T(8,128)(2,1)} custom-call(bf16[256,256]{1,0:T(8,128)(2,1)S(1)} %collective-permute-done.5.stretch_ref, bf16[64,256]{1,0:T(8,128)(2,1)S(1)} %collective-permute-done.3.pages_ref, f32[1,8,160]{2,1,0:T(8,128)S(1)} %get-tuple-element.133.tally_ref, bf16[128,256]{1,0:T(8,128)(2,1)S(1)} %get-tuple-element.103.refs_3_.wide_ref, ...), custom_call_target="tpu_custom_call" | custom-call | flops 67108864 | bytes 1048576 | tf_op jit(solution)/shard_map/decode_last_pages/pallas_call | solution.py:579
  39.8 1.1 %last_values.1 = bf16[128,2048]{1,0:T(8,128)(2,1)} custom-call(bf16[2,256,1024]{2,1,0:T(8,128)(2,1)S(1)} %get-tuple-element.131.weights_ref, f32[2,1,1024]{2,1,0:T(1,128)S(1)} %get-tuple-element.142.total_ref, f32[2,128,1024]{2,1,0:T(8,128)S(1)} %get-tuple-element.143.accum_ref, bf16[256,256]{1,0:T(8,128)(2,1)S(1)} %collective-permute-done.6.values_ref), custom_call_target="tpu_custom_call" | custom-call | flops 134217728 | bytes 1048576 | tf_op jit(solution)/shard_map/last_values/pallas_call | solution.py:590
  (15 shorter events, 0.0 us)
Async XLA Ops:
  0.6 4.8 %copy-start.6 = (bf16[128,2048]{1,0:T(8,128)(2,1)S(1)}, bf16[128,2048]{1,0:T(8,128)(2,1)}, u32[]{:S(2)}) copy-start(bf16[128,2048]{1,0:T(8,128)(2,1)} %q_ref.2) | copy-start | bytes 1572868
  1.7 14.7 %collective-permute-start = (bf16[768,256]{1,0:T(8,128)(2,1)S(1)}, bf16[768,256]{1,0:T(8,128)(2,1)S(1)}, u32[]{:S(2)}, u32[]{:S(2)}) collective-permute-start(bf16[768,256]{1,0:T(8,128)(2,1)S(1)} %pad_maximum_fusion.shard_ref.rest_ref), channel_id=1, source_target_pairs={{0,4},{4,8},{8,12},{12,0},{1,5},{5,9},{9,13},{13,1},{2,6},{6,10},{... | collective-permute-start | bytes 1179656 | tf_op jit(solution)/shard_map/ppermute | solution.py:436
  5.5 0.7 %copy-start.4 = (s32[32]{0:T(128)S(1)}, s32[32]{0:T(128)}, u32[]{:S(2)}) copy-start(s32[32]{0:T(128)} %targets_ref.5) | copy-start | bytes 388
  6.1 2.5 %copy-start = (bf16[128,16,256]{2,1,0:T(8,128)(2,1)S(1)}, bf16[128,16,256]{2,1,0:T(8,128)(2,1)}, u32[]{:S(2)}) copy-start(bf16[128,16,256]{2,1,0:T(8,128)(2,1)} %pool_k.1) | copy-start | bytes 3145732
  6.1 2.5 %copy-start.1 = (bf16[128,16,256]{2,1,0:T(8,128)(2,1)S(1)}, bf16[128,16,256]{2,1,0:T(8,128)(2,1)}, u32[]{:S(2)}) copy-start(bf16[128,16,256]{2,1,0:T(8,128)(2,1)} %pool_v.1) | copy-start | bytes 3145732
  8.5 0.8 %copy-start.2 = (bf16[8,2048]{1,0:T(8,128)(2,1)S(1)}, bf16[8,2048]{1,0:T(8,128)(2,1)}, u32[]{:S(2)}) copy-start(bf16[8,2048]{1,0:T(8,128)(2,1)} %q_ref.3) | copy-start | bytes 98308
  8.5 0.8 %copy-start.3 = (s32[8,32]{1,0:T(8,128)S(1)}, s32[8,32]{1,0:T(8,128)}, u32[]{:S(2)}) copy-start(s32[8,32]{1,0:T(8,128)} %lists_ref.3) | copy-start | bytes 3076
  8.5 0.7 %copy-start.5 = (s32[8]{0:T(128)S(1)}, s32[8]{0:T(128)}, u32[]{:S(2)}) copy-start(s32[8]{0:T(128)} %length_ref.3) | copy-start | bytes 100
  11.2 17.1 %collective-permute-start.1 = (bf16[768,256]{1,0:T(8,128)(2,1)S(1)}, bf16[768,256]{1,0:T(8,128)(2,1)S(1)}, u32[]{:S(2)}, u32[]{:S(2)}) collective-permute-start(bf16[768,256]{1,0:T(8,128)(2,1)S(1)} %pad_maximum_fusion.shard_ref.rest_ref), channel_id=1, source_target_pairs={{0,12},{1,13},{2,14},{3,15},{16,28},{17,29},{18,30},{19,31}} | collective-permute-start | bytes 1179656 | tf_op jit(solution)/shard_map/ppermute | solution.py:505
  15.1 13.2 %collective-permute-start.2 = (bf16[576,256]{1,0:T(8,128)(2,1)S(1)}, bf16[576,256]{1,0:T(8,128)(2,1)S(1)}, u32[]{:S(2)}, u32[]{:S(2)}) collective-permute-start(bf16[576,256]{1,0:T(8,128)(2,1)S(1)} %rows_to_send_down.1), channel_id=1, source_target_pairs={{4,0},{8,4},{12,8},{5,1},{9,5},{13,9},{6,2},{10,6},{14,10},{7,3},{... | collective-permute-start | bytes 884744 | tf_op jit(solution)/shard_map/ppermute | solution.py:504
  16.6 20.5 %collective-permute-start.4 = (bf16[256,256]{1,0:T(8,128)(2,1)S(1)}, bf16[256,256]{1,0:T(8,128)(2,1)S(1)}, u32[]{:S(2)}, u32[]{:S(2)}) collective-permute-start(bf16[256,256]{1,0:T(8,128)(2,1)S(1)} %get-tuple-element.129), channel_id=1, source_target_pairs={{0,4},{4,8},{8,12},{12,0},{1,5},{5,9},{9,13},{13,1},{2,6},{6,10},{... | collective-permute-start | bytes 393224 | tf_op jit(solution)/shard_map/ppermute | solution.py:436
  19.3 17.8 %collective-permute-start.5 = (bf16[256,256]{1,0:T(8,128)(2,1)S(1)}, bf16[256,256]{1,0:T(8,128)(2,1)S(1)}, u32[]{:S(2)}, u32[]{:S(2)}) collective-permute-start(bf16[256,256]{1,0:T(8,128)(2,1)S(1)} %get-tuple-element.130), channel_id=1, source_target_pairs={{4,8},{8,12},{5,9},{9,13},{6,10},{10,14},{7,11},{11,15},{20,24},{2... | collective-permute-start | bytes 393224 | tf_op jit(solution)/shard_map/ppermute | solution.py:531
  28.3 11.5 %collective-permute-start.6 = (bf16[256,256]{1,0:T(8,128)(2,1)S(1)}, bf16[256,256]{1,0:T(8,128)(2,1)S(1)}, u32[]{:S(2)}, u32[]{:S(2)}) collective-permute-start(bf16[256,256]{1,0:T(8,128)(2,1)S(1)} %get-tuple-element.144), channel_id=1, source_target_pairs={{0,4},{4,8},{8,12},{12,0},{1,5},{5,9},{9,13},{13,1},{2,6},{6,10},{... | collective-permute-start | bytes 393224 | tf_op jit(solution)/shard_map/ppermute | solution.py:436
  28.3 7.6 %collective-permute-start.3 = (bf16[64,256]{1,0:T(8,128)(2,1)S(1)}, bf16[64,256]{1,0:T(8,128)(2,1)S(1)}, u32[]{:S(2)}, u32[]{:S(2)}) collective-permute-start(bf16[64,256]{1,0:T(8,128)(2,1)S(1)} %get-tuple-element.104), channel_id=1, source_target_pairs={{0,4},{12,0},{1,5},{13,1},{2,6},{14,2},{3,7},{15,3},{16,20},{28,16... | collective-permute-start | bytes 98312 | tf_op jit(solution)/shard_map/ppermute | solution.py:532

commit v18 on v10

--- a/solution.py
+++ b/solution.py
@@ -210,11 +210,7 @@
         shard = shard_of(own, hop, count)
         near_ref[place] = stretch_mask(shard, own, tokens)
         far_ref[place] = cache_mask(shard, limit, c_rows, tokens)
-    onward = 1 if hops[-1] < 0 else -1
-    pages = tokens // PAGE
-    one, two = sent_pages(
-        targets_ref, shard_of(own, hops[-1] + onward, count), shard_of(own, onward, count), pages
-    )
+    one, two = sent_pages(targets_ref, own, shard_of(own, -hops[-1], count), tokens // PAGE)
     row = lax.broadcasted_iota(jnp.int32, pick_ref.shape, 0)
     token = lax.broadcasted_iota(jnp.int32, pick_ref.shape, 1)
     sent = ((row < PAGE) & (one >= 0) & (token == row + one * PAGE)) | (
@@ -270,41 +266,42 @@
     attend(qt_ref, keys, values_t, (high_in, total_in, accum_in), outs)
 
 
-def split_kernel(pick_ref, shard_ref, keys_ref, stretch_ref, values_ref, pages_ref):
+def pick_kernel(pick_ref, shard_ref, pages_ref):
     tokens = pick_ref.shape[1]
-    half = shard_ref.shape[0] // 2
     sent = pick_ref.shape[0]
+    for place, start in enumerate((0, shard_ref.shape[0] // 2)):
+        rows = jnp.dot(pick_ref[...], shard_ref[start : start + tokens], preferred_element_type=jnp.float32)
+        pages_ref[place * sent : (place + 1) * sent] = rows.astype(jnp.bfloat16)
+
+
+def split_kernel(shard_ref, keys_ref, stretch_ref, values_ref):
+    c_rows = keys_ref.shape[0]
+    tokens = stretch_ref.shape[0] // 2
+    half = tokens + c_rows
     for place, start in enumerate((0, half)):
         stretch_ref[place * tokens : (place + 1) * tokens] = shard_ref[start : start + tokens]
-        rows = jnp.dot(pick_ref[...], shard_ref[start : start + tokens], preferred_element_type=jnp.float32)
-        pages_ref[place * sent : (place + 1) * sent] = rows.astype(jnp.bfloat16)
     keys_ref[...] = shard_ref[tokens:half]
     values_ref[...] = shard_ref[half + tokens :]
 
 
-def pages_kernel(count, hops, tokens, pool, own_ref, targets_ref, length_ref, lists_ref, *refs):
-    shard_refs, refs = refs[: len(hops) + 1], refs[len(hops) + 1 :]
-    wide_ref, dec_high, dec_total, dec_mixed, dec_out = refs
+def new_pages_kernel(count, hops, tokens, pool, own_ref, targets_ref, length_ref, lists_ref, *refs):
+    shard_refs, refs = refs[: len(hops) - 1], refs[len(hops) - 1 :]
+    pages_ref, wide_ref, dec_high, dec_total, dec_mixed, dec_out = refs
     own = own_ref[0]
-    pages = tokens // PAGE
     lists = lists_ref[...]
     lengths = length_column(length_ref)
     parts = []
-    for hop, ref in zip(hops[:-1], shard_refs):
+    for hop, ref in zip(hops, shard_refs):
         half = ref.shape[0] // 2
         slot = slot_row(targets_ref, shard_of(own, hop, count), own, tokens, pool)
         parts.append((ref[:tokens], ref[half : half + tokens], tally_of(lists, lengths, slot)))
-    stretch_ref, pages_ref = shard_refs[-2:]
-    shard = shard_of(own, hops[-1], count)
-    attended = shard < own
-    slot = jnp.where(attended, slot_row(targets_ref, shard, own, tokens, pool), -1)
-    parts.append((stretch_ref[:tokens], stretch_ref[tokens:], tally_of(lists, lengths, slot)))
     sent = pages_ref.shape[0] // 2
-    slot = jnp.where(attended, -1, sent_slots(targets_ref, shard, own, pages, pool))
+    slot = sent_slots(targets_ref, shard_of(own, hops[-1], count), own, tokens // PAGE, pool)
     parts.append((pages_ref[:sent], pages_ref[sent:], tally_of(lists, lengths, slot)))
     _, total, mixed = decode_attend(wide_ref[...], parts, (dec_high[...], dec_total[...], dec_mixed[...]))
+    share = 1.0 / total
     for head in range(dec_high.shape[0]):
-        piece = mixed[head, :, features(head // GROUP)] / total[head]
+        piece = mixed[head, :, features(head // GROUP)] * share[head]
         dec_out[:, features(head)] = piece.astype(jnp.bfloat16)
 
 
@@ -358,6 +355,7 @@
         copies.append(copy)
 
     walk(blocks_of(weights_ref), first, second)
+
     for copy in copies:
         copy.wait()
 
@@ -436,14 +434,14 @@
         name="own_shard",
     )(own_array, prefix_length, page_targets, queries, shard[0])
 
+    dec_shapes = (
+        shape((heads, dec_rows, 1), f32),
+        shape((heads, dec_rows, 1), f32),
+        shape((heads, dec_rows, kv_width), f32),
+    )
     wide, *dec_state = pl.pallas_call(
         held_kernel,
-        out_shape=(
-            shape((heads * dec_rows, kv_width), bf16),
-            shape((heads, dec_rows, 1), f32),
-            shape((heads, dec_rows, 1), f32),
-            shape((heads, dec_rows, kv_width), f32),
-        ),
+        out_shape=(shape((heads * dec_rows, kv_width), bf16),) + dec_shapes,
         in_specs=[SMEM] * 3 + [VMEM] * 5,
         out_specs=(VMEM,) * 4,
         compiler_params=params,
@@ -467,48 +465,55 @@
             shape((c_rows, kv_width), bf16),
             shape((2 * tokens, kv_width), bf16),
             shape((c_rows, kv_width), bf16),
-            shape((2 * SEND_CAP * PAGE, kv_width), bf16),
         ),
+        in_specs=[VMEM],
+        out_specs=(VMEM,) * 3,
+        compiler_params=params,
+        name="pieces_to_send_on",
+    )(nearer)
+    far_pages = pl.pallas_call(
+        pick_kernel,
+        out_shape=shape((2 * SEND_CAP * PAGE, kv_width), bf16),
         in_specs=[VMEM] * 2,
-        out_specs=(VMEM,) * 4,
-        compiler_params=params,
-        name="pieces_to_send_on",
-    )(pick, nearer)
+        out_specs=VMEM,
+        compiler_params=params,
+        name="pages_to_send",
+    )(pick, shard[0])
+    far_pages = lax.ppermute(far_pages, "ctx", [(i, (i - hop) % count) for i in range(count)])
     last_keys = send(pieces[0], hop)
-    attending, others = [], []
-    for pair in up_pairs if hop < 0 else down_pairs:
-        (attending if (pair[1] + hop) % count < pair[1] else others).append(pair)
+    attending = [pair for pair in (up_pairs if hop < 0 else down_pairs) if (pair[1] + hop) % count < pair[1]]
     last_stretch = lax.ppermute(pieces[1], "ctx", attending)
-    last_pages = lax.ppermute(pieces[3], "ctx", others)
-    last_values = send(pieces[2], hop)
-
-    for first in range(len(hops) - 1):
-        places = [first]
+
+    for place, hop in enumerate(hops[:-1]):
+        if place == 1:
+            last_piece, far_pages, state = lax.optimization_barrier((pieces[2], far_pages, state))
+            last_values = send(last_piece, hops[-1])
         state = pl.pallas_call(
-            functools.partial(hop_kernel, places),
+            functools.partial(hop_kernel, [place]),
             out_shape=state_shapes,
-            in_specs=[VMEM] * (6 + len(places)),
+            in_specs=[VMEM] * 7,
             out_specs=(VMEM,) * 3,
             compiler_params=params,
-            cost_estimate=cost((c_rows + tokens) * len(places)),
-            name="whole_shards_" + str(first),
-        )(qt, near, far, *state, *[shard[hops[place]] for place in places])
+            cost_estimate=cost(half),
+            name="whole_shards_" + str(place),
+        )(qt, near, far, *state, shard[hop])
 
     final = len(hops) - 1
+    dec_state, state = lax.optimization_barrier((dec_state, state))
     decoded = pl.pallas_call(
-        functools.partial(pages_kernel, count, hops, tokens, pool),
+        functools.partial(new_pages_kernel, count, hops, tokens, pool),
         out_shape=shape(decode_queries.shape, bf16),
-        in_specs=[SMEM] * 3 + [VMEM] * (6 + len(hops)),
+        in_specs=[SMEM] * 3 + [VMEM] * (6 + len(hops) - 1),
         out_specs=VMEM,
         compiler_params=params,
         cost_estimate=cost(tokens),
         name="decode_new_pages",
     )(
-        own_array, page_targets, context_length, page_lists, *[shard[hop] for hop in hops[:-1]], last_stretch, last_pages,
+        own_array, page_targets, context_length, page_lists, *[shard[hop] for hop in hops[:-1]], far_pages,
         wide, *dec_state,
     )
-
     decoded, state = lax.optimization_barrier((decoded, state))
+
     weights, total, accum = pl.pallas_call(
         functools.partial(score_kernel, final),
         out_shape=(shape((kv_local, c_rows, rows), bf16),) + state_shapes[1:],

time: 36.7 us -> 34.6 us (0.943)
  starting transfers between devices: 11.9 us -> 10.3 us
    ppermute x4, waiting for transfers between devices: 1.16 us -> 0.01 us  [send(): return lax.ppermute(array, 'ctx', up_pairs if hop < 0 else down_pairs)]
    ppermute x1, starting transfers between devices: 1.96 us -> 1.01 us  [per_device(): lax.ppermute(far_pages, 'ctx', [(i, (i - hop) % count) for i in range(cou...]
    ppermute x1, waiting for transfers between devices: 5.4 us -> 6.2 us  [per_device(): lax.ppermute(far_pages, 'ctx', [(i, (i - hop) % count) for i in range(cou...]
    ppermute x4, starting transfers between devices: 9.24 us -> 8.63 us  [send(): return lax.ppermute(array, 'ctx', up_pairs if hop < 0 else down_pairs)]
    pallas_call x3 -> x4, Pallas kernels: 5.28 us -> 5.34 us  [the longest x2 3.45 us: per_device(): pl.pallas_call(functools.partial(hop_kernel, [place]), out_shape=state_sh...]
  transfers between devices with their start and end apart: 6 -> 6, of which waited for: 3 -> 1; matrix products, arithmetic and copies ran while one was open for 0% -> 0% of each run, Pallas kernels for 31% -> 33%
where the time goes in v18:
time: 34.6 us; the launch traced here: 34.4 us
  Pallas kernels  12.3 us (36%)
  starting transfers between devices  10.3 us (30%)
  waiting for transfers between devices  6.21 us (18%)
  local copies, waits for them, and re-layouts  3.1 us (9%)
  between operations  1.41 us (4%)
  other arithmetic  1.03 us (3%)
    ppermute x4, starting transfers between devices, send(): return lax.ppermute(array, 'ctx', up_pairs if hop < 0 else down_pairs)  8.63 us
    ppermute x1, waiting for transfers between devices, per_device(): lax.ppermute(far_pages, 'ctx', [(i, (i - hop) % count) for i in range(cou...  6.2 us
    pallas_call x2, Pallas kernels, per_device(): pl.pallas_call(functools.partial(hop_kernel, [place]), out_shape=state_sh...  3.45 us
    unnamed x14, local copies, waits for them, and re-layouts  3.1 us
    pallas_call x1, Pallas kernels, per_device(): pl.pallas_call(functools.partial(own_kernel, count, hops), out_shape=(sha...  2.36 us
    pallas_call x1, Pallas kernels, per_device(): pl.pallas_call(held_kernel, out_shape=(shape((heads * dec_rows, kv_width)...  1.86 us
    pallas_call x1, Pallas kernels, per_device(): pl.pallas_call(functools.partial(new_pages_kernel, count, hops, tokens, p...  1.76 us
    pallas_call x1, Pallas kernels, per_device(): pl.pallas_call(functools.partial(score_kernel, final), out_shape=(shape((...  1.6 us
  transfers between devices with their start and end apart: 6, of which 1 were waited for; matrix products, arithmetic and copies ran while one was open for 0% of the time, Pallas kernels for 33%

profile of v18, /device:TPU:0, one launch (start us, length us, event | category | flops | bytes accessed | tf_op | source)
XLA Modules:
  0.0 34.4 jit_solution(6246239874281496888)
XLA Ops:
  0.6 1.0 %pad_maximum_fusion.shard_ref.rest_ref = bf16[768,256]{1,0:T(8,128)(2,1)S(1)} fusion(bf16[256,256]{1,0:T(8,128)(2,1)} %param.16, bf16[128,256]{1,0:T(8,128)(2,1)} %param.14, bf16[256,256]{1,0:T(8,128)(2,1)} %param.15, bf16[128,256]{1,0:T(8,128)(2,1)} %param.13), kind=kLoop, calls=%fused_computation | loop fusion | flops 1572864 | bytes 786432 | tf_op jit(solution)/shard_map/max | solution.py:413
  1.7 3.1 %collective-permute-start = (bf16[768,256]{1,0:T(8,128)(2,1)S(1)}, bf16[768,256]{1,0:T(8,128)(2,1)S(1)}, u32[]{:S(2)}, u32[]{:S(2)}) collective-permute-start(bf16[768,256]{1,0:T(8,128)(2,1)S(1)} %pad_maximum_fusion.shard_ref.rest_ref), channel_id=1, source_target_pairs={{0,4},{4,8},{8,12},{12,0},{1,5},{5,9},{9,13},{13,1},{2,6},{6,10},{... | collective-permute-start | bytes 1179656 | tf_op jit(solution)/shard_map/ppermute | solution.py:398
  5.4 0.0 copy-start.4
  5.4 0.0 copy-start.5
  5.5 0.6 %copy-done.4 = s32[32]{0:T(128)S(1)} copy-done((s32[32]{0:T(128)S(1)}, s32[32]{0:T(128)}, u32[]{:S(2)}) %copy-start.4) | copy-done | bytes 152
  6.1 0.0 copy-done.5
  6.1 1.2 %copy-done = bf16[128,16,256]{2,1,0:T(8,128)(2,1)S(1)} copy-done((bf16[128,16,256]{2,1,0:T(8,128)(2,1)S(1)}, bf16[128,16,256]{2,1,0:T(8,128)(2,1)}, u32[]{:S(2)}) %copy-start) | copy-done | bytes 1048600
  7.3 1.2 %copy-done.1 = bf16[128,16,256]{2,1,0:T(8,128)(2,1)S(1)} copy-done((bf16[128,16,256]{2,1,0:T(8,128)(2,1)S(1)}, bf16[128,16,256]{2,1,0:T(8,128)(2,1)}, u32[]{:S(2)}) %copy-start.1) | copy-done | bytes 1048600
  8.5 1.9 %decode_held_pages.1 = (bf16[128,256]{1,0:T(8,128)(2,1)S(1)}, f32[16,8,1]{2,1,0:T(8,128)S(1)}, f32[16,8,1]{2,1,0:T(8,128)S(1)}, f32[16,8,256]{2,1,0:T(8,128)S(1)}) custom-call(s32[1]{0:T(128)} %bitcast.own_ref, s32[32]{0:T(128)S(1)} %copy-done.4, s32[8]{0:T(128)S(1)} %copy-done.5, bf16[8,2048]{1,0:T(8,128)(2,1)S(1)} %copy-done.2, s32[8,32]{1,0:T(8,128)S(1)} %copy-done.3, ...), custom_call_target="tpu_custom_call" | custom-call | flops 268435456 | bytes 2097152 | tf_op jit(solution)/shard_map/decode_held_pages/pallas_call | solution.py:442
  10.4 2.4 %own_shard.1 = (bf16[2,256,1024]{2,1,0:T(8,128)(2,1)S(1)}, bf16[3,128,128]{2,1,0:T(8,128)(2,1)S(1)}, bf16[3,256,128]{2,1,0:T(8,128)(2,1)S(1)}, bf16[32,128]{1,0:...) custom-call(s32[1]{0:T(128)} %bitcast.own_ref, ...), custom_call_target="tpu_custom_call" | custom-call | flops 402653184 | bytes 1048576 | tf_op jit(solution)/shard_map/own_shard/pallas_call | solution.py:421
  12.8 2.1 %collective-permute-start.1 = (bf16[768,256]{1,0:T(8,128)(2,1)S(1)}, bf16[768,256]{1,0:T(8,128)(2,1)S(1)}, u32[]{:S(2)}, u32[]{:S(2)}) collective-permute-start(bf16[768,256]{1,0:T(8,128)(2,1)S(1)} %pad_maximum_fusion.shard_ref.rest_ref), channel_id=1, source_target_pairs={{0,12},{4,0},{8,4},{12,8},{1,13},{5,1},{9,5},{13,9},{2,14},{6,2},{... | collective-permute-start | bytes 1179656 | tf_op jit(solution)/shard_map/ppermute | solution.py:398
  14.9 0.1 pages_to_send.1
  15.0 1.0 %collective-permute-start.2 = (bf16[64,256]{1,0:T(8,128)(2,1)S(1)}, bf16[64,256]{1,0:T(8,128)(2,1)S(1)}, u32[]{:S(2)}, u32[]{:S(2)}) collective-permute-start(bf16[64,256]{1,0:T(8,128)(2,1)S(1)} %pages_to_send.1), channel_id=1, source_target_pairs={{0,8},{4,12},{8,0},{12,4},{1,9},{5,13},{9,1},{13,5},{2,10},{6,14},... | collective-permute-start | bytes 98312 | tf_op jit(solution)/shard_map/ppermute | solution.py:482
  16.1 1.6 %collective-permute-start.3 = (bf16[256,256]{1,0:T(8,128)(2,1)S(1)}, bf16[256,256]{1,0:T(8,128)(2,1)S(1)}, u32[]{:S(2)}, u32[]{:S(2)}) collective-permute-start(bf16[256,256]{1,0:T(8,128)(2,1)S(1)} %get-tuple-element.99), channel_id=1, source_target_pairs={{0,4},{4,8},{8,12},{12,0},{1,5},{5,9},{9,13},{13,1},{2,6},{6,10},{... | collective-permute-start | bytes 393224 | tf_op jit(solution)/shard_map/ppermute | solution.py:398
  17.7 0.7 %collective-permute-start.4 = (bf16[256,256]{1,0:T(8,128)(2,1)S(1)}, bf16[256,256]{1,0:T(8,128)(2,1)S(1)}, u32[]{:S(2)}, u32[]{:S(2)}) collective-permute-start(bf16[256,256]{1,0:T(8,128)(2,1)S(1)} %get-tuple-element.100), channel_id=1, source_target_pairs={{4,8},{8,12},{5,9},{9,13},{6,10},{10,14},{7,11},{11,15},{20,24},{2... | collective-permute-start | bytes 393224 | tf_op jit(solution)/shard_map/ppermute | solution.py:485
  18.4 1.7 %whole_shards_0.1 = (f32[2,1,1024]{2,1,0:T(1,128)S(1)}, f32[2,1,1024]{2,1,0:T(1,128)S(1)}, f32[2,128,1024]{2,1,0:T(8,128)S(1)}) custom-call(bf16[2,256,1024]{2,1,0:T(8,128)(2,1)S(1)} %get-tuple-element.54.qt_ref, bf16[3,128,128]{2,1,0:T(8,128)(2,1)S(1)} %get-tuple-element.55.near_ref, bf16[3,256,128]{2,1,0:T(8,128)(2,1)S(1)} %get-tuple-element.56.far_ref, ...), custom_call_target="tpu_custom_call" | custom-call | flops 402653184 | bytes 1048576 | tf_op jit(solution)/shard_map/whole_shards_0/pallas_call | solution.py:491
  20.1 6.2 %collective-permute-done.2.refs_2_ = bf16[64,256]{1,0:T(8,128)(2,1)S(1)} collective-permute-done((bf16[64,256]{1,0:T(8,128)(2,1)S(1)}, bf16[64,256]{1,0:T(8,128)(2,1)S(1)}, u32[]{:S(2)}, u32[]{:S(2)}) %collective-permute-start.2) | collective-permute-done | bytes 32800 | tf_op jit(solution)/shard_map/ppermute | solution.py:482
  26.3 1.8 %collective-permute-start.5 = (bf16[256,256]{1,0:T(8,128)(2,1)S(1)}, bf16[256,256]{1,0:T(8,128)(2,1)S(1)}, u32[]{:S(2)}, u32[]{:S(2)}) collective-permute-start(bf16[256,256]{1,0:T(8,128)(2,1)S(1)} %get-tuple-element.104), channel_id=1, source_target_pairs={{0,4},{4,8},{8,12},{12,0},{1,5},{5,9},{9,13},{13,1},{2,6},{6,10},{... | collective-permute-start | bytes 393224 | tf_op jit(solution)/shard_map/ppermute | solution.py:398
  28.1 0.0 collective-permute-done.1.refs_0_.refs_1_
  28.1 1.7 %whole_shards_1.1 = (f32[2,1,1024]{2,1,0:T(1,128)S(1)}, f32[2,1,1024]{2,1,0:T(1,128)S(1)}, f32[2,128,1024]{2,1,0:T(8,128)S(1)}) custom-call(bf16[2,256,1024]{2,1,0:T(8,128)(2,1)S(1)} %get-tuple-element.54.qt_ref, bf16[3,128,128]{2,1,0:T(8,128)(2,1)S(1)} %get-tuple-element.55.near_ref, bf16[3,256,128]{2,1,0:T(8,128)(2,1)S(1)} %get-tuple-element.56.far_ref, ...), custom_call_target="tpu_custom_call" | custom-call | flops 402653184 | bytes 1048576 | tf_op jit(solution)/shard_map/whole_shards_1/pallas_call | solution.py:491
  29.8 1.8 %decode_new_pages.1 = bf16[8,2048]{1,0:T(8,128)(2,1)} custom-call(s32[1]{0:T(128)} %bitcast.own_ref, s32[32]{0:T(128)S(1)} %copy-done.4, s32[8]{0:T(128)S(1)} %copy-done.5, s32[8,32]{1,0:T(8,128)S(1)} %copy-done.3, bf16[768,256]{1,0:T(8,128)(2,1)S(1)} %collective-permute-done.shard_ref.refs_0_, bf16[768,256]{1,0:T(8,128)(2,1)S(1)} %collective-permute-done.1.refs_0_.refs_1_, ...), custom_call_target="tpu_custom_call" | custom-call | flops 134217728 | bytes 1048576 | tf_op jit(solution)/shard_map/decode_new_pages/pallas_call | solution.py:503
  31.6 0.0 collective-permute-done.3.keys_ref
  31.6 1.6 %last_scores.1 = (bf16[2,256,1024]{2,1,0:T(8,128)(2,1)S(1)}, f32[2,1,1024]{2,1,0:T(1,128)S(1)}, f32[2,128,1024]{2,1,0:T(8,128)S(1)}) custom-call(bf16[2,256,1024]{2,1,0:T(8,128)(2,1)S(1)} %get-tuple-element.54.qt_ref, bf16[3,128,128]{2,1,0:T(8,128)(2,1)S(1)} %get-tuple-element.55.near_ref, bf16[3,256,128]{2,1,0:T(8,128)(2,1)S(1)} %get-tuple-element.56.far_ref, ...), custom_call_target="tpu_custom_call" | custom-call | flops 402653184 | bytes 1048576 | tf_op jit(solution)/shard_map/last_scores/pallas_call | solution.py:517
  33.2 1.1 %last_values.1 = bf16[128,2048]{1,0:T(8,128)(2,1)} custom-call(bf16[2,256,1024]{2,1,0:T(8,128)(2,1)S(1)} %get-tuple-element.101.weights_ref, f32[2,1,1024]{2,1,0:T(1,128)S(1)} %get-tuple-element.102.total_ref, f32[2,128,1024]{2,1,0:T(8,128)S(1)} %get-tuple-element.103.accum_ref, bf16[256,256]{1,0:T(8,128)(2,1)S(1)} %collective-permute-done.5.values_ref), custom_call_target="tpu_custom_call" | custom-call | flops 134217728 | bytes 1048576 | tf_op jit(solution)/shard_map/last_values/pallas_call | solution.py:527
  (12 shorter events, 0.0 us)
Async XLA Ops:
  0.6 4.8 %copy-start.2 = (bf16[8,2048]{1,0:T(8,128)(2,1)S(1)}, bf16[8,2048]{1,0:T(8,128)(2,1)}, u32[]{:S(2)}) copy-start(bf16[8,2048]{1,0:T(8,128)(2,1)} %q_ref.3) | copy-start | bytes 98308
  1.7 14.4 %collective-permute-start = (bf16[768,256]{1,0:T(8,128)(2,1)S(1)}, bf16[768,256]{1,0:T(8,128)(2,1)S(1)}, u32[]{:S(2)}, u32[]{:S(2)}) collective-permute-start(bf16[768,256]{1,0:T(8,128)(2,1)S(1)} %pad_maximum_fusion.shard_ref.rest_ref), channel_id=1, source_target_pairs={{0,4},{4,8},{8,12},{12,0},{1,5},{5,9},{9,13},{13,1},{2,6},{6,10},{... | collective-permute-start | bytes 1179656 | tf_op jit(solution)/shard_map/ppermute | solution.py:398
  4.8 0.7 %copy-start.3 = (s32[8,32]{1,0:T(8,128)S(1)}, s32[8,32]{1,0:T(8,128)}, u32[]{:S(2)}) copy-start(s32[8,32]{1,0:T(8,128)} %lists_ref.3) | copy-start | bytes 3076
  5.4 0.7 %copy-start.4 = (s32[32]{0:T(128)S(1)}, s32[32]{0:T(128)}, u32[]{:S(2)}) copy-start(s32[32]{0:T(128)} %targets_ref.5) | copy-start | bytes 388
  5.4 0.7 %copy-start.5 = (s32[8]{0:T(128)S(1)}, s32[8]{0:T(128)}, u32[]{:S(2)}) copy-start(s32[8]{0:T(128)} %length_ref.3) | copy-start | bytes 100
  6.1 1.2 %copy-start = (bf16[128,16,256]{2,1,0:T(8,128)(2,1)S(1)}, bf16[128,16,256]{2,1,0:T(8,128)(2,1)}, u32[]{:S(2)}) copy-start(bf16[128,16,256]{2,1,0:T(8,128)(2,1)} %pool_k.1) | copy-start | bytes 3145732
  7.3 1.2 %copy-start.1 = (bf16[128,16,256]{2,1,0:T(8,128)(2,1)S(1)}, bf16[128,16,256]{2,1,0:T(8,128)(2,1)}, u32[]{:S(2)}) copy-start(bf16[128,16,256]{2,1,0:T(8,128)(2,1)} %pool_v.1) | copy-start | bytes 3145732
  8.5 1.9 %copy-start.6 = (bf16[128,2048]{1,0:T(8,128)(2,1)S(1)}, bf16[128,2048]{1,0:T(8,128)(2,1)}, u32[]{:S(2)}) copy-start(bf16[128,2048]{1,0:T(8,128)(2,1)} %q_ref.2) | copy-start | bytes 1572868
  12.8 15.3 %collective-permute-start.1 = (bf16[768,256]{1,0:T(8,128)(2,1)S(1)}, bf16[768,256]{1,0:T(8,128)(2,1)S(1)}, u32[]{:S(2)}, u32[]{:S(2)}) collective-permute-start(bf16[768,256]{1,0:T(8,128)(2,1)S(1)} %pad_maximum_fusion.shard_ref.rest_ref), channel_id=1, source_target_pairs={{0,12},{4,0},{8,4},{12,8},{1,13},{5,1},{9,5},{13,9},{2,14},{6,2},{... | collective-permute-start | bytes 1179656 | tf_op jit(solution)/shard_map/ppermute | solution.py:398
  15.0 11.3 %collective-permute-start.2 = (bf16[64,256]{1,0:T(8,128)(2,1)S(1)}, bf16[64,256]{1,0:T(8,128)(2,1)S(1)}, u32[]{:S(2)}, u32[]{:S(2)}) collective-permute-start(bf16[64,256]{1,0:T(8,128)(2,1)S(1)} %pages_to_send.1), channel_id=1, source_target_pairs={{0,8},{4,12},{8,0},{12,4},{1,9},{5,13},{9,1},{13,5},{2,10},{6,14},... | collective-permute-start | bytes 98312 | tf_op jit(solution)/shard_map/ppermute | solution.py:482
  16.1 15.5 %collective-permute-start.3 = (bf16[256,256]{1,0:T(8,128)(2,1)S(1)}, bf16[256,256]{1,0:T(8,128)(2,1)S(1)}, u32[]{:S(2)}, u32[]{:S(2)}) collective-permute-start(bf16[256,256]{1,0:T(8,128)(2,1)S(1)} %get-tuple-element.99), channel_id=1, source_target_pairs={{0,4},{4,8},{8,12},{12,0},{1,5},{5,9},{9,13},{13,1},{2,6},{6,10},{... | collective-permute-start | bytes 393224 | tf_op jit(solution)/shard_map/ppermute | solution.py:398
  17.7 13.9 %collective-permute-start.4 = (bf16[256,256]{1,0:T(8,128)(2,1)S(1)}, bf16[256,256]{1,0:T(8,128)(2,1)S(1)}, u32[]{:S(2)}, u32[]{:S(2)}) collective-permute-start(bf16[256,256]{1,0:T(8,128)(2,1)S(1)} %get-tuple-element.100), channel_id=1, source_target_pairs={{4,8},{8,12},{5,9},{9,13},{6,10},{10,14},{7,11},{11,15},{20,24},{2... | collective-permute-start | bytes 393224 | tf_op jit(solution)/shard_map/ppermute | solution.py:485
  26.3 6.9 %collective-permute-start.5 = (bf16[256,256]{1,0:T(8,128)(2,1)S(1)}, bf16[256,256]{1,0:T(8,128)(2,1)S(1)}, u32[]{:S(2)}, u32[]{:S(2)}) collective-permute-start(bf16[256,256]{1,0:T(8,128)(2,1)S(1)} %get-tuple-element.104), channel_id=1, source_target_pairs={{0,4},{4,8},{8,12},{12,0},{1,5},{5,9},{9,13},{13,1},{2,6},{6,10},{... | collective-permute-start | bytes 393224 | tf_op jit(solution)/shard_map/ppermute | solution.py:398

commit v19 on v16

--- a/solution.py
+++ b/solution.py
@@ -210,11 +210,7 @@
         shard = shard_of(own, hop, count)
         near_ref[place] = stretch_mask(shard, own, tokens)
         far_ref[place] = cache_mask(shard, limit, c_rows, tokens)
-    onward = 1 if hops[-1] < 0 else -1
-    pages = tokens // PAGE
-    one, two = sent_pages(
-        targets_ref, shard_of(own, hops[-1] + onward, count), shard_of(own, onward, count), pages
-    )
+    one, two = sent_pages(targets_ref, own, shard_of(own, -hops[-1], count), tokens // PAGE)
     row = lax.broadcasted_iota(jnp.int32, pick_ref.shape, 0)
     token = lax.broadcasted_iota(jnp.int32, pick_ref.shape, 1)
     sent = ((row < PAGE) & (one >= 0) & (token == row + one * PAGE)) | (
@@ -270,14 +266,20 @@
     attend(qt_ref, keys, values_t, (high_in, total_in, accum_in), outs)
 
 
-def split_kernel(pick_ref, shard_ref, keys_ref, stretch_ref, values_ref, pages_ref):
+def pick_kernel(pick_ref, shard_ref, pages_ref):
     tokens = pick_ref.shape[1]
-    half = shard_ref.shape[0] // 2
     sent = pick_ref.shape[0]
+    for place, start in enumerate((0, shard_ref.shape[0] // 2)):
+        rows = jnp.dot(pick_ref[...], shard_ref[start : start + tokens], preferred_element_type=jnp.float32)
+        pages_ref[place * sent : (place + 1) * sent] = rows.astype(jnp.bfloat16)
+
+
+def split_kernel(shard_ref, keys_ref, stretch_ref, values_ref):
+    c_rows = keys_ref.shape[0]
+    tokens = stretch_ref.shape[0] // 2
+    half = tokens + c_rows
     for place, start in enumerate((0, half)):
         stretch_ref[place * tokens : (place + 1) * tokens] = shard_ref[start : start + tokens]
-        rows = jnp.dot(pick_ref[...], shard_ref[start : start + tokens], preferred_element_type=jnp.float32)
-        pages_ref[place * sent : (place + 1) * sent] = rows.astype(jnp.bfloat16)
     keys_ref[...] = shard_ref[tokens:half]
     values_ref[...] = shard_ref[half + tokens :]
 
@@ -478,20 +480,25 @@
             shape((c_rows, kv_width), bf16),
             shape((2 * tokens, kv_width), bf16),
             shape((c_rows, kv_width), bf16),
-            shape((2 * SEND_CAP * PAGE, kv_width), bf16),
         ),
+        in_specs=[VMEM],
+        out_specs=(VMEM,) * 3,
+        compiler_params=params,
+        name="pieces_to_send_on",
+    )(nearer)
+    far_pages = pl.pallas_call(
+        pick_kernel,
+        out_shape=shape((2 * SEND_CAP * PAGE, kv_width), bf16),
         in_specs=[VMEM] * 2,
-        out_specs=(VMEM,) * 4,
-        compiler_params=params,
-        name="pieces_to_send_on",
-    )(pick, nearer)
+        out_specs=VMEM,
+        compiler_params=params,
+        name="pages_to_send",
+    )(pick, shard[0])
+    straight = [(i, (i - hop) % count) for i in range(count) if i > (i - hop) % count]
+    last_pages = lax.ppermute(far_pages, "ctx", straight)
     last_keys = send(pieces[0], hop)
-    attending, others = [], []
-    for pair in up_pairs if hop < 0 else down_pairs:
-        (attending if (pair[1] + hop) % count < pair[1] else others).append(pair)
+    attending = [pair for pair in (up_pairs if hop < 0 else down_pairs) if (pair[1] + hop) % count < pair[1]]
     last_stretch = lax.ppermute(pieces[1], "ctx", attending)
-    last_pages = lax.ppermute(pieces[3], "ctx", others)
-    last_values = send(pieces[2], hop)
 
     for first in range(len(hops) - 1):
         places = [first]
@@ -505,6 +512,9 @@
             name="whole_shards_" + str(first),
         )(qt, near, far, *state, *[shard[hops[place]] for place in places])
 
+    last_piece, last_pages, state = lax.optimization_barrier((pieces[2], last_pages, state))
+    last_values = send(last_piece, hops[-1])
+
     final = len(hops) - 1
     dec_state, state = lax.optimization_barrier((dec_state, state))
     near_hops = hops[:-1]
@@ -523,6 +533,17 @@
     )
     dec_state, state = lax.optimization_barrier((dec_state, state))
 
+    decoded = pl.pallas_call(
+        last_pages_kernel,
+        out_shape=shape(decode_queries.shape, bf16),
+        in_specs=[VMEM] * 7,
+        out_specs=VMEM,
+        compiler_params=params,
+        cost_estimate=cost(tokens // 2),
+        name="decode_last_pages",
+    )(last_stretch, last_pages, tally, wide, *dec_state)
+    decoded, state = lax.optimization_barrier((decoded, state))
+
     weights, total, accum = pl.pallas_call(
         functools.partial(score_kernel, final),
         out_shape=(shape((kv_local, c_rows, rows), bf16),) + state_shapes[1:],
@@ -532,18 +553,6 @@
         cost_estimate=cost(half),
         name="last_scores",
     )(qt, near, far, *state, last_keys, last_stretch)
-
-    dec_state, total = lax.optimization_barrier((dec_state, total))
-    decoded = pl.pallas_call(
-        last_pages_kernel,
-        out_shape=shape(decode_queries.shape, bf16),
-        in_specs=[VMEM] * 7,
-        out_specs=VMEM,
-        compiler_params=params,
-        cost_estimate=cost(tokens // 2),
-        name="decode_last_pages",
-    )(last_stretch, last_pages, tally, wide, *dec_state)
-    decoded, total = lax.optimization_barrier((decoded, total))
 
     prefill = pl.pallas_call(
         last_kernel,

time: 33.9 us -> 34.9 us (1.029)
  starting transfers between devices: 11.9 us -> 14.2 us
  waiting for transfers between devices: 3.43 us -> 2.04 us
    ppermute x4, starting transfers between devices: 5.29 us -> 12.3 us  [send(): return lax.ppermute(array, 'ctx', up_pairs if hop < 0 else down_pairs)]
    ppermute x1, starting transfers between devices: 5.9 us -> 1.29 us  [per_device(): last_pages = lax.ppermute(far_pages, 'ctx', straight)]
    ppermute x4, waiting for transfers between devices: 3.42 us -> 2.04 us  [send(): return lax.ppermute(array, 'ctx', up_pairs if hop < 0 else down_pairs)]
  transfers between devices with their start and end apart: 6 -> 6, of which waited for: 3 -> 2; matrix products, arithmetic and copies ran while one was open for 0% -> 0% of each run, Pallas kernels for 35% -> 34%
where the time goes in v19:
time: 34.9 us; the launch traced here: 34.6 us
  starting transfers between devices  14.2 us (41%)
  Pallas kernels  12.8 us (37%)
  local copies, waits for them, and re-layouts  3.14 us (9%)
  waiting for transfers between devices  2.04 us (6%)
  between operations  1.41 us (4%)
  other arithmetic  1.03 us (3%)
    ppermute x4, starting transfers between devices, send(): return lax.ppermute(array, 'ctx', up_pairs if hop < 0 else down_pairs)  12.3 us
    pallas_call x2, Pallas kernels, per_device(): pl.pallas_call(functools.partial(hop_kernel, places), out_shape=state_sha...  3.45 us
    unnamed x14, local copies, waits for them, and re-layouts  3.14 us
    pallas_call x1, Pallas kernels, per_device(): pl.pallas_call(functools.partial(own_kernel, count, hops), out_shape=(sha...  2.36 us
    ppermute x4, waiting for transfers between devices, send(): return lax.ppermute(array, 'ctx', up_pairs if hop < 0 else down_pairs)  2.04 us
    pallas_call x1, Pallas kernels, per_device(): pl.pallas_call(held_kernel, out_shape=(shape((heads * dec_rows, kv_width)...  1.86 us
    pallas_call x1, Pallas kernels, per_device(): pl.pallas_call(functools.partial(score_kernel, final), out_shape=(shape((...  1.61 us
    ppermute x1, starting transfers between devices, per_device(): last_pages = lax.ppermute(far_pages, 'ctx', straight)  1.29 us
  transfers between devices with their start and end apart: 6, of which 2 were waited for; matrix products, arithmetic and copies ran while one was open for 0% of the time, Pallas kernels for 34%

profile of v19, /device:TPU:0, one launch (start us, length us, event | category | flops | bytes accessed | tf_op | source)
XLA Modules:
  0.0 34.6 jit_solution(2720159215807355385)
XLA Ops:
  0.6 1.0 %pad_maximum_fusion.shard_ref.rest_ref = bf16[768,256]{1,0:T(8,128)(2,1)S(1)} fusion(bf16[256,256]{1,0:T(8,128)(2,1)} %param.16, bf16[128,256]{1,0:T(8,128)(2,1)} %param.14, bf16[256,256]{1,0:T(8,128)(2,1)} %param.15, bf16[128,256]{1,0:T(8,128)(2,1)} %param.13), kind=kLoop, calls=%fused_computation | loop fusion | flops 1572864 | bytes 786432 | tf_op jit(solution)/shard_map/max | solution.py:428
  1.7 3.1 %collective-permute-start = (bf16[768,256]{1,0:T(8,128)(2,1)S(1)}, bf16[768,256]{1,0:T(8,128)(2,1)S(1)}, u32[]{:S(2)}, u32[]{:S(2)}) collective-permute-start(bf16[768,256]{1,0:T(8,128)(2,1)S(1)} %pad_maximum_fusion.shard_ref.rest_ref), channel_id=1, source_target_pairs={{0,4},{4,8},{8,12},{12,0},{1,5},{5,9},{9,13},{13,1},{2,6},{6,10},{... | collective-permute-start | bytes 1179656 | tf_op jit(solution)/shard_map/ppermute | solution.py:413
  4.8 0.7 %copy-done.3 = s32[8,32]{1,0:T(8,128)S(1)} copy-done((s32[8,32]{1,0:T(8,128)S(1)}, s32[8,32]{1,0:T(8,128)}, u32[]{:S(2)}) %copy-start.3) | copy-done | bytes 1048
  5.4 1.2 %copy-done = bf16[128,16,256]{2,1,0:T(8,128)(2,1)S(1)} copy-done((bf16[128,16,256]{2,1,0:T(8,128)(2,1)S(1)}, bf16[128,16,256]{2,1,0:T(8,128)(2,1)}, u32[]{:S(2)}) %copy-start) | copy-done | bytes 1048600
  6.7 1.2 %copy-done.1 = bf16[128,16,256]{2,1,0:T(8,128)(2,1)S(1)} copy-done((bf16[128,16,256]{2,1,0:T(8,128)(2,1)S(1)}, bf16[128,16,256]{2,1,0:T(8,128)(2,1)}, u32[]{:S(2)}) %copy-start.1) | copy-done | bytes 1048600
  7.9 1.9 %decode_held_pages.1 = (bf16[128,256]{1,0:T(8,128)(2,1)S(1)}, f32[16,8,1]{2,1,0:T(8,128)S(1)}, f32[16,8,1]{2,1,0:T(8,128)S(1)}, f32[16,8,256]{2,1,0:T(8,128)S(1)}) custom-call(s32[1]{0:T(128)} %bitcast.own_ref, s32[32]{0:T(128)S(1)} %copy-done.4, s32[8]{0:T(128)S(1)} %copy-done.5, bf16[8,2048]{1,0:T(8,128)(2,1)S(1)} %copy-done.2, s32[8,32]{1,0:T(8,128)S(1)} %copy-done.3, ...), custom_call_target="tpu_custom_call" | custom-call | flops 268435456 | bytes 2097152 | tf_op jit(solution)/shard_map/decode_held_pages/pallas_call | solution.py:457
  10.4 2.4 %own_shard.1 = (bf16[2,256,1024]{2,1,0:T(8,128)(2,1)S(1)}, bf16[3,128,128]{2,1,0:T(8,128)(2,1)S(1)}, bf16[3,256,128]{2,1,0:T(8,128)(2,1)S(1)}, bf16[32,128]{1,0:...) custom-call(s32[1]{0:T(128)} %bitcast.own_ref, ...), custom_call_target="tpu_custom_call" | custom-call | flops 402653184 | bytes 1048576 | tf_op jit(solution)/shard_map/own_shard/pallas_call | solution.py:436
  12.8 2.1 %collective-permute-start.3 = (bf16[768,256]{1,0:T(8,128)(2,1)S(1)}, bf16[768,256]{1,0:T(8,128)(2,1)S(1)}, u32[]{:S(2)}, u32[]{:S(2)}) collective-permute-start(bf16[768,256]{1,0:T(8,128)(2,1)S(1)} %pad_maximum_fusion.shard_ref.rest_ref), channel_id=1, source_target_pairs={{0,12},{4,0},{8,4},{12,8},{1,13},{5,1},{9,5},{13,9},{2,14},{6,2},{... | collective-permute-start | bytes 1179656 | tf_op jit(solution)/shard_map/ppermute | solution.py:413
  14.9 0.1 pages_to_send.1
  15.0 1.3 %collective-permute-start.2 = (bf16[64,256]{1,0:T(8,128)(2,1)S(1)}, bf16[64,256]{1,0:T(8,128)(2,1)S(1)}, u32[]{:S(2)}, u32[]{:S(2)}) collective-permute-start(bf16[64,256]{1,0:T(8,128)(2,1)S(1)} %pages_to_send.1), channel_id=1, source_target_pairs={{8,0},{12,4},{9,1},{13,5},{10,2},{14,6},{11,3},{15,7},{24,16},{28,... | collective-permute-start | bytes 98312 | tf_op jit(solution)/shard_map/ppermute | solution.py:498
  16.3 0.0 collective-permute-done.shard_ref.refs_0_
  16.4 0.7 %collective-permute-start.1 = (bf16[256,256]{1,0:T(8,128)(2,1)S(1)}, bf16[256,256]{1,0:T(8,128)(2,1)S(1)}, u32[]{:S(2)}, u32[]{:S(2)}) collective-permute-start(bf16[256,256]{1,0:T(8,128)(2,1)S(1)} %get-tuple-element.80), channel_id=1, source_target_pairs={{4,8},{8,12},{5,9},{9,13},{6,10},{10,14},{7,11},{11,15},{20,24},{2... | collective-permute-start | bytes 393224 | tf_op jit(solution)/shard_map/ppermute | solution.py:501
  17.1 5.4 %collective-permute-start.4 = (bf16[256,256]{1,0:T(8,128)(2,1)S(1)}, bf16[256,256]{1,0:T(8,128)(2,1)S(1)}, u32[]{:S(2)}, u32[]{:S(2)}) collective-permute-start(bf16[256,256]{1,0:T(8,128)(2,1)S(1)} %get-tuple-element.120), channel_id=1, source_target_pairs={{0,4},{4,8},{8,12},{12,0},{1,5},{5,9},{9,13},{13,1},{2,6},{6,10},{... | collective-permute-start | bytes 393224 | tf_op jit(solution)/shard_map/ppermute | solution.py:413
  22.4 1.7 %whole_shards_0.1 = (f32[2,1,1024]{2,1,0:T(1,128)S(1)}, f32[2,1,1024]{2,1,0:T(1,128)S(1)}, f32[2,128,1024]{2,1,0:T(8,128)S(1)}) custom-call(bf16[2,256,1024]{2,1,0:T(8,128)(2,1)S(1)} %get-tuple-element.64.qt_ref, bf16[3,128,128]{2,1,0:T(8,128)(2,1)S(1)} %get-tuple-element.65.near_ref, bf16[3,256,128]{2,1,0:T(8,128)(2,1)S(1)} %get-tuple-element.66.far_ref, ...), custom_call_target="tpu_custom_call" | custom-call | flops 402653184 | bytes 1048576 | tf_op jit(solution)/shard_map/whole_shards_0/pallas_call | solution.py:505
  24.2 0.5 %collective-permute-done.3.refs_0_.refs_1_ = bf16[768,256]{1,0:T(8,128)(2,1)S(1)} collective-permute-done((bf16[768,256]{1,0:T(8,128)(2,1)S(1)}, bf16[768,256]{1,0:T(8,128)(2,1)S(1)}, u32[]{:S(2)}, u32[]{:S(2)}) %collective-permute-start.3) | collective-permute-done | bytes 393248 | tf_op jit(solution)/shard_map/ppermute | solution.py:413
  24.7 1.7 %whole_shards_1.1 = (f32[2,1,1024]{2,1,0:T(1,128)S(1)}, f32[2,1,1024]{2,1,0:T(1,128)S(1)}, f32[2,128,1024]{2,1,0:T(8,128)S(1)}) custom-call(bf16[2,256,1024]{2,1,0:T(8,128)(2,1)S(1)} %get-tuple-element.64.qt_ref, bf16[3,128,128]{2,1,0:T(8,128)(2,1)S(1)} %get-tuple-element.65.near_ref, bf16[3,256,128]{2,1,0:T(8,128)(2,1)S(1)} %get-tuple-element.66.far_ref, ...), custom_call_target="tpu_custom_call" | custom-call | flops 402653184 | bytes 1048576 | tf_op jit(solution)/shard_map/whole_shards_1/pallas_call | solution.py:505
  26.4 1.7 %collective-permute-start.5 = (bf16[256,256]{1,0:T(8,128)(2,1)S(1)}, bf16[256,256]{1,0:T(8,128)(2,1)S(1)}, u32[]{:S(2)}, u32[]{:S(2)}) collective-permute-start(bf16[256,256]{1,0:T(8,128)(2,1)S(1)} %get-tuple-element.124), channel_id=1, source_target_pairs={{0,4},{4,8},{8,12},{12,0},{1,5},{5,9},{9,13},{13,1},{2,6},{6,10},{... | collective-permute-start | bytes 393224 | tf_op jit(solution)/shard_map/ppermute | solution.py:413
  28.1 1.1 %decode_near_pages.1 = (f32[16,8,1]{2,1,0:T(8,128)S(1)}, f32[16,8,1]{2,1,0:T(8,128)S(1)}, f32[16,8,256]{2,1,0:T(8,128)S(1)}, f32[1,8,160]{2,1,0:T(8,128)S(1)}) custom-call(s32[1]{0:T(128)} %bitcast.own_ref, s32[32]{0:T(128)S(1)} %copy-done.4, s32[8]{0:T(128)S(1)} %copy-done.5, s32[8,32]{1,0:T(8,128)S(1)} %copy-done.3, ...), custom_call_target="tpu_custom_call" | custom-call | flops 134217728 | bytes 1048576 | tf_op jit(solution)/shard_map/decode_near_pages/pallas_call | solution.py:521
  29.2 0.0 collective-permute-done.1.stretch_ref
  29.2 1.1 %decode_last_pages.1 = bf16[8,2048]{1,0:T(8,128)(2,1)} custom-call(bf16[256,256]{1,0:T(8,128)(2,1)S(1)} %collective-permute-done.1.stretch_ref, bf16[64,256]{1,0:T(8,128)(2,1)S(1)} %collective-permute-done.2.pages_ref, f32[1,8,160]{2,1,0:T(8,128)S(1)} %get-tuple-element.104.tally_ref, bf16[128,256]{1,0:T(8,128)(2,1)S(1)} %get-tuple-element.94.refs_2_.wide_ref, ...), custom_call_target="tpu_custom_call" | custom-call | flops 67108864 | bytes 1048576 | tf_op jit(solution)/shard_map/decode_last_pages/pallas_call | solution.py:536
  30.3 0.0 collective-permute-done.4.keys_ref
  30.3 1.6 %last_scores.1 = (bf16[2,256,1024]{2,1,0:T(8,128)(2,1)S(1)}, f32[2,1,1024]{2,1,0:T(1,128)S(1)}, f32[2,128,1024]{2,1,0:T(8,128)S(1)}) custom-call(bf16[2,256,1024]{2,1,0:T(8,128)(2,1)S(1)} %get-tuple-element.64.qt_ref, bf16[3,128,128]{2,1,0:T(8,128)(2,1)S(1)} %get-tuple-element.65.near_ref, bf16[3,256,128]{2,1,0:T(8,128)(2,1)S(1)} %get-tuple-element.66.far_ref, ...), custom_call_target="tpu_custom_call" | custom-call | flops 402653184 | bytes 1048576 | tf_op jit(solution)/shard_map/last_scores/pallas_call | solution.py:547
  31.9 1.5 %collective-permute-done.5.values_ref = bf16[256,256]{1,0:T(8,128)(2,1)S(1)} collective-permute-done((bf16[256,256]{1,0:T(8,128)(2,1)S(1)}, bf16[256,256]{1,0:T(8,128)(2,1)S(1)}, u32[]{:S(2)}, u32[]{:S(2)}) %collective-permute-start.5) | collective-permute-done | bytes 131104 | tf_op jit(solution)/shard_map/ppermute | solution.py:413
  33.5 1.1 %last_values.1 = bf16[128,2048]{1,0:T(8,128)(2,1)} custom-call(bf16[2,256,1024]{2,1,0:T(8,128)(2,1)S(1)} %get-tuple-element.121.weights_ref, f32[2,1,1024]{2,1,0:T(1,128)S(1)} %get-tuple-element.122.total_ref, f32[2,128,1024]{2,1,0:T(8,128)S(1)} %get-tuple-element.123.accum_ref, bf16[256,256]{1,0:T(8,128)(2,1)S(1)} %collective-permute-done.5.values_ref), custom_call_target="tpu_custom_call" | custom-call | flops 134217728 | bytes 1048576 | tf_op jit(solution)/shard_map/last_values/pallas_call | solution.py:557
  (13 shorter events, 0.1 us)
Async XLA Ops:
  0.6 4.1 %copy-start.2 = (bf16[8,2048]{1,0:T(8,128)(2,1)S(1)}, bf16[8,2048]{1,0:T(8,128)(2,1)}, u32[]{:S(2)}) copy-start(bf16[8,2048]{1,0:T(8,128)(2,1)} %q_ref.3) | copy-start | bytes 98308
  1.7 14.7 %collective-permute-start = (bf16[768,256]{1,0:T(8,128)(2,1)S(1)}, bf16[768,256]{1,0:T(8,128)(2,1)S(1)}, u32[]{:S(2)}, u32[]{:S(2)}) collective-permute-start(bf16[768,256]{1,0:T(8,128)(2,1)S(1)} %pad_maximum_fusion.shard_ref.rest_ref), channel_id=1, source_target_pairs={{0,4},{4,8},{8,12},{12,0},{1,5},{5,9},{9,13},{13,1},{2,6},{6,10},{... | collective-permute-start | bytes 1179656 | tf_op jit(solution)/shard_map/ppermute | solution.py:413
  4.8 0.7 %copy-start.3 = (s32[8,32]{1,0:T(8,128)S(1)}, s32[8,32]{1,0:T(8,128)}, u32[]{:S(2)}) copy-start(s32[8,32]{1,0:T(8,128)} %lists_ref.3) | copy-start | bytes 3076
  4.8 0.7 %copy-start.4 = (s32[32]{0:T(128)S(1)}, s32[32]{0:T(128)}, u32[]{:S(2)}) copy-start(s32[32]{0:T(128)} %targets_ref.5) | copy-start | bytes 388
  4.8 0.7 %copy-start.5 = (s32[8]{0:T(128)S(1)}, s32[8]{0:T(128)}, u32[]{:S(2)}) copy-start(s32[8]{0:T(128)} %length_ref.3) | copy-start | bytes 100
  5.4 1.2 %copy-start = (bf16[128,16,256]{2,1,0:T(8,128)(2,1)S(1)}, bf16[128,16,256]{2,1,0:T(8,128)(2,1)}, u32[]{:S(2)}) copy-start(bf16[128,16,256]{2,1,0:T(8,128)(2,1)} %pool_k.1) | copy-start | bytes 3145732
  6.7 1.2 %copy-start.1 = (bf16[128,16,256]{2,1,0:T(8,128)(2,1)S(1)}, bf16[128,16,256]{2,1,0:T(8,128)(2,1)}, u32[]{:S(2)}) copy-start(bf16[128,16,256]{2,1,0:T(8,128)(2,1)} %pool_v.1) | copy-start | bytes 3145732
  7.9 2.5 %copy-start.6 = (bf16[128,2048]{1,0:T(8,128)(2,1)S(1)}, bf16[128,2048]{1,0:T(8,128)(2,1)}, u32[]{:S(2)}) copy-start(bf16[128,2048]{1,0:T(8,128)(2,1)} %q_ref.2) | copy-start | bytes 1572868
  12.8 11.9 %collective-permute-start.3 = (bf16[768,256]{1,0:T(8,128)(2,1)S(1)}, bf16[768,256]{1,0:T(8,128)(2,1)S(1)}, u32[]{:S(2)}, u32[]{:S(2)}) collective-permute-start(bf16[768,256]{1,0:T(8,128)(2,1)S(1)} %pad_maximum_fusion.shard_ref.rest_ref), channel_id=1, source_target_pairs={{0,12},{4,0},{8,4},{12,8},{1,13},{5,1},{9,5},{13,9},{2,14},{6,2},{... | collective-permute-start | bytes 1179656 | tf_op jit(solution)/shard_map/ppermute | solution.py:413
  15.0 11.4 %collective-permute-start.2 = (bf16[64,256]{1,0:T(8,128)(2,1)S(1)}, bf16[64,256]{1,0:T(8,128)(2,1)S(1)}, u32[]{:S(2)}, u32[]{:S(2)}) collective-permute-start(bf16[64,256]{1,0:T(8,128)(2,1)S(1)} %pages_to_send.1), channel_id=1, source_target_pairs={{8,0},{12,4},{9,1},{13,5},{10,2},{14,6},{11,3},{15,7},{24,16},{28,... | collective-permute-start | bytes 98312 | tf_op jit(solution)/shard_map/ppermute | solution.py:498
  16.4 12.8 %collective-permute-start.1 = (bf16[256,256]{1,0:T(8,128)(2,1)S(1)}, bf16[256,256]{1,0:T(8,128)(2,1)S(1)}, u32[]{:S(2)}, u32[]{:S(2)}) collective-permute-start(bf16[256,256]{1,0:T(8,128)(2,1)S(1)} %get-tuple-element.80), channel_id=1, source_target_pairs={{4,8},{8,12},{5,9},{9,13},{6,10},{10,14},{7,11},{11,15},{20,24},{2... | collective-permute-start | bytes 393224 | tf_op jit(solution)/shard_map/ppermute | solution.py:501
  17.1 13.3 %collective-permute-start.4 = (bf16[256,256]{1,0:T(8,128)(2,1)S(1)}, bf16[256,256]{1,0:T(8,128)(2,1)S(1)}, u32[]{:S(2)}, u32[]{:S(2)}) collective-permute-start(bf16[256,256]{1,0:T(8,128)(2,1)S(1)} %get-tuple-element.120), channel_id=1, source_target_pairs={{0,4},{4,8},{8,12},{12,0},{1,5},{5,9},{9,13},{13,1},{2,6},{6,10},{... | collective-permute-start | bytes 393224 | tf_op jit(solution)/shard_map/ppermute | solution.py:413
  26.4 7.1 %collective-permute-start.5 = (bf16[256,256]{1,0:T(8,128)(2,1)S(1)}, bf16[256,256]{1,0:T(8,128)(2,1)S(1)}, u32[]{:S(2)}, u32[]{:S(2)}) collective-permute-start(bf16[256,256]{1,0:T(8,128)(2,1)S(1)} %get-tuple-element.124), channel_id=1, source_target_pairs={{0,4},{4,8},{8,12},{12,0},{1,5},{5,9},{9,13},{13,1},{2,6},{6,10},{... | collective-permute-start | bytes 393224 | tf_op jit(solution)/shard_map/ppermute | solution.py:413

commit v20 on v19

--- a/solution.py
+++ b/solution.py
@@ -511,9 +511,9 @@
             cost_estimate=cost((c_rows + tokens) * len(places)),
             name="whole_shards_" + str(first),
         )(qt, near, far, *state, *[shard[hops[place]] for place in places])
-
-    last_piece, last_pages, state = lax.optimization_barrier((pieces[2], last_pages, state))
-    last_values = send(last_piece, hops[-1])
+        if first == 0:
+            last_piece, last_pages, state = lax.optimization_barrier((pieces[2], last_pages, state))
+            last_values = send(last_piece, hops[-1])
 
     final = len(hops) - 1
     dec_state, state = lax.optimization_barrier((dec_state, state))

time: 34.9 us -> 35.1 us (level)
  waiting for transfers between devices: 2.04 us -> 5.05 us
  starting transfers between devices: 14.2 us -> 11.5 us
    ppermute x1, waiting for transfers between devices: 0.01 us -> 3.94 us  [per_device(): last_pages = lax.ppermute(far_pages, 'ctx', straight)]
    ppermute x4, starting transfers between devices: 12.3 us -> 9.5 us  [send(): return lax.ppermute(array, 'ctx', up_pairs if hop < 0 else down_pairs)]
    ppermute x4, waiting for transfers between devices: 2.04 us -> 1.1 us  [send(): return lax.ppermute(array, 'ctx', up_pairs if hop < 0 else down_pairs)]
  transfers between devices with their start and end apart: 6 -> 6, of which waited for: 2 -> 2; matrix products, arithmetic and copies ran while one was open for 0% -> 0% of each run, Pallas kernels for 34% -> 33%
where the time goes in v20:
time: 35.1 us; the launch traced here: 34.8 us
  Pallas kernels  12.8 us (36%)
  starting transfers between devices  11.5 us (33%)
  waiting for transfers between devices  5.05 us (14%)
  local copies, waits for them, and re-layouts  3.1 us (9%)
  between operations  1.44 us (4%)
  other arithmetic  1.03 us (3%)
    ppermute x4, starting transfers between devices, send(): return lax.ppermute(array, 'ctx', up_pairs if hop < 0 else down_pairs)  9.5 us
    ppermute x1, waiting for transfers between devices, per_device(): last_pages = lax.ppermute(far_pages, 'ctx', straight)  3.94 us
    pallas_call x2, Pallas kernels, per_device(): pl.pallas_call(functools.partial(hop_kernel, places), out_shape=state_sha...  3.45 us
    unnamed x14, local copies, waits for them, and re-layouts  3.1 us
    pallas_call x1, Pallas kernels, per_device(): pl.pallas_call(functools.partial(own_kernel, count, hops), out_shape=(sha...  2.36 us
    pallas_call x1, Pallas kernels, per_device(): pl.pallas_call(held_kernel, out_shape=(shape((heads * dec_rows, kv_width)...  1.86 us
    pallas_call x1, Pallas kernels, per_device(): pl.pallas_call(functools.partial(score_kernel, final), out_shape=(shape((...  1.61 us
    ppermute x1, starting transfers between devices, per_device(): last_pages = lax.ppermute(far_pages, 'ctx', straight)  1.29 us
  transfers between devices with their start and end apart: 6, of which 2 were waited for; matrix products, arithmetic and copies ran while one was open for 0% of the time, Pallas kernels for 33%

profile of v20, /device:TPU:0, one launch (start us, length us, event | category | flops | bytes accessed | tf_op | source)
XLA Modules:
  0.0 34.8 jit_solution(17411576659878818439)
XLA Ops:
  0.6 1.0 %pad_maximum_fusion.shard_ref.rest_ref = bf16[768,256]{1,0:T(8,128)(2,1)S(1)} fusion(bf16[256,256]{1,0:T(8,128)(2,1)} %param.16, bf16[128,256]{1,0:T(8,128)(2,1)} %param.14, bf16[256,256]{1,0:T(8,128)(2,1)} %param.15, bf16[128,256]{1,0:T(8,128)(2,1)} %param.13), kind=kLoop, calls=%fused_computation | loop fusion | flops 1572864 | bytes 786432 | tf_op jit(solution)/shard_map/max | solution.py:428
  1.7 3.1 %collective-permute-start = (bf16[768,256]{1,0:T(8,128)(2,1)S(1)}, bf16[768,256]{1,0:T(8,128)(2,1)S(1)}, u32[]{:S(2)}, u32[]{:S(2)}) collective-permute-start(bf16[768,256]{1,0:T(8,128)(2,1)S(1)} %pad_maximum_fusion.shard_ref.rest_ref), channel_id=1, source_target_pairs={{0,4},{4,8},{8,12},{12,0},{1,5},{5,9},{9,13},{13,1},{2,6},{6,10},{... | collective-permute-start | bytes 1179656 | tf_op jit(solution)/shard_map/ppermute | solution.py:413
  5.4 0.0 copy-start.4
  5.4 0.0 copy-start.5
  5.5 0.6 %copy-done.4 = s32[32]{0:T(128)S(1)} copy-done((s32[32]{0:T(128)S(1)}, s32[32]{0:T(128)}, u32[]{:S(2)}) %copy-start.4) | copy-done | bytes 152
  6.1 0.0 copy-done.5
  6.1 1.2 %copy-done = bf16[128,16,256]{2,1,0:T(8,128)(2,1)S(1)} copy-done((bf16[128,16,256]{2,1,0:T(8,128)(2,1)S(1)}, bf16[128,16,256]{2,1,0:T(8,128)(2,1)}, u32[]{:S(2)}) %copy-start) | copy-done | bytes 1048600
  7.3 1.2 %copy-done.1 = bf16[128,16,256]{2,1,0:T(8,128)(2,1)S(1)} copy-done((bf16[128,16,256]{2,1,0:T(8,128)(2,1)S(1)}, bf16[128,16,256]{2,1,0:T(8,128)(2,1)}, u32[]{:S(2)}) %copy-start.1) | copy-done | bytes 1048600
  8.5 1.9 %decode_held_pages.1 = (bf16[128,256]{1,0:T(8,128)(2,1)S(1)}, f32[16,8,1]{2,1,0:T(8,128)S(1)}, f32[16,8,1]{2,1,0:T(8,128)S(1)}, f32[16,8,256]{2,1,0:T(8,128)S(1)}) custom-call(s32[1]{0:T(128)} %bitcast.own_ref, s32[32]{0:T(128)S(1)} %copy-done.4, s32[8]{0:T(128)S(1)} %copy-done.5, bf16[8,2048]{1,0:T(8,128)(2,1)S(1)} %copy-done.2, s32[8,32]{1,0:T(8,128)S(1)} %copy-done.3, ...), custom_call_target="tpu_custom_call" | custom-call | flops 268435456 | bytes 2097152 | tf_op jit(solution)/shard_map/decode_held_pages/pallas_call | solution.py:457
  10.4 2.4 %own_shard.1 = (bf16[2,256,1024]{2,1,0:T(8,128)(2,1)S(1)}, bf16[3,128,128]{2,1,0:T(8,128)(2,1)S(1)}, bf16[3,256,128]{2,1,0:T(8,128)(2,1)S(1)}, bf16[32,128]{1,0:...) custom-call(s32[1]{0:T(128)} %bitcast.own_ref, ...), custom_call_target="tpu_custom_call" | custom-call | flops 402653184 | bytes 1048576 | tf_op jit(solution)/shard_map/own_shard/pallas_call | solution.py:436
  12.8 2.1 %collective-permute-start.3 = (bf16[768,256]{1,0:T(8,128)(2,1)S(1)}, bf16[768,256]{1,0:T(8,128)(2,1)S(1)}, u32[]{:S(2)}, u32[]{:S(2)}) collective-permute-start(bf16[768,256]{1,0:T(8,128)(2,1)S(1)} %pad_maximum_fusion.shard_ref.rest_ref), channel_id=1, source_target_pairs={{0,12},{4,0},{8,4},{12,8},{1,13},{5,1},{9,5},{13,9},{2,14},{6,2},{... | collective-permute-start | bytes 1179656 | tf_op jit(solution)/shard_map/ppermute | solution.py:413
  14.9 1.1 %collective-permute-done.shard_ref.refs_0_ = bf16[768,256]{1,0:T(8,128)(2,1)S(1)} collective-permute-done((bf16[768,256]{1,0:T(8,128)(2,1)S(1)}, bf16[768,256]{1,0:T(8,128)(2,1)S(1)}, u32[]{:S(2)}, u32[]{:S(2)}) %collective-permute-start) | collective-permute-done | bytes 393248 | tf_op jit(solution)/shard_map/ppermute | solution.py:413
  16.0 0.7 %collective-permute-start.1 = (bf16[256,256]{1,0:T(8,128)(2,1)S(1)}, bf16[256,256]{1,0:T(8,128)(2,1)S(1)}, u32[]{:S(2)}, u32[]{:S(2)}) collective-permute-start(bf16[256,256]{1,0:T(8,128)(2,1)S(1)} %get-tuple-element.80), channel_id=1, source_target_pairs={{4,8},{8,12},{5,9},{9,13},{6,10},{10,14},{7,11},{11,15},{20,24},{2... | collective-permute-start | bytes 393224 | tf_op jit(solution)/shard_map/ppermute | solution.py:501
  16.7 0.1 pages_to_send.1
  16.8 1.3 %collective-permute-start.2 = (bf16[64,256]{1,0:T(8,128)(2,1)S(1)}, bf16[64,256]{1,0:T(8,128)(2,1)S(1)}, u32[]{:S(2)}, u32[]{:S(2)}) collective-permute-start(bf16[64,256]{1,0:T(8,128)(2,1)S(1)} %pages_to_send.1), channel_id=1, source_target_pairs={{8,0},{12,4},{9,1},{13,5},{10,2},{14,6},{11,3},{15,7},{24,16},{28,... | collective-permute-start | bytes 98312 | tf_op jit(solution)/shard_map/ppermute | solution.py:498
  18.1 2.5 %collective-permute-start.4 = (bf16[256,256]{1,0:T(8,128)(2,1)S(1)}, bf16[256,256]{1,0:T(8,128)(2,1)S(1)}, u32[]{:S(2)}, u32[]{:S(2)}) collective-permute-start(bf16[256,256]{1,0:T(8,128)(2,1)S(1)} %get-tuple-element.120), channel_id=1, source_target_pairs={{0,4},{4,8},{8,12},{12,0},{1,5},{5,9},{9,13},{13,1},{2,6},{6,10},{... | collective-permute-start | bytes 393224 | tf_op jit(solution)/shard_map/ppermute | solution.py:413
  20.6 1.7 %whole_shards_0.1 = (f32[2,1,1024]{2,1,0:T(1,128)S(1)}, f32[2,1,1024]{2,1,0:T(1,128)S(1)}, f32[2,128,1024]{2,1,0:T(8,128)S(1)}) custom-call(bf16[2,256,1024]{2,1,0:T(8,128)(2,1)S(1)} %get-tuple-element.64.qt_ref, bf16[3,128,128]{2,1,0:T(8,128)(2,1)S(1)} %get-tuple-element.65.near_ref, bf16[3,256,128]{2,1,0:T(8,128)(2,1)S(1)} %get-tuple-element.66.far_ref, ...), custom_call_target="tpu_custom_call" | custom-call | flops 402653184 | bytes 1048576 | tf_op jit(solution)/shard_map/whole_shards_0/pallas_call | solution.py:505
  22.3 3.9 %collective-permute-done.2.pages_ref = bf16[64,256]{1,0:T(8,128)(2,1)S(1)} collective-permute-done((bf16[64,256]{1,0:T(8,128)(2,1)S(1)}, bf16[64,256]{1,0:T(8,128)(2,1)S(1)}, u32[]{:S(2)}, u32[]{:S(2)}) %collective-permute-start.2) | collective-permute-done | bytes 32800 | tf_op jit(solution)/shard_map/ppermute | solution.py:498
  26.3 1.8 %collective-permute-start.5 = (bf16[256,256]{1,0:T(8,128)(2,1)S(1)}, bf16[256,256]{1,0:T(8,128)(2,1)S(1)}, u32[]{:S(2)}, u32[]{:S(2)}) collective-permute-start(bf16[256,256]{1,0:T(8,128)(2,1)S(1)} %get-tuple-element.124), channel_id=1, source_target_pairs={{0,4},{4,8},{8,12},{12,0},{1,5},{5,9},{9,13},{13,1},{2,6},{6,10},{... | collective-permute-start | bytes 393224 | tf_op jit(solution)/shard_map/ppermute | solution.py:413
  28.1 1.7 %whole_shards_1.1 = (f32[2,1,1024]{2,1,0:T(1,128)S(1)}, f32[2,1,1024]{2,1,0:T(1,128)S(1)}, f32[2,128,1024]{2,1,0:T(8,128)S(1)}) custom-call(bf16[2,256,1024]{2,1,0:T(8,128)(2,1)S(1)} %get-tuple-element.64.qt_ref, bf16[3,128,128]{2,1,0:T(8,128)(2,1)S(1)} %get-tuple-element.65.near_ref, bf16[3,256,128]{2,1,0:T(8,128)(2,1)S(1)} %get-tuple-element.66.far_ref, ...), custom_call_target="tpu_custom_call" | custom-call | flops 402653184 | bytes 1048576 | tf_op jit(solution)/shard_map/whole_shards_1/pallas_call | solution.py:505
  29.9 1.1 %decode_near_pages.1 = (f32[16,8,1]{2,1,0:T(8,128)S(1)}, f32[16,8,1]{2,1,0:T(8,128)S(1)}, f32[16,8,256]{2,1,0:T(8,128)S(1)}, f32[1,8,160]{2,1,0:T(8,128)S(1)}) custom-call(s32[1]{0:T(128)} %bitcast.own_ref, s32[32]{0:T(128)S(1)} %copy-done.4, s32[8]{0:T(128)S(1)} %copy-done.5, s32[8,32]{1,0:T(8,128)S(1)} %copy-done.3, ...), custom_call_target="tpu_custom_call" | custom-call | flops 134217728 | bytes 1048576 | tf_op jit(solution)/shard_map/decode_near_pages/pallas_call | solution.py:521
  30.9 1.1 %decode_last_pages.1 = bf16[8,2048]{1,0:T(8,128)(2,1)} custom-call(bf16[256,256]{1,0:T(8,128)(2,1)S(1)} %collective-permute-done.1.stretch_ref, bf16[64,256]{1,0:T(8,128)(2,1)S(1)} %collective-permute-done.2.pages_ref, f32[1,8,160]{2,1,0:T(8,128)S(1)} %get-tuple-element.104.tally_ref, bf16[128,256]{1,0:T(8,128)(2,1)S(1)} %get-tuple-element.91.refs_2_.wide_ref, ...), custom_call_target="tpu_custom_call" | custom-call | flops 67108864 | bytes 1048576 | tf_op jit(solution)/shard_map/decode_last_pages/pallas_call | solution.py:536
  32.1 1.6 %last_scores.1 = (bf16[2,256,1024]{2,1,0:T(8,128)(2,1)S(1)}, f32[2,1,1024]{2,1,0:T(1,128)S(1)}, f32[2,128,1024]{2,1,0:T(8,128)S(1)}) custom-call(bf16[2,256,1024]{2,1,0:T(8,128)(2,1)S(1)} %get-tuple-element.64.qt_ref, bf16[3,128,128]{2,1,0:T(8,128)(2,1)S(1)} %get-tuple-element.65.near_ref, bf16[3,256,128]{2,1,0:T(8,128)(2,1)S(1)} %get-tuple-element.66.far_ref, ...), custom_call_target="tpu_custom_call" | custom-call | flops 402653184 | bytes 1048576 | tf_op jit(solution)/shard_map/last_scores/pallas_call | solution.py:547
  33.7 1.1 %last_values.1 = bf16[128,2048]{1,0:T(8,128)(2,1)} custom-call(bf16[2,256,1024]{2,1,0:T(8,128)(2,1)S(1)} %get-tuple-element.121.weights_ref, f32[2,1,1024]{2,1,0:T(1,128)S(1)} %get-tuple-element.122.total_ref, f32[2,128,1024]{2,1,0:T(8,128)S(1)} %get-tuple-element.123.accum_ref, bf16[256,256]{1,0:T(8,128)(2,1)S(1)} %collective-permute-done.5.values_ref), custom_call_target="tpu_custom_call" | custom-call | flops 134217728 | bytes 1048576 | tf_op jit(solution)/shard_map/last_values/pallas_call | solution.py:557
  (13 shorter events, 0.1 us)
Async XLA Ops:
  0.6 4.8 %copy-start.2 = (bf16[8,2048]{1,0:T(8,128)(2,1)S(1)}, bf16[8,2048]{1,0:T(8,128)(2,1)}, u32[]{:S(2)}) copy-start(bf16[8,2048]{1,0:T(8,128)(2,1)} %q_ref.3) | copy-start | bytes 98308
  1.7 14.3 %collective-permute-start = (bf16[768,256]{1,0:T(8,128)(2,1)S(1)}, bf16[768,256]{1,0:T(8,128)(2,1)S(1)}, u32[]{:S(2)}, u32[]{:S(2)}) collective-permute-start(bf16[768,256]{1,0:T(8,128)(2,1)S(1)} %pad_maximum_fusion.shard_ref.rest_ref), channel_id=1, source_target_pairs={{0,4},{4,8},{8,12},{12,0},{1,5},{5,9},{9,13},{13,1},{2,6},{6,10},{... | collective-permute-start | bytes 1179656 | tf_op jit(solution)/shard_map/ppermute | solution.py:413
  4.8 0.7 %copy-start.3 = (s32[8,32]{1,0:T(8,128)S(1)}, s32[8,32]{1,0:T(8,128)}, u32[]{:S(2)}) copy-start(s32[8,32]{1,0:T(8,128)} %lists_ref.3) | copy-start | bytes 3076
  5.4 0.7 %copy-start.4 = (s32[32]{0:T(128)S(1)}, s32[32]{0:T(128)}, u32[]{:S(2)}) copy-start(s32[32]{0:T(128)} %targets_ref.5) | copy-start | bytes 388
  5.4 0.7 %copy-start.5 = (s32[8]{0:T(128)S(1)}, s32[8]{0:T(128)}, u32[]{:S(2)}) copy-start(s32[8]{0:T(128)} %length_ref.3) | copy-start | bytes 100
  6.1 1.2 %copy-start = (bf16[128,16,256]{2,1,0:T(8,128)(2,1)S(1)}, bf16[128,16,256]{2,1,0:T(8,128)(2,1)}, u32[]{:S(2)}) copy-start(bf16[128,16,256]{2,1,0:T(8,128)(2,1)} %pool_k.1) | copy-start | bytes 3145732
  7.3 1.2 %copy-start.1 = (bf16[128,16,256]{2,1,0:T(8,128)(2,1)S(1)}, bf16[128,16,256]{2,1,0:T(8,128)(2,1)}, u32[]{:S(2)}) copy-start(bf16[128,16,256]{2,1,0:T(8,128)(2,1)} %pool_v.1) | copy-start | bytes 3145732
  8.5 1.9 %copy-start.6 = (bf16[128,2048]{1,0:T(8,128)(2,1)S(1)}, bf16[128,2048]{1,0:T(8,128)(2,1)}, u32[]{:S(2)}) copy-start(bf16[128,2048]{1,0:T(8,128)(2,1)} %q_ref.2) | copy-start | bytes 1572868
  12.8 15.3 %collective-permute-start.3 = (bf16[768,256]{1,0:T(8,128)(2,1)S(1)}, bf16[768,256]{1,0:T(8,128)(2,1)S(1)}, u32[]{:S(2)}, u32[]{:S(2)}) collective-permute-start(bf16[768,256]{1,0:T(8,128)(2,1)S(1)} %pad_maximum_fusion.shard_ref.rest_ref), channel_id=1, source_target_pairs={{0,12},{4,0},{8,4},{12,8},{1,13},{5,1},{9,5},{13,9},{2,14},{6,2},{... | collective-permute-start | bytes 1179656 | tf_op jit(solution)/shard_map/ppermute | solution.py:413
  16.0 14.9 %collective-permute-start.1 = (bf16[256,256]{1,0:T(8,128)(2,1)S(1)}, bf16[256,256]{1,0:T(8,128)(2,1)S(1)}, u32[]{:S(2)}, u32[]{:S(2)}) collective-permute-start(bf16[256,256]{1,0:T(8,128)(2,1)S(1)} %get-tuple-element.80), channel_id=1, source_target_pairs={{4,8},{8,12},{5,9},{9,13},{6,10},{10,14},{7,11},{11,15},{20,24},{2... | collective-permute-start | bytes 393224 | tf_op jit(solution)/shard_map/ppermute | solution.py:501
  16.8 9.5 %collective-permute-start.2 = (bf16[64,256]{1,0:T(8,128)(2,1)S(1)}, bf16[64,256]{1,0:T(8,128)(2,1)S(1)}, u32[]{:S(2)}, u32[]{:S(2)}) collective-permute-start(bf16[64,256]{1,0:T(8,128)(2,1)S(1)} %pages_to_send.1), channel_id=1, source_target_pairs={{8,0},{12,4},{9,1},{13,5},{10,2},{14,6},{11,3},{15,7},{24,16},{28,... | collective-permute-start | bytes 98312 | tf_op jit(solution)/shard_map/ppermute | solution.py:498
  18.1 13.9 %collective-permute-start.4 = (bf16[256,256]{1,0:T(8,128)(2,1)S(1)}, bf16[256,256]{1,0:T(8,128)(2,1)S(1)}, u32[]{:S(2)}, u32[]{:S(2)}) collective-permute-start(bf16[256,256]{1,0:T(8,128)(2,1)S(1)} %get-tuple-element.120), channel_id=1, source_target_pairs={{0,4},{4,8},{8,12},{12,0},{1,5},{5,9},{9,13},{13,1},{2,6},{6,10},{... | collective-permute-start | bytes 393224 | tf_op jit(solution)/shard_map/ppermute | solution.py:413
  26.3 7.4 %collective-permute-start.5 = (bf16[256,256]{1,0:T(8,128)(2,1)S(1)}, bf16[256,256]{1,0:T(8,128)(2,1)S(1)}, u32[]{:S(2)}, u32[]{:S(2)}) collective-permute-start(bf16[256,256]{1,0:T(8,128)(2,1)S(1)} %get-tuple-element.124), channel_id=1, source_target_pairs={{0,4},{4,8},{8,12},{12,0},{1,5},{5,9},{9,13},{13,1},{2,6},{6,10},{... | collective-permute-start | bytes 393224 | tf_op jit(solution)/shard_map/ppermute | solution.py:413

commit v21 on v16

--- a/solution.py
+++ b/solution.py
@@ -106,13 +106,14 @@
     return one, two
 
 
-def sent_slots(targets_ref, shard, owner, pages, pool):
-    place = lax.broadcasted_iota(jnp.int32, (1, SEND_CAP * PAGE), 1)
-    slots = []
-    for index in sent_pages(targets_ref, shard, owner, pages):
-        target = targets_ref[shard * pages + jnp.maximum(index, 0)]
-        slots.append(jnp.where(index >= 0, pool + lax.rem(target, P_DEV), -1))
-    return jnp.where(place < PAGE, slots[0], slots[1])
+def sent_slots(targets_ref, shard, owner, tokens, pool):
+    page = lax.broadcasted_iota(jnp.int32, (1, tokens), 1) // PAGE
+    row = jnp.full((1, tokens), -1, jnp.int32)
+    for place, index in enumerate(sent_pages(targets_ref, shard, owner, tokens // PAGE)):
+        target = targets_ref[shard * (tokens // PAGE) + jnp.maximum(index, 0)]
+        slot = jnp.where(index >= 0, pool + lax.rem(target, P_DEV), -1)
+        row = jnp.where(page == place, slot, row)
+    return row
 
 
 def length_column(length_ref):
@@ -297,10 +298,9 @@
     high_ref[...], total_ref[...], mixed_ref[...] = decode_attend(wide_ref[...], parts, state)
     shard = shard_of(own, hops[-1], count)
     attended = shard < own
-    whole = jnp.where(attended, slot_row(targets_ref, shard, own, tokens, pool), -1)
-    alone = jnp.where(attended, -1, sent_slots(targets_ref, shard, own, tokens // PAGE, pool))
-    tally_ref[:, :, :tokens] = tally_of(lists, lengths, whole)
-    tally_ref[:, :, tokens:] = tally_of(lists, lengths, alone)
+    whole = slot_row(targets_ref, shard, own, tokens, pool)
+    alone = sent_slots(targets_ref, shard, own, tokens, pool)
+    tally_ref[...] = tally_of(lists, lengths, jnp.where(attended, whole, alone))
 
 
 def score_kernel(
@@ -309,24 +309,34 @@
 ):
     kv_local = qt_ref.shape[0]
     tokens, c_rows = near_ref.shape[1], far_ref.shape[1]
-    mask = jnp.concatenate([near_ref[final], far_ref[final]], axis=0)
-    keys, values_t = [], []
-    for head in range(kv_local):
-        pieces = [stretch_ref[:tokens, features(head)], keys_ref[:, features(head)]]
-        keys.append(jnp.concatenate([jnp.concatenate(pieces, axis=0), mask], axis=1))
-        values_t.append(stretch_ref[tokens:, features(head)].T)
-
-    def second(block, scores):
-        head, cols = block
-        before = (high_in[head, :, cols], total_in[head, :, cols])
-        weights, _, total, decay = soften(scores, before)
-        weights_ref[head, :, cols] = weights[tokens:]
-        total_ref[head, :, cols] = total
-        accum_ref[head, :, cols] = accum_in[head, :, cols] * decay + jnp.dot(
-            values_t[head], weights[:tokens], preferred_element_type=jnp.float32
-        )
-
-    walk(blocks_of(qt_ref), lambda block: scores_of(qt_ref, block[0], block[1], keys[block[0]]), second)
+    def run(attended):
+        mask = far_ref[final]
+        if attended:
+            mask = jnp.concatenate([near_ref[final], mask], axis=0)
+        keys, values_t = [], []
+        for head in range(kv_local):
+            rows = keys_ref[:, features(head)]
+            if attended:
+                rows = jnp.concatenate([stretch_ref[:tokens, features(head)], rows], axis=0)
+                values_t.append(stretch_ref[tokens:, features(head)].T)
+            keys.append(jnp.concatenate([rows, mask], axis=1))
+
+        def second(block, scores):
+            head, cols = block
+            before = (high_in[head, :, cols], total_in[head, :, cols])
+            weights, _, total, decay = soften(scores, before)
+            weights_ref[head, :, cols] = weights[-c_rows:]
+            total_ref[head, :, cols] = total
+            accum = accum_in[head, :, cols] * decay
+            if attended:
+                accum = accum + jnp.dot(values_t[head], weights[:tokens], preferred_element_type=jnp.float32)
+            accum_ref[head, :, cols] = accum
+
+        walk(blocks_of(qt_ref), lambda block: scores_of(qt_ref, block[0], block[1], keys[block[0]]), second)
+
+    attended = jnp.max(near_ref[final].astype(jnp.float32)) > HIDDEN / 2
+    pl.when(attended)(functools.partial(run, True))
+    pl.when(jnp.logical_not(attended))(functools.partial(run, False))
 
 
 def last_pages_kernel(
@@ -334,8 +344,10 @@
 ):
     tokens = stretch_ref.shape[0] // 2
     sent = pages_ref.shape[0] // 2
-    keys = jnp.concatenate([stretch_ref[:tokens], pages_ref[:sent]], axis=0)
-    values = jnp.concatenate([stretch_ref[tokens:], pages_ref[sent:]], axis=0)
+    keys = jnp.concatenate([stretch_ref[:sent] + pages_ref[:sent], stretch_ref[sent:tokens]], axis=0)
+    values = jnp.concatenate(
+        [stretch_ref[tokens : tokens + sent] + pages_ref[sent:], stretch_ref[tokens + sent :]], axis=0
+    )
     state = (dec_high[...], dec_total[...], dec_mixed[...])
     _, total, mixed = decode_attend(wide_ref[...], [(keys, values, tally_ref[...])], state)
     share = 1.0 / total
@@ -511,7 +523,7 @@
     *dec_state, tally = pl.pallas_call(
         functools.partial(near_pages_kernel, count, hops, tokens, pool),
         out_shape=dec_shapes
-        + (shape((1, dec_rows, tokens + SEND_CAP * PAGE), f32),),
+        + (shape((1, dec_rows, tokens), f32),),
         in_specs=[SMEM] * 3 + [VMEM] * (5 + len(near_hops)),
         out_specs=(VMEM,) * 4,
         compiler_params=params,

time: 33.9 us -> 33.3 us (0.982)
  Pallas kernels: 12.8 us -> 12.2 us
    pallas_call x1, Pallas kernels: 1.6 us -> 1.02 us  [per_device(): pl.pallas_call(functools.partial(score_kernel, final), out_shape=(shape((...]
  transfers between devices with their start and end apart: 6 -> 6, of which waited for: 3 -> 3; matrix products, arithmetic and copies ran while one was open for 0% -> 0% of each run, Pallas kernels for 35% -> 33%
where the time goes in v21:
time: 33.3 us; the launch traced here: 33 us
  Pallas kernels  12.2 us (37%)
  starting transfers between devices  11.9 us (36%)
  waiting for transfers between devices  3.43 us (10%)
  local copies, waits for them, and re-layouts  3.1 us (9%)
  between operations  1.44 us (4%)
  other arithmetic  1.03 us (3%)
    ppermute x1, starting transfers between devices, per_device(): last_pages = lax.ppermute(pieces[3], 'ctx', others)  5.9 us
    ppermute x4, starting transfers between devices, send(): return lax.ppermute(array, 'ctx', up_pairs if hop < 0 else down_pairs)  5.29 us
    pallas_call x2, Pallas kernels, per_device(): pl.pallas_call(functools.partial(hop_kernel, places), out_shape=state_sha...  3.45 us
    ppermute x4, waiting for transfers between devices, send(): return lax.ppermute(array, 'ctx', up_pairs if hop < 0 else down_pairs)  3.42 us
    unnamed x14, local copies, waits for them, and re-layouts  3.1 us
    pallas_call x1, Pallas kernels, per_device(): pl.pallas_call(functools.partial(own_kernel, count, hops), out_shape=(sha...  2.36 us
    pallas_call x1, Pallas kernels, per_device(): pl.pallas_call(held_kernel, out_shape=(shape((heads * dec_rows, kv_width)...  1.86 us
    pallas_call x1, Pallas kernels, per_device(): pl.pallas_call(last_kernel, out_shape=shape((tokens, width), bf16), in_sp...  1.14 us
  transfers between devices with their start and end apart: 6, of which 3 were waited for; matrix products, arithmetic and copies ran while one was open for 0% of the time, Pallas kernels for 33%

profile of v21, /device:TPU:0, one launch (start us, length us, event | category | flops | bytes accessed | tf_op | source)
XLA Modules:
  0.0 33.0 jit_solution(7897077621003104385)
XLA Ops:
  0.6 1.0 %pad_maximum_fusion.shard_ref.rest_ref = bf16[768,256]{1,0:T(8,128)(2,1)S(1)} fusion(bf16[256,256]{1,0:T(8,128)(2,1)} %param.16, bf16[128,256]{1,0:T(8,128)(2,1)} %param.14, bf16[256,256]{1,0:T(8,128)(2,1)} %param.15, bf16[128,256]{1,0:T(8,128)(2,1)} %param.13), kind=kLoop, calls=%fused_computation | loop fusion | flops 1572864 | bytes 786432 | tf_op jit(solution)/shard_map/max | solution.py:438
  1.7 3.1 %collective-permute-start = (bf16[768,256]{1,0:T(8,128)(2,1)S(1)}, bf16[768,256]{1,0:T(8,128)(2,1)S(1)}, u32[]{:S(2)}, u32[]{:S(2)}) collective-permute-start(bf16[768,256]{1,0:T(8,128)(2,1)S(1)} %pad_maximum_fusion.shard_ref.rest_ref), channel_id=1, source_target_pairs={{0,4},{4,8},{8,12},{12,0},{1,5},{5,9},{9,13},{13,1},{2,6},{6,10},{... | collective-permute-start | bytes 1179656 | tf_op jit(solution)/shard_map/ppermute | solution.py:423
  5.4 0.0 copy-start.4
  5.5 0.6 %copy-done.4 = s32[32]{0:T(128)S(1)} copy-done((s32[32]{0:T(128)S(1)}, s32[32]{0:T(128)}, u32[]{:S(2)}) %copy-start.4) | copy-done | bytes 152
  6.1 0.0 copy-done.5
  6.1 1.2 %copy-done = bf16[128,16,256]{2,1,0:T(8,128)(2,1)S(1)} copy-done((bf16[128,16,256]{2,1,0:T(8,128)(2,1)S(1)}, bf16[128,16,256]{2,1,0:T(8,128)(2,1)}, u32[]{:S(2)}) %copy-start) | copy-done | bytes 1048600
  7.3 1.2 %copy-done.1 = bf16[128,16,256]{2,1,0:T(8,128)(2,1)S(1)} copy-done((bf16[128,16,256]{2,1,0:T(8,128)(2,1)S(1)}, bf16[128,16,256]{2,1,0:T(8,128)(2,1)}, u32[]{:S(2)}) %copy-start.1) | copy-done | bytes 1048600
  8.5 1.9 %decode_held_pages.1 = (bf16[128,256]{1,0:T(8,128)(2,1)S(1)}, f32[16,8,1]{2,1,0:T(8,128)S(1)}, f32[16,8,1]{2,1,0:T(8,128)S(1)}, f32[16,8,256]{2,1,0:T(8,128)S(1)}) custom-call(s32[1]{0:T(128)} %bitcast.own_ref, s32[32]{0:T(128)S(1)} %copy-done.4, s32[8]{0:T(128)S(1)} %copy-done.5, bf16[8,2048]{1,0:T(8,128)(2,1)S(1)} %copy-done.2, s32[8,32]{1,0:T(8,128)S(1)} %copy-done.3, ...), custom_call_target="tpu_custom_call" | custom-call | flops 268435456 | bytes 2097152 | tf_op jit(solution)/shard_map/decode_held_pages/pallas_call | solution.py:467
  10.4 2.4 %own_shard.1 = (bf16[2,256,1024]{2,1,0:T(8,128)(2,1)S(1)}, bf16[3,128,128]{2,1,0:T(8,128)(2,1)S(1)}, bf16[3,256,128]{2,1,0:T(8,128)(2,1)S(1)}, bf16[32,128]{1,0:...) custom-call(s32[1]{0:T(128)} %bitcast.own_ref, ...), custom_call_target="tpu_custom_call" | custom-call | flops 402653184 | bytes 1048576 | tf_op jit(solution)/shard_map/own_shard/pallas_call | solution.py:446
  12.8 2.1 %collective-permute-start.1 = (bf16[768,256]{1,0:T(8,128)(2,1)S(1)}, bf16[768,256]{1,0:T(8,128)(2,1)S(1)}, u32[]{:S(2)}, u32[]{:S(2)}) collective-permute-start(bf16[768,256]{1,0:T(8,128)(2,1)S(1)} %pad_maximum_fusion.shard_ref.rest_ref), channel_id=1, source_target_pairs={{0,12},{4,0},{8,4},{12,8},{1,13},{5,1},{9,5},{13,9},{2,14},{6,2},{... | collective-permute-start | bytes 1179656 | tf_op jit(solution)/shard_map/ppermute | solution.py:423
  14.9 1.1 %collective-permute-done.refs_0_.shard_ref = bf16[768,256]{1,0:T(8,128)(2,1)S(1)} collective-permute-done((bf16[768,256]{1,0:T(8,128)(2,1)S(1)}, bf16[768,256]{1,0:T(8,128)(2,1)S(1)}, u32[]{:S(2)}, u32[]{:S(2)}) %collective-permute-start) | collective-permute-done | bytes 393248 | tf_op jit(solution)/shard_map/ppermute | solution.py:423
  16.0 0.1 pieces_to_send_on.1
  16.1 0.1 collective-permute-start.2
  16.2 0.7 %collective-permute-start.3 = (bf16[256,256]{1,0:T(8,128)(2,1)S(1)}, bf16[256,256]{1,0:T(8,128)(2,1)S(1)}, u32[]{:S(2)}, u32[]{:S(2)}) collective-permute-start(bf16[256,256]{1,0:T(8,128)(2,1)S(1)} %get-tuple-element.106), channel_id=1, source_target_pairs={{4,8},{8,12},{5,9},{9,13},{6,10},{10,14},{7,11},{11,15},{20,24},{2... | collective-permute-start | bytes 393224 | tf_op jit(solution)/shard_map/ppermute | solution.py:504
  16.9 5.9 %collective-permute-start.4 = (bf16[64,256]{1,0:T(8,128)(2,1)S(1)}, bf16[64,256]{1,0:T(8,128)(2,1)S(1)}, u32[]{:S(2)}, u32[]{:S(2)}) collective-permute-start(bf16[64,256]{1,0:T(8,128)(2,1)S(1)} %get-tuple-element.108), channel_id=1, source_target_pairs={{0,4},{12,0},{1,5},{13,1},{2,6},{14,2},{3,7},{15,3},{16,20},{28,16... | collective-permute-start | bytes 98312 | tf_op jit(solution)/shard_map/ppermute | solution.py:505
  22.8 0.1 collective-permute-start.5
  22.8 1.7 %whole_shards_0.1 = (f32[2,1,1024]{2,1,0:T(1,128)S(1)}, f32[2,1,1024]{2,1,0:T(1,128)S(1)}, f32[2,128,1024]{2,1,0:T(8,128)S(1)}) custom-call(bf16[2,256,1024]{2,1,0:T(8,128)(2,1)S(1)} %get-tuple-element.62.qt_ref, bf16[3,128,128]{2,1,0:T(8,128)(2,1)S(1)} %get-tuple-element.63.near_ref, bf16[3,256,128]{2,1,0:T(8,128)(2,1)S(1)} %get-tuple-element.64.far_ref, ...), custom_call_target="tpu_custom_call" | custom-call | flops 402653184 | bytes 1048576 | tf_op jit(solution)/shard_map/whole_shards_0/pallas_call | solution.py:510
  24.6 0.1 collective-permute-done.1.refs_0_.refs_1_
  24.6 1.7 %whole_shards_1.1 = (f32[2,1,1024]{2,1,0:T(1,128)S(1)}, f32[2,1,1024]{2,1,0:T(1,128)S(1)}, f32[2,128,1024]{2,1,0:T(8,128)S(1)}) custom-call(bf16[2,256,1024]{2,1,0:T(8,128)(2,1)S(1)} %get-tuple-element.62.qt_ref, bf16[3,128,128]{2,1,0:T(8,128)(2,1)S(1)} %get-tuple-element.63.near_ref, bf16[3,256,128]{2,1,0:T(8,128)(2,1)S(1)} %get-tuple-element.64.far_ref, ...), custom_call_target="tpu_custom_call" | custom-call | flops 402653184 | bytes 1048576 | tf_op jit(solution)/shard_map/whole_shards_1/pallas_call | solution.py:510
  26.4 1.1 %decode_near_pages.1 = (f32[16,8,1]{2,1,0:T(8,128)S(1)}, f32[16,8,1]{2,1,0:T(8,128)S(1)}, f32[16,8,256]{2,1,0:T(8,128)S(1)}, f32[1,8,128]{2,1,0:T(8,128)S(1)}) custom-call(s32[1]{0:T(128)} %bitcast.own_ref, s32[32]{0:T(128)S(1)} %copy-done.4, s32[8]{0:T(128)S(1)} %copy-done.5, s32[8,32]{1,0:T(8,128)S(1)} %copy-done.3, ...), custom_call_target="tpu_custom_call" | custom-call | flops 134217728 | bytes 1048576 | tf_op jit(solution)/shard_map/decode_near_pages/pallas_call | solution.py:523
  27.5 2.3 %collective-permute-done.2.keys_ref = bf16[256,256]{1,0:T(8,128)(2,1)S(1)} collective-permute-done((bf16[256,256]{1,0:T(8,128)(2,1)S(1)}, bf16[256,256]{1,0:T(8,128)(2,1)S(1)}, u32[]{:S(2)}, u32[]{:S(2)}) %collective-permute-start.2) | collective-permute-done | bytes 131104 | tf_op jit(solution)/shard_map/ppermute | solution.py:423
  29.7 1.0 %last_scores.1 = (bf16[2,256,1024]{2,1,0:T(8,128)(2,1)S(1)}, f32[2,1,1024]{2,1,0:T(1,128)S(1)}, f32[2,128,1024]{2,1,0:T(8,128)S(1)}) custom-call(bf16[2,256,1024]{2,1,0:T(8,128)(2,1)S(1)} %get-tuple-element.62.qt_ref, bf16[3,128,128]{2,1,0:T(8,128)(2,1)S(1)} %get-tuple-element.63.near_ref, bf16[3,256,128]{2,1,0:T(8,128)(2,1)S(1)} %get-tuple-element.64.far_ref, ...), custom_call_target="tpu_custom_call" | custom-call | flops 402653184 | bytes 1048576 | tf_op jit(solution)/shard_map/last_scores/pallas_call | solution.py:538
  30.8 1.1 %decode_last_pages.1 = bf16[8,2048]{1,0:T(8,128)(2,1)} custom-call(bf16[256,256]{1,0:T(8,128)(2,1)S(1)} %collective-permute-done.3.stretch_ref, bf16[64,256]{1,0:T(8,128)(2,1)S(1)} %collective-permute-done.4.pages_ref, f32[1,8,128]{2,1,0:T(8,128)S(1)} %get-tuple-element.109.tally_ref, bf16[128,256]{1,0:T(8,128)(2,1)S(1)} %get-tuple-element.79.refs_2_.wide_ref, ...), custom_call_target="tpu_custom_call" | custom-call | flops 67108864 | bytes 1048576 | tf_op jit(solution)/shard_map/decode_last_pages/pallas_call | solution.py:549
  31.9 1.1 %last_values.1 = bf16[128,2048]{1,0:T(8,128)(2,1)} custom-call(bf16[2,256,1024]{2,1,0:T(8,128)(2,1)S(1)} %get-tuple-element.107.weights_ref, f32[2,1,1024]{2,1,0:T(1,128)S(1)} %get-tuple-element.118.total_ref, f32[2,128,1024]{2,1,0:T(8,128)S(1)} %get-tuple-element.119.accum_ref, bf16[256,256]{1,0:T(8,128)(2,1)S(1)} %collective-permute-done.5.values_ref), custom_call_target="tpu_custom_call" | custom-call | flops 134217728 | bytes 1048576 | tf_op jit(solution)/shard_map/last_values/pallas_call | solution.py:560
  (12 shorter events, 0.0 us)
Async XLA Ops:
  0.6 4.8 %copy-start.2 = (bf16[8,2048]{1,0:T(8,128)(2,1)S(1)}, bf16[8,2048]{1,0:T(8,128)(2,1)}, u32[]{:S(2)}) copy-start(bf16[8,2048]{1,0:T(8,128)(2,1)} %q_ref.3) | copy-start | bytes 98308
  1.7 14.3 %collective-permute-start = (bf16[768,256]{1,0:T(8,128)(2,1)S(1)}, bf16[768,256]{1,0:T(8,128)(2,1)S(1)}, u32[]{:S(2)}, u32[]{:S(2)}) collective-permute-start(bf16[768,256]{1,0:T(8,128)(2,1)S(1)} %pad_maximum_fusion.shard_ref.rest_ref), channel_id=1, source_target_pairs={{0,4},{4,8},{8,12},{12,0},{1,5},{5,9},{9,13},{13,1},{2,6},{6,10},{... | collective-permute-start | bytes 1179656 | tf_op jit(solution)/shard_map/ppermute | solution.py:423
  4.8 0.7 %copy-start.3 = (s32[8,32]{1,0:T(8,128)S(1)}, s32[8,32]{1,0:T(8,128)}, u32[]{:S(2)}) copy-start(s32[8,32]{1,0:T(8,128)} %lists_ref.3) | copy-start | bytes 3076
  5.4 0.7 %copy-start.4 = (s32[32]{0:T(128)S(1)}, s32[32]{0:T(128)}, u32[]{:S(2)}) copy-start(s32[32]{0:T(128)} %targets_ref.5) | copy-start | bytes 388
  5.4 0.7 %copy-start.5 = (s32[8]{0:T(128)S(1)}, s32[8]{0:T(128)}, u32[]{:S(2)}) copy-start(s32[8]{0:T(128)} %length_ref.3) | copy-start | bytes 100
  6.1 1.2 %copy-start = (bf16[128,16,256]{2,1,0:T(8,128)(2,1)S(1)}, bf16[128,16,256]{2,1,0:T(8,128)(2,1)}, u32[]{:S(2)}) copy-start(bf16[128,16,256]{2,1,0:T(8,128)(2,1)} %pool_k.1) | copy-start | bytes 3145732
  7.3 1.2 %copy-start.1 = (bf16[128,16,256]{2,1,0:T(8,128)(2,1)S(1)}, bf16[128,16,256]{2,1,0:T(8,128)(2,1)}, u32[]{:S(2)}) copy-start(bf16[128,16,256]{2,1,0:T(8,128)(2,1)} %pool_v.1) | copy-start | bytes 3145732
  8.5 1.9 %copy-start.6 = (bf16[128,2048]{1,0:T(8,128)(2,1)S(1)}, bf16[128,2048]{1,0:T(8,128)(2,1)}, u32[]{:S(2)}) copy-start(bf16[128,2048]{1,0:T(8,128)(2,1)} %q_ref.2) | copy-start | bytes 1572868
  12.8 11.8 %collective-permute-start.1 = (bf16[768,256]{1,0:T(8,128)(2,1)S(1)}, bf16[768,256]{1,0:T(8,128)(2,1)S(1)}, u32[]{:S(2)}, u32[]{:S(2)}) collective-permute-start(bf16[768,256]{1,0:T(8,128)(2,1)S(1)} %pad_maximum_fusion.shard_ref.rest_ref), channel_id=1, source_target_pairs={{0,12},{4,0},{8,4},{12,8},{1,13},{5,1},{9,5},{13,9},{2,14},{6,2},{... | collective-permute-start | bytes 1179656 | tf_op jit(solution)/shard_map/ppermute | solution.py:423
  16.1 13.6 %collective-permute-start.2 = (bf16[256,256]{1,0:T(8,128)(2,1)S(1)}, bf16[256,256]{1,0:T(8,128)(2,1)S(1)}, u32[]{:S(2)}, u32[]{:S(2)}) collective-permute-start(bf16[256,256]{1,0:T(8,128)(2,1)S(1)} %get-tuple-element.105), channel_id=1, source_target_pairs={{0,4},{4,8},{8,12},{12,0},{1,5},{5,9},{9,13},{13,1},{2,6},{6,10},{... | collective-permute-start | bytes 393224 | tf_op jit(solution)/shard_map/ppermute | solution.py:423
  16.2 13.5 %collective-permute-start.3 = (bf16[256,256]{1,0:T(8,128)(2,1)S(1)}, bf16[256,256]{1,0:T(8,128)(2,1)S(1)}, u32[]{:S(2)}, u32[]{:S(2)}) collective-permute-start(bf16[256,256]{1,0:T(8,128)(2,1)S(1)} %get-tuple-element.106), channel_id=1, source_target_pairs={{4,8},{8,12},{5,9},{9,13},{6,10},{10,14},{7,11},{11,15},{20,24},{2... | collective-permute-start | bytes 393224 | tf_op jit(solution)/shard_map/ppermute | solution.py:504
  16.9 13.9 %collective-permute-start.4 = (bf16[64,256]{1,0:T(8,128)(2,1)S(1)}, bf16[64,256]{1,0:T(8,128)(2,1)S(1)}, u32[]{:S(2)}, u32[]{:S(2)}) collective-permute-start(bf16[64,256]{1,0:T(8,128)(2,1)S(1)} %get-tuple-element.108), channel_id=1, source_target_pairs={{0,4},{12,0},{1,5},{13,1},{2,6},{14,2},{3,7},{15,3},{16,20},{28,16... | collective-permute-start | bytes 98312 | tf_op jit(solution)/shard_map/ppermute | solution.py:505
  22.8 9.1 %collective-permute-start.5 = (bf16[256,256]{1,0:T(8,128)(2,1)S(1)}, bf16[256,256]{1,0:T(8,128)(2,1)S(1)}, u32[]{:S(2)}, u32[]{:S(2)}) collective-permute-start(bf16[256,256]{1,0:T(8,128)(2,1)S(1)} %get-tuple-element.120), channel_id=1, source_target_pairs={{0,4},{4,8},{8,12},{12,0},{1,5},{5,9},{9,13},{13,1},{2,6},{6,10},{... | collective-permute-start | bytes 393224 | tf_op jit(solution)/shard_map/ppermute | solution.py:423

commit v22 on v21

--- a/solution.py
+++ b/solution.py
@@ -51,7 +51,7 @@
 
 def blocks_of(qt_ref):
     kv_local, _, rows = qt_ref.shape
-    width = min(2 * (rows // GROUP), rows)
+    width = min(4 * (rows // GROUP), rows)
     return [(head, slice(start, start + width)) for head in range(kv_local) for start in range(0, rows, width)]
 
 

time: 33.3 us -> 33 us (level)
  Pallas kernels: 12.2 us -> 11.5 us
  waiting for transfers between devices: 3.43 us -> 3.84 us
    ppermute x4, waiting for transfers between devices: 3.42 us -> 3.83 us  [send(): return lax.ppermute(array, 'ctx', up_pairs if hop < 0 else down_pairs)]
    pallas_call x2, Pallas kernels: 3.45 us -> 3.05 us  [per_device(): pl.pallas_call(functools.partial(hop_kernel, places), out_shape=state_sha...]
  transfers between devices with their start and end apart: 6 -> 6, of which waited for: 3 -> 3; matrix products, arithmetic and copies ran while one was open for 0% -> 0% of each run, Pallas kernels for 33% -> 32%
where the time goes in v22:
time: 33 us; the launch traced here: 32.7 us
  starting transfers between devices  11.9 us (36%)
  Pallas kernels  11.5 us (35%)
  waiting for transfers between devices  3.84 us (12%)
  local copies, waits for them, and re-layouts  3.1 us (9%)
  between operations  1.44 us (4%)
  other arithmetic  1.03 us (3%)
    ppermute x1, starting transfers between devices, per_device(): last_pages = lax.ppermute(pieces[3], 'ctx', others)  5.89 us
    ppermute x4, starting transfers between devices, send(): return lax.ppermute(array, 'ctx', up_pairs if hop < 0 else down_pairs)  5.29 us
    ppermute x4, waiting for transfers between devices, send(): return lax.ppermute(array, 'ctx', up_pairs if hop < 0 else down_pairs)  3.83 us
    unnamed x14, local copies, waits for them, and re-layouts  3.1 us
    pallas_call x2, Pallas kernels, per_device(): pl.pallas_call(functools.partial(hop_kernel, places), out_shape=state_sha...  3.05 us
    pallas_call x1, Pallas kernels, per_device(): pl.pallas_call(functools.partial(own_kernel, count, hops), out_shape=(sha...  2.07 us
    pallas_call x1, Pallas kernels, per_device(): pl.pallas_call(held_kernel, out_shape=(shape((heads * dec_rows, kv_width)...  1.86 us
    pallas_call x1, Pallas kernels, per_device(): pl.pallas_call(last_kernel, out_shape=shape((tokens, width), bf16), in_sp...  1.16 us
  transfers between devices with their start and end apart: 6, of which 3 were waited for; matrix products, arithmetic and copies ran while one was open for 0% of the time, Pallas kernels for 32%

profile of v22, /device:TPU:0, one launch (start us, length us, event | category | flops | bytes accessed | tf_op | source)
XLA Modules:
  0.0 32.7 jit_solution(4276299955380916946)
XLA Ops:
  0.6 1.0 %pad_maximum_fusion.shard_ref.rest_ref = bf16[768,256]{1,0:T(8,128)(2,1)S(1)} fusion(bf16[256,256]{1,0:T(8,128)(2,1)} %param.16, bf16[128,256]{1,0:T(8,128)(2,1)} %param.14, bf16[256,256]{1,0:T(8,128)(2,1)} %param.15, bf16[128,256]{1,0:T(8,128)(2,1)} %param.13), kind=kLoop, calls=%fused_computation | loop fusion | flops 1572864 | bytes 786432 | tf_op jit(solution)/shard_map/max | solution.py:438
  1.7 3.1 %collective-permute-start = (bf16[768,256]{1,0:T(8,128)(2,1)S(1)}, bf16[768,256]{1,0:T(8,128)(2,1)S(1)}, u32[]{:S(2)}, u32[]{:S(2)}) collective-permute-start(bf16[768,256]{1,0:T(8,128)(2,1)S(1)} %pad_maximum_fusion.shard_ref.rest_ref), channel_id=1, source_target_pairs={{0,4},{4,8},{8,12},{12,0},{1,5},{5,9},{9,13},{13,1},{2,6},{6,10},{... | collective-permute-start | bytes 1179656 | tf_op jit(solution)/shard_map/ppermute | solution.py:423
  5.4 0.0 copy-start.5
  5.5 0.6 %copy-done.4 = s32[32]{0:T(128)S(1)} copy-done((s32[32]{0:T(128)S(1)}, s32[32]{0:T(128)}, u32[]{:S(2)}) %copy-start.4) | copy-done | bytes 152
  6.1 0.0 copy-done.5
  6.1 1.2 %copy-done = bf16[128,16,256]{2,1,0:T(8,128)(2,1)S(1)} copy-done((bf16[128,16,256]{2,1,0:T(8,128)(2,1)S(1)}, bf16[128,16,256]{2,1,0:T(8,128)(2,1)}, u32[]{:S(2)}) %copy-start) | copy-done | bytes 1048600
  7.3 1.2 %copy-done.1 = bf16[128,16,256]{2,1,0:T(8,128)(2,1)S(1)} copy-done((bf16[128,16,256]{2,1,0:T(8,128)(2,1)S(1)}, bf16[128,16,256]{2,1,0:T(8,128)(2,1)}, u32[]{:S(2)}) %copy-start.1) | copy-done | bytes 1048600
  8.5 1.9 %decode_held_pages.1 = (bf16[128,256]{1,0:T(8,128)(2,1)S(1)}, f32[16,8,1]{2,1,0:T(8,128)S(1)}, f32[16,8,1]{2,1,0:T(8,128)S(1)}, f32[16,8,256]{2,1,0:T(8,128)S(1)}) custom-call(s32[1]{0:T(128)} %bitcast.own_ref, s32[32]{0:T(128)S(1)} %copy-done.4, s32[8]{0:T(128)S(1)} %copy-done.5, bf16[8,2048]{1,0:T(8,128)(2,1)S(1)} %copy-done.2, s32[8,32]{1,0:T(8,128)S(1)} %copy-done.3, ...), custom_call_target="tpu_custom_call" | custom-call | flops 268435456 | bytes 2097152 | tf_op jit(solution)/shard_map/decode_held_pages/pallas_call | solution.py:467
  10.4 2.1 %own_shard.1 = (bf16[2,256,1024]{2,1,0:T(8,128)(2,1)S(1)}, bf16[3,128,128]{2,1,0:T(8,128)(2,1)S(1)}, bf16[3,256,128]{2,1,0:T(8,128)(2,1)S(1)}, bf16[32,128]{1,0:...) custom-call(s32[1]{0:T(128)} %bitcast.own_ref, ...), custom_call_target="tpu_custom_call" | custom-call | flops 402653184 | bytes 1048576 | tf_op jit(solution)/shard_map/own_shard/pallas_call | solution.py:446
  12.5 2.1 %collective-permute-start.1 = (bf16[768,256]{1,0:T(8,128)(2,1)S(1)}, bf16[768,256]{1,0:T(8,128)(2,1)S(1)}, u32[]{:S(2)}, u32[]{:S(2)}) collective-permute-start(bf16[768,256]{1,0:T(8,128)(2,1)S(1)} %pad_maximum_fusion.shard_ref.rest_ref), channel_id=1, source_target_pairs={{0,12},{4,0},{8,4},{12,8},{1,13},{5,1},{9,5},{13,9},{2,14},{6,2},{... | collective-permute-start | bytes 1179656 | tf_op jit(solution)/shard_map/ppermute | solution.py:423
  14.6 1.4 %collective-permute-done.refs_0_.shard_ref = bf16[768,256]{1,0:T(8,128)(2,1)S(1)} collective-permute-done((bf16[768,256]{1,0:T(8,128)(2,1)S(1)}, bf16[768,256]{1,0:T(8,128)(2,1)S(1)}, u32[]{:S(2)}, u32[]{:S(2)}) %collective-permute-start) | collective-permute-done | bytes 393248 | tf_op jit(solution)/shard_map/ppermute | solution.py:423
  16.0 0.1 pieces_to_send_on.1
  16.1 0.1 collective-permute-start.2
  16.2 0.7 %collective-permute-start.3 = (bf16[256,256]{1,0:T(8,128)(2,1)S(1)}, bf16[256,256]{1,0:T(8,128)(2,1)S(1)}, u32[]{:S(2)}, u32[]{:S(2)}) collective-permute-start(bf16[256,256]{1,0:T(8,128)(2,1)S(1)} %get-tuple-element.106), channel_id=1, source_target_pairs={{4,8},{8,12},{5,9},{9,13},{6,10},{10,14},{7,11},{11,15},{20,24},{2... | collective-permute-start | bytes 393224 | tf_op jit(solution)/shard_map/ppermute | solution.py:504
  16.9 5.9 %collective-permute-start.4 = (bf16[64,256]{1,0:T(8,128)(2,1)S(1)}, bf16[64,256]{1,0:T(8,128)(2,1)S(1)}, u32[]{:S(2)}, u32[]{:S(2)}) collective-permute-start(bf16[64,256]{1,0:T(8,128)(2,1)S(1)} %get-tuple-element.108), channel_id=1, source_target_pairs={{0,4},{12,0},{1,5},{13,1},{2,6},{14,2},{3,7},{15,3},{16,20},{28,16... | collective-permute-start | bytes 98312 | tf_op jit(solution)/shard_map/ppermute | solution.py:505
  22.8 0.1 collective-permute-start.5
  22.8 1.5 %whole_shards_0.1 = (f32[2,1,1024]{2,1,0:T(1,128)S(1)}, f32[2,1,1024]{2,1,0:T(1,128)S(1)}, f32[2,128,1024]{2,1,0:T(8,128)S(1)}) custom-call(bf16[2,256,1024]{2,1,0:T(8,128)(2,1)S(1)} %get-tuple-element.62.qt_ref, bf16[3,128,128]{2,1,0:T(8,128)(2,1)S(1)} %get-tuple-element.63.near_ref, bf16[3,256,128]{2,1,0:T(8,128)(2,1)S(1)} %get-tuple-element.64.far_ref, ...), custom_call_target="tpu_custom_call" | custom-call | flops 402653184 | bytes 1048576 | tf_op jit(solution)/shard_map/whole_shards_0/pallas_call | solution.py:510
  24.4 0.6 %collective-permute-done.1.refs_0_.refs_1_ = bf16[768,256]{1,0:T(8,128)(2,1)S(1)} collective-permute-done((bf16[768,256]{1,0:T(8,128)(2,1)S(1)}, bf16[768,256]{1,0:T(8,128)(2,1)S(1)}, u32[]{:S(2)}, u32[]{:S(2)}) %collective-permute-start.1) | collective-permute-done | bytes 393248 | tf_op jit(solution)/shard_map/ppermute | solution.py:423
  24.9 1.5 %whole_shards_1.1 = (f32[2,1,1024]{2,1,0:T(1,128)S(1)}, f32[2,1,1024]{2,1,0:T(1,128)S(1)}, f32[2,128,1024]{2,1,0:T(8,128)S(1)}) custom-call(bf16[2,256,1024]{2,1,0:T(8,128)(2,1)S(1)} %get-tuple-element.62.qt_ref, bf16[3,128,128]{2,1,0:T(8,128)(2,1)S(1)} %get-tuple-element.63.near_ref, bf16[3,256,128]{2,1,0:T(8,128)(2,1)S(1)} %get-tuple-element.64.far_ref, ...), custom_call_target="tpu_custom_call" | custom-call | flops 402653184 | bytes 1048576 | tf_op jit(solution)/shard_map/whole_shards_1/pallas_call | solution.py:510
  26.5 1.1 %decode_near_pages.1 = (f32[16,8,1]{2,1,0:T(8,128)S(1)}, f32[16,8,1]{2,1,0:T(8,128)S(1)}, f32[16,8,256]{2,1,0:T(8,128)S(1)}, f32[1,8,128]{2,1,0:T(8,128)S(1)}) custom-call(s32[1]{0:T(128)} %bitcast.own_ref, s32[32]{0:T(128)S(1)} %copy-done.4, s32[8]{0:T(128)S(1)} %copy-done.5, s32[8,32]{1,0:T(8,128)S(1)} %copy-done.3, ...), custom_call_target="tpu_custom_call" | custom-call | flops 134217728 | bytes 1048576 | tf_op jit(solution)/shard_map/decode_near_pages/pallas_call | solution.py:523
  27.6 1.9 %collective-permute-done.2.keys_ref = bf16[256,256]{1,0:T(8,128)(2,1)S(1)} collective-permute-done((bf16[256,256]{1,0:T(8,128)(2,1)S(1)}, bf16[256,256]{1,0:T(8,128)(2,1)S(1)}, u32[]{:S(2)}, u32[]{:S(2)}) %collective-permute-start.2) | collective-permute-done | bytes 131104 | tf_op jit(solution)/shard_map/ppermute | solution.py:423
  29.4 1.0 %last_scores.1 = (bf16[2,256,1024]{2,1,0:T(8,128)(2,1)S(1)}, f32[2,1,1024]{2,1,0:T(1,128)S(1)}, f32[2,128,1024]{2,1,0:T(8,128)S(1)}) custom-call(bf16[2,256,1024]{2,1,0:T(8,128)(2,1)S(1)} %get-tuple-element.62.qt_ref, bf16[3,128,128]{2,1,0:T(8,128)(2,1)S(1)} %get-tuple-element.63.near_ref, bf16[3,256,128]{2,1,0:T(8,128)(2,1)S(1)} %get-tuple-element.64.far_ref, ...), custom_call_target="tpu_custom_call" | custom-call | flops 402653184 | bytes 1048576 | tf_op jit(solution)/shard_map/last_scores/pallas_call | solution.py:538
  30.5 1.1 %decode_last_pages.1 = bf16[8,2048]{1,0:T(8,128)(2,1)} custom-call(bf16[256,256]{1,0:T(8,128)(2,1)S(1)} %collective-permute-done.3.stretch_ref, bf16[64,256]{1,0:T(8,128)(2,1)S(1)} %collective-permute-done.4.pages_ref, f32[1,8,128]{2,1,0:T(8,128)S(1)} %get-tuple-element.109.tally_ref, bf16[128,256]{1,0:T(8,128)(2,1)S(1)} %get-tuple-element.79.refs_2_.wide_ref, ...), custom_call_target="tpu_custom_call" | custom-call | flops 67108864 | bytes 1048576 | tf_op jit(solution)/shard_map/decode_last_pages/pallas_call | solution.py:549
  31.6 1.2 %last_values.1 = bf16[128,2048]{1,0:T(8,128)(2,1)} custom-call(bf16[2,256,1024]{2,1,0:T(8,128)(2,1)S(1)} %get-tuple-element.107.weights_ref, f32[2,1,1024]{2,1,0:T(1,128)S(1)} %get-tuple-element.118.total_ref, f32[2,128,1024]{2,1,0:T(8,128)S(1)} %get-tuple-element.119.accum_ref, bf16[256,256]{1,0:T(8,128)(2,1)S(1)} %collective-permute-done.5.values_ref), custom_call_target="tpu_custom_call" | custom-call | flops 134217728 | bytes 1048576 | tf_op jit(solution)/shard_map/last_values/pallas_call | solution.py:560
  (12 shorter events, 0.0 us)
Async XLA Ops:
  0.6 4.8 %copy-start.2 = (bf16[8,2048]{1,0:T(8,128)(2,1)S(1)}, bf16[8,2048]{1,0:T(8,128)(2,1)}, u32[]{:S(2)}) copy-start(bf16[8,2048]{1,0:T(8,128)(2,1)} %q_ref.3) | copy-start | bytes 98308
  1.7 14.3 %collective-permute-start = (bf16[768,256]{1,0:T(8,128)(2,1)S(1)}, bf16[768,256]{1,0:T(8,128)(2,1)S(1)}, u32[]{:S(2)}, u32[]{:S(2)}) collective-permute-start(bf16[768,256]{1,0:T(8,128)(2,1)S(1)} %pad_maximum_fusion.shard_ref.rest_ref), channel_id=1, source_target_pairs={{0,4},{4,8},{8,12},{12,0},{1,5},{5,9},{9,13},{13,1},{2,6},{6,10},{... | collective-permute-start | bytes 1179656 | tf_op jit(solution)/shard_map/ppermute | solution.py:423
  4.8 0.7 %copy-start.3 = (s32[8,32]{1,0:T(8,128)S(1)}, s32[8,32]{1,0:T(8,128)}, u32[]{:S(2)}) copy-start(s32[8,32]{1,0:T(8,128)} %lists_ref.3) | copy-start | bytes 3076
  5.4 0.7 %copy-start.4 = (s32[32]{0:T(128)S(1)}, s32[32]{0:T(128)}, u32[]{:S(2)}) copy-start(s32[32]{0:T(128)} %targets_ref.5) | copy-start | bytes 388
  5.4 0.7 %copy-start.5 = (s32[8]{0:T(128)S(1)}, s32[8]{0:T(128)}, u32[]{:S(2)}) copy-start(s32[8]{0:T(128)} %length_ref.3) | copy-start | bytes 100
  6.1 1.2 %copy-start = (bf16[128,16,256]{2,1,0:T(8,128)(2,1)S(1)}, bf16[128,16,256]{2,1,0:T(8,128)(2,1)}, u32[]{:S(2)}) copy-start(bf16[128,16,256]{2,1,0:T(8,128)(2,1)} %pool_k.1) | copy-start | bytes 3145732
  7.3 1.2 %copy-start.1 = (bf16[128,16,256]{2,1,0:T(8,128)(2,1)S(1)}, bf16[128,16,256]{2,1,0:T(8,128)(2,1)}, u32[]{:S(2)}) copy-start(bf16[128,16,256]{2,1,0:T(8,128)(2,1)} %pool_v.1) | copy-start | bytes 3145732
  8.5 1.9 %copy-start.6 = (bf16[128,2048]{1,0:T(8,128)(2,1)S(1)}, bf16[128,2048]{1,0:T(8,128)(2,1)}, u32[]{:S(2)}) copy-start(bf16[128,2048]{1,0:T(8,128)(2,1)} %q_ref.2) | copy-start | bytes 1572868
  12.5 12.4 %collective-permute-start.1 = (bf16[768,256]{1,0:T(8,128)(2,1)S(1)}, bf16[768,256]{1,0:T(8,128)(2,1)S(1)}, u32[]{:S(2)}, u32[]{:S(2)}) collective-permute-start(bf16[768,256]{1,0:T(8,128)(2,1)S(1)} %pad_maximum_fusion.shard_ref.rest_ref), channel_id=1, source_target_pairs={{0,12},{4,0},{8,4},{12,8},{1,13},{5,1},{9,5},{13,9},{2,14},{6,2},{... | collective-permute-start | bytes 1179656 | tf_op jit(solution)/shard_map/ppermute | solution.py:423
  16.1 13.3 %collective-permute-start.2 = (bf16[256,256]{1,0:T(8,128)(2,1)S(1)}, bf16[256,256]{1,0:T(8,128)(2,1)S(1)}, u32[]{:S(2)}, u32[]{:S(2)}) collective-permute-start(bf16[256,256]{1,0:T(8,128)(2,1)S(1)} %get-tuple-element.105), channel_id=1, source_target_pairs={{0,4},{4,8},{8,12},{12,0},{1,5},{5,9},{9,13},{13,1},{2,6},{6,10},{... | collective-permute-start | bytes 393224 | tf_op jit(solution)/shard_map/ppermute | solution.py:423
  16.2 13.2 %collective-permute-start.3 = (bf16[256,256]{1,0:T(8,128)(2,1)S(1)}, bf16[256,256]{1,0:T(8,128)(2,1)S(1)}, u32[]{:S(2)}, u32[]{:S(2)}) collective-permute-start(bf16[256,256]{1,0:T(8,128)(2,1)S(1)} %get-tuple-element.106), channel_id=1, source_target_pairs={{4,8},{8,12},{5,9},{9,13},{6,10},{10,14},{7,11},{11,15},{20,24},{2... | collective-permute-start | bytes 393224 | tf_op jit(solution)/shard_map/ppermute | solution.py:504
  16.9 13.6 %collective-permute-start.4 = (bf16[64,256]{1,0:T(8,128)(2,1)S(1)}, bf16[64,256]{1,0:T(8,128)(2,1)S(1)}, u32[]{:S(2)}, u32[]{:S(2)}) collective-permute-start(bf16[64,256]{1,0:T(8,128)(2,1)S(1)} %get-tuple-element.108), channel_id=1, source_target_pairs={{0,4},{12,0},{1,5},{13,1},{2,6},{14,2},{3,7},{15,3},{16,20},{28,16... | collective-permute-start | bytes 98312 | tf_op jit(solution)/shard_map/ppermute | solution.py:505
  22.8 8.8 %collective-permute-start.5 = (bf16[256,256]{1,0:T(8,128)(2,1)S(1)}, bf16[256,256]{1,0:T(8,128)(2,1)S(1)}, u32[]{:S(2)}, u32[]{:S(2)}) collective-permute-start(bf16[256,256]{1,0:T(8,128)(2,1)S(1)} %get-tuple-element.120), channel_id=1, source_target_pairs={{0,4},{4,8},{8,12},{12,0},{1,5},{5,9},{9,13},{13,1},{2,6},{6,10},{... | collective-permute-start | bytes 393224 | tf_op jit(solution)/shard_map/ppermute | solution.py:423

commit v23 on v22

--- a/solution.py
+++ b/solution.py
@@ -49,9 +49,9 @@
         second(block, current)
 
 
-def blocks_of(qt_ref):
-    kv_local, _, rows = qt_ref.shape
-    width = min(4 * (rows // GROUP), rows)
+def blocks_of(ref, groups=GROUP):
+    kv_local, _, rows = ref.shape
+    width = groups * (rows // GROUP)
     return [(head, slice(start, start + width)) for head in range(kv_local) for start in range(0, rows, width)]
 
 
@@ -379,7 +379,7 @@
         copy.start()
         copies.append(copy)
 
-    walk(blocks_of(weights_ref), first, second)
+    walk(blocks_of(weights_ref, 2), first, second)
 
     for copy in copies:
         copy.wait()
@@ -564,7 +564,7 @@
         out_specs=HBM,
         scratch_shapes=[
             pltpu.VMEM((tokens, width), bf16),
-            pltpu.SemaphoreType.DMA((kv_local * max(GROUP // 2, 1),)),
+            pltpu.SemaphoreType.DMA((kv_local * GROUP // 2,)),
         ],
         compiler_params=params,
         cost_estimate=cost(c_rows // 2),

time: 33 us -> 32.9 us (level)
  Pallas kernels: 11.5 us -> 11.1 us
  transfers between devices with their start and end apart: 6 -> 6, of which waited for: 3 -> 3; matrix products, arithmetic and copies ran while one was open for 0% -> 0% of each run, Pallas kernels for 32% -> 30%
where the time goes in v23:
time: 32.9 us; the launch traced here: 32.6 us
  starting transfers between devices  11.9 us (36%)
  Pallas kernels  11.1 us (34%)
  waiting for transfers between devices  4.12 us (13%)
  local copies, waits for them, and re-layouts  3.1 us (9%)
  between operations  1.44 us (4%)
  other arithmetic  1.03 us (3%)
    ppermute x1, starting transfers between devices, per_device(): last_pages = lax.ppermute(pieces[3], 'ctx', others)  5.89 us
    ppermute x4, starting transfers between devices, send(): return lax.ppermute(array, 'ctx', up_pairs if hop < 0 else down_pairs)  5.29 us
    ppermute x4, waiting for transfers between devices, send(): return lax.ppermute(array, 'ctx', up_pairs if hop < 0 else down_pairs)  4.11 us
    unnamed x14, local copies, waits for them, and re-layouts  3.1 us
    pallas_call x2, Pallas kernels, per_device(): pl.pallas_call(functools.partial(hop_kernel, places), out_shape=state_sha...  2.78 us
    pallas_call x1, Pallas kernels, per_device(): pl.pallas_call(functools.partial(own_kernel, count, hops), out_shape=(sha...  1.99 us
    pallas_call x1, Pallas kernels, per_device(): pl.pallas_call(held_kernel, out_shape=(shape((heads * dec_rows, kv_width)...  1.86 us
    pallas_call x1, Pallas kernels, per_device(): pl.pallas_call(last_kernel, out_shape=shape((tokens, width), bf16), in_sp...  1.14 us
  transfers between devices with their start and end apart: 6, of which 3 were waited for; matrix products, arithmetic and copies ran while one was open for 0% of the time, Pallas kernels for 30%

profile of v23, /device:TPU:0, one launch (start us, length us, event | category | flops | bytes accessed | tf_op | source)
XLA Modules:
  0.0 32.6 jit_solution(4577822988916586723)
XLA Ops:
  0.6 1.0 %pad_maximum_fusion.shard_ref.rest_ref = bf16[768,256]{1,0:T(8,128)(2,1)S(1)} fusion(bf16[256,256]{1,0:T(8,128)(2,1)} %param.16, bf16[128,256]{1,0:T(8,128)(2,1)} %param.14, bf16[256,256]{1,0:T(8,128)(2,1)} %param.15, bf16[128,256]{1,0:T(8,128)(2,1)} %param.13), kind=kLoop, calls=%fused_computation | loop fusion | flops 1572864 | bytes 786432 | tf_op jit(solution)/shard_map/max | solution.py:438
  1.7 3.1 %collective-permute-start = (bf16[768,256]{1,0:T(8,128)(2,1)S(1)}, bf16[768,256]{1,0:T(8,128)(2,1)S(1)}, u32[]{:S(2)}, u32[]{:S(2)}) collective-permute-start(bf16[768,256]{1,0:T(8,128)(2,1)S(1)} %pad_maximum_fusion.shard_ref.rest_ref), channel_id=1, source_target_pairs={{0,4},{4,8},{8,12},{12,0},{1,5},{5,9},{9,13},{13,1},{2,6},{6,10},{... | collective-permute-start | bytes 1179656 | tf_op jit(solution)/shard_map/ppermute | solution.py:423
  5.4 0.0 copy-start.4
  5.5 0.6 %copy-done.4 = s32[32]{0:T(128)S(1)} copy-done((s32[32]{0:T(128)S(1)}, s32[32]{0:T(128)}, u32[]{:S(2)}) %copy-start.4) | copy-done | bytes 152
  6.1 0.0 copy-done.5
  6.1 1.2 %copy-done = bf16[128,16,256]{2,1,0:T(8,128)(2,1)S(1)} copy-done((bf16[128,16,256]{2,1,0:T(8,128)(2,1)S(1)}, bf16[128,16,256]{2,1,0:T(8,128)(2,1)}, u32[]{:S(2)}) %copy-start) | copy-done | bytes 1048600
  7.3 1.2 %copy-done.1 = bf16[128,16,256]{2,1,0:T(8,128)(2,1)S(1)} copy-done((bf16[128,16,256]{2,1,0:T(8,128)(2,1)S(1)}, bf16[128,16,256]{2,1,0:T(8,128)(2,1)}, u32[]{:S(2)}) %copy-start.1) | copy-done | bytes 1048600
  8.5 1.9 %decode_held_pages.1 = (bf16[128,256]{1,0:T(8,128)(2,1)S(1)}, f32[16,8,1]{2,1,0:T(8,128)S(1)}, f32[16,8,1]{2,1,0:T(8,128)S(1)}, f32[16,8,256]{2,1,0:T(8,128)S(1)}) custom-call(s32[1]{0:T(128)} %bitcast.own_ref, s32[32]{0:T(128)S(1)} %copy-done.4, s32[8]{0:T(128)S(1)} %copy-done.5, bf16[8,2048]{1,0:T(8,128)(2,1)S(1)} %copy-done.2, s32[8,32]{1,0:T(8,128)S(1)} %copy-done.3, ...), custom_call_target="tpu_custom_call" | custom-call | flops 268435456 | bytes 2097152 | tf_op jit(solution)/shard_map/decode_held_pages/pallas_call | solution.py:467
  10.4 2.0 %own_shard.1 = (bf16[2,256,1024]{2,1,0:T(8,128)(2,1)S(1)}, bf16[3,128,128]{2,1,0:T(8,128)(2,1)S(1)}, bf16[3,256,128]{2,1,0:T(8,128)(2,1)S(1)}, bf16[32,128]{1,0:...) custom-call(s32[1]{0:T(128)} %bitcast.own_ref, ...), custom_call_target="tpu_custom_call" | custom-call | flops 402653184 | bytes 1048576 | tf_op jit(solution)/shard_map/own_shard/pallas_call | solution.py:446
  12.4 2.1 %collective-permute-start.1 = (bf16[768,256]{1,0:T(8,128)(2,1)S(1)}, bf16[768,256]{1,0:T(8,128)(2,1)S(1)}, u32[]{:S(2)}, u32[]{:S(2)}) collective-permute-start(bf16[768,256]{1,0:T(8,128)(2,1)S(1)} %pad_maximum_fusion.shard_ref.rest_ref), channel_id=1, source_target_pairs={{0,12},{4,0},{8,4},{12,8},{1,13},{5,1},{9,5},{13,9},{2,14},{6,2},{... | collective-permute-start | bytes 1179656 | tf_op jit(solution)/shard_map/ppermute | solution.py:423
  14.5 1.5 %collective-permute-done.refs_0_.shard_ref = bf16[768,256]{1,0:T(8,128)(2,1)S(1)} collective-permute-done((bf16[768,256]{1,0:T(8,128)(2,1)S(1)}, bf16[768,256]{1,0:T(8,128)(2,1)S(1)}, u32[]{:S(2)}, u32[]{:S(2)}) %collective-permute-start) | collective-permute-done | bytes 393248 | tf_op jit(solution)/shard_map/ppermute | solution.py:423
  16.0 0.1 pieces_to_send_on.1
  16.1 0.1 collective-permute-start.2
  16.2 0.7 %collective-permute-start.3 = (bf16[256,256]{1,0:T(8,128)(2,1)S(1)}, bf16[256,256]{1,0:T(8,128)(2,1)S(1)}, u32[]{:S(2)}, u32[]{:S(2)}) collective-permute-start(bf16[256,256]{1,0:T(8,128)(2,1)S(1)} %get-tuple-element.106), channel_id=1, source_target_pairs={{4,8},{8,12},{5,9},{9,13},{6,10},{10,14},{7,11},{11,15},{20,24},{2... | collective-permute-start | bytes 393224 | tf_op jit(solution)/shard_map/ppermute | solution.py:504
  16.9 5.9 %collective-permute-start.4 = (bf16[64,256]{1,0:T(8,128)(2,1)S(1)}, bf16[64,256]{1,0:T(8,128)(2,1)S(1)}, u32[]{:S(2)}, u32[]{:S(2)}) collective-permute-start(bf16[64,256]{1,0:T(8,128)(2,1)S(1)} %get-tuple-element.108), channel_id=1, source_target_pairs={{0,4},{12,0},{1,5},{13,1},{2,6},{14,2},{3,7},{15,3},{16,20},{28,16... | collective-permute-start | bytes 98312 | tf_op jit(solution)/shard_map/ppermute | solution.py:505
  22.8 0.1 collective-permute-start.5
  22.8 1.4 %whole_shards_0.1 = (f32[2,1,1024]{2,1,0:T(1,128)S(1)}, f32[2,1,1024]{2,1,0:T(1,128)S(1)}, f32[2,128,1024]{2,1,0:T(8,128)S(1)}) custom-call(bf16[2,256,1024]{2,1,0:T(8,128)(2,1)S(1)} %get-tuple-element.62.qt_ref, bf16[3,128,128]{2,1,0:T(8,128)(2,1)S(1)} %get-tuple-element.63.near_ref, bf16[3,256,128]{2,1,0:T(8,128)(2,1)S(1)} %get-tuple-element.64.far_ref, ...), custom_call_target="tpu_custom_call" | custom-call | flops 402653184 | bytes 1048576 | tf_op jit(solution)/shard_map/whole_shards_0/pallas_call | solution.py:510
  24.2 0.8 %collective-permute-done.1.refs_0_.refs_1_ = bf16[768,256]{1,0:T(8,128)(2,1)S(1)} collective-permute-done((bf16[768,256]{1,0:T(8,128)(2,1)S(1)}, bf16[768,256]{1,0:T(8,128)(2,1)S(1)}, u32[]{:S(2)}, u32[]{:S(2)}) %collective-permute-start.1) | collective-permute-done | bytes 393248 | tf_op jit(solution)/shard_map/ppermute | solution.py:423
  25.0 1.4 %whole_shards_1.1 = (f32[2,1,1024]{2,1,0:T(1,128)S(1)}, f32[2,1,1024]{2,1,0:T(1,128)S(1)}, f32[2,128,1024]{2,1,0:T(8,128)S(1)}) custom-call(bf16[2,256,1024]{2,1,0:T(8,128)(2,1)S(1)} %get-tuple-element.62.qt_ref, bf16[3,128,128]{2,1,0:T(8,128)(2,1)S(1)} %get-tuple-element.63.near_ref, bf16[3,256,128]{2,1,0:T(8,128)(2,1)S(1)} %get-tuple-element.64.far_ref, ...), custom_call_target="tpu_custom_call" | custom-call | flops 402653184 | bytes 1048576 | tf_op jit(solution)/shard_map/whole_shards_1/pallas_call | solution.py:510
  26.4 1.1 %decode_near_pages.1 = (f32[16,8,1]{2,1,0:T(8,128)S(1)}, f32[16,8,1]{2,1,0:T(8,128)S(1)}, f32[16,8,256]{2,1,0:T(8,128)S(1)}, f32[1,8,128]{2,1,0:T(8,128)S(1)}) custom-call(s32[1]{0:T(128)} %bitcast.own_ref, s32[32]{0:T(128)S(1)} %copy-done.4, s32[8]{0:T(128)S(1)} %copy-done.5, s32[8,32]{1,0:T(8,128)S(1)} %copy-done.3, ...), custom_call_target="tpu_custom_call" | custom-call | flops 134217728 | bytes 1048576 | tf_op jit(solution)/shard_map/decode_near_pages/pallas_call | solution.py:523
  27.5 1.8 %collective-permute-done.2.keys_ref = bf16[256,256]{1,0:T(8,128)(2,1)S(1)} collective-permute-done((bf16[256,256]{1,0:T(8,128)(2,1)S(1)}, bf16[256,256]{1,0:T(8,128)(2,1)S(1)}, u32[]{:S(2)}, u32[]{:S(2)}) %collective-permute-start.2) | collective-permute-done | bytes 131104 | tf_op jit(solution)/shard_map/ppermute | solution.py:423
  29.4 1.0 %last_scores.1 = (bf16[2,256,1024]{2,1,0:T(8,128)(2,1)S(1)}, f32[2,1,1024]{2,1,0:T(1,128)S(1)}, f32[2,128,1024]{2,1,0:T(8,128)S(1)}) custom-call(bf16[2,256,1024]{2,1,0:T(8,128)(2,1)S(1)} %get-tuple-element.62.qt_ref, bf16[3,128,128]{2,1,0:T(8,128)(2,1)S(1)} %get-tuple-element.63.near_ref, bf16[3,256,128]{2,1,0:T(8,128)(2,1)S(1)} %get-tuple-element.64.far_ref, ...), custom_call_target="tpu_custom_call" | custom-call | flops 402653184 | bytes 1048576 | tf_op jit(solution)/shard_map/last_scores/pallas_call | solution.py:538
  30.4 1.1 %decode_last_pages.1 = bf16[8,2048]{1,0:T(8,128)(2,1)} custom-call(bf16[256,256]{1,0:T(8,128)(2,1)S(1)} %collective-permute-done.3.stretch_ref, bf16[64,256]{1,0:T(8,128)(2,1)S(1)} %collective-permute-done.4.pages_ref, f32[1,8,128]{2,1,0:T(8,128)S(1)} %get-tuple-element.109.tally_ref, bf16[128,256]{1,0:T(8,128)(2,1)S(1)} %get-tuple-element.79.refs_2_.wide_ref, ...), custom_call_target="tpu_custom_call" | custom-call | flops 67108864 | bytes 1048576 | tf_op jit(solution)/shard_map/decode_last_pages/pallas_call | solution.py:549
  31.5 1.1 %last_values.1 = bf16[128,2048]{1,0:T(8,128)(2,1)} custom-call(bf16[2,256,1024]{2,1,0:T(8,128)(2,1)S(1)} %get-tuple-element.107.weights_ref, f32[2,1,1024]{2,1,0:T(1,128)S(1)} %get-tuple-element.118.total_ref, f32[2,128,1024]{2,1,0:T(8,128)S(1)} %get-tuple-element.119.accum_ref, bf16[256,256]{1,0:T(8,128)(2,1)S(1)} %collective-permute-done.5.values_ref), custom_call_target="tpu_custom_call" | custom-call | flops 134217728 | bytes 1048576 | tf_op jit(solution)/shard_map/last_values/pallas_call | solution.py:560
  (12 shorter events, 0.0 us)
Async XLA Ops:
  0.6 4.8 %copy-start.2 = (bf16[8,2048]{1,0:T(8,128)(2,1)S(1)}, bf16[8,2048]{1,0:T(8,128)(2,1)}, u32[]{:S(2)}) copy-start(bf16[8,2048]{1,0:T(8,128)(2,1)} %q_ref.3) | copy-start | bytes 98308
  1.7 14.3 %collective-permute-start = (bf16[768,256]{1,0:T(8,128)(2,1)S(1)}, bf16[768,256]{1,0:T(8,128)(2,1)S(1)}, u32[]{:S(2)}, u32[]{:S(2)}) collective-permute-start(bf16[768,256]{1,0:T(8,128)(2,1)S(1)} %pad_maximum_fusion.shard_ref.rest_ref), channel_id=1, source_target_pairs={{0,4},{4,8},{8,12},{12,0},{1,5},{5,9},{9,13},{13,1},{2,6},{6,10},{... | collective-permute-start | bytes 1179656 | tf_op jit(solution)/shard_map/ppermute | solution.py:423
  4.8 0.7 %copy-start.3 = (s32[8,32]{1,0:T(8,128)S(1)}, s32[8,32]{1,0:T(8,128)}, u32[]{:S(2)}) copy-start(s32[8,32]{1,0:T(8,128)} %lists_ref.3) | copy-start | bytes 3076
  5.4 0.7 %copy-start.4 = (s32[32]{0:T(128)S(1)}, s32[32]{0:T(128)}, u32[]{:S(2)}) copy-start(s32[32]{0:T(128)} %targets_ref.5) | copy-start | bytes 388
  5.4 0.7 %copy-start.5 = (s32[8]{0:T(128)S(1)}, s32[8]{0:T(128)}, u32[]{:S(2)}) copy-start(s32[8]{0:T(128)} %length_ref.3) | copy-start | bytes 100
  6.1 1.2 %copy-start = (bf16[128,16,256]{2,1,0:T(8,128)(2,1)S(1)}, bf16[128,16,256]{2,1,0:T(8,128)(2,1)}, u32[]{:S(2)}) copy-start(bf16[128,16,256]{2,1,0:T(8,128)(2,1)} %pool_k.1) | copy-start | bytes 3145732
  7.3 1.2 %copy-start.1 = (bf16[128,16,256]{2,1,0:T(8,128)(2,1)S(1)}, bf16[128,16,256]{2,1,0:T(8,128)(2,1)}, u32[]{:S(2)}) copy-start(bf16[128,16,256]{2,1,0:T(8,128)(2,1)} %pool_v.1) | copy-start | bytes 3145732
  8.5 1.9 %copy-start.6 = (bf16[128,2048]{1,0:T(8,128)(2,1)S(1)}, bf16[128,2048]{1,0:T(8,128)(2,1)}, u32[]{:S(2)}) copy-start(bf16[128,2048]{1,0:T(8,128)(2,1)} %q_ref.2) | copy-start | bytes 1572868
  12.4 12.6 %collective-permute-start.1 = (bf16[768,256]{1,0:T(8,128)(2,1)S(1)}, bf16[768,256]{1,0:T(8,128)(2,1)S(1)}, u32[]{:S(2)}, u32[]{:S(2)}) collective-permute-start(bf16[768,256]{1,0:T(8,128)(2,1)S(1)} %pad_maximum_fusion.shard_ref.rest_ref), channel_id=1, source_target_pairs={{0,12},{4,0},{8,4},{12,8},{1,13},{5,1},{9,5},{13,9},{2,14},{6,2},{... | collective-permute-start | bytes 1179656 | tf_op jit(solution)/shard_map/ppermute | solution.py:423
  16.1 13.2 %collective-permute-start.2 = (bf16[256,256]{1,0:T(8,128)(2,1)S(1)}, bf16[256,256]{1,0:T(8,128)(2,1)S(1)}, u32[]{:S(2)}, u32[]{:S(2)}) collective-permute-start(bf16[256,256]{1,0:T(8,128)(2,1)S(1)} %get-tuple-element.105), channel_id=1, source_target_pairs={{0,4},{4,8},{8,12},{12,0},{1,5},{5,9},{9,13},{13,1},{2,6},{6,10},{... | collective-permute-start | bytes 393224 | tf_op jit(solution)/shard_map/ppermute | solution.py:423
  16.2 13.1 %collective-permute-start.3 = (bf16[256,256]{1,0:T(8,128)(2,1)S(1)}, bf16[256,256]{1,0:T(8,128)(2,1)S(1)}, u32[]{:S(2)}, u32[]{:S(2)}) collective-permute-start(bf16[256,256]{1,0:T(8,128)(2,1)S(1)} %get-tuple-element.106), channel_id=1, source_target_pairs={{4,8},{8,12},{5,9},{9,13},{6,10},{10,14},{7,11},{11,15},{20,24},{2... | collective-permute-start | bytes 393224 | tf_op jit(solution)/shard_map/ppermute | solution.py:504
  16.9 13.5 %collective-permute-start.4 = (bf16[64,256]{1,0:T(8,128)(2,1)S(1)}, bf16[64,256]{1,0:T(8,128)(2,1)S(1)}, u32[]{:S(2)}, u32[]{:S(2)}) collective-permute-start(bf16[64,256]{1,0:T(8,128)(2,1)S(1)} %get-tuple-element.108), channel_id=1, source_target_pairs={{0,4},{12,0},{1,5},{13,1},{2,6},{14,2},{3,7},{15,3},{16,20},{28,16... | collective-permute-start | bytes 98312 | tf_op jit(solution)/shard_map/ppermute | solution.py:505
  22.8 8.7 %collective-permute-start.5 = (bf16[256,256]{1,0:T(8,128)(2,1)S(1)}, bf16[256,256]{1,0:T(8,128)(2,1)S(1)}, u32[]{:S(2)}, u32[]{:S(2)}) collective-permute-start(bf16[256,256]{1,0:T(8,128)(2,1)S(1)} %get-tuple-element.120), channel_id=1, source_target_pairs={{0,4},{4,8},{8,12},{12,0},{1,5},{5,9},{9,13},{13,1},{2,6},{6,10},{... | collective-permute-start | bytes 393224 | tf_op jit(solution)/shard_map/ppermute | solution.py:423

commit v24 on v23

--- a/solution.py
+++ b/solution.py
@@ -49,7 +49,7 @@
         second(block, current)
 
 
-def blocks_of(ref, groups=GROUP):
+def blocks_of(ref, groups=GROUP // 2):
     kv_local, _, rows = ref.shape
     width = groups * (rows // GROUP)
     return [(head, slice(start, start + width)) for head in range(kv_local) for start in range(0, rows, width)]

time: 32.9 us -> 33 us (level)
  Pallas kernels: 11.1 us -> 11.5 us
  transfers between devices with their start and end apart: 6 -> 6, of which waited for: 3 -> 3; matrix products, arithmetic and copies ran while one was open for 0% -> 0% of each run, Pallas kernels for 30% -> 32%
where the time goes in v24:
time: 33 us; the launch traced here: 32.7 us
  starting transfers between devices  11.9 us (36%)
  Pallas kernels  11.5 us (35%)
  waiting for transfers between devices  3.84 us (12%)
  local copies, waits for them, and re-layouts  3.1 us (9%)
  between operations  1.44 us (4%)
  other arithmetic  1.03 us (3%)
    ppermute x1, starting transfers between devices, per_device(): last_pages = lax.ppermute(pieces[3], 'ctx', others)  5.89 us
    ppermute x4, starting transfers between devices, send(): return lax.ppermute(array, 'ctx', up_pairs if hop < 0 else down_pairs)  5.29 us
    ppermute x4, waiting for transfers between devices, send(): return lax.ppermute(array, 'ctx', up_pairs if hop < 0 else down_pairs)  3.83 us
    unnamed x14, local copies, waits for them, and re-layouts  3.1 us
    pallas_call x2, Pallas kernels, per_device(): pl.pallas_call(functools.partial(hop_kernel, places), out_shape=state_sha...  3.05 us
    pallas_call x1, Pallas kernels, per_device(): pl.pallas_call(functools.partial(own_kernel, count, hops), out_shape=(sha...  2.07 us
    pallas_call x1, Pallas kernels, per_device(): pl.pallas_call(held_kernel, out_shape=(shape((heads * dec_rows, kv_width)...  1.86 us
    pallas_call x1, Pallas kernels, per_device(): pl.pallas_call(last_kernel, out_shape=shape((tokens, width), bf16), in_sp...  1.14 us
  transfers between devices with their start and end apart: 6, of which 3 were waited for; matrix products, arithmetic and copies ran while one was open for 0% of the time, Pallas kernels for 32%

profile of v24, /device:TPU:0, one launch (start us, length us, event | category | flops | bytes accessed | tf_op | source)
XLA Modules:
  0.0 32.7 jit_solution(1818503021531827223)
XLA Ops:
  0.6 1.0 %pad_maximum_fusion.shard_ref.rest_ref = bf16[768,256]{1,0:T(8,128)(2,1)S(1)} fusion(bf16[256,256]{1,0:T(8,128)(2,1)} %param.16, bf16[128,256]{1,0:T(8,128)(2,1)} %param.14, bf16[256,256]{1,0:T(8,128)(2,1)} %param.15, bf16[128,256]{1,0:T(8,128)(2,1)} %param.13), kind=kLoop, calls=%fused_computation | loop fusion | flops 1572864 | bytes 786432 | tf_op jit(solution)/shard_map/max | solution.py:438
  1.7 3.1 %collective-permute-start = (bf16[768,256]{1,0:T(8,128)(2,1)S(1)}, bf16[768,256]{1,0:T(8,128)(2,1)S(1)}, u32[]{:S(2)}, u32[]{:S(2)}) collective-permute-start(bf16[768,256]{1,0:T(8,128)(2,1)S(1)} %pad_maximum_fusion.shard_ref.rest_ref), channel_id=1, source_target_pairs={{0,4},{4,8},{8,12},{12,0},{1,5},{5,9},{9,13},{13,1},{2,6},{6,10},{... | collective-permute-start | bytes 1179656 | tf_op jit(solution)/shard_map/ppermute | solution.py:423
  5.4 0.0 copy-start.5
  5.5 0.6 %copy-done.4 = s32[32]{0:T(128)S(1)} copy-done((s32[32]{0:T(128)S(1)}, s32[32]{0:T(128)}, u32[]{:S(2)}) %copy-start.4) | copy-done | bytes 152
  6.1 0.0 copy-done.5
  6.1 1.2 %copy-done = bf16[128,16,256]{2,1,0:T(8,128)(2,1)S(1)} copy-done((bf16[128,16,256]{2,1,0:T(8,128)(2,1)S(1)}, bf16[128,16,256]{2,1,0:T(8,128)(2,1)}, u32[]{:S(2)}) %copy-start) | copy-done | bytes 1048600
  7.3 1.2 %copy-done.1 = bf16[128,16,256]{2,1,0:T(8,128)(2,1)S(1)} copy-done((bf16[128,16,256]{2,1,0:T(8,128)(2,1)S(1)}, bf16[128,16,256]{2,1,0:T(8,128)(2,1)}, u32[]{:S(2)}) %copy-start.1) | copy-done | bytes 1048600
  8.5 1.9 %decode_held_pages.1 = (bf16[128,256]{1,0:T(8,128)(2,1)S(1)}, f32[16,8,1]{2,1,0:T(8,128)S(1)}, f32[16,8,1]{2,1,0:T(8,128)S(1)}, f32[16,8,256]{2,1,0:T(8,128)S(1)}) custom-call(s32[1]{0:T(128)} %bitcast.own_ref, s32[32]{0:T(128)S(1)} %copy-done.4, s32[8]{0:T(128)S(1)} %copy-done.5, bf16[8,2048]{1,0:T(8,128)(2,1)S(1)} %copy-done.2, s32[8,32]{1,0:T(8,128)S(1)} %copy-done.3, ...), custom_call_target="tpu_custom_call" | custom-call | flops 268435456 | bytes 2097152 | tf_op jit(solution)/shard_map/decode_held_pages/pallas_call | solution.py:467
  10.4 2.1 %own_shard.1 = (bf16[2,256,1024]{2,1,0:T(8,128)(2,1)S(1)}, bf16[3,128,128]{2,1,0:T(8,128)(2,1)S(1)}, bf16[3,256,128]{2,1,0:T(8,128)(2,1)S(1)}, bf16[32,128]{1,0:...) custom-call(s32[1]{0:T(128)} %bitcast.own_ref, ...), custom_call_target="tpu_custom_call" | custom-call | flops 402653184 | bytes 1048576 | tf_op jit(solution)/shard_map/own_shard/pallas_call | solution.py:446
  12.5 2.1 %collective-permute-start.1 = (bf16[768,256]{1,0:T(8,128)(2,1)S(1)}, bf16[768,256]{1,0:T(8,128)(2,1)S(1)}, u32[]{:S(2)}, u32[]{:S(2)}) collective-permute-start(bf16[768,256]{1,0:T(8,128)(2,1)S(1)} %pad_maximum_fusion.shard_ref.rest_ref), channel_id=1, source_target_pairs={{0,12},{4,0},{8,4},{12,8},{1,13},{5,1},{9,5},{13,9},{2,14},{6,2},{... | collective-permute-start | bytes 1179656 | tf_op jit(solution)/shard_map/ppermute | solution.py:423
  14.6 1.4 %collective-permute-done.refs_0_.shard_ref = bf16[768,256]{1,0:T(8,128)(2,1)S(1)} collective-permute-done((bf16[768,256]{1,0:T(8,128)(2,1)S(1)}, bf16[768,256]{1,0:T(8,128)(2,1)S(1)}, u32[]{:S(2)}, u32[]{:S(2)}) %collective-permute-start) | collective-permute-done | bytes 393248 | tf_op jit(solution)/shard_map/ppermute | solution.py:423
  16.0 0.1 pieces_to_send_on.1
  16.1 0.1 collective-permute-start.2
  16.2 0.7 %collective-permute-start.3 = (bf16[256,256]{1,0:T(8,128)(2,1)S(1)}, bf16[256,256]{1,0:T(8,128)(2,1)S(1)}, u32[]{:S(2)}, u32[]{:S(2)}) collective-permute-start(bf16[256,256]{1,0:T(8,128)(2,1)S(1)} %get-tuple-element.106), channel_id=1, source_target_pairs={{4,8},{8,12},{5,9},{9,13},{6,10},{10,14},{7,11},{11,15},{20,24},{2... | collective-permute-start | bytes 393224 | tf_op jit(solution)/shard_map/ppermute | solution.py:504
  16.9 5.9 %collective-permute-start.4 = (bf16[64,256]{1,0:T(8,128)(2,1)S(1)}, bf16[64,256]{1,0:T(8,128)(2,1)S(1)}, u32[]{:S(2)}, u32[]{:S(2)}) collective-permute-start(bf16[64,256]{1,0:T(8,128)(2,1)S(1)} %get-tuple-element.108), channel_id=1, source_target_pairs={{0,4},{12,0},{1,5},{13,1},{2,6},{14,2},{3,7},{15,3},{16,20},{28,16... | collective-permute-start | bytes 98312 | tf_op jit(solution)/shard_map/ppermute | solution.py:505
  22.8 0.1 collective-permute-start.5
  22.8 1.5 %whole_shards_0.1 = (f32[2,1,1024]{2,1,0:T(1,128)S(1)}, f32[2,1,1024]{2,1,0:T(1,128)S(1)}, f32[2,128,1024]{2,1,0:T(8,128)S(1)}) custom-call(bf16[2,256,1024]{2,1,0:T(8,128)(2,1)S(1)} %get-tuple-element.62.qt_ref, bf16[3,128,128]{2,1,0:T(8,128)(2,1)S(1)} %get-tuple-element.63.near_ref, bf16[3,256,128]{2,1,0:T(8,128)(2,1)S(1)} %get-tuple-element.64.far_ref, ...), custom_call_target="tpu_custom_call" | custom-call | flops 402653184 | bytes 1048576 | tf_op jit(solution)/shard_map/whole_shards_0/pallas_call | solution.py:510
  24.4 0.6 %collective-permute-done.1.refs_0_.refs_1_ = bf16[768,256]{1,0:T(8,128)(2,1)S(1)} collective-permute-done((bf16[768,256]{1,0:T(8,128)(2,1)S(1)}, bf16[768,256]{1,0:T(8,128)(2,1)S(1)}, u32[]{:S(2)}, u32[]{:S(2)}) %collective-permute-start.1) | collective-permute-done | bytes 393248 | tf_op jit(solution)/shard_map/ppermute | solution.py:423
  24.9 1.5 %whole_shards_1.1 = (f32[2,1,1024]{2,1,0:T(1,128)S(1)}, f32[2,1,1024]{2,1,0:T(1,128)S(1)}, f32[2,128,1024]{2,1,0:T(8,128)S(1)}) custom-call(bf16[2,256,1024]{2,1,0:T(8,128)(2,1)S(1)} %get-tuple-element.62.qt_ref, bf16[3,128,128]{2,1,0:T(8,128)(2,1)S(1)} %get-tuple-element.63.near_ref, bf16[3,256,128]{2,1,0:T(8,128)(2,1)S(1)} %get-tuple-element.64.far_ref, ...), custom_call_target="tpu_custom_call" | custom-call | flops 402653184 | bytes 1048576 | tf_op jit(solution)/shard_map/whole_shards_1/pallas_call | solution.py:510
  26.5 1.1 %decode_near_pages.1 = (f32[16,8,1]{2,1,0:T(8,128)S(1)}, f32[16,8,1]{2,1,0:T(8,128)S(1)}, f32[16,8,256]{2,1,0:T(8,128)S(1)}, f32[1,8,128]{2,1,0:T(8,128)S(1)}) custom-call(s32[1]{0:T(128)} %bitcast.own_ref, s32[32]{0:T(128)S(1)} %copy-done.4, s32[8]{0:T(128)S(1)} %copy-done.5, s32[8,32]{1,0:T(8,128)S(1)} %copy-done.3, ...), custom_call_target="tpu_custom_call" | custom-call | flops 134217728 | bytes 1048576 | tf_op jit(solution)/shard_map/decode_near_pages/pallas_call | solution.py:523
  27.6 1.9 %collective-permute-done.2.keys_ref = bf16[256,256]{1,0:T(8,128)(2,1)S(1)} collective-permute-done((bf16[256,256]{1,0:T(8,128)(2,1)S(1)}, bf16[256,256]{1,0:T(8,128)(2,1)S(1)}, u32[]{:S(2)}, u32[]{:S(2)}) %collective-permute-start.2) | collective-permute-done | bytes 131104 | tf_op jit(solution)/shard_map/ppermute | solution.py:423
  29.4 1.0 %last_scores.1 = (bf16[2,256,1024]{2,1,0:T(8,128)(2,1)S(1)}, f32[2,1,1024]{2,1,0:T(1,128)S(1)}, f32[2,128,1024]{2,1,0:T(8,128)S(1)}) custom-call(bf16[2,256,1024]{2,1,0:T(8,128)(2,1)S(1)} %get-tuple-element.62.qt_ref, bf16[3,128,128]{2,1,0:T(8,128)(2,1)S(1)} %get-tuple-element.63.near_ref, bf16[3,256,128]{2,1,0:T(8,128)(2,1)S(1)} %get-tuple-element.64.far_ref, ...), custom_call_target="tpu_custom_call" | custom-call | flops 402653184 | bytes 1048576 | tf_op jit(solution)/shard_map/last_scores/pallas_call | solution.py:538
  30.5 1.1 %decode_last_pages.1 = bf16[8,2048]{1,0:T(8,128)(2,1)} custom-call(bf16[256,256]{1,0:T(8,128)(2,1)S(1)} %collective-permute-done.3.stretch_ref, bf16[64,256]{1,0:T(8,128)(2,1)S(1)} %collective-permute-done.4.pages_ref, f32[1,8,128]{2,1,0:T(8,128)S(1)} %get-tuple-element.109.tally_ref, bf16[128,256]{1,0:T(8,128)(2,1)S(1)} %get-tuple-element.79.refs_2_.wide_ref, ...), custom_call_target="tpu_custom_call" | custom-call | flops 67108864 | bytes 1048576 | tf_op jit(solution)/shard_map/decode_last_pages/pallas_call | solution.py:549
  31.6 1.1 %last_values.1 = bf16[128,2048]{1,0:T(8,128)(2,1)} custom-call(bf16[2,256,1024]{2,1,0:T(8,128)(2,1)S(1)} %get-tuple-element.107.weights_ref, f32[2,1,1024]{2,1,0:T(1,128)S(1)} %get-tuple-element.118.total_ref, f32[2,128,1024]{2,1,0:T(8,128)S(1)} %get-tuple-element.119.accum_ref, bf16[256,256]{1,0:T(8,128)(2,1)S(1)} %collective-permute-done.5.values_ref), custom_call_target="tpu_custom_call" | custom-call | flops 134217728 | bytes 1048576 | tf_op jit(solution)/shard_map/last_values/pallas_call | solution.py:560
  (12 shorter events, 0.0 us)
Async XLA Ops:
  0.6 4.8 %copy-start.2 = (bf16[8,2048]{1,0:T(8,128)(2,1)S(1)}, bf16[8,2048]{1,0:T(8,128)(2,1)}, u32[]{:S(2)}) copy-start(bf16[8,2048]{1,0:T(8,128)(2,1)} %q_ref.3) | copy-start | bytes 98308
  1.7 14.3 %collective-permute-start = (bf16[768,256]{1,0:T(8,128)(2,1)S(1)}, bf16[768,256]{1,0:T(8,128)(2,1)S(1)}, u32[]{:S(2)}, u32[]{:S(2)}) collective-permute-start(bf16[768,256]{1,0:T(8,128)(2,1)S(1)} %pad_maximum_fusion.shard_ref.rest_ref), channel_id=1, source_target_pairs={{0,4},{4,8},{8,12},{12,0},{1,5},{5,9},{9,13},{13,1},{2,6},{6,10},{... | collective-permute-start | bytes 1179656 | tf_op jit(solution)/shard_map/ppermute | solution.py:423
  4.8 0.7 %copy-start.3 = (s32[8,32]{1,0:T(8,128)S(1)}, s32[8,32]{1,0:T(8,128)}, u32[]{:S(2)}) copy-start(s32[8,32]{1,0:T(8,128)} %lists_ref.3) | copy-start | bytes 3076
  5.4 0.7 %copy-start.4 = (s32[32]{0:T(128)S(1)}, s32[32]{0:T(128)}, u32[]{:S(2)}) copy-start(s32[32]{0:T(128)} %targets_ref.5) | copy-start | bytes 388
  5.4 0.7 %copy-start.5 = (s32[8]{0:T(128)S(1)}, s32[8]{0:T(128)}, u32[]{:S(2)}) copy-start(s32[8]{0:T(128)} %length_ref.3) | copy-start | bytes 100
  6.1 1.2 %copy-start = (bf16[128,16,256]{2,1,0:T(8,128)(2,1)S(1)}, bf16[128,16,256]{2,1,0:T(8,128)(2,1)}, u32[]{:S(2)}) copy-start(bf16[128,16,256]{2,1,0:T(8,128)(2,1)} %pool_k.1) | copy-start | bytes 3145732
  7.3 1.2 %copy-start.1 = (bf16[128,16,256]{2,1,0:T(8,128)(2,1)S(1)}, bf16[128,16,256]{2,1,0:T(8,128)(2,1)}, u32[]{:S(2)}) copy-start(bf16[128,16,256]{2,1,0:T(8,128)(2,1)} %pool_v.1) | copy-start | bytes 3145732
  8.5 1.9 %copy-start.6 = (bf16[128,2048]{1,0:T(8,128)(2,1)S(1)}, bf16[128,2048]{1,0:T(8,128)(2,1)}, u32[]{:S(2)}) copy-start(bf16[128,2048]{1,0:T(8,128)(2,1)} %q_ref.2) | copy-start | bytes 1572868
  12.5 12.4 %collective-permute-start.1 = (bf16[768,256]{1,0:T(8,128)(2,1)S(1)}, bf16[768,256]{1,0:T(8,128)(2,1)S(1)}, u32[]{:S(2)}, u32[]{:S(2)}) collective-permute-start(bf16[768,256]{1,0:T(8,128)(2,1)S(1)} %pad_maximum_fusion.shard_ref.rest_ref), channel_id=1, source_target_pairs={{0,12},{4,0},{8,4},{12,8},{1,13},{5,1},{9,5},{13,9},{2,14},{6,2},{... | collective-permute-start | bytes 1179656 | tf_op jit(solution)/shard_map/ppermute | solution.py:423
  16.1 13.3 %collective-permute-start.2 = (bf16[256,256]{1,0:T(8,128)(2,1)S(1)}, bf16[256,256]{1,0:T(8,128)(2,1)S(1)}, u32[]{:S(2)}, u32[]{:S(2)}) collective-permute-start(bf16[256,256]{1,0:T(8,128)(2,1)S(1)} %get-tuple-element.105), channel_id=1, source_target_pairs={{0,4},{4,8},{8,12},{12,0},{1,5},{5,9},{9,13},{13,1},{2,6},{6,10},{... | collective-permute-start | bytes 393224 | tf_op jit(solution)/shard_map/ppermute | solution.py:423
  16.2 13.2 %collective-permute-start.3 = (bf16[256,256]{1,0:T(8,128)(2,1)S(1)}, bf16[256,256]{1,0:T(8,128)(2,1)S(1)}, u32[]{:S(2)}, u32[]{:S(2)}) collective-permute-start(bf16[256,256]{1,0:T(8,128)(2,1)S(1)} %get-tuple-element.106), channel_id=1, source_target_pairs={{4,8},{8,12},{5,9},{9,13},{6,10},{10,14},{7,11},{11,15},{20,24},{2... | collective-permute-start | bytes 393224 | tf_op jit(solution)/shard_map/ppermute | solution.py:504
  16.9 13.6 %collective-permute-start.4 = (bf16[64,256]{1,0:T(8,128)(2,1)S(1)}, bf16[64,256]{1,0:T(8,128)(2,1)S(1)}, u32[]{:S(2)}, u32[]{:S(2)}) collective-permute-start(bf16[64,256]{1,0:T(8,128)(2,1)S(1)} %get-tuple-element.108), channel_id=1, source_target_pairs={{0,4},{12,0},{1,5},{13,1},{2,6},{14,2},{3,7},{15,3},{16,20},{28,16... | collective-permute-start | bytes 98312 | tf_op jit(solution)/shard_map/ppermute | solution.py:505
  22.8 8.8 %collective-permute-start.5 = (bf16[256,256]{1,0:T(8,128)(2,1)S(1)}, bf16[256,256]{1,0:T(8,128)(2,1)S(1)}, u32[]{:S(2)}, u32[]{:S(2)}) collective-permute-start(bf16[256,256]{1,0:T(8,128)(2,1)S(1)} %get-tuple-element.120), channel_id=1, source_target_pairs={{0,4},{4,8},{8,12},{12,0},{1,5},{5,9},{9,13},{13,1},{2,6},{6,10},{... | collective-permute-start | bytes 393224 | tf_op jit(solution)/shard_map/ppermute | solution.py:423
